TPU v7x, 32 devices: a whole 2x2x4 slice. The times are simulated.
32 devices in a mesh: groups: 2 (over y), grid: 4 (over z), atoms: 4 (over x, core).
Axes of the slice: x: 2, y: 2, z: 4, core: 2. Of those that a mesh axis runs over, the one named last changes fastest.
Arguments:
- basis: bfloat16 [512, 128, 4, 128], P(('groups', 'grid', 'atoms')), parts along dimension 0, may hold values from -6 to 6
- basis_grad: bfloat16 [3, 512, 128, 4, 128], P(None, ('groups', 'grid', 'atoms')), parts along dimension 1, may hold values from -6 to 6
- exchange_field: bfloat16 [512, 128, 4, 128], P(('groups', 'grid', 'atoms')), parts along dimension 0, may hold values from -6 to 6
- weights: float32 [512, 128], P(('groups', 'grid', 'atoms')), parts along dimension 0, may hold values from 0.0005 to 0.02
- weight_grad: float32 [3, 512, 128], P(None, ('groups', 'grid', 'atoms')), parts along dimension 1, may hold values from -0.06 to 0.06
- density: bfloat16 [120, 3, 128, 128], P(('groups', 'grid')), parts along dimension 0, may hold values from -0.375 to 0.375
- region: int32 [8, 4], P('groups'), parts along dimension 0, may hold values from 0 to 59, as said below
- pattern: int32 [512, 4], P(('groups', 'grid', 'atoms')), parts along dimension 0, may hold values from 0 to 3, as said below
- fn_atom: int32 [15360], P('groups'), parts along dimension 0, may hold values from 0 to 767, never falling along the last dimension, each value on 1 to 18 neighbouring positions
- batch_atom: int32 [512], P(('groups', 'grid', 'atoms')), parts along dimension 0, may hold values from 0 to 767
Outputs:
- contracted: bfloat16 [512, 128, 4, 128], P(('groups', 'grid', 'atoms')), parts along dimension 0
- gradient: float32 [3, 1536], P(None, ('groups', 'atoms')), parts along dimension 1
There are 2 independent parts, one for each index of `groups`. A program takes and returns all parts, laid end to end along the dimension named above; each array names one. Nothing has to cross between parts.
Inputs may be any that keep to these rules, and one draw needn't show every extreme that they name: `region`: each row lists 4 increasing basis blocks; block r lies on grid index r // 15; at most 2 blocks of a row lie on one grid index, and in every row some grid index holds exactly 2; two blocks of a row on one grid index are consecutive blocks. `pattern`: each row names 4 different positions. `fn_atom`: never falls along the functions; each atom owns 1 to 18 consecutive functions.
All inputs are finite; a program needn't handle non-finite values.
Results may differ from a plain program's by a relative error of at most 0.008.
Values may be sent and summed in bfloat16 or wider, within the bound.
No kernel may reach another device: no remote copies, remote signals or barrier semaphores. Data moves between devices by JAX's collectives and lax.ppermute only.
A program may use at most 128 MiB of HBM per device.

v0:
```python
import jax
import jax.numpy as jnp
from jax import lax
from jax.sharding import PartitionSpec as P

CAP = 2


def region_slots(owners):
    region_size = owners.shape[1]
    same_owner = owners[:, :, None] == owners[:, None, :]
    before = jnp.arange(region_size)[None, :] < jnp.arange(region_size)[:, None]
    return jnp.sum(jnp.logical_and(same_owner, before[None]), axis=2)


def atom_sum(values, atom_ids, atom_total):
    return jax.ops.segment_sum(values, atom_ids, atom_total)


def local(
    basis,
    basis_grad,
    exchange_field,
    weights,
    weight_grad,
    density,
    region,
    pattern,
    fn_atom,
    batch_atom,
):
    blocks_here = density.shape[0]
    band_width = density.shape[1]
    half_band = (band_width - 1) // 2
    block_size = density.shape[2]
    region_size = region.shape[1]
    grid_here = lax.axis_index("grid")
    grid_count = lax.axis_size("grid")
    atom_devices = lax.axis_size("atoms")
    owners = region // blocks_here
    local_rows = region - grid_here * blocks_here
    owned_here = owners == grid_here
    positions = jnp.arange(region_size)
    nothing = jnp.zeros((), density.dtype)
    slot_index = region_slots(owners)
    chosen = jnp.logical_and(
        owned_here[:, None, :], slot_index[:, None, :] == jnp.arange(CAP)[None, :, None]
    )
    present = jnp.any(chosen, axis=2)
    source = jnp.sum(jnp.where(chosen, local_rows[:, None, :], 0), axis=2)
    outgoing = jnp.where(present[:, :, None, None, None], density[source], nothing)
    arrived = lax.all_to_all(outgoing, "grid", split_axis=0, concat_axis=0, tiled=True)
    held_rows = arrived[owners[grid_here], slot_index[grid_here]]
    block_rows = region[grid_here][pattern]
    density_tiles = held_rows[positions[pattern]]
    offsets = jnp.arange(band_width) - half_band
    matches = block_rows[:, None, :, None] == block_rows[:, :, None, None] + offsets
    spread = jnp.einsum(
        "bgsm,bskmn->bgskn", basis, density_tiles, preferred_element_type=jnp.float32
    )
    product = jnp.einsum("bgskn,bstk->bgtn", spread, matches.astype(jnp.float32))
    energy = jnp.sum(product * exchange_field.astype(jnp.float32), axis=(2, 3))
    picked = jnp.einsum(
        "bgtn,bstk->bgskn",
        exchange_field,
        matches.astype(jnp.bfloat16),
        preferred_element_type=jnp.float32,
    ).astype(jnp.bfloat16)
    potential = jnp.einsum(
        "bgskn,bskmn->bgsm", picked, density_tiles, preferred_element_type=jnp.float32
    )
    scaled = weights[:, :, None, None] * potential
    contribution = jnp.sum(basis_grad.astype(jnp.float32) * scaled[None], axis=2)
    weight_term = jnp.sum(weight_grad * energy[None], axis=2)
    atom_ids = fn_atom.reshape(-1, block_size)[block_rows].reshape(-1)
    atom_total = fn_atom.shape[0] // (10 * grid_count * atom_devices) * grid_count * atom_devices
    derivative_part = jax.vmap(atom_sum, in_axes=(0, None, None))(
        contribution.reshape(3, -1), atom_ids, atom_total
    )
    weight_part = jax.vmap(atom_sum, in_axes=(0, None, None))(weight_term, batch_atom, atom_total)
    partial_grad = -2.0 * derivative_part + weight_part
    reduced = lax.psum_scatter(partial_grad, "atoms", scatter_dimension=1, tiled=True)
    gradient = lax.psum(reduced, "grid")
    return (product.astype(jnp.bfloat16), gradient)


def solution(mesh):
    placed = (
        P(("groups", "grid", "atoms"), None, None, None),
        P(None, ("groups", "grid", "atoms"), None, None, None),
        P(("groups", "grid", "atoms"), None, None, None),
        P(("groups", "grid", "atoms"), None),
        P(None, ("groups", "grid", "atoms"), None),
        P(("groups", "grid"), None, None, None),
        P("groups", None),
        P(("groups", "grid", "atoms"), None),
        P("groups"),
        P(("groups", "grid", "atoms")),
    )
    return jax.shard_map(
        local,
        mesh=mesh,
        in_specs=placed,
        out_specs=(P(("groups", "grid", "atoms"), None, None, None), P(None, ("groups", "atoms"))),
        check_vma=False,
    )
```

profile of v0, /device:TPU:0, one launch (start us, length us, event | category | flops | bytes accessed | tf_op | source)
XLA Modules:
  0.0 202.1 jit_solution(14489054648999043945)
XLA Ops:
  7.2 0.0 copy-start
  7.2 0.0 copy-start.6
  7.2 0.8 broadcast_compare_fusion
  8.0 0.7 broadcast_subtract_fusion
  8.7 0.2 convert_reduce_fusion
  8.9 0.2 fusion.16
  9.1 0.2 select_reduce_fusion
  9.3 0.1 copy.33
  9.4 0.1 reshape.150
  9.5 0.1 copy.32
  9.6 2.1 %gather_fusion.1 = bf16[8,3,128,128]{3,2,1,0:T(8,128)(2,1)S(1)} fusion(bf16[15,3,128,128]{3,2,1,0:T(8,128)(2,1)} %param.15, s32[1024]{0:T(1024)S(1)} %pad_clamp_fusion.2), kind=kCustom, calls=%fused_computation.1 | custom fusion | bytes 1572896 | tf_op jit(solution)/shard_map/gather | solution.py:51
  11.6 1.0 broadcast_select_fusion
  12.7 6.3 %all-to-all-start = ((bf16[4,2,3,128,128]{4,3,2,1,0:T(8,128)(2,1)}), bf16[4,2,3,128,128]{4,3,2,1,0:T(8,128)(2,1)S(1)}, u32[]{:S(2)}, u32[]{:S(2)}) async-start(bf16[4,2,3,128,128]{4,3,2,1,0:T(8,128)(2,1)} %broadcast_select_fusion), calls=%async_computation | async-start | bytes 1572864 | tf_op jit(solution)/shard_map/all_to_all | solution.py:52
  19.0 0.0 reduce-scatter.2.cloned.1.call-start
  19.0 0.0 copy-done.6
  19.0 0.1 copy.31
  19.1 0.1 reshape.142
  19.2 0.8 gather_fusion.3
  20.0 0.1 gather.26
  20.1 0.7 fusion.18
  20.7 0.0 copy-start.2
  20.7 0.8 gather_fusion
  21.5 0.1 gather.28
  21.6 0.1 reshape.141
  21.7 0.1 reshape.172
  21.8 0.1 reshape.180
  21.9 0.0 copy-done.2
  21.9 0.6 gather_fusion.5
  22.6 0.1 broadcast_add_fusion
  22.6 6.6 %convert_bitcast_fusion = bf16[16,128,4,3,128]{4,2,1,3,0:T(4,128)(2,1)} fusion(bf16[16,128,4,128]{3,2,1,0:T(4,128)(2,1)} %param.12, s32[16,4,3]{1,2,0:T(4,128)S(1)} %broadcast_add_fusion, s32[16,4]{1,0:T(8,128)S(1)} %reshape.141), kind=kOutput, calls=%fused_computation.11 | convolution fusion | flops 28312320 | bytes 8389632 | tf_op jit(solution)/shard_map/bgtn,bstk->bgskn/dot_general | solution.py:63
  29.3 9.8 %all-to-all-done = bf16[4,2,3,128,128]{4,3,2,1,0:T(8,128)(2,1)S(1)} async-done(((bf16[4,2,3,128,128]{4,3,2,1,0:T(8,128)(2,1)}), bf16[4,2,3,128,128]{4,3,2,1,0:T(8,128)(2,1)S(1)}, u32[]{:S(2)}, u32[]{:S(2)}) %all-to-all-start) | async-done | bytes 786464 | tf_op jit(solution)/shard_map/all_to_all | solution.py:52
  39.1 0.6 gather_fusion.2
  39.7 0.0 copy-start.5
  39.7 4.0 %gather_fusion.4 = bf16[64,3,128,128]{3,2,1,0:T(8,128)(2,1)} fusion(bf16[4,3,128,128]{3,2,1,0:T(8,128)(2,1)S(1)} %gather_fusion.2, s32[1024]{0:T(1024)S(1)} %pad_clamp_fusion.1), kind=kCustom, calls=%fused_computation.4 | custom fusion | bytes 12583168 | tf_op jit(solution)/shard_map/gather | solution.py:55
  43.7 0.0 copy-done.5
  43.7 9.3 %fusion.3 = f32[16,128,4,128]{1,3,2,0:T(8,128)} fusion(bf16[16,4,3,128,128]{4,3,2,1,0:T(8,128)(2,1)} %bitcast.73, bf16[16,128,4,3,128]{4,2,1,3,0:T(4,128)(2,1)} %convert_bitcast_fusion, f32[16,128]{1,0:T(8,128)S(1)} %copy-done.5), kind=kOutput, calls=%fused_computation.17 | convolution fusion | flops 806354944 | bytes 16785408 | tf_op jit(solution)/shard_map/bgskn,bskmn->bgsm/dot_general | solution.py:69
  53.0 5.3 %copy.39 = f32[16,128,4,128]{3,2,1,0:T(4,128)} copy(f32[16,128,4,128]{1,3,2,0:T(8,128)} %fusion.3) | data formatting | bytes 8388608 | tf_op jit(solution)/shard_map/mul | solution.py:72
  58.3 7.4 %multiply_reduce_fusion = f32[3,16,4,128]{3,2,1,0:T(4,128)S(1)} fusion(bf16[3,16,128,4,128]{4,3,2,1,0:T(4,128)(2,1)} %param.11, f32[16,128,4,128]{3,2,1,0:T(4,128)} %copy.39), kind=kLoop, calls=%fused_computation.8 | loop fusion | flops 9412608 | bytes 10584064 | tf_op jit(solution)/shard_map/reduce_sum | solution.py:73
  65.7 2.7 %copy.54 = f32[3,16,4,128]{0,3,2,1:T(8,128)} copy(f32[3,16,4,128]{3,2,1,0:T(4,128)S(1)} %multiply_reduce_fusion) | data formatting | bytes 196608 | tf_op jit(solution)/shard_map/reshape | solution.py:78
  68.4 53.5 %scatter_custom_fusion = f32[3,768]{0,1:T(8,128)S(1)} fusion(s32[8192]{0:T(1024)S(1)} %bitcast.78, f32[8192,3]{1,0:T(8,128)} %bitcast.75, f32[]{:T(128)} %constant.10.clone.1), kind=kCustom, calls=%fused_computation.22 | custom fusion | flops 24576 | bytes 9728 | tf_op jit(solution)/shard_map/vmap()/scatter-add | solution.py:17
  122.0 0.0 copy-done
  122.0 7.4 %convolution_bitcast_fusion = bf16[16,128,4,3,128]{1,4,3,2,0:T(8,128)(2,1)} fusion(bf16[16,4,3,128,128]{4,3,2,1,0:T(8,128)(2,1)} %bitcast.74, bf16[16,128,4,128,1]{3,2,1,0,4:T(4,128)(2,1)S(1)} %bitcast.72), kind=kOutput, calls=%fused_computation.12 | convolution fusion | flops 805306368 | bytes 14680064 | tf_op jit(solution)/shard_map/bgsm,bskmn->bgskn/dot_general | solution.py:58
  129.4 10.7 %copy.37 = bf16[16,128,4,3,128]{4,2,3,1,0:T(4,128)(2,1)} copy(bf16[16,128,4,3,128]{1,4,3,2,0:T(8,128)(2,1)} %convolution_bitcast_fusion) | data formatting | bytes 12582912 | tf_op jit(solution)/shard_map/bgsm,bskmn->bgskn/transpose | solution.py:58
  140.0 0.0 copy-start.1
  140.0 7.8 %bitcast_convert_fusion = (bf16[16,128,4,128]{3,2,1,0:T(4,128)(2,1)}, f32[16,4,128,128,1]{3,1,4,2,0:T(4,128)S(1)}) fusion(bf16[16,128,4,3,128]{4,2,3,1,0:T(4,128)(2,1)} %copy.37, s32[16,4,3]{1,2,0:T(4,128)S(1)} %broadcast_add_fusion, s32[16,4]{1,0:T(8,128)S(1)} %reshape.141), kind=kOutput, calls=%fused_computation.14 | convolution fusion | flops 26215168 | bytes 12583936 | tf_op jit(solution)/shard_map/bgskn,bstk->bgtn/dot_general | solution.py:61
  147.8 0.0 copy-start.4
  147.8 0.0 copy-start.7
  147.8 0.0 copy-done.1
  147.8 4.4 %fusion.2 = f32[16,128]{1,0:T(8,128)S(1)} fusion(f32[16,4,128,128,1]{3,1,4,2,0:T(4,128)S(1)} %get-tuple-element.13, bf16[16,128,4,128]{3,2,1,0:T(4,128)(2,1)S(1)} %copy-done.1), kind=kLoop, calls=%fused_computation.15 | loop fusion | flops 3143680 | bytes 6299648 | tf_op jit(solution)/shard_map/reduce_sum | solution.py:62
  152.3 0.0 copy-done.4
  152.3 0.1 multiply_reduce_fusion.1
  152.4 0.1 copy.41
  152.5 0.0 copy-done.7
  152.5 0.8 scatter_fusion
  153.3 0.0 copy-start.3
  153.3 0.7 copy-done.3
  154.0 0.0 reduce-scatter.2.cloned.1.call-update
  154.1 19.6 %reduce-scatter.2.cloned.1.call-done = f32[3,192]{0,1:T(8,128)} async-done(((f32[3,768]{0,1:T(8,128)}), f32[3,192]{0,1:T(8,128)}) %reduce-scatter.2.cloned.1.call-update) | async-done | bytes 2320 | tf_op jit(solution)/shard_map/reduce_scatter | solution.py:82
  173.7 20.9 %psum.7 = f32[3,192]{0,1:T(8,128)S(1)} all-reduce(f32[3,192]{0,1:T(8,128)} %reduce-scatter.2.cloned.1.call-done), channel_id=1, replica_groups=mesh['groups'=2,'grid'=4,'atoms'=4] {'grid'}, use_global_device_ids=true, to_apply=%region_9.10 | all-reduce | flops 576 | bytes 4608 | tf_op jit(solution)/shard_map/psum | solution.py:83
  194.6 0.7 copy.42
  (12 shorter events, 0.1 us)
Async XLA Ops:
  7.2 114.8 %copy-start = (bf16[16,128,4,128]{3,2,1,0:T(4,128)(2,1)S(1)}, bf16[16,128,4,128]{3,2,1,0:T(4,128)(2,1)}, u32[]{:S(2)}) copy-start(bf16[16,128,4,128]{3,2,1,0:T(4,128)(2,1)} %param.10) | copy-start | bytes 6291460
  7.2 11.8 %copy-start.6 = (s32[16,4]{0,1:T(4,128)S(1)}, s32[16,4]{0,1:T(4,128)}, u32[]{:S(2)}) copy-start(s32[16,4]{0,1:T(4,128)} %param.17) | copy-start | bytes 772
  12.7 26.4 %all-to-all-start = ((bf16[4,2,3,128,128]{4,3,2,1,0:T(8,128)(2,1)}), bf16[4,2,3,128,128]{4,3,2,1,0:T(8,128)(2,1)S(1)}, u32[]{:S(2)}, u32[]{:S(2)}) async-start(bf16[4,2,3,128,128]{4,3,2,1,0:T(8,128)(2,1)} %broadcast_select_fusion), calls=%async_computation | async-start | bytes 1572864 | tf_op jit(solution)/shard_map/all_to_all | solution.py:52
  19.0 154.7 %reduce-scatter.2.cloned.1.call-start = ((), (), s32[]{:S(2)}) async-start(), calls=%async_computation.2 | async-start | bytes 491520 | tf_op jit(solution)/shard_map/reduce_scatter | solution.py:82
  20.7 1.2 copy-start.2
  39.7 4.0 %copy-start.5 = (f32[16,128]{1,0:T(8,128)S(1)}, f32[16,128]{1,0:T(8,128)}, u32[]{:S(2)}) copy-start(f32[16,128]{1,0:T(8,128)} %param.13) | copy-start | bytes 24580
  140.0 7.8 %copy-start.1 = (bf16[16,128,4,128]{3,2,1,0:T(4,128)(2,1)S(1)}, bf16[16,128,4,128]{3,2,1,0:T(4,128)(2,1)}, u32[]{:S(2)}) copy-start(bf16[16,128,4,128]{3,2,1,0:T(4,128)(2,1)} %param.12) | copy-start | bytes 6291460
  147.8 4.4 %copy-start.4 = (f32[3,16,128]{2,1,0:T(8,128)S(1)}, f32[3,16,128]{2,1,0:T(8,128)}, u32[]{:S(2)}) copy-start(f32[3,16,128]{2,1,0:T(8,128)} %param.14) | copy-start | bytes 73732
  147.8 4.6 %copy-start.7 = (s32[16]{0:T(128)S(1)}, s32[16]{0:T(128)}, u32[]{:S(2)}) copy-start(s32[16]{0:T(128)} %param.19) | copy-start | bytes 196
  153.3 0.7 copy-start.3
Sparse Core Ops, SparseCore 0:
  154.2 19.4 reduce-scatter.1
where the time goes:
time: 203 us; the launch traced here: 202 us
  other arithmetic  69.5 us (34%)
  matrix products  31.1 us (15%)
  local copies, waits for them, and re-layouts  30.6 us (15%)
  waiting for transfers between devices  29.5 us (15%)
  blocking collectives  20.9 us (10%)
  between operations  14.2 us (7%)
  starting transfers between devices  6.32 us (3%)
    scatter-add x2, other arithmetic, atom_sum(): return jax.ops.segment_sum(values, atom_ids, atom_total)  54.3 us
    psum x1, blocking collectives, local(): gradient = lax.psum(reduced, 'grid')  20.9 us
    reduce_scatter x1, waiting for transfers between devices, local(): lax.psum_scatter(partial_grad, 'atoms', scatter_dimension=1, tiled=True)  19.6 us
    transpose x1, local copies, waits for them, and re-layouts, local(): jnp.einsum('bgsm,bskmn->bgskn', basis, density_tiles, preferred_element_t...  10.7 us
    all_to_all x1, waiting for transfers between devices, local(): lax.all_to_all(outgoing, 'grid', split_axis=0, concat_axis=0, tiled=True)  9.8 us
    dot_general x1, matrix products, local(): jnp.einsum('bgskn,bskmn->bgsm', picked, density_tiles, preferred_element_...  9.28 us
    dot_general x1, matrix products, local(): jnp.einsum('bgskn,bstk->bgtn', spread, matches.astype(jnp.float32))  7.79 us
    reduce_sum x1, other arithmetic, local(): jnp.sum(basis_grad.astype(jnp.float32) * scaled[None], axis=2)  7.4 us
  transfers between devices with their start and end apart: 2, of which 2 were waited for; matrix products, arithmetic and copies ran while one was open for 5% of the time, Pallas kernels for 0%

commit v1 on v0

v1 whole, which is shorter than its diff:
```python
import functools

import jax
import jax.numpy as jnp
from jax import lax
from jax.experimental import pallas as pl
from jax.experimental.pallas import tpu as pltpu
from jax.sharding import PartitionSpec as P

CAP = 2
PARTS = 3
F32 = jnp.float32
BF16 = jnp.bfloat16
NT = (((1,), (1,)), ((), ()))
VMEM_LIMIT = 32 * 1024 * 1024


def owner_and_slot(region, slab, position, owner_rows):
    row = region[slab, position]
    owner = lax.div(row, owner_rows)
    slot = jnp.int32(0)
    for earlier in range(position):
        same = lax.div(region[slab, earlier], owner_rows) == owner
        slot = slot + jnp.where(same, 1, 0)
    return owner, slot


def pick_kernel(region, density, out, sems, *, owner_rows, quarter):
    me = lax.axis_index("grid")
    part = lax.axis_index("atoms")
    slabs, size = region.shape
    first = pl.multiple_of(part * quarter, quarter)

    def copies(slab):
        found = []
        for position in range(size):
            owner, slot = owner_and_slot(region, slab, position, owner_rows)
            mine = owner == me
            local_row = jnp.where(mine, region[slab, position] - me * owner_rows, 0)
            copy = pltpu.make_async_copy(
                density.at[local_row, :, pl.ds(first, quarter), :],
                out.at[slab, jnp.minimum(slot, CAP - 1)],
                sems.at[slab, position],
            )
            found.append((mine, copy))
        return found

    @pl.loop(0, slabs)
    def _(slab):
        for mine, copy in copies(slab):
            pl.when(mine)(copy.start)

    @pl.loop(0, slabs)
    def _(slab):
        for mine, copy in copies(slab):
            pl.when(mine)(copy.wait)


def pick_rows(region, density, slabs, atom_devices):
    owner_rows, width, size, _ = density.shape
    quarter = size // atom_devices
    return pl.pallas_call(
        functools.partial(pick_kernel, owner_rows=owner_rows, quarter=quarter),
        out_shape=jax.ShapeDtypeStruct((slabs, CAP, width, quarter, size), density.dtype),
        in_specs=[pl.BlockSpec(memory_space=pltpu.SMEM), pl.BlockSpec(memory_space=pl.ANY)],
        out_specs=pl.BlockSpec(memory_space=pltpu.VMEM),
        scratch_shapes=[pltpu.SemaphoreType.DMA(region.shape)],
        compiler_params=pltpu.CompilerParams(vmem_limit_bytes=VMEM_LIMIT),
    )(region, density)


def block_major(x_ref, wide, points, blocks):
    wide[...] = x_ref[0].astype(F32)
    return [wide[pl.ds(s, points, stride=blocks), :] for s in range(blocks)]


def relayout_kernel(basis, field, basis_out, field_out, wide, *, points, blocks):
    size = basis.shape[-1]
    for source, target in ((basis, basis_out), (field, field_out)):
        for s, part in enumerate(block_major(source, wide, points, blocks)):
            target[0, :, s * size : (s + 1) * size] = part.astype(BF16)


def relayout(basis, field, points, blocks):
    batches, rows, size = basis.shape
    here = pl.BlockSpec((1, rows, size), lambda b: (b, 0, 0))
    there = pl.BlockSpec((1, points, blocks * size), lambda b: (b, 0, 0))
    shape = jax.ShapeDtypeStruct((batches, points, blocks * size), BF16)
    return pl.pallas_call(
        functools.partial(relayout_kernel, points=points, blocks=blocks),
        grid=(batches,),
        out_shape=(shape, shape),
        in_specs=[here, here],
        out_specs=(there, there),
        scratch_shapes=[pltpu.VMEM((rows, size), F32)],
        compiler_params=pltpu.CompilerParams(vmem_limit_bytes=VMEM_LIMIT),
        cost_estimate=pl.CostEstimate(flops=0, bytes_accessed=8 * batches * rows * size, transcendentals=0),
    )(basis, field)


def batch_matrix(region, pattern, tiles, slab, batch, blocks, width):
    half = (width - 1) // 2
    none = tiles.shape[0] - 1
    places = [pattern[batch, s] for s in range(blocks)]
    rows = [region[slab, place] for place in places]
    strips = []
    for s in range(blocks):
        strip = []
        for t in range(blocks):
            k = rows[t] - rows[s] + half
            inside = jnp.logical_and(k >= 0, k < width)
            strip.append(tiles[jnp.where(inside, places[s] * width + k, none)])
        strips.append(jnp.concatenate(strip, axis=1))
    return jnp.concatenate(strips, axis=0)


def split(values):
    high = values.astype(BF16)
    rest = values - high.astype(F32)
    middle = rest.astype(BF16)
    low = (rest - middle.astype(F32)).astype(BF16)
    return high, middle, low


def gradient_kernel(
    region,
    pattern,
    basis,
    field,
    basis_grad,
    weights,
    weight_grad,
    fn_atom,
    batch_atom,
    places,
    *rest,
    points,
    blocks,
    width,
    owner_rows,
    slabs,
):
    *pieces, tiles, out, spread, sums, energy_sums = rest
    batch = pl.program_id(0)
    batches = pl.num_programs(0)
    me = lax.axis_index("grid")
    part = lax.axis_index("atoms")
    size = tiles.shape[-1]
    quarter = pieces[0].shape[-2]
    region_size = region.shape[1]

    @pl.when(batch == 0)
    def _():
        tiles[region_size * width] = jnp.zeros((size, size), BF16)
        for position in range(region_size):
            owner, slot = owner_and_slot(region, me, position, owner_rows)
            for step, piece in enumerate(pieces):
                first = pl.multiple_of(jnp.bitwise_xor(part, step) * quarter, quarter)
                for k in range(width):
                    tiles[position * width + k, pl.ds(first, quarter), :] = piece[owner, slot, k]

    matrix = batch_matrix(region, pattern, tiles, me, batch, blocks, width)
    potential = lax.dot_general(field[0], matrix, NT, preferred_element_type=F32)
    rows = jnp.concatenate(
        [weights[pl.ds(batch, 1), :]]
        + [weight_grad[c, pl.ds(batch, 1), :] for c in range(PARTS)]
        + [jnp.zeros((8 - 1 - PARTS, points), F32)],
        axis=0,
    )
    columns = rows.T
    weight = columns[:, 0:1]
    energy = jnp.zeros((points, size), F32)
    for s in range(blocks):
        here = potential[:, s * size : (s + 1) * size]
        energy = energy + basis[0, :, s * size : (s + 1) * size].astype(F32) * here
        spread[pl.ds(s, points, stride=blocks), :] = here * weight
    scaled = spread[...]
    place = pl.ds(pl.multiple_of(batch * 8, 8), 8)
    for c in range(PARTS):
        terms = basis_grad[c, 0].astype(F32) * scaled
        sums[c, place, :] = jnp.sum(terms.reshape(-1, 8, size), axis=0)
        terms = energy * columns[:, 1 + c : 2 + c]
        energy_sums[c, place, :] = jnp.sum(terms.reshape(-1, 8, size), axis=0)

    @pl.when(batch == batches - 1)
    def _():
        padded = max(8, region_size)
        chosen = lax.broadcasted_iota(jnp.int32, (padded, places.shape[1]), 0) == places[...]
        chosen = chosen.astype(BF16)
        blocks_sum = []
        for c in range(PARTS):
            total = jnp.zeros((padded, size), F32)
            for piece in split(sums[c]):
                total = total + jnp.dot(chosen, piece, preferred_element_type=F32)
            blocks_sum.append(-2.0 * total)
        lefts = []
        for position in range(region_size):
            stack = jnp.concatenate([total[position : position + 1] for total in blocks_sum], axis=0)
            high, middle, low = (piece.astype(F32) for piece in split(stack))
            lefts.append(jnp.concatenate([high, middle, low, jnp.zeros((16 - 3 * PARTS, size), F32)], axis=0))
        left = jnp.concatenate(lefts, axis=1).astype(BF16)
        chunk = out.shape[-1]
        scale = [jnp.sum(energy_sums[c], axis=1, keepdims=True) for c in range(PARTS)]
        for device in range(out.shape[1]):
            atoms = lax.broadcasted_iota(jnp.int32, (chunk, size), 0) + device * chunk
            hot = [
                jnp.where(atoms == fn_atom[pl.ds(region[me, position], 1), :], 1.0, 0.0).astype(BF16)
                for position in range(region_size)
            ]
            found = lax.dot_general(left, jnp.concatenate(hot, axis=1), NT, preferred_element_type=F32)
            atoms = lax.broadcasted_iota(jnp.int32, (batch_atom.shape[0], chunk), 1) + device * chunk
            mine = atoms == batch_atom[...]
            for c in range(PARTS):
                value = found[c : c + 1] + found[PARTS + c : PARTS + c + 1] + found[2 * PARTS + c : 2 * PARTS + c + 1]
                value = value + jnp.sum(jnp.where(mine, scale[c], 0.0), axis=0, keepdims=True)
                for slab in range(slabs):
                    out[slab, device, c : c + 1, :] = value


def partial_gradient(
    region, pattern, basis, field, basis_grad, weights, weight_grad, fn_atom, batch_atom, pieces, shapes
):
    slabs, atom_devices, atom_total, points, blocks, width, owner_rows = shapes
    batches, _, columns = basis.shape
    size = columns // blocks
    region_size = region.shape[1]
    fn_atom = fn_atom.reshape(-1, size)
    places = jnp.broadcast_to(pattern[:, None, :], (batches, 8 // blocks, blocks)).reshape(1, -1)
    batch_atom = jnp.broadcast_to(batch_atom[:, None], (batches, 8)).reshape(-1, 1)
    block = pl.BlockSpec((1, points, columns), lambda b, *_: (b, 0, 0))
    whole = pl.BlockSpec(memory_space=pltpu.VMEM)
    tile_shape = (region_size * width + 1, size, size)
    out_shape = (slabs, atom_devices, PARTS, atom_total // atom_devices)
    return pl.pallas_call(
        functools.partial(
            gradient_kernel, points=points, blocks=blocks, width=width, owner_rows=owner_rows, slabs=slabs
        ),
        grid_spec=pltpu.PrefetchScalarGridSpec(
            num_scalar_prefetch=2,
            grid=(batches,),
            in_specs=[
                block,
                block,
                pl.BlockSpec((PARTS, 1, points * blocks, size), lambda b, *_: (0, b, 0, 0)),
            ]
            + [whole] * (5 + len(pieces)),
            out_specs=(whole, whole),
            scratch_shapes=[
                pltpu.VMEM((points * blocks, size), F32),
                pltpu.VMEM((PARTS, batches * 8, size), F32),
                pltpu.VMEM((PARTS, batches * 8, size), F32),
            ],
        ),
        out_shape=(jax.ShapeDtypeStruct(tile_shape, BF16), jax.ShapeDtypeStruct(out_shape, F32)),
        compiler_params=pltpu.CompilerParams(vmem_limit_bytes=VMEM_LIMIT),
    )(region, pattern, basis, field, basis_grad, weights, weight_grad, fn_atom, batch_atom, places, *pieces)


def product_kernel(region, pattern, basis, tiles, out, spread, *, points, blocks, width):
    me = lax.axis_index("grid")
    size = tiles.shape[-1]
    matrix = batch_matrix(region, pattern, tiles, me, pl.program_id(0), blocks, width)
    product = jnp.dot(basis[0], matrix, preferred_element_type=F32)
    for t in range(blocks):
        spread[pl.ds(t, points, stride=blocks), :] = product[:, t * size : (t + 1) * size]
    out[0] = spread[...].astype(BF16)


def contract(region, pattern, basis, tiles, points, blocks, width):
    batches, _, columns = basis.shape
    size = columns // blocks
    return pl.pallas_call(
        functools.partial(product_kernel, points=points, blocks=blocks, width=width),
        grid_spec=pltpu.PrefetchScalarGridSpec(
            num_scalar_prefetch=2,
            grid=(batches,),
            in_specs=[
                pl.BlockSpec((1, points, columns), lambda b, *_: (b, 0, 0)),
                pl.BlockSpec(memory_space=pltpu.VMEM),
            ],
            out_specs=pl.BlockSpec((1, points * blocks, size), lambda b, *_: (b, 0, 0)),
            scratch_shapes=[pltpu.VMEM((points * blocks, size), F32)],
        ),
        out_shape=jax.ShapeDtypeStruct((batches, points * blocks, size), BF16),
        compiler_params=pltpu.CompilerParams(vmem_limit_bytes=VMEM_LIMIT),
        cost_estimate=pl.CostEstimate(
            flops=2 * batches * points * columns * columns,
            bytes_accessed=4 * batches * points * columns,
            transcendentals=0,
        ),
    )(region, pattern, basis, tiles)


def gather_atoms(piece, atom_devices):
    pieces = {0: piece}
    bit = atom_devices // 2
    while bit:
        swap = [(i, i ^ bit) for i in range(atom_devices)]
        for step in list(pieces):
            pieces[step ^ bit] = lax.ppermute(pieces[step], "atoms", swap)
        bit //= 2
    return [pieces[step] for step in range(atom_devices)]


def local(
    basis,
    basis_grad,
    exchange_field,
    weights,
    weight_grad,
    density,
    region,
    pattern,
    fn_atom,
    batch_atom,
):
    batches, points, blocks, size = basis.shape
    owner_rows, width = density.shape[:2]
    slabs = lax.axis_size("grid")
    atom_devices = lax.axis_size("atoms")
    atom_total = fn_atom.shape[0] // (10 * slabs * atom_devices) * slabs * atom_devices
    outgoing = pick_rows(region, density, slabs, atom_devices)
    arrived = lax.all_to_all(outgoing, "grid", split_axis=0, concat_axis=0, tiled=True)
    pieces = gather_atoms(arrived, atom_devices)
    basis_wide, field_wide = relayout(
        basis.reshape(batches, points * blocks, size),
        exchange_field.reshape(batches, points * blocks, size),
        points,
        blocks,
    )
    shapes = (slabs, atom_devices, atom_total, points, blocks, width, owner_rows)
    tiles, partial_grad = partial_gradient(
        region,
        pattern,
        basis_wide,
        field_wide,
        basis_grad.reshape(PARTS, batches, points * blocks, size),
        weights,
        weight_grad,
        fn_atom,
        batch_atom,
        pieces,
        shapes,
    )
    chunk = atom_total // atom_devices
    parts = lax.all_to_all(
        partial_grad.reshape(slabs * atom_devices, PARTS, chunk),
        ("grid", "atoms"),
        split_axis=0,
        concat_axis=0,
        tiled=True,
    )
    contracted = contract(region, pattern, basis_wide, tiles, points, blocks, width)
    return contracted.reshape(basis.shape), jnp.sum(parts, axis=0)


def solution(mesh):
    placed = (
        P(("groups", "grid", "atoms"), None, None, None),
        P(None, ("groups", "grid", "atoms"), None, None, None),
        P(("groups", "grid", "atoms"), None, None, None),
        P(("groups", "grid", "atoms"), None),
        P(None, ("groups", "grid", "atoms"), None),
        P(("groups", "grid"), None, None, None),
        P("groups", None),
        P(("groups", "grid", "atoms"), None),
        P("groups"),
        P(("groups", "grid", "atoms")),
    )
    return jax.shard_map(
        local,
        mesh=mesh,
        in_specs=placed,
        out_specs=(P(("groups", "grid", "atoms"), None, None, None), P(None, ("groups", "atoms"))),
        check_vma=False,
    )
```

time: 203 us -> 55.8 us (0.27)
  other arithmetic: 69.5 us -> 0.62 us
  matrix products: 31.1 us -> 0 us
  waiting for transfers between devices: 29.5 us -> 4.18 us
  local copies, waits for them, and re-layouts: 30.6 us -> 9.05 us
  Pallas kernels: 0 us -> 21.2 us
  between operations: 14.2 us -> 0.76 us
  blocking collectives: 20.9 us -> 13.6 us
    scatter-add x2 -> x0, other arithmetic: 54.3 us -> none  [atom_sum(): return jax.ops.segment_sum(values, atom_ids, atom_total)]
    dot_general x4 -> x0, matrix products: 31.1 us -> none  [the longest x1 9.28 us: local(): jnp.einsum('bgskn,bskmn->bgsm', picked, density_tiles, preferred_element_...]
    pallas_call x0 -> x4, Pallas kernels: none -> 21.2 us  [the longest x1 10.3 us: partial_gradient(): pl.pallas_call(functools.partial(gradient_kernel, points=points, blocks=b...]
    psum x1 -> x0, blocking collectives: 20.9 us -> none  [local(): gradient = lax.psum(reduced, 'grid')]
    reduce_scatter x1 -> x0, waiting for transfers between devices: 19.6 us -> none  [local(): lax.psum_scatter(partial_grad, 'atoms', scatter_dimension=1, tiled=True)]
    all_to_all x0 -> x1, blocking collectives: none -> 13.6 us  [local(): lax.all_to_all(outgoing, 'grid', split_axis=0, concat_axis=0, tiled=True)]
    reduce_sum x5 -> x1, other arithmetic: 12.3 us -> 0.62 us  [local(): return (contracted.reshape(basis.shape), jnp.sum(parts, axis=0))]
    transpose x1 -> x0, local copies, waits for them, and re-layouts: 10.7 us -> none  [local(): jnp.einsum('bgsm,bskmn->bgskn', basis, density_tiles, preferred_element_t...]
  transfers between devices with their start and end apart: 2 -> 4, of which waited for: 2 -> 1; matrix products, arithmetic and copies ran while one was open for 5% -> 2% of each run, Pallas kernels for 0% -> 18%
where the time goes in v1:
time: 55.8 us; the launch traced here: 55.4 us
  Pallas kernels  21.2 us (38%)
  blocking collectives  13.6 us (24%)
  local copies, waits for them, and re-layouts  9.05 us (16%)
  starting transfers between devices  6.04 us (11%)
  waiting for transfers between devices  4.18 us (7%)
  between operations  0.76 us (1%)
  other arithmetic  0.62 us (1%)
    all_to_all x1, blocking collectives, local(): lax.all_to_all(outgoing, 'grid', split_axis=0, concat_axis=0, tiled=True)  13.6 us
    pallas_call x1, Pallas kernels, partial_gradient(): pl.pallas_call(functools.partial(gradient_kernel, points=points, blocks=b...  10.3 us
    unnamed x21, local copies, waits for them, and re-layouts  8.78 us
    pallas_call x1, Pallas kernels, contract(): pl.pallas_call(functools.partial(product_kernel, points=points, blocks=bl...  8.36 us
    all_to_all x1, starting transfers between devices, local(): lax.all_to_all(partial_grad.reshape(slabs * atom_devices, PARTS, chunk),...  4.54 us
    ppermute x3, waiting for transfers between devices, gather_atoms(): pieces[step ^ bit] = lax.ppermute(pieces[step], 'atoms', swap)  4.18 us
    ppermute x3, starting transfers between devices, gather_atoms(): pieces[step ^ bit] = lax.ppermute(pieces[step], 'atoms', swap)  1.5 us
    pallas_call x1, Pallas kernels, relayout(): pl.pallas_call(functools.partial(relayout_kernel, points=points, blocks=b...  1.47 us
  transfers between devices with their start and end apart: 4, of which 1 were waited for; matrix products, arithmetic and copies ran while one was open for 2% of the time, Pallas kernels for 18%

profile of v1, /device:TPU:0, one launch (start us, length us, event | category | flops | bytes accessed | tf_op | source)
XLA Modules:
  0.0 55.4 jit_solution(15523237197384553001)
XLA Ops:
  0.6 0.0 copy-start.3
  0.6 1.4 %copy-done.3 = bf16[15,3,128,128]{3,2,1,0:T(8,128)(2,1)S(1)} copy-done((bf16[15,3,128,128]{3,2,1,0:T(8,128)(2,1)S(1)}, bf16[15,3,128,128]{3,2,1,0:T(8,128)(2,1)}, u32[]{:S(2)}) %copy-start.3) | copy-done | bytes 1474584
  2.0 0.0 copy-start.6
  2.0 0.7 %copy-done.6 = s32[4,4]{1,0:T(4,128)S(1)} copy-done((s32[4,4]{1,0:T(4,128)S(1)}, s32[4,4]{1,0:T(4,128)}, u32[]{:S(2)}) %copy-start.6) | copy-done | bytes 88
  2.7 0.0 copy-start.9
  2.7 1.1 %shard_map.114 = bf16[4,2,3,32,128]{4,3,2,1,0:T(8,128)(2,1)S(1)} custom-call(s32[4,4]{1,0:T(4,128)S(1)} %copy-done.6, bf16[15,3,128,128]{3,2,1,0:T(8,128)(2,1)S(1)} %copy-done.3), custom_call_target="tpu_custom_call" | custom-call | tf_op jit(solution)/shard_map/pallas_call | solution.py:62
  3.7 13.6 %all_to_all.10.rest_0_ = bf16[4,2,3,32,128]{4,3,2,1,0:T(8,128)(2,1)S(1)} all-to-all(bf16[4,2,3,32,128]{4,3,2,1,0:T(8,128)(2,1)S(1)} %shard_map.114), channel_id=1, replica_groups=mesh['groups'=2,'grid'=4,'atoms'=4] {'grid'}, dimensions={0} | all-to-all | bytes 393216 | tf_op jit(solution)/shard_map/all_to_all | solution.py:323
  17.3 1.5 %collective-permute-start.1 = (bf16[4,2,3,32,128]{4,3,2,1,0:T(8,128)(2,1)S(1)}, bf16[4,2,3,32,128]{4,3,2,1,0:T(8,128)(2,1)S(1)}, u32[]{:S(2)}, u32[]{:S(2)}) collective-permute-start(bf16[4,2,3,32,128]{4,3,2,1,0:T(8,128)(2,1)S(1)} %all_to_all.10.rest_0_), channel_id=1, source_target_pairs={{0,2},{1,3},{2,0},{3,1},{4,6},{5,7},{6,4},{7,5},{8,10},{9,11},{10,... | collective-permute-start | bytes 589832 | tf_op jit(solution)/shard_map/ppermute | solution.py:300
  18.8 0.0 collective-permute-start
  18.8 4.2 %collective-permute-done.1.rest_2_ = bf16[4,2,3,32,128]{4,3,2,1,0:T(8,128)(2,1)S(1)} collective-permute-done((bf16[4,2,3,32,128]{4,3,2,1,0:T(8,128)(2,1)S(1)}, bf16[4,2,3,32,128]{4,3,2,1,0:T(8,128)(2,1)S(1)}, u32[]{:S(2)}, u32[]{:S(2)}) %collective-permute-start.1) | collective-permute-done | bytes 196640 | tf_op jit(solution)/shard_map/ppermute | solution.py:300
  23.0 0.0 collective-permute-start.2
  23.0 0.8 %copy.19.pattern = s32[16,4]{1,0:T(8,128)S(1)} copy(s32[16,4]{0,1:T(4,128)} %param.17) | data formatting | bytes 512 | tf_op args[7]
  23.8 0.1 reshape.35.places
  23.9 0.0 copy-done.9
  23.9 0.1 broadcast_in_dim.4
  24.0 0.1 reshape.38.batch_atom
  24.1 0.0 copy-start.1
  24.1 1.6 %copy-done.1 = bf16[16,128,4,128]{3,2,1,0:T(4,128)(2,1)S(1)} copy-done((bf16[16,128,4,128]{3,2,1,0:T(4,128)(2,1)S(1)}, bf16[16,128,4,128]{3,2,1,0:T(4,128)(2,1)}, u32[]{:S(2)}) %copy-start.1) | copy-done | bytes 2097176
  25.6 0.0 copy-start.2
  25.6 1.6 %copy-done.2 = bf16[16,128,4,128]{3,2,1,0:T(4,128)(2,1)S(1)} copy-done((bf16[16,128,4,128]{3,2,1,0:T(4,128)(2,1)S(1)}, bf16[16,128,4,128]{3,2,1,0:T(4,128)(2,1)}, u32[]{:S(2)}) %copy-start.2) | copy-done | bytes 2097176
  27.2 0.0 copy-start.4
  27.2 0.0 copy-start.5
  27.2 0.0 copy-start.7
  27.2 0.0 copy-start.8
  27.2 1.5 %shard_map.113 = (bf16[16,128,512]{2,1,0:T(8,128)(2,1)S(1)}, bf16[16,128,512]{2,1,0:T(8,128)(2,1)S(1)}) custom-call(bf16[16,512,128]{2,1,0:T(8,128)(2,1)S(1)} %bitcast.7, bf16[16,512,128]{2,1,0:T(8,128)(2,1)S(1)} %bitcast.8), custom_call_target="tpu_custom_call" | custom-call | bytes 8388608 | tf_op jit(solution)/shard_map/pallas_call | solution.py:89
  28.7 0.0 collective-permute-done.rest_1_
  28.7 0.0 collective-permute-done.2.rest_3_
  28.8 0.0 copy-done.4
  28.8 0.0 copy-done.5
  28.8 0.0 copy-done.7
  28.8 0.0 copy-done.8
  28.8 0.0 copy-start
  28.8 2.8 %copy-done = bf16[3,16,128,4,128]{4,3,2,1,0:T(4,128)(2,1)S(1)} copy-done((bf16[3,16,128,4,128]{4,3,2,1,0:T(4,128)(2,1)S(1)}, bf16[3,16,128,4,128]{4,3,2,1,0:T(4,128)(2,1)}, u32[]{:S(2)}) %copy-start) | copy-done | bytes 6291480
  31.6 10.3 %shard_map.115 = (bf16[13,128,128]{2,1,0:T(8,128)(2,1)S(1)}, f32[4,4,3,192]{3,2,1,0:T(4,128)}) custom-call(s32[4,4]{1,0:T(4,128)S(1)} %copy-done.7, s32[16,4]{1,0:T(8,128)S(1)} %copy.19.pattern, bf16[16,128,512]{2,1,0:T(8,128)(2,1)S(1)} %get-tuple-element.6.basis, bf16[16,128,512]{2,1,0:T(8,128)(2,1)S(1)} %get-tuple-element.7.field, ...), custom_call_target="tpu_custom_call" | custom-call | tf_op jit(solution)/shard_map/pallas_call | solution.py:234
  41.9 4.5 %all-to-all-start.1 = ((f32[16,3,192]{2,1,0:T(4,128)}), f32[16,3,192]{2,1,0:T(4,128)S(1)}, u32[]{:S(2)}, u32[]{:S(2)}) async-start(f32[16,3,192]{2,1,0:T(4,128)} %bitcast.5), calls=%async_computation.1 | async-start | bytes 131072 | tf_op jit(solution)/shard_map/all_to_all | solution.py:346
  46.4 8.4 %shard_map.116 = bf16[16,512,128]{2,1,0:T(8,128)(2,1)} custom-call(s32[4,4]{1,0:T(4,128)S(1)} %copy-done.7, s32[16,4]{1,0:T(8,128)S(1)} %copy.19.pattern, bf16[16,128,512]{2,1,0:T(8,128)(2,1)S(1)} %get-tuple-element.6.basis, bf16[13,128,128]{2,1,0:T(8,128)(2,1)S(1)} %get-tuple-element.8.tiles), custom_call_target="tpu_custom_call" | custom-call | flops 1073741824 | bytes 4194304 | tf_op jit(solution)/shard_map/pallas_call | solution.py:272
  54.8 0.0 all-to-all-done.1
  54.8 0.6 %reduce_sum.9 = f32[3,192]{1,0:T(4,128)} reduce(f32[16,3,192]{2,1,0:T(4,128)S(1)} %all-to-all-done.1, f32[]{:T(128)} %constant.0.clone.1), dimensions={0}, to_apply=%region_0.0 | reduce | flops 8640 | bytes 39172 | tf_op jit(solution)/shard_map/reduce_sum | solution.py:354
  (1 shorter events, 0.0 us)
Async XLA Ops:
  0.6 1.4 %copy-start.3 = (bf16[15,3,128,128]{3,2,1,0:T(8,128)(2,1)S(1)}, bf16[15,3,128,128]{3,2,1,0:T(8,128)(2,1)}, u32[]{:S(2)}) copy-start(bf16[15,3,128,128]{3,2,1,0:T(8,128)(2,1)} %density.1) | copy-start | bytes 4423684
  2.0 0.7 %copy-start.6 = (s32[4,4]{1,0:T(4,128)S(1)}, s32[4,4]{1,0:T(4,128)}, u32[]{:S(2)}) copy-start(s32[4,4]{1,0:T(4,128)} %region.5) | copy-start | bytes 196
  2.7 21.2 %copy-start.9 = (s32[16]{0:T(128)S(1)}, s32[16]{0:T(128)}, u32[]{:S(2)}) copy-start(s32[16]{0:T(128)} %param.19) | copy-start | bytes 196
  17.3 5.7 %collective-permute-start.1 = (bf16[4,2,3,32,128]{4,3,2,1,0:T(8,128)(2,1)S(1)}, bf16[4,2,3,32,128]{4,3,2,1,0:T(8,128)(2,1)S(1)}, u32[]{:S(2)}, u32[]{:S(2)}) collective-permute-start(bf16[4,2,3,32,128]{4,3,2,1,0:T(8,128)(2,1)S(1)} %all_to_all.10.rest_0_), channel_id=1, source_target_pairs={{0,2},{1,3},{2,0},{3,1},{4,6},{5,7},{6,4},{7,5},{8,10},{9,11},{10,... | collective-permute-start | bytes 589832 | tf_op jit(solution)/shard_map/ppermute | solution.py:300
  18.8 9.9 %collective-permute-start = (bf16[4,2,3,32,128]{4,3,2,1,0:T(8,128)(2,1)S(1)}, bf16[4,2,3,32,128]{4,3,2,1,0:T(8,128)(2,1)S(1)}, u32[]{:S(2)}, u32[]{:S(2)}) collective-permute-start(bf16[4,2,3,32,128]{4,3,2,1,0:T(8,128)(2,1)S(1)} %all_to_all.10.rest_0_), channel_id=1, source_target_pairs={{0,1},{1,0},{2,3},{3,2},{4,5},{5,4},{6,7},{7,6},{8,9},{9,8},{10,11... | collective-permute-start | bytes 589832 | tf_op jit(solution)/shard_map/ppermute | solution.py:300
  23.0 5.7 %collective-permute-start.2 = (bf16[4,2,3,32,128]{4,3,2,1,0:T(8,128)(2,1)S(1)}, bf16[4,2,3,32,128]{4,3,2,1,0:T(8,128)(2,1)S(1)}, u32[]{:S(2)}, u32[]{:S(2)}) collective-permute-start(bf16[4,2,3,32,128]{4,3,2,1,0:T(8,128)(2,1)S(1)} %collective-permute-done.1.rest_2_), channel_id=1, source_target_pairs={{0,1},{1,0},{2,3},{3,2},{4,5},{5,4},{6,7},{7,6},{8,9},{9,8},{10,11... | collective-permute-start | bytes 589832 | tf_op jit(solution)/shard_map/ppermute | solution.py:300
  24.1 1.6 %copy-start.1 = (bf16[16,128,4,128]{3,2,1,0:T(4,128)(2,1)S(1)}, bf16[16,128,4,128]{3,2,1,0:T(4,128)(2,1)}, u32[]{:S(2)}) copy-start(bf16[16,128,4,128]{3,2,1,0:T(4,128)(2,1)} %param.10) | copy-start | bytes 6291460
  25.6 1.6 %copy-start.2 = (bf16[16,128,4,128]{3,2,1,0:T(4,128)(2,1)S(1)}, bf16[16,128,4,128]{3,2,1,0:T(4,128)(2,1)}, u32[]{:S(2)}) copy-start(bf16[16,128,4,128]{3,2,1,0:T(4,128)(2,1)} %param.12) | copy-start | bytes 6291460
  27.2 1.5 %copy-start.4 = (s32[7680]{0:T(1024)S(1)}, s32[7680]{0:T(1024)}, u32[]{:S(2)}) copy-start(s32[7680]{0:T(1024)} %param.18) | copy-start | bytes 92164
  27.2 1.5 %copy-start.5 = (f32[3,16,128]{2,1,0:T(8,128)S(1)}, f32[3,16,128]{2,1,0:T(8,128)}, u32[]{:S(2)}) copy-start(f32[3,16,128]{2,1,0:T(8,128)} %weight_grad.1) | copy-start | bytes 73732
  27.2 1.5 %copy-start.7 = (s32[4,4]{1,0:T(4,128)S(1)}, s32[4,4]{1,0:T(4,128)}, u32[]{:S(2)}) copy-start(s32[4,4]{1,0:T(4,128)} %region.5) | copy-start | bytes 196
  27.2 1.5 %copy-start.8 = (f32[16,128]{1,0:T(8,128)S(1)}, f32[16,128]{1,0:T(8,128)}, u32[]{:S(2)}) copy-start(f32[16,128]{1,0:T(8,128)} %weights.1) | copy-start | bytes 24580
  28.8 2.8 %copy-start = (bf16[3,16,128,4,128]{4,3,2,1,0:T(4,128)(2,1)S(1)}, bf16[3,16,128,4,128]{4,3,2,1,0:T(4,128)(2,1)}, u32[]{:S(2)}) copy-start(bf16[3,16,128,4,128]{4,3,2,1,0:T(4,128)(2,1)} %param.11) | copy-start | bytes 18874372
  41.9 12.9 %all-to-all-start.1 = ((f32[16,3,192]{2,1,0:T(4,128)}), f32[16,3,192]{2,1,0:T(4,128)S(1)}, u32[]{:S(2)}, u32[]{:S(2)}) async-start(f32[16,3,192]{2,1,0:T(4,128)} %bitcast.5), calls=%async_computation.1 | async-start | bytes 131072 | tf_op jit(solution)/shard_map/all_to_all | solution.py:346

commit v2 on v1

--- a/solution.py
+++ b/solution.py
@@ -7,7 +7,8 @@
 from jax.experimental.pallas import tpu as pltpu
 from jax.sharding import PartitionSpec as P
 
-CAP = 2
+TRAVEL = 5
+SHARE = 2
 PARTS = 3
 F32 = jnp.float32
 BF16 = jnp.bfloat16
@@ -16,57 +17,95 @@
 
 
 def owner_and_slot(region, slab, position, owner_rows):
-    row = region[slab, position]
-    owner = lax.div(row, owner_rows)
+    owner = lax.div(region[slab, position], owner_rows)
     slot = jnp.int32(0)
-    for earlier in range(position):
-        same = lax.div(region[slab, earlier], owner_rows) == owner
-        slot = slot + jnp.where(same, 1, 0)
-    return owner, slot
-
-
-def pick_kernel(region, density, out, sems, *, owner_rows, quarter):
+    count = jnp.int32(0)
+    for other in range(region.shape[1]):
+        same = jnp.where(lax.div(region[slab, other], owner_rows) == owner, 1, 0)
+        count = count + same
+        if other < position:
+            slot = slot + same
+    return owner, slot, count
+
+
+def travel_place(slot, count, k):
+    if k == 0:
+        return jnp.where(slot == 0, 4, 2)
+    if k == 1:
+        return jnp.where(slot == 0, 0, 3)
+    return jnp.where(jnp.logical_and(slot == 0, count == 2), 1, 4)
+
+
+def send_kernel(region, density, *rest, share):
+    *outs, sems = rest
     me = lax.axis_index("grid")
-    part = lax.axis_index("atoms")
+    part = lax.rem(lax.axis_index("atoms"), share)
     slabs, size = region.shape
-    first = pl.multiple_of(part * quarter, quarter)
-
-    def copies(slab):
-        found = []
+    owner_rows = density.shape[0]
+    rows = density.shape[-2]
+    copies = []
+    for shift, out in enumerate(outs):
+        slab = lax.rem(me + shift, slabs)
+        base = jnp.int32(owner_rows)
+        count = jnp.int32(0)
         for position in range(size):
-            owner, slot = owner_and_slot(region, slab, position, owner_rows)
-            mine = owner == me
-            local_row = jnp.where(mine, region[slab, position] - me * owner_rows, 0)
-            copy = pltpu.make_async_copy(
-                density.at[local_row, :, pl.ds(first, quarter), :],
-                out.at[slab, jnp.minimum(slot, CAP - 1)],
-                sems.at[slab, position],
-            )
-            found.append((mine, copy))
-        return found
-
-    @pl.loop(0, slabs)
-    def _(slab):
-        for mine, copy in copies(slab):
-            pl.when(mine)(copy.start)
-
-    @pl.loop(0, slabs)
-    def _(slab):
-        for mine, copy in copies(slab):
-            pl.when(mine)(copy.wait)
-
-
-def pick_rows(region, density, slabs, atom_devices):
-    owner_rows, width, size, _ = density.shape
-    quarter = size // atom_devices
+            row = region[slab, position] - me * owner_rows
+            mine = jnp.logical_and(row >= 0, row < owner_rows)
+            base = jnp.minimum(base, jnp.where(mine, row, owner_rows))
+            count = count + jnp.where(mine, 1, 0)
+        base = jnp.where(count == 0, 0, base)
+        after = jnp.minimum(base + 1, owner_rows - 1)
+        lower = base == 0
+        edge = jnp.where(jnp.logical_and(count == 2, jnp.logical_not(lower)), after, base)
+        kept = out.shape[1]
+        first = 0 if kept == rows else pl.multiple_of(part * kept, kept)
+        here = pl.ds(first, kept)
+        pairs = (
+            (density.at[base, pl.ds(1, 2), here, :], out.at[pl.ds(0, 2)]),
+            (density.at[after, pl.ds(0, 2), here, :], out.at[pl.ds(2, 2)]),
+            (density.at[edge, jnp.where(lower, 0, 2), here, :], out.at[4]),
+        )
+        for number, (source, target) in enumerate(pairs):
+            copies.append(pltpu.make_async_copy(source, target, sems.at[shift, number]))
+    for copy in copies:
+        copy.start()
+    for copy in copies:
+        copy.wait()
+
+
+def in_hbm(array):
+    return pltpu.with_memory_space_constraint(array, pltpu.HBM)
+
+
+def rows_to_send(region, density, slabs, share):
+    size = density.shape[-1]
+    kept = [size] + [size // share] * (slabs - 1)
     return pl.pallas_call(
-        functools.partial(pick_kernel, owner_rows=owner_rows, quarter=quarter),
-        out_shape=jax.ShapeDtypeStruct((slabs, CAP, width, quarter, size), density.dtype),
+        functools.partial(send_kernel, share=share),
+        out_shape=[jax.ShapeDtypeStruct((TRAVEL, rows, size), density.dtype) for rows in kept],
         in_specs=[pl.BlockSpec(memory_space=pltpu.SMEM), pl.BlockSpec(memory_space=pl.ANY)],
-        out_specs=pl.BlockSpec(memory_space=pltpu.VMEM),
-        scratch_shapes=[pltpu.SemaphoreType.DMA(region.shape)],
+        out_specs=[pl.BlockSpec(memory_space=pltpu.VMEM)] * slabs,
+        scratch_shapes=[pltpu.SemaphoreType.DMA((slabs, 3))],
         compiler_params=pltpu.CompilerParams(vmem_limit_bytes=VMEM_LIMIT),
-    )(region, density)
+    )(in_hbm(region), in_hbm(density))
+
+
+def fetch_rows(region, density, slabs, share):
+    own, *outgoing = rows_to_send(region, density, slabs, share)
+    near = []
+    for shift, piece in enumerate(outgoing, 1):
+        near.append(lax.ppermute(piece, "grid", [(i, (i + shift) % slabs) for i in range(slabs)]))
+    return own, near
+
+
+def stage_rows(stage, own, near, far, share):
+    part = lax.rem(lax.axis_index("atoms"), share)
+    kept = near[0].shape[1]
+    for place in range(TRAVEL):
+        stage[place] = own[place]
+        for shift, (here, there) in enumerate(zip(near, far), 1):
+            stage[shift * TRAVEL + place, pl.ds(pl.multiple_of(part * kept, kept), kept), :] = here[place]
+            stage[shift * TRAVEL + place, pl.ds(pl.multiple_of((1 - part) * kept, kept), kept), :] = there[place]
 
 
 def block_major(x_ref, wide, points, blocks):
@@ -140,24 +179,22 @@
     owner_rows,
     slabs,
 ):
-    *pieces, tiles, out, spread, sums, energy_sums = rest
+    *pieces, tiles, out, stage, spread, sums, energy_sums = rest
     batch = pl.program_id(0)
     batches = pl.num_programs(0)
     me = lax.axis_index("grid")
-    part = lax.axis_index("atoms")
     size = tiles.shape[-1]
-    quarter = pieces[0].shape[-2]
     region_size = region.shape[1]
 
     @pl.when(batch == 0)
     def _():
         tiles[region_size * width] = jnp.zeros((size, size), BF16)
+        stage_rows(stage, pieces[0], pieces[1:slabs], pieces[slabs:], SHARE)
         for position in range(region_size):
-            owner, slot = owner_and_slot(region, me, position, owner_rows)
-            for step, piece in enumerate(pieces):
-                first = pl.multiple_of(jnp.bitwise_xor(part, step) * quarter, quarter)
-                for k in range(width):
-                    tiles[position * width + k, pl.ds(first, quarter), :] = piece[owner, slot, k]
+            owner, slot, count = owner_and_slot(region, me, position, owner_rows)
+            shift = lax.rem(me - owner + slabs, slabs)
+            for k in range(width):
+                tiles[position * width + k] = stage[shift * TRAVEL + travel_place(slot, count, k)]
 
     matrix = batch_matrix(region, pattern, tiles, me, batch, blocks, width)
     potential = lax.dot_general(field[0], matrix, NT, preferred_element_type=F32)
@@ -246,6 +283,7 @@
             + [whole] * (5 + len(pieces)),
             out_specs=(whole, whole),
             scratch_shapes=[
+                pltpu.VMEM((slabs * TRAVEL, size, size), BF16),
                 pltpu.VMEM((points * blocks, size), F32),
                 pltpu.VMEM((PARTS, batches * 8, size), F32),
                 pltpu.VMEM((PARTS, batches * 8, size), F32),
@@ -291,17 +329,6 @@
     )(region, pattern, basis, tiles)
 
 
-def gather_atoms(piece, atom_devices):
-    pieces = {0: piece}
-    bit = atom_devices // 2
-    while bit:
-        swap = [(i, i ^ bit) for i in range(atom_devices)]
-        for step in list(pieces):
-            pieces[step ^ bit] = lax.ppermute(pieces[step], "atoms", swap)
-        bit //= 2
-    return [pieces[step] for step in range(atom_devices)]
-
-
 def local(
     basis,
     basis_grad,
@@ -319,22 +346,24 @@
     slabs = lax.axis_size("grid")
     atom_devices = lax.axis_size("atoms")
     atom_total = fn_atom.shape[0] // (10 * slabs * atom_devices) * slabs * atom_devices
-    outgoing = pick_rows(region, density, slabs, atom_devices)
-    arrived = lax.all_to_all(outgoing, "grid", split_axis=0, concat_axis=0, tiled=True)
-    pieces = gather_atoms(arrived, atom_devices)
+    own, near = fetch_rows(region, density, slabs, SHARE)
     basis_wide, field_wide = relayout(
-        basis.reshape(batches, points * blocks, size),
-        exchange_field.reshape(batches, points * blocks, size),
+        in_hbm(basis.reshape(batches, points * blocks, size)),
+        in_hbm(exchange_field.reshape(batches, points * blocks, size)),
         points,
         blocks,
     )
+    near, basis_wide, field_wide = lax.optimization_barrier((near, basis_wide, field_wide))
+    swap = [(i, i ^ 1) for i in range(atom_devices)]
+    far = [lax.ppermute(piece, "atoms", swap) for piece in near]
+    pieces = [own, *near, *far]
     shapes = (slabs, atom_devices, atom_total, points, blocks, width, owner_rows)
     tiles, partial_grad = partial_gradient(
         region,
         pattern,
         basis_wide,
         field_wide,
-        basis_grad.reshape(PARTS, batches, points * blocks, size),
+        in_hbm(basis_grad.reshape(PARTS, batches, points * blocks, size)),
         weights,
         weight_grad,
         fn_atom,

time: 55.8 us -> 50.9 us (0.912)
  blocking collectives: 13.6 us -> 0 us
  Pallas kernels: 21.2 us -> 33.5 us
  local copies, waits for them, and re-layouts: 9.05 us -> 3.28 us
  starting transfers between devices: 6.04 us -> 11.3 us
  waiting for transfers between devices: 4.18 us -> 0.83 us
    all_to_all x1 -> x0, blocking collectives: 13.6 us -> none  [local(): lax.all_to_all(outgoing, 'grid', split_axis=0, concat_axis=0, tiled=True)]
    pallas_call x1, Pallas kernels: 1.47 us -> 8.86 us  [relayout(): pl.pallas_call(functools.partial(relayout_kernel, points=points, blocks=b...]
    ppermute x3 -> x6, starting transfers between devices: 1.5 us -> 7.78 us  [the longest x3 7.13 us: fetch_rows(): lax.ppermute(piece, 'grid', [(i, (i + shift) % slabs) for i in range(slab...]
    unnamed x21 -> x17, local copies, waits for them, and re-layouts: 8.78 us -> 3.01 us
    pallas_call x1, Pallas kernels: 10.3 us -> 14.5 us  [partial_gradient(): pl.pallas_call(functools.partial(gradient_kernel, points=points, blocks=b...]
    ppermute x3 -> x6, waiting for transfers between devices: 4.18 us -> 0.83 us  [the longest x3 0.82 us: local(): far = [lax.ppermute(piece, 'atoms', swap) for piece in near]]
    all_to_all x1, starting transfers between devices: 4.54 us -> 3.5 us  [local(): lax.all_to_all(partial_grad.reshape(slabs * atom_devices, PARTS, chunk),...]
    pallas_call x1, Pallas kernels: 1.05 us -> 1.78 us  [rows_to_send(): pl.pallas_call(functools.partial(send_kernel, share=share), out_shape=[ja...]
  transfers between devices with their start and end apart: 4 -> 7, of which waited for: 1 -> 3; matrix products, arithmetic and copies ran while one was open for 2% -> 1% of each run, Pallas kernels for 18% -> 34%
where the time goes in v2:
time: 50.9 us; the launch traced here: 50.3 us
  Pallas kernels  33.5 us (66%)
  starting transfers between devices  11.3 us (22%)
  local copies, waits for them, and re-layouts  3.28 us (6%)
  waiting for transfers between devices  0.83 us (2%)
  between operations  0.74 us (1%)
  other arithmetic  0.62 us (1%)
    pallas_call x1, Pallas kernels, partial_gradient(): pl.pallas_call(functools.partial(gradient_kernel, points=points, blocks=b...  14.5 us
    pallas_call x1, Pallas kernels, relayout(): pl.pallas_call(functools.partial(relayout_kernel, points=points, blocks=b...  8.86 us
    pallas_call x1, Pallas kernels, contract(): pl.pallas_call(functools.partial(product_kernel, points=points, blocks=bl...  8.36 us
    ppermute x3, starting transfers between devices, fetch_rows(): lax.ppermute(piece, 'grid', [(i, (i + shift) % slabs) for i in range(slab...  7.13 us
    all_to_all x1, starting transfers between devices, local(): lax.all_to_all(partial_grad.reshape(slabs * atom_devices, PARTS, chunk),...  3.5 us
    unnamed x17, local copies, waits for them, and re-layouts  3.01 us
    pallas_call x1, Pallas kernels, rows_to_send(): pl.pallas_call(functools.partial(send_kernel, share=share), out_shape=[ja...  1.78 us
  transfers between devices with their start and end apart: 7, of which 3 were waited for; matrix products, arithmetic and copies ran while one was open for 1% of the time, Pallas kernels for 34%

profile of v2, /device:TPU:0, one launch (start us, length us, event | category | flops | bytes accessed | tf_op | source)
XLA Modules:
  0.0 50.3 jit_solution(12513496147909043210)
XLA Ops:
  0.6 1.8 %shard_map.113 = (bf16[5,128,128]{2,1,0:T(8,128)(2,1)S(1)}, bf16[5,64,128]{2,1,0:T(8,128)(2,1)S(1)}, bf16[5,64,128]{2,1,0:T(8,128)(2,1)S(1)}, bf16[5,64,128]{2,1,0:T(8,128)(2,1)S(1)}) custom-call(s32[4,4]{1,0:T(4,128)} %region.5, bf16[15,3,128,128]{3,2,1,0:T(8,128)(2,1)} %density.1), custom_call_target="tpu_custom_call" | custom-call | tf_op jit(solution)/shard_map/pallas_call | solution.py:83
  2.4 3.1 %collective-permute-start = (bf16[5,64,128]{2,1,0:T(8,128)(2,1)S(1)}, bf16[5,64,128]{2,1,0:T(8,128)(2,1)S(1)}, u32[]{:S(2)}, u32[]{:S(2)}) collective-permute-start(bf16[5,64,128]{2,1,0:T(8,128)(2,1)S(1)} %get-tuple-element.15), channel_id=1, source_target_pairs={{0,4},{4,8},{8,12},{12,0},{1,5},{5,9},{9,13},{13,1},{2,6},{6,10},{... | collective-permute-start | bytes 245768 | tf_op jit(solution)/shard_map/ppermute | solution.py:97
  5.5 2.6 %collective-permute-start.1 = (bf16[5,64,128]{2,1,0:T(8,128)(2,1)S(1)}, bf16[5,64,128]{2,1,0:T(8,128)(2,1)S(1)}, u32[]{:S(2)}, u32[]{:S(2)}) collective-permute-start(bf16[5,64,128]{2,1,0:T(8,128)(2,1)S(1)} %get-tuple-element.16), channel_id=1, source_target_pairs={{0,8},{4,12},{8,0},{12,4},{1,9},{5,13},{9,1},{13,5},{2,10},{6,14},... | collective-permute-start | bytes 245768 | tf_op jit(solution)/shard_map/ppermute | solution.py:97
  8.1 1.5 %collective-permute-start.2 = (bf16[5,64,128]{2,1,0:T(8,128)(2,1)S(1)}, bf16[5,64,128]{2,1,0:T(8,128)(2,1)S(1)}, u32[]{:S(2)}, u32[]{:S(2)}) collective-permute-start(bf16[5,64,128]{2,1,0:T(8,128)(2,1)S(1)} %get-tuple-element.17), channel_id=1, source_target_pairs={{0,12},{4,0},{8,4},{12,8},{1,13},{5,1},{9,5},{13,9},{2,14},{6,2},{... | collective-permute-start | bytes 245768 | tf_op jit(solution)/shard_map/ppermute | solution.py:97
  9.6 0.0 copy-start.6
  9.6 0.0 copy-start.7
  9.6 0.0 copy-start.2
  9.6 0.0 copy-start.3
  9.6 0.0 copy-start.4
  9.6 0.0 copy-start.5
  9.6 8.9 %shard_map.114 = (bf16[16,128,512]{2,1,0:T(8,128)(2,1)S(1)}, bf16[16,128,512]{2,1,0:T(8,128)(2,1)S(1)}) custom-call(bf16[16,512,128]{2,1,0:T(8,128)(2,1)} %bitcast.8, bf16[16,512,128]{2,1,0:T(8,128)(2,1)} %bitcast.9), custom_call_target="tpu_custom_call" | custom-call | bytes 8388608 | tf_op jit(solution)/shard_map/pallas_call | solution.py:128
  18.5 0.0 copy-start
  18.5 1.3 %copy-done = bf16[16,128,512]{2,1,0:T(8,128)(2,1)} copy-done((bf16[16,128,512]{2,1,0:T(8,128)(2,1)}, bf16[16,128,512]{2,1,0:T(8,128)(2,1)S(1)}, u32[]{:S(2)}) %copy-start) | copy-done | bytes 2097176
  19.8 0.0 collective-permute-done.rest_1_
  19.8 0.0 collective-permute-done.1.rest_2_
  19.8 0.0 collective-permute-done.2.rest_3_
  19.8 0.1 collective-permute-start.3
  19.9 0.5 collective-permute-start.4
  20.4 0.1 collective-permute-start.5
  20.5 0.0 copy-done.6
  20.5 0.1 copy.19.pattern
  20.5 0.1 reshape.35.places
  20.7 0.0 copy-done.7
  20.7 0.1 broadcast_in_dim.4
  20.7 0.1 reshape.38.batch_atom
  20.8 0.3 collective-permute-done.3.rest_4_
  21.1 0.2 collective-permute-done.4.rest_5_
  21.3 0.4 collective-permute-done.5.rest_6_
  21.6 0.0 copy-done.2
  21.7 0.0 copy-done.3
  21.7 0.0 copy-done.4
  21.7 0.0 copy-done.5
  21.7 0.0 copy-start.1
  21.7 1.6 %copy-done.1 = bf16[16,128,512]{2,1,0:T(8,128)(2,1)S(1)} copy-done((bf16[16,128,512]{2,1,0:T(8,128)(2,1)S(1)}, bf16[16,128,512]{2,1,0:T(8,128)(2,1)}, u32[]{:S(2)}) %copy-start.1) | copy-done | bytes 2097176
  23.3 14.5 %shard_map.115 = (bf16[13,128,128]{2,1,0:T(8,128)(2,1)S(1)}, f32[4,4,3,192]{3,2,1,0:T(4,128)}) custom-call(s32[4,4]{1,0:T(4,128)S(1)} %copy-done.4, s32[16,4]{1,0:T(8,128)S(1)} %copy.19.pattern, bf16[16,128,512]{2,1,0:T(8,128)(2,1)S(1)} %get-tuple-element.20.basis, bf16[16,128,512]{2,1,0:T(8,128)(2,1)S(1)} %copy-done.1, bf16[3,16,512,128]{3,2,1,0:T(8,128)(2,1)} %bitcast.7, ...), custom_call_target="tpu_custom_call" | custom-call | tf_op jit(solution)/shard_map/pallas_call | solution.py:271
  37.8 3.5 %all-to-all-start = ((f32[16,3,192]{2,1,0:T(4,128)}), f32[16,3,192]{2,1,0:T(4,128)S(1)}, u32[]{:S(2)}, u32[]{:S(2)}) async-start(f32[16,3,192]{2,1,0:T(4,128)} %bitcast.5), calls=%async_computation | async-start | bytes 131072 | tf_op jit(solution)/shard_map/all_to_all | solution.py:375
  41.3 8.4 %shard_map.116 = bf16[16,512,128]{2,1,0:T(8,128)(2,1)} custom-call(s32[4,4]{1,0:T(4,128)S(1)} %copy-done.4, s32[16,4]{1,0:T(8,128)S(1)} %copy.19.pattern, bf16[16,128,512]{2,1,0:T(8,128)(2,1)S(1)} %get-tuple-element.20.basis, bf16[13,128,128]{2,1,0:T(8,128)(2,1)S(1)} %get-tuple-element.26.tiles), custom_call_target="tpu_custom_call" | custom-call | flops 1073741824 | bytes 4194304 | tf_op jit(solution)/shard_map/pallas_call | solution.py:310
  49.6 0.0 all-to-all-done
  49.6 0.6 %reduce_sum.9 = f32[3,192]{1,0:T(4,128)} reduce(f32[16,3,192]{2,1,0:T(4,128)S(1)} %all-to-all-done, f32[]{:T(128)} %constant.0.clone.1), dimensions={0}, to_apply=%region_0.0 | reduce | flops 8640 | bytes 39172 | tf_op jit(solution)/shard_map/reduce_sum | solution.py:383
  (1 shorter events, 0.0 us)
Async XLA Ops:
  2.4 17.4 %collective-permute-start = (bf16[5,64,128]{2,1,0:T(8,128)(2,1)S(1)}, bf16[5,64,128]{2,1,0:T(8,128)(2,1)S(1)}, u32[]{:S(2)}, u32[]{:S(2)}) collective-permute-start(bf16[5,64,128]{2,1,0:T(8,128)(2,1)S(1)} %get-tuple-element.15), channel_id=1, source_target_pairs={{0,4},{4,8},{8,12},{12,0},{1,5},{5,9},{9,13},{13,1},{2,6},{6,10},{... | collective-permute-start | bytes 245768 | tf_op jit(solution)/shard_map/ppermute | solution.py:97
  5.5 14.3 %collective-permute-start.1 = (bf16[5,64,128]{2,1,0:T(8,128)(2,1)S(1)}, bf16[5,64,128]{2,1,0:T(8,128)(2,1)S(1)}, u32[]{:S(2)}, u32[]{:S(2)}) collective-permute-start(bf16[5,64,128]{2,1,0:T(8,128)(2,1)S(1)} %get-tuple-element.16), channel_id=1, source_target_pairs={{0,8},{4,12},{8,0},{12,4},{1,9},{5,13},{9,1},{13,5},{2,10},{6,14},... | collective-permute-start | bytes 245768 | tf_op jit(solution)/shard_map/ppermute | solution.py:97
  8.1 11.7 %collective-permute-start.2 = (bf16[5,64,128]{2,1,0:T(8,128)(2,1)S(1)}, bf16[5,64,128]{2,1,0:T(8,128)(2,1)S(1)}, u32[]{:S(2)}, u32[]{:S(2)}) collective-permute-start(bf16[5,64,128]{2,1,0:T(8,128)(2,1)S(1)} %get-tuple-element.17), channel_id=1, source_target_pairs={{0,12},{4,0},{8,4},{12,8},{1,13},{5,1},{9,5},{13,9},{2,14},{6,2},{... | collective-permute-start | bytes 245768 | tf_op jit(solution)/shard_map/ppermute | solution.py:97
  9.6 10.9 %copy-start.6 = (s32[16,4]{0,1:T(4,128)S(1)}, s32[16,4]{0,1:T(4,128)}, u32[]{:S(2)}) copy-start(s32[16,4]{0,1:T(4,128)} %param.17) | copy-start | bytes 772
  9.6 11.1 %copy-start.7 = (s32[16]{0:T(128)S(1)}, s32[16]{0:T(128)}, u32[]{:S(2)}) copy-start(s32[16]{0:T(128)} %param.19) | copy-start | bytes 196
  9.6 12.1 %copy-start.2 = (s32[7680]{0:T(1024)S(1)}, s32[7680]{0:T(1024)}, u32[]{:S(2)}) copy-start(s32[7680]{0:T(1024)} %param.18) | copy-start | bytes 92164
  9.6 12.1 %copy-start.3 = (f32[3,16,128]{2,1,0:T(8,128)S(1)}, f32[3,16,128]{2,1,0:T(8,128)}, u32[]{:S(2)}) copy-start(f32[3,16,128]{2,1,0:T(8,128)} %weight_grad.1) | copy-start | bytes 73732
  9.6 12.1 %copy-start.4 = (s32[4,4]{1,0:T(4,128)S(1)}, s32[4,4]{1,0:T(4,128)}, u32[]{:S(2)}) copy-start(s32[4,4]{1,0:T(4,128)} %region.5) | copy-start | bytes 196
  9.6 12.1 %copy-start.5 = (f32[16,128]{1,0:T(8,128)S(1)}, f32[16,128]{1,0:T(8,128)}, u32[]{:S(2)}) copy-start(f32[16,128]{1,0:T(8,128)} %weights.1) | copy-start | bytes 24580
  18.5 1.3 %copy-start = (bf16[16,128,512]{2,1,0:T(8,128)(2,1)}, bf16[16,128,512]{2,1,0:T(8,128)(2,1)S(1)}, u32[]{:S(2)}) copy-start(bf16[16,128,512]{2,1,0:T(8,128)(2,1)S(1)} %get-tuple-element.21.field) | copy-start | bytes 6291460
  19.8 1.3 %collective-permute-start.3 = (bf16[5,64,128]{2,1,0:T(8,128)(2,1)S(1)}, bf16[5,64,128]{2,1,0:T(8,128)(2,1)S(1)}, u32[]{:S(2)}, u32[]{:S(2)}) collective-permute-start(bf16[5,64,128]{2,1,0:T(8,128)(2,1)S(1)} %collective-permute-done.rest_1_), channel_id=1, source_target_pairs={{0,1},{1,0},{2,3},{3,2},{4,5},{5,4},{6,7},{7,6},{8,9},{9,8},{10,11... | collective-permute-start | bytes 245768 | tf_op jit(solution)/shard_map/ppermute | solution.py:358
  19.9 1.4 %collective-permute-start.4 = (bf16[5,64,128]{2,1,0:T(8,128)(2,1)S(1)}, bf16[5,64,128]{2,1,0:T(8,128)(2,1)S(1)}, u32[]{:S(2)}, u32[]{:S(2)}) collective-permute-start(bf16[5,64,128]{2,1,0:T(8,128)(2,1)S(1)} %collective-permute-done.1.rest_2_), channel_id=1, source_target_pairs={{0,1},{1,0},{2,3},{3,2},{4,5},{5,4},{6,7},{7,6},{8,9},{9,8},{10,11... | collective-permute-start | bytes 245768 | tf_op jit(solution)/shard_map/ppermute | solution.py:358
  20.4 1.3 %collective-permute-start.5 = (bf16[5,64,128]{2,1,0:T(8,128)(2,1)S(1)}, bf16[5,64,128]{2,1,0:T(8,128)(2,1)S(1)}, u32[]{:S(2)}, u32[]{:S(2)}) collective-permute-start(bf16[5,64,128]{2,1,0:T(8,128)(2,1)S(1)} %collective-permute-done.2.rest_3_), channel_id=1, source_target_pairs={{0,1},{1,0},{2,3},{3,2},{4,5},{5,4},{6,7},{7,6},{8,9},{9,8},{10,11... | collective-permute-start | bytes 245768 | tf_op jit(solution)/shard_map/ppermute | solution.py:358
  21.7 1.6 %copy-start.1 = (bf16[16,128,512]{2,1,0:T(8,128)(2,1)S(1)}, bf16[16,128,512]{2,1,0:T(8,128)(2,1)}, u32[]{:S(2)}) copy-start(bf16[16,128,512]{2,1,0:T(8,128)(2,1)} %copy-done) | copy-start | bytes 6291460
  37.8 11.9 %all-to-all-start = ((f32[16,3,192]{2,1,0:T(4,128)}), f32[16,3,192]{2,1,0:T(4,128)S(1)}, u32[]{:S(2)}, u32[]{:S(2)}) async-start(f32[16,3,192]{2,1,0:T(4,128)} %bitcast.5), calls=%async_computation | async-start | bytes 131072 | tf_op jit(solution)/shard_map/all_to_all | solution.py:375

commit v3 on v2

--- a/solution.py
+++ b/solution.py
@@ -1,4 +1,5 @@
 import functools
+import math
 
 import jax
 import jax.numpy as jnp
@@ -40,12 +41,12 @@
     *outs, sems = rest
     me = lax.axis_index("grid")
     part = lax.rem(lax.axis_index("atoms"), share)
-    slabs, size = region.shape
+    size = region.shape[1]
     owner_rows = density.shape[0]
     rows = density.shape[-2]
     copies = []
     for shift, out in enumerate(outs):
-        slab = lax.rem(me + shift, slabs)
+        slab = jnp.bitwise_xor(me, shift)
         base = jnp.int32(owner_rows)
         count = jnp.int32(0)
         for position in range(size):
@@ -94,7 +95,7 @@
     own, *outgoing = rows_to_send(region, density, slabs, share)
     near = []
     for shift, piece in enumerate(outgoing, 1):
-        near.append(lax.ppermute(piece, "grid", [(i, (i + shift) % slabs) for i in range(slabs)]))
+        near.append(lax.ppermute(piece, "grid", [(i, i ^ shift) for i in range(slabs)]))
     return own, near
 
 
@@ -192,7 +193,7 @@
         stage_rows(stage, pieces[0], pieces[1:slabs], pieces[slabs:], SHARE)
         for position in range(region_size):
             owner, slot, count = owner_and_slot(region, me, position, owner_rows)
-            shift = lax.rem(me - owner + slabs, slabs)
+            shift = jnp.bitwise_xor(me, owner)
             for k in range(width):
                 tiles[position * width + k] = stage[shift * TRAVEL + travel_place(slot, count, k)]
 
@@ -329,6 +330,275 @@
     )(region, pattern, basis, tiles)
 
 
+def prepare_kernel(
+    region,
+    pattern,
+    basis,
+    field,
+    basis_grad,
+    weights,
+    weight_grad,
+    fn_atom,
+    batch_atom,
+    basis_out,
+    field_out,
+    moments,
+    hot,
+    grad_columns,
+    basis_in,
+    field_in,
+    grad_in,
+    wide,
+    turned,
+    grad_wide,
+    sems,
+    *,
+    points,
+    blocks,
+    step,
+):
+    batches, _, size = basis.shape
+    groups = batches // step
+    me = lax.axis_index("grid")
+
+    def copies(group):
+        here = pl.ds(group * step, step)
+        return (
+            pltpu.make_async_copy(field.at[here], field_in.at[here], sems.at[group, 0]),
+            pltpu.make_async_copy(basis_grad.at[:, here], grad_in.at[:, here], sems.at[group, 1]),
+            pltpu.make_async_copy(basis.at[here], basis_in.at[here], sems.at[group, 2]),
+        )
+
+    for group in range(groups):
+        for copy in copies(group):
+            copy.start()
+
+    atoms = lax.broadcasted_iota(jnp.int32, (hot.shape[0], size), 0)
+    for position in range(blocks):
+        ids = fn_atom[pl.ds(region[me, position], 1), :]
+        hot[:, position * size : (position + 1) * size] = jnp.where(atoms == ids, 1.0, 0.0).astype(BF16)
+    ids = jnp.concatenate([batch_atom[...], jnp.full((1, size - batches), -1, jnp.int32)], axis=1)
+    hot[:, blocks * size :] = jnp.where(atoms == ids, 1.0, 0.0).astype(BF16)
+    for c in range(PARTS):
+        rows = jnp.concatenate([weight_grad[c], jnp.zeros((size - batches, points), F32)], axis=0)
+        grad_columns[c] = rows.T
+
+    @pl.loop(0, groups)
+    def _(group):
+        for copy in copies(group):
+            copy.wait()
+        for inner in range(step):
+            batch = group * step + inner
+            points_here = pl.ds(pl.multiple_of(batch * points, points), points)
+            places = [pattern[s, batch] for s in range(blocks)]
+            weight = weights[pl.ds(batch, 1), :]
+            wide[0] = field_in[batch].astype(F32)
+            wide[1] = basis_in[batch].astype(F32)
+            for c in range(PARTS):
+                wide[2 + c] = grad_in[c, batch].astype(F32)
+            for s, place in enumerate(places):
+                strided = pl.ds(s, points, stride=blocks)
+                values = wide[0, strided, :]
+                field_out[batch, place] = values.astype(BF16)
+                turned[pl.ds(pl.multiple_of(place * size, size), size), points_here] = (values.T * weight).astype(BF16)
+                basis_out[batch, place] = wide[1, strided, :].astype(BF16)
+                for c in range(PARTS):
+                    grad_wide[c, place, points_here, :] = wide[2 + c, strided, :].astype(BF16)
+
+    for c in range(PARTS):
+        right = jnp.concatenate([grad_wide[c, place] for place in range(blocks)], axis=1)
+        moments[c] = jnp.dot(turned[...], right, preferred_element_type=F32)
+
+
+def prepare(region, pattern, basis, field, basis_grad, weights, weight_grad, fn_atom, batch_atom, atom_total):
+    batches, points, blocks, size = basis.shape
+    rows = points * blocks
+    step = 2 if batches % 2 == 0 else 1
+    smem = pl.BlockSpec(memory_space=pltpu.SMEM)
+    hbm = pl.BlockSpec(memory_space=pl.ANY)
+    vmem = pl.BlockSpec(memory_space=pltpu.VMEM)
+    ordered = jax.ShapeDtypeStruct((batches, blocks, points, size), BF16)
+    return pl.pallas_call(
+        functools.partial(prepare_kernel, points=points, blocks=blocks, step=step),
+        out_shape=(
+            ordered,
+            ordered,
+            jax.ShapeDtypeStruct((PARTS, blocks * size, blocks * size), F32),
+            jax.ShapeDtypeStruct((atom_total, (blocks + 1) * size), BF16),
+            jax.ShapeDtypeStruct((PARTS, points, size), F32),
+        ),
+        in_specs=[smem, smem, hbm, hbm, hbm, vmem, vmem, vmem, vmem],
+        out_specs=(vmem,) * 5,
+        scratch_shapes=[
+            pltpu.VMEM((batches, rows, size), BF16),
+            pltpu.VMEM((batches, rows, size), BF16),
+            pltpu.VMEM((PARTS, batches, rows, size), BF16),
+            pltpu.VMEM((2 + PARTS, rows, size), F32),
+            pltpu.VMEM((blocks * size, batches * points), BF16),
+            pltpu.VMEM((PARTS, blocks, batches * points, size), BF16),
+            pltpu.SemaphoreType.DMA((batches // step, 3)),
+        ],
+        compiler_params=pltpu.CompilerParams(vmem_limit_bytes=VMEM_LIMIT),
+        cost_estimate=pl.CostEstimate(
+            flops=2 * PARTS * batches * points * (blocks * size) ** 2,
+            bytes_accessed=2 * (2 + PARTS) * batches * rows * size,
+            transcendentals=0,
+        ),
+    )(
+        in_hbm(region),
+        in_hbm(pattern.T),
+        in_hbm(basis.reshape(batches, rows, size)),
+        in_hbm(field.reshape(batches, rows, size)),
+        in_hbm(basis_grad.reshape(PARTS, batches, rows, size)),
+        in_hbm(weights),
+        in_hbm(weight_grad),
+        in_hbm(fn_atom.reshape(-1, size)),
+        in_hbm(batch_atom.reshape(1, -1)),
+    )
+
+
+def combine_kernel(
+    region, basis, field, moments, hot, grad_columns, *rest, owner_rows, slabs, width, step
+):
+    *pieces, product_out, out, stage, matrix, energies = rest
+    batches, blocks, points, size = basis.shape
+    me = lax.axis_index("grid")
+    half = (width - 1) // 2
+    stage_rows(stage, pieces[0], pieces[1:slabs], pieces[slabs:], SHARE)
+    rows = [region[me, position] for position in range(blocks)]
+    found = [owner_and_slot(region, me, position, owner_rows) for position in range(blocks)]
+    totals = [[jnp.zeros((8, size), F32) for _ in range(blocks)] for _ in range(PARTS)]
+    for p in range(blocks):
+        owner, slot, count = found[p]
+        first = jnp.bitwise_xor(me, owner) * TRAVEL
+        for q in range(blocks):
+            k = rows[q] - rows[p] + half
+            place = jnp.where(
+                k == 0,
+                travel_place(slot, count, 0),
+                jnp.where(k == 1, travel_place(slot, count, 1), travel_place(slot, count, 2)),
+            )
+            inside = jnp.logical_and(k >= 0, k < width)
+            tile = stage[first + place].astype(F32)
+            tile = jnp.where(inside, tile, 0.0)
+            matrix[p * size : (p + 1) * size, q * size : (q + 1) * size] = tile.astype(BF16)
+            turned = tile.T
+            for c in range(PARTS):
+                terms = turned * moments[c, q * size : (q + 1) * size, p * size : (p + 1) * size]
+                totals[c][p] = totals[c][p] + jnp.sum(terms.reshape(-1, 8, size), axis=0)
+    derivative = [
+        jnp.concatenate([jnp.sum(total, axis=0, keepdims=True) for total in totals[c]], axis=1) for c in range(PARTS)
+    ]
+
+    energies[...] = jnp.zeros_like(energies)
+    lanes = lax.broadcasted_iota(jnp.int32, (points, size), 1)
+
+    @pl.loop(0, batches // step)
+    def _(group):
+        left = [
+            jnp.concatenate([basis[group * step + inner, p] for p in range(blocks)], axis=1) for inner in range(step)
+        ]
+        product = jnp.dot(jnp.concatenate(left, axis=0), matrix[...], preferred_element_type=F32)
+        for inner in range(step):
+            batch = group * step + inner
+            energy = jnp.zeros((points, size), F32)
+            for q in range(blocks):
+                part = product[inner * points : (inner + 1) * points, q * size : (q + 1) * size]
+                product_out[batch, q] = part.astype(BF16)
+                energy = energy + part * field[batch, q].astype(F32)
+            energy = jnp.sum(energy, axis=1, keepdims=True)
+            energies[...] = jnp.where(lanes == batch, energy, energies[...])
+
+    lefts = []
+    for c in range(PARTS):
+        term = jnp.sum(energies[...] * grad_columns[c], axis=0, keepdims=True)
+        lefts.append(jnp.concatenate([-2.0 * derivative[c], term], axis=1))
+    left = jnp.concatenate(lefts, axis=0)
+    high, middle, low = (piece.astype(F32) for piece in split(left))
+    left = jnp.concatenate([high, middle, low, jnp.zeros((16 - 3 * PARTS, left.shape[1]), F32)], axis=0).astype(BF16)
+    chunk = out.shape[-1]
+    for device in range(out.shape[1]):
+        sums = lax.dot_general(
+            left, hot[device * chunk : (device + 1) * chunk, :], NT, preferred_element_type=F32
+        )
+        value = sums[:PARTS] + sums[PARTS : 2 * PARTS] + sums[2 * PARTS : 3 * PARTS]
+        for slab in range(slabs):
+            out[slab, device] = value
+
+
+def combine(region, prepared, pieces, shapes):
+    basis, field, moments, hot, grad_columns = prepared
+    slabs, atom_devices, atom_total, points, blocks, width, owner_rows = shapes
+    batches, _, _, size = basis.shape
+    step = 4 if batches % 4 == 0 else 1
+    vmem = pl.BlockSpec(memory_space=pltpu.VMEM)
+    return pl.pallas_call(
+        functools.partial(combine_kernel, owner_rows=owner_rows, slabs=slabs, width=width, step=step),
+        out_shape=(
+            jax.ShapeDtypeStruct(basis.shape, BF16),
+            jax.ShapeDtypeStruct((slabs, atom_devices, PARTS, atom_total // atom_devices), F32),
+        ),
+        in_specs=[pl.BlockSpec(memory_space=pltpu.SMEM)] + [vmem] * (5 + len(pieces)),
+        out_specs=(vmem, vmem),
+        scratch_shapes=[
+            pltpu.VMEM((slabs * TRAVEL, size, size), BF16),
+            pltpu.VMEM((blocks * size, blocks * size), BF16),
+            pltpu.VMEM((points, size), F32),
+        ],
+        compiler_params=pltpu.CompilerParams(vmem_limit_bytes=VMEM_LIMIT),
+    )(in_hbm(region), basis, field, moments, hot, grad_columns, *pieces)
+
+
+def write_kernel(pattern, product, out, wide, staged, sems):
+    batches, blocks, points, size = product.shape
+
+    def copy(batch):
+        return pltpu.make_async_copy(staged.at[batch], out.at[batch], sems.at[batch])
+
+    @pl.loop(0, batches // 2)
+    def _(pair):
+        for inner in range(2):
+            batch = pair * 2 + inner
+            for t in range(blocks):
+                wide[inner, pl.ds(t, points, stride=blocks), :] = product[batch, pattern[t, batch]].astype(F32)
+            staged[batch] = wide[inner].astype(BF16)
+            copy(batch).start()
+
+    @pl.loop(0, batches)
+    def _(batch):
+        copy(batch).wait()
+
+
+def write(pattern, product):
+    batches, blocks, points, size = product.shape
+    shape = (batches, points * blocks, size)
+    return pl.pallas_call(
+        write_kernel,
+        out_shape=jax.ShapeDtypeStruct(shape, BF16),
+        in_specs=[pl.BlockSpec(memory_space=pltpu.SMEM), pl.BlockSpec(memory_space=pltpu.VMEM)],
+        out_specs=pl.BlockSpec(memory_space=pl.ANY),
+        scratch_shapes=[
+            pltpu.VMEM((2, points * blocks, size), F32),
+            pltpu.VMEM(shape, BF16),
+            pltpu.SemaphoreType.DMA((batches,)),
+        ],
+        compiler_params=pltpu.CompilerParams(vmem_limit_bytes=VMEM_LIMIT),
+        cost_estimate=pl.CostEstimate(flops=0, bytes_accessed=4 * math.prod(shape), transcendentals=0),
+    )(in_hbm(pattern.T), product)
+
+
+def swap_halves(near, ready, atom_devices):
+    near, ready = lax.optimization_barrier((near, ready))
+    swap = [(i, i ^ 1) for i in range(atom_devices)]
+    return near, [lax.ppermute(piece, "atoms", swap) for piece in near], ready
+
+
+def sum_parts(partial_grad):
+    parts = partial_grad.reshape((-1,) + partial_grad.shape[2:])
+    parts = lax.all_to_all(parts, ("grid", "atoms"), split_axis=0, concat_axis=0, tiled=True)
+    return jnp.sum(parts, axis=0)
+
+
 def local(
     basis,
     basis_grad,
@@ -346,18 +616,24 @@
     slabs = lax.axis_size("grid")
     atom_devices = lax.axis_size("atoms")
     atom_total = fn_atom.shape[0] // (10 * slabs * atom_devices) * slabs * atom_devices
+    shapes = (slabs, atom_devices, atom_total, points, blocks, width, owner_rows)
     own, near = fetch_rows(region, density, slabs, SHARE)
-    basis_wide, field_wide = relayout(
+    if region.shape[1] == blocks:
+        ready = prepare(
+            region, pattern, basis, exchange_field, basis_grad, weights, weight_grad, fn_atom, batch_atom, atom_total
+        )
+        near, far, ready = swap_halves(near, ready, atom_devices)
+        product, partial_grad = combine(region, ready, [own, *near, *far], shapes)
+        gradient = sum_parts(partial_grad)
+        contracted = write(pattern, product)
+        return contracted.reshape(basis.shape), gradient
+    ready = relayout(
         in_hbm(basis.reshape(batches, points * blocks, size)),
         in_hbm(exchange_field.reshape(batches, points * blocks, size)),
         points,
         blocks,
     )
-    near, basis_wide, field_wide = lax.optimization_barrier((near, basis_wide, field_wide))
-    swap = [(i, i ^ 1) for i in range(atom_devices)]
-    far = [lax.ppermute(piece, "atoms", swap) for piece in near]
-    pieces = [own, *near, *far]
-    shapes = (slabs, atom_devices, atom_total, points, blocks, width, owner_rows)
+    near, far, (basis_wide, field_wide) = swap_halves(near, ready, atom_devices)
     tiles, partial_grad = partial_gradient(
         region,
         pattern,
@@ -368,19 +644,12 @@
         weight_grad,
         fn_atom,
         batch_atom,
-        pieces,
+        [own, *near, *far],
         shapes,
     )
-    chunk = atom_total // atom_devices
-    parts = lax.all_to_all(
-        partial_grad.reshape(slabs * atom_devices, PARTS, chunk),
-        ("grid", "atoms"),
-        split_axis=0,
-        concat_axis=0,
-        tiled=True,
-    )
+    gradient = sum_parts(partial_grad)
     contracted = contract(region, pattern, basis_wide, tiles, points, blocks, width)
-    return contracted.reshape(basis.shape), jnp.sum(parts, axis=0)
+    return contracted.reshape(basis.shape), gradient
 
 
 def solution(mesh):

time: 50.9 us -> 38.5 us (0.76)
  Pallas kernels: 33.5 us -> 18.5 us
  waiting for transfers between devices: 0.83 us -> 5.91 us
  local copies, waits for them, and re-layouts: 3.28 us -> 0 us
  starting transfers between devices: 11.3 us -> 12.4 us
    pallas_call x3, Pallas kernels: 31.7 us -> 16.7 us  [the longest x1 10.2 us: prepare(): pl.pallas_call(functools.partial(prepare_kernel, points=points, blocks=bl...]
    all_to_all x1, waiting for transfers between devices: 0.01 us -> 4.71 us  [sum_parts(): lax.all_to_all(parts, ('grid', 'atoms'), split_axis=0, concat_axis=0, til...]
    unnamed x17 -> x0, local copies, waits for them, and re-layouts: 3.01 us -> none
    all_to_all x1, starting transfers between devices: 3.5 us -> 6.13 us  [sum_parts(): lax.all_to_all(parts, ('grid', 'atoms'), split_axis=0, concat_axis=0, til...]
    ppermute x6, starting transfers between devices: 7.78 us -> 6.27 us  [the longest x3 5.62 us: fetch_rows(): lax.ppermute(piece, 'grid', [(i, i ^ shift) for i in range(slabs)])]
  transfers between devices with their start and end apart: 7 -> 7, of which waited for: 3 -> 4; matrix products, arithmetic and copies ran while one was open for 1% -> 0% of each run, Pallas kernels for 34% -> 32%
where the time goes in v3:
time: 38.5 us; the launch traced here: 38.1 us
  Pallas kernels  18.5 us (48%)
  starting transfers between devices  12.4 us (32%)
  waiting for transfers between devices  5.91 us (15%)
  between operations  0.7 us (2%)
  other arithmetic  0.62 us (2%)
    pallas_call x1, Pallas kernels, prepare(): pl.pallas_call(functools.partial(prepare_kernel, points=points, blocks=bl...  10.2 us
    all_to_all x1, starting transfers between devices, sum_parts(): lax.all_to_all(parts, ('grid', 'atoms'), split_axis=0, concat_axis=0, til...  6.13 us
    ppermute x3, starting transfers between devices, fetch_rows(): lax.ppermute(piece, 'grid', [(i, i ^ shift) for i in range(slabs)])  5.62 us
    all_to_all x1, waiting for transfers between devices, sum_parts(): lax.all_to_all(parts, ('grid', 'atoms'), split_axis=0, concat_axis=0, til...  4.71 us
    pallas_call x1, Pallas kernels, combine(): pl.pallas_call(functools.partial(combine_kernel, owner_rows=owner_rows, s...  4.32 us
    pallas_call x1, Pallas kernels, write(): pl.pallas_call(write_kernel, out_shape=jax.ShapeDtypeStruct(shape, BF16),...  2.18 us
    pallas_call x1, Pallas kernels, rows_to_send(): pl.pallas_call(functools.partial(send_kernel, share=share), out_shape=[ja...  1.84 us
    ppermute x3, waiting for transfers between devices, swap_halves(): return (near, [lax.ppermute(piece, 'atoms', swap) for piece in near], ready)  1.2 us
  transfers between devices with their start and end apart: 7, of which 4 were waited for; matrix products, arithmetic and copies ran while one was open for 0% of the time, Pallas kernels for 32%

profile of v3, /device:TPU:0, one launch (start us, length us, event | category | flops | bytes accessed | tf_op | source)
XLA Modules:
  0.0 38.1 jit_solution(8848281529593024229)
XLA Ops:
  0.6 1.8 %shard_map.113 = (bf16[5,128,128]{2,1,0:T(8,128)(2,1)S(1)}, bf16[5,64,128]{2,1,0:T(8,128)(2,1)S(1)}, bf16[5,64,128]{2,1,0:T(8,128)(2,1)S(1)}, bf16[5,64,128]{2,1,0:T(8,128)(2,1)S(1)}) custom-call(s32[4,4]{1,0:T(4,128)} %region.5, bf16[15,3,128,128]{3,2,1,0:T(8,128)(2,1)} %density.1), custom_call_target="tpu_custom_call" | custom-call | tf_op jit(solution)/shard_map/pallas_call | solution.py:84
  2.5 3.0 %collective-permute-start = (bf16[5,64,128]{2,1,0:T(8,128)(2,1)S(1)}, bf16[5,64,128]{2,1,0:T(8,128)(2,1)S(1)}, u32[]{:S(2)}, u32[]{:S(2)}) collective-permute-start(bf16[5,64,128]{2,1,0:T(8,128)(2,1)S(1)} %get-tuple-element.21), channel_id=1, source_target_pairs={{0,4},{4,0},{8,12},{12,8},{1,5},{5,1},{9,13},{13,9},{2,6},{6,2},{1... | collective-permute-start | bytes 245768 | tf_op jit(solution)/shard_map/ppermute | solution.py:98
  5.5 2.6 %collective-permute-start.1 = (bf16[5,64,128]{2,1,0:T(8,128)(2,1)S(1)}, bf16[5,64,128]{2,1,0:T(8,128)(2,1)S(1)}, u32[]{:S(2)}, u32[]{:S(2)}) collective-permute-start(bf16[5,64,128]{2,1,0:T(8,128)(2,1)S(1)} %get-tuple-element.22), channel_id=1, source_target_pairs={{0,8},{4,12},{8,0},{12,4},{1,9},{5,13},{9,1},{13,5},{2,10},{6,14},... | collective-permute-start | bytes 245768 | tf_op jit(solution)/shard_map/ppermute | solution.py:98
  8.1 0.0 collective-permute-start.2
  8.1 10.2 %shard_map.114 = (bf16[16,4,128,128]{3,2,1,0:T(8,128)(2,1)S(1)}, bf16[16,4,128,128]{3,2,1,0:T(8,128)(2,1)S(1)}, f32[3,512,512]{2,1,0:T(8,128)S(1)}, bf16[768,640]{1,0:T(8,128)(2,1)S(1)}, f32[3,128,128]{2,1,0:T(8,128)S(1)}) custom-call(s32[4,4]{1,0:T(4,128)} %region.5, s32[4,16]{1,0:T(4,128)} %bitcast.9, bf16[16,512,128]{2,1,0:T(8,128)(2,1)} %bitcast.12, ...), custom_call_target="tpu_custom_call" | custom-call | flops 3221225472 | bytes 10485760 | tf_op jit(solution)/shard_map/pallas_call | solution.py:421
  18.3 0.0 collective-permute-done.rest_1_
  18.3 0.0 collective-permute-done.1.rest_2_
  18.3 0.0 collective-permute-done.2.rest_3_
  18.3 0.1 collective-permute-start.3
  18.4 0.5 %collective-permute-start.4 = (bf16[5,64,128]{2,1,0:T(8,128)(2,1)S(1)}, bf16[5,64,128]{2,1,0:T(8,128)(2,1)S(1)}, u32[]{:S(2)}, u32[]{:S(2)}) collective-permute-start(bf16[5,64,128]{2,1,0:T(8,128)(2,1)S(1)} %collective-permute-done.1.rest_2_), channel_id=1, source_target_pairs={{0,1},{1,0},{2,3},{3,2},{4,5},{5,4},{6,7},{7,6},{8,9},{9,8},{10,11... | collective-permute-start | bytes 245768 | tf_op jit(solution)/shard_map/ppermute | solution.py:593
  18.9 0.1 collective-permute-start.5
  18.9 0.7 %collective-permute-done.3.rest_4_ = bf16[5,64,128]{2,1,0:T(8,128)(2,1)S(1)} collective-permute-done((bf16[5,64,128]{2,1,0:T(8,128)(2,1)S(1)}, bf16[5,64,128]{2,1,0:T(8,128)(2,1)S(1)}, u32[]{:S(2)}, u32[]{:S(2)}) %collective-permute-start.3) | collective-permute-done | bytes 81952 | tf_op jit(solution)/shard_map/ppermute | solution.py:593
  19.6 0.2 collective-permute-done.4.rest_5_
  19.8 0.4 collective-permute-done.5.rest_6_
  20.1 4.3 %shard_map.115 = (bf16[16,4,128,128]{3,2,1,0:T(8,128)(2,1)S(1)}, f32[4,4,3,192]{3,2,1,0:T(4,128)}) custom-call(s32[4,4]{1,0:T(4,128)} %region.5, bf16[16,4,128,128]{3,2,1,0:T(8,128)(2,1)S(1)} %get-tuple-element.29.basis, bf16[16,4,128,128]{3,2,1,0:T(8,128)(2,1)S(1)} %get-tuple-element.30.field, f32[3,512,512]{2,1,0:T(8,128)S(1)} %get-tuple-element.31.moments, ...), custom_call_target="tpu_custom_call" | custom-call | tf_op jit(solution)/shard_map/pallas_call | solution.py:535
  24.5 6.1 %all-to-all-start = ((f32[16,3,192]{2,1,0:T(4,128)}), f32[16,3,192]{2,1,0:T(4,128)S(1)}, u32[]{:S(2)}, u32[]{:S(2)}) async-start(f32[16,3,192]{2,1,0:T(4,128)} %bitcast.7), calls=%async_computation | async-start | bytes 131072 | tf_op jit(solution)/shard_map/all_to_all | solution.py:598
  30.6 2.2 %shard_map.116 = bf16[16,512,128]{2,1,0:T(8,128)(2,1)} custom-call(s32[4,16]{1,0:T(4,128)} %bitcast.10, bf16[16,4,128,128]{3,2,1,0:T(8,128)(2,1)S(1)} %get-tuple-element.38.product), custom_call_target="tpu_custom_call" | custom-call | bytes 4194304 | tf_op jit(solution)/shard_map/pallas_call | solution.py:575
  32.8 4.7 %all-to-all-done = f32[16,3,192]{2,1,0:T(4,128)S(1)} async-done(((f32[16,3,192]{2,1,0:T(4,128)}), f32[16,3,192]{2,1,0:T(4,128)S(1)}, u32[]{:S(2)}, u32[]{:S(2)}) %all-to-all-start) | async-done | bytes 36896 | tf_op jit(solution)/shard_map/all_to_all | solution.py:598
  37.5 0.6 %reduce_sum.9 = f32[3,192]{1,0:T(4,128)} reduce(f32[16,3,192]{2,1,0:T(4,128)S(1)} %all-to-all-done, f32[]{:T(128)} %constant.0.clone.1), dimensions={0}, to_apply=%region_0.0 | reduce | flops 8640 | bytes 39172 | tf_op jit(solution)/shard_map/reduce_sum | solution.py:599
Async XLA Ops:
  2.5 15.8 %collective-permute-start = (bf16[5,64,128]{2,1,0:T(8,128)(2,1)S(1)}, bf16[5,64,128]{2,1,0:T(8,128)(2,1)S(1)}, u32[]{:S(2)}, u32[]{:S(2)}) collective-permute-start(bf16[5,64,128]{2,1,0:T(8,128)(2,1)S(1)} %get-tuple-element.21), channel_id=1, source_target_pairs={{0,4},{4,0},{8,12},{12,8},{1,5},{5,1},{9,13},{13,9},{2,6},{6,2},{1... | collective-permute-start | bytes 245768 | tf_op jit(solution)/shard_map/ppermute | solution.py:98
  5.5 12.8 %collective-permute-start.1 = (bf16[5,64,128]{2,1,0:T(8,128)(2,1)S(1)}, bf16[5,64,128]{2,1,0:T(8,128)(2,1)S(1)}, u32[]{:S(2)}, u32[]{:S(2)}) collective-permute-start(bf16[5,64,128]{2,1,0:T(8,128)(2,1)S(1)} %get-tuple-element.22), channel_id=1, source_target_pairs={{0,8},{4,12},{8,0},{12,4},{1,9},{5,13},{9,1},{13,5},{2,10},{6,14},... | collective-permute-start | bytes 245768 | tf_op jit(solution)/shard_map/ppermute | solution.py:98
  8.1 10.2 %collective-permute-start.2 = (bf16[5,64,128]{2,1,0:T(8,128)(2,1)S(1)}, bf16[5,64,128]{2,1,0:T(8,128)(2,1)S(1)}, u32[]{:S(2)}, u32[]{:S(2)}) collective-permute-start(bf16[5,64,128]{2,1,0:T(8,128)(2,1)S(1)} %get-tuple-element.23), channel_id=1, source_target_pairs={{0,12},{4,8},{8,4},{12,0},{1,13},{5,9},{9,5},{13,1},{2,14},{6,10},... | collective-permute-start | bytes 245768 | tf_op jit(solution)/shard_map/ppermute | solution.py:98
  18.3 1.3 %collective-permute-start.3 = (bf16[5,64,128]{2,1,0:T(8,128)(2,1)S(1)}, bf16[5,64,128]{2,1,0:T(8,128)(2,1)S(1)}, u32[]{:S(2)}, u32[]{:S(2)}) collective-permute-start(bf16[5,64,128]{2,1,0:T(8,128)(2,1)S(1)} %collective-permute-done.rest_1_), channel_id=1, source_target_pairs={{0,1},{1,0},{2,3},{3,2},{4,5},{5,4},{6,7},{7,6},{8,9},{9,8},{10,11... | collective-permute-start | bytes 245768 | tf_op jit(solution)/shard_map/ppermute | solution.py:593
  18.4 1.4 %collective-permute-start.4 = (bf16[5,64,128]{2,1,0:T(8,128)(2,1)S(1)}, bf16[5,64,128]{2,1,0:T(8,128)(2,1)S(1)}, u32[]{:S(2)}, u32[]{:S(2)}) collective-permute-start(bf16[5,64,128]{2,1,0:T(8,128)(2,1)S(1)} %collective-permute-done.1.rest_2_), channel_id=1, source_target_pairs={{0,1},{1,0},{2,3},{3,2},{4,5},{5,4},{6,7},{7,6},{8,9},{9,8},{10,11... | collective-permute-start | bytes 245768 | tf_op jit(solution)/shard_map/ppermute | solution.py:593
  18.9 1.3 %collective-permute-start.5 = (bf16[5,64,128]{2,1,0:T(8,128)(2,1)S(1)}, bf16[5,64,128]{2,1,0:T(8,128)(2,1)S(1)}, u32[]{:S(2)}, u32[]{:S(2)}) collective-permute-start(bf16[5,64,128]{2,1,0:T(8,128)(2,1)S(1)} %collective-permute-done.2.rest_3_), channel_id=1, source_target_pairs={{0,1},{1,0},{2,3},{3,2},{4,5},{5,4},{6,7},{7,6},{8,9},{9,8},{10,11... | collective-permute-start | bytes 245768 | tf_op jit(solution)/shard_map/ppermute | solution.py:593
  24.5 13.0 %all-to-all-start = ((f32[16,3,192]{2,1,0:T(4,128)}), f32[16,3,192]{2,1,0:T(4,128)S(1)}, u32[]{:S(2)}, u32[]{:S(2)}) async-start(f32[16,3,192]{2,1,0:T(4,128)} %bitcast.7), calls=%async_computation | async-start | bytes 131072 | tf_op jit(solution)/shard_map/all_to_all | solution.py:598

commit v4 on v3

--- a/solution.py
+++ b/solution.py
@@ -184,6 +184,7 @@
     batch = pl.program_id(0)
     batches = pl.num_programs(0)
     me = lax.axis_index("grid")
+    me_atoms = lax.axis_index("atoms")
     size = tiles.shape[-1]
     region_size = region.shape[1]
 
@@ -239,7 +240,7 @@
         left = jnp.concatenate(lefts, axis=1).astype(BF16)
         chunk = out.shape[-1]
         scale = [jnp.sum(energy_sums[c], axis=1, keepdims=True) for c in range(PARTS)]
-        for device in range(out.shape[1]):
+        for device in range(out.shape[0]):
             atoms = lax.broadcasted_iota(jnp.int32, (chunk, size), 0) + device * chunk
             hot = [
                 jnp.where(atoms == fn_atom[pl.ds(region[me, position], 1), :], 1.0, 0.0).astype(BF16)
@@ -251,8 +252,7 @@
             for c in range(PARTS):
                 value = found[c : c + 1] + found[PARTS + c : PARTS + c + 1] + found[2 * PARTS + c : 2 * PARTS + c + 1]
                 value = value + jnp.sum(jnp.where(mine, scale[c], 0.0), axis=0, keepdims=True)
-                for slab in range(slabs):
-                    out[slab, device, c : c + 1, :] = value
+                out[jnp.bitwise_xor(me_atoms, device), c : c + 1, :] = value
 
 
 def partial_gradient(
@@ -268,7 +268,7 @@
     block = pl.BlockSpec((1, points, columns), lambda b, *_: (b, 0, 0))
     whole = pl.BlockSpec(memory_space=pltpu.VMEM)
     tile_shape = (region_size * width + 1, size, size)
-    out_shape = (slabs, atom_devices, PARTS, atom_total // atom_devices)
+    out_shape = (atom_devices, PARTS, atom_total // atom_devices)
     return pl.pallas_call(
         functools.partial(
             gradient_kernel, points=points, blocks=blocks, width=width, owner_rows=owner_rows, slabs=slabs
@@ -463,6 +463,7 @@
     *pieces, product_out, out, stage, matrix, energies = rest
     batches, blocks, points, size = basis.shape
     me = lax.axis_index("grid")
+    me_atoms = lax.axis_index("atoms")
     half = (width - 1) // 2
     stage_rows(stage, pieces[0], pieces[1:slabs], pieces[slabs:], SHARE)
     rows = [region[me, position] for position in range(blocks)]
@@ -472,6 +473,9 @@
         owner, slot, count = found[p]
         first = jnp.bitwise_xor(me, owner) * TRAVEL
         for q in range(blocks):
+            if abs(q - p) > half:
+                matrix[p * size : (p + 1) * size, q * size : (q + 1) * size] = jnp.zeros((size, size), BF16)
+                continue
             k = rows[q] - rows[p] + half
             place = jnp.where(
                 k == 0,
@@ -517,13 +521,12 @@
     high, middle, low = (piece.astype(F32) for piece in split(left))
     left = jnp.concatenate([high, middle, low, jnp.zeros((16 - 3 * PARTS, left.shape[1]), F32)], axis=0).astype(BF16)
     chunk = out.shape[-1]
-    for device in range(out.shape[1]):
+    for device in range(out.shape[0]):
         sums = lax.dot_general(
             left, hot[device * chunk : (device + 1) * chunk, :], NT, preferred_element_type=F32
         )
         value = sums[:PARTS] + sums[PARTS : 2 * PARTS] + sums[2 * PARTS : 3 * PARTS]
-        for slab in range(slabs):
-            out[slab, device] = value
+        out[jnp.bitwise_xor(me_atoms, device)] = value
 
 
 def combine(region, prepared, pieces, shapes):
@@ -536,7 +539,7 @@
         functools.partial(combine_kernel, owner_rows=owner_rows, slabs=slabs, width=width, step=step),
         out_shape=(
             jax.ShapeDtypeStruct(basis.shape, BF16),
-            jax.ShapeDtypeStruct((slabs, atom_devices, PARTS, atom_total // atom_devices), F32),
+            jax.ShapeDtypeStruct((atom_devices, PARTS, atom_total // atom_devices), F32),
         ),
         in_specs=[pl.BlockSpec(memory_space=pltpu.SMEM)] + [vmem] * (5 + len(pieces)),
         out_specs=(vmem, vmem),
@@ -593,10 +596,21 @@
     return near, [lax.ppermute(piece, "atoms", swap) for piece in near], ready
 
 
-def sum_parts(partial_grad):
-    parts = partial_grad.reshape((-1,) + partial_grad.shape[2:])
-    parts = lax.all_to_all(parts, ("grid", "atoms"), split_axis=0, concat_axis=0, tiled=True)
-    return jnp.sum(parts, axis=0)
+def exchange(values, axis, bit):
+    return lax.ppermute(values, axis, [(i, i ^ bit) for i in range(lax.axis_size(axis))])
+
+
+def sum_parts(partial_grad, slabs):
+    parts = partial_grad
+    while parts.shape[0] > 1:
+        half = parts.shape[0] // 2
+        parts = parts[:half] + exchange(parts[half:], "atoms", half)
+    total = parts[0]
+    bit = 1
+    while bit < slabs:
+        total = total + exchange(total, "grid", bit)
+        bit *= 2
+    return total
 
 
 def local(
@@ -624,7 +638,7 @@
         )
         near, far, ready = swap_halves(near, ready, atom_devices)
         product, partial_grad = combine(region, ready, [own, *near, *far], shapes)
-        gradient = sum_parts(partial_grad)
+        gradient = sum_parts(partial_grad, slabs)
         contracted = write(pattern, product)
         return contracted.reshape(basis.shape), gradient
     ready = relayout(
@@ -647,7 +661,7 @@
         [own, *near, *far],
         shapes,
     )
-    gradient = sum_parts(partial_grad)
+    gradient = sum_parts(partial_grad, slabs)
     contracted = contract(region, pattern, basis_wide, tiles, points, blocks, width)
     return contracted.reshape(basis.shape), gradient
 

time: 38.5 us -> 37.6 us (0.977)
  waiting for transfers between devices: 5.91 us -> 7.14 us
  starting transfers between devices: 12.4 us -> 11.3 us
  Pallas kernels: 18.5 us -> 17.6 us
    all_to_all x1 -> x0, starting transfers between devices: 6.13 us -> none  [sum_parts(): lax.all_to_all(parts, ('grid', 'atoms'), split_axis=0, concat_axis=0, til...]
    ppermute x0 -> x4, waiting for transfers between devices: none -> 5.93 us  [exchange(): lax.ppermute(values, axis, [(i, i ^ bit) for i in range(lax.axis_size(axi...]
    ppermute x0 -> x4, starting transfers between devices: none -> 4.87 us  [exchange(): lax.ppermute(values, axis, [(i, i ^ bit) for i in range(lax.axis_size(axi...]
    all_to_all x1 -> x0, waiting for transfers between devices: 4.71 us -> none  [sum_parts(): lax.all_to_all(parts, ('grid', 'atoms'), split_axis=0, concat_axis=0, til...]
    pallas_call x1, Pallas kernels: 4.32 us -> 3.47 us  [combine(): pl.pallas_call(functools.partial(combine_kernel, owner_rows=owner_rows, s...]
    reduce_sum x1 -> x0, other arithmetic: 0.62 us -> none  [sum_parts(): return jnp.sum(parts, axis=0)]
    add x0 -> x3, other arithmetic: none -> 0.6 us  [the longest x2 0.6 us: sum_parts(): total = total + exchange(total, 'grid', bit)]
  transfers between devices with their start and end apart: 7 -> 10, of which waited for: 4 -> 6; matrix products, arithmetic and copies ran while one was open for 0% -> 0% of each run, Pallas kernels for 32% -> 33%
where the time goes in v4:
time: 37.6 us; the launch traced here: 37.3 us
  Pallas kernels  17.6 us (47%)
  starting transfers between devices  11.3 us (30%)
  waiting for transfers between devices  7.14 us (19%)
  between operations  0.7 us (2%)
  other arithmetic  0.61 us (2%)
    pallas_call x1, Pallas kernels, prepare(): pl.pallas_call(functools.partial(prepare_kernel, points=points, blocks=bl...  10.2 us
    ppermute x4, waiting for transfers between devices, exchange(): lax.ppermute(values, axis, [(i, i ^ bit) for i in range(lax.axis_size(axi...  5.93 us
    ppermute x3, starting transfers between devices, fetch_rows(): lax.ppermute(piece, 'grid', [(i, i ^ shift) for i in range(slabs)])  5.73 us
    ppermute x4, starting transfers between devices, exchange(): lax.ppermute(values, axis, [(i, i ^ bit) for i in range(lax.axis_size(axi...  4.87 us
    pallas_call x1, Pallas kernels, combine(): pl.pallas_call(functools.partial(combine_kernel, owner_rows=owner_rows, s...  3.47 us
    pallas_call x1, Pallas kernels, write(): pl.pallas_call(write_kernel, out_shape=jax.ShapeDtypeStruct(shape, BF16),...  2.18 us
    pallas_call x1, Pallas kernels, rows_to_send(): pl.pallas_call(functools.partial(send_kernel, share=share), out_shape=[ja...  1.78 us
    ppermute x3, waiting for transfers between devices, swap_halves(): return (near, [lax.ppermute(piece, 'atoms', swap) for piece in near], ready)  1.2 us
  transfers between devices with their start and end apart: 10, of which 6 were waited for; matrix products, arithmetic and copies ran while one was open for 0% of the time, Pallas kernels for 33%

profile of v4, /device:TPU:0, one launch (start us, length us, event | category | flops | bytes accessed | tf_op | source)
XLA Modules:
  0.0 37.3 jit_solution(14004780321973367467)
XLA Ops:
  0.6 1.8 %shard_map.113 = (bf16[5,128,128]{2,1,0:T(8,128)(2,1)S(1)}, bf16[5,64,128]{2,1,0:T(8,128)(2,1)S(1)}, bf16[5,64,128]{2,1,0:T(8,128)(2,1)S(1)}, bf16[5,64,128]{2,1,0:T(8,128)(2,1)S(1)}) custom-call(s32[4,4]{1,0:T(4,128)} %region.5, bf16[15,3,128,128]{3,2,1,0:T(8,128)(2,1)} %density.1), custom_call_target="tpu_custom_call" | custom-call | tf_op jit(solution)/shard_map/pallas_call | solution.py:84
  2.4 3.1 %collective-permute-start = (bf16[5,64,128]{2,1,0:T(8,128)(2,1)S(1)}, bf16[5,64,128]{2,1,0:T(8,128)(2,1)S(1)}, u32[]{:S(2)}, u32[]{:S(2)}) collective-permute-start(bf16[5,64,128]{2,1,0:T(8,128)(2,1)S(1)} %get-tuple-element.21), channel_id=1, source_target_pairs={{0,4},{4,0},{8,12},{12,8},{1,5},{5,1},{9,13},{13,9},{2,6},{6,2},{1... | collective-permute-start | bytes 245768 | tf_op jit(solution)/shard_map/ppermute | solution.py:98
  5.5 2.6 %collective-permute-start.1 = (bf16[5,64,128]{2,1,0:T(8,128)(2,1)S(1)}, bf16[5,64,128]{2,1,0:T(8,128)(2,1)S(1)}, u32[]{:S(2)}, u32[]{:S(2)}) collective-permute-start(bf16[5,64,128]{2,1,0:T(8,128)(2,1)S(1)} %get-tuple-element.22), channel_id=1, source_target_pairs={{0,8},{4,12},{8,0},{12,4},{1,9},{5,13},{9,1},{13,5},{2,10},{6,14},... | collective-permute-start | bytes 245768 | tf_op jit(solution)/shard_map/ppermute | solution.py:98
  8.1 0.1 collective-permute-start.2
  8.2 10.2 %shard_map.114 = (bf16[16,4,128,128]{3,2,1,0:T(8,128)(2,1)S(1)}, bf16[16,4,128,128]{3,2,1,0:T(8,128)(2,1)S(1)}, f32[3,512,512]{2,1,0:T(8,128)S(1)}, bf16[768,640]{1,0:T(8,128)(2,1)S(1)}, f32[3,128,128]{2,1,0:T(8,128)S(1)}) custom-call(s32[4,4]{1,0:T(4,128)} %region.5, s32[4,16]{1,0:T(4,128)} %bitcast.10, bf16[16,512,128]{2,1,0:T(8,128)(2,1)} %bitcast.13, ...), custom_call_target="tpu_custom_call" | custom-call | flops 3221225472 | bytes 10485760 | tf_op jit(solution)/shard_map/pallas_call | solution.py:421
  18.3 0.0 collective-permute-done.rest_1_
  18.3 0.0 collective-permute-done.1.rest_2_
  18.3 0.0 collective-permute-done.2.rest_3_
  18.3 0.1 collective-permute-start.3
  18.4 0.5 %collective-permute-start.4 = (bf16[5,64,128]{2,1,0:T(8,128)(2,1)S(1)}, bf16[5,64,128]{2,1,0:T(8,128)(2,1)S(1)}, u32[]{:S(2)}, u32[]{:S(2)}) collective-permute-start(bf16[5,64,128]{2,1,0:T(8,128)(2,1)S(1)} %collective-permute-done.1.rest_2_), channel_id=1, source_target_pairs={{0,1},{1,0},{2,3},{3,2},{4,5},{5,4},{6,7},{7,6},{8,9},{9,8},{10,11... | collective-permute-start | bytes 245768 | tf_op jit(solution)/shard_map/ppermute | solution.py:596
  18.9 0.1 collective-permute-start.5
  19.0 0.7 %collective-permute-done.3.rest_4_ = bf16[5,64,128]{2,1,0:T(8,128)(2,1)S(1)} collective-permute-done((bf16[5,64,128]{2,1,0:T(8,128)(2,1)S(1)}, bf16[5,64,128]{2,1,0:T(8,128)(2,1)S(1)}, u32[]{:S(2)}, u32[]{:S(2)}) %collective-permute-start.3) | collective-permute-done | bytes 81952 | tf_op jit(solution)/shard_map/ppermute | solution.py:596
  19.7 0.2 collective-permute-done.4.rest_5_
  19.8 0.4 collective-permute-done.5.rest_6_
  20.2 3.5 %shard_map.115 = (bf16[16,4,128,128]{3,2,1,0:T(8,128)(2,1)S(1)}, f32[4,3,192]{2,1,0:T(4,128)S(1)}) custom-call(s32[4,4]{1,0:T(4,128)} %region.5, bf16[16,4,128,128]{3,2,1,0:T(8,128)(2,1)S(1)} %get-tuple-element.29.basis, bf16[16,4,128,128]{3,2,1,0:T(8,128)(2,1)S(1)} %get-tuple-element.30.field, f32[3,512,512]{2,1,0:T(8,128)S(1)} %get-tuple-element.31.moments, ...), custom_call_target="tpu_custom_call" | custom-call | tf_op jit(solution)/shard_map/pallas_call | solution.py:538
  23.7 1.7 %collective-permute-start.6 = (f32[2,3,192]{2,1,0:T(4,128)S(1)}, f32[2,3,192]{2,1,0:T(4,128)S(1)}, u32[]{:S(2)}, u32[]{:S(2)}) collective-permute-start(f32[2,3,192]{2,1,0:T(4,128)S(1)} %slice.13), channel_id=1, source_target_pairs={{0,2},{1,3},{2,0},{3,1},{4,6},{5,7},{6,4},{7,5},{8,10},{9,11},{10,... | collective-permute-start | bytes 13832 | tf_op jit(solution)/shard_map/ppermute | solution.py:600
  25.4 2.0 %collective-permute-done.6 = f32[2,3,192]{2,1,0:T(4,128)S(1)} collective-permute-done((f32[2,3,192]{2,1,0:T(4,128)S(1)}, f32[2,3,192]{2,1,0:T(4,128)S(1)}, u32[]{:S(2)}, u32[]{:S(2)}) %collective-permute-start.6) | collective-permute-done | bytes 4640 | tf_op jit(solution)/shard_map/ppermute | solution.py:600
  27.4 0.0 collective-permute-start.7
  27.4 1.2 %collective-permute-done.7 = f32[1,3,192]{2,1,0:T(4,128)S(1)} collective-permute-done((f32[1,3,192]{2,1,0:T(4,128)S(1)}, f32[1,3,192]{2,1,0:T(4,128)S(1)}, u32[]{:S(2)}, u32[]{:S(2)}) %collective-permute-start.7) | collective-permute-done | bytes 2336 | tf_op jit(solution)/shard_map/ppermute | solution.py:600
  28.6 0.8 %collective-permute-start.8 = (f32[3,192]{1,0:T(4,128)S(1)}, f32[3,192]{1,0:T(4,128)S(1)}, u32[]{:S(2)}, u32[]{:S(2)}) collective-permute-start(f32[3,192]{1,0:T(4,128)S(1)} %fusion), channel_id=1, source_target_pairs={{0,4},{4,0},{8,12},{12,8},{1,5},{5,1},{9,13},{13,9},{2,6},{6,2},{1... | collective-permute-start | bytes 6920 | tf_op jit(solution)/shard_map/ppermute | solution.py:600
  29.4 2.8 %collective-permute-done.8 = f32[3,192]{1,0:T(4,128)S(1)} collective-permute-done((f32[3,192]{1,0:T(4,128)S(1)}, f32[3,192]{1,0:T(4,128)S(1)}, u32[]{:S(2)}, u32[]{:S(2)}) %collective-permute-start.8) | collective-permute-done | bytes 2336 | tf_op jit(solution)/shard_map/ppermute | solution.py:600
  32.2 2.3 %collective-permute-start.9 = (f32[3,192]{1,0:T(4,128)S(1)}, f32[3,192]{1,0:T(4,128)S(1)}, u32[]{:S(2)}, u32[]{:S(2)}) collective-permute-start(f32[3,192]{1,0:T(4,128)S(1)} %add.14), channel_id=1, source_target_pairs={{0,8},{4,12},{8,0},{12,4},{1,9},{5,13},{9,1},{13,5},{2,10},{6,14},... | collective-permute-start | bytes 6920 | tf_op jit(solution)/shard_map/ppermute | solution.py:600
  34.5 2.2 %shard_map.116 = bf16[16,512,128]{2,1,0:T(8,128)(2,1)} custom-call(s32[4,16]{1,0:T(4,128)} %bitcast.11, bf16[16,4,128,128]{3,2,1,0:T(8,128)(2,1)S(1)} %get-tuple-element.38.product), custom_call_target="tpu_custom_call" | custom-call | bytes 4194304 | tf_op jit(solution)/shard_map/pallas_call | solution.py:578
  36.7 0.0 collective-permute-done.9
  36.7 0.6 %add.15 = f32[3,192]{1,0:T(4,128)} add(f32[3,192]{1,0:T(4,128)S(1)} %add.14, f32[3,192]{1,0:T(4,128)S(1)} %collective-permute-done.9) | non-fusion elementwise | flops 576 | bytes 6912 | tf_op jit(solution)/shard_map/add | solution.py:611
  (5 shorter events, 0.0 us)
Async XLA Ops:
  2.4 15.9 %collective-permute-start = (bf16[5,64,128]{2,1,0:T(8,128)(2,1)S(1)}, bf16[5,64,128]{2,1,0:T(8,128)(2,1)S(1)}, u32[]{:S(2)}, u32[]{:S(2)}) collective-permute-start(bf16[5,64,128]{2,1,0:T(8,128)(2,1)S(1)} %get-tuple-element.21), channel_id=1, source_target_pairs={{0,4},{4,0},{8,12},{12,8},{1,5},{5,1},{9,13},{13,9},{2,6},{6,2},{1... | collective-permute-start | bytes 245768 | tf_op jit(solution)/shard_map/ppermute | solution.py:98
  5.5 12.8 %collective-permute-start.1 = (bf16[5,64,128]{2,1,0:T(8,128)(2,1)S(1)}, bf16[5,64,128]{2,1,0:T(8,128)(2,1)S(1)}, u32[]{:S(2)}, u32[]{:S(2)}) collective-permute-start(bf16[5,64,128]{2,1,0:T(8,128)(2,1)S(1)} %get-tuple-element.22), channel_id=1, source_target_pairs={{0,8},{4,12},{8,0},{12,4},{1,9},{5,13},{9,1},{13,5},{2,10},{6,14},... | collective-permute-start | bytes 245768 | tf_op jit(solution)/shard_map/ppermute | solution.py:98
  8.1 10.2 %collective-permute-start.2 = (bf16[5,64,128]{2,1,0:T(8,128)(2,1)S(1)}, bf16[5,64,128]{2,1,0:T(8,128)(2,1)S(1)}, u32[]{:S(2)}, u32[]{:S(2)}) collective-permute-start(bf16[5,64,128]{2,1,0:T(8,128)(2,1)S(1)} %get-tuple-element.23), channel_id=1, source_target_pairs={{0,12},{4,8},{8,4},{12,0},{1,13},{5,9},{9,5},{13,1},{2,14},{6,10},... | collective-permute-start | bytes 245768 | tf_op jit(solution)/shard_map/ppermute | solution.py:98
  18.3 1.3 %collective-permute-start.3 = (bf16[5,64,128]{2,1,0:T(8,128)(2,1)S(1)}, bf16[5,64,128]{2,1,0:T(8,128)(2,1)S(1)}, u32[]{:S(2)}, u32[]{:S(2)}) collective-permute-start(bf16[5,64,128]{2,1,0:T(8,128)(2,1)S(1)} %collective-permute-done.rest_1_), channel_id=1, source_target_pairs={{0,1},{1,0},{2,3},{3,2},{4,5},{5,4},{6,7},{7,6},{8,9},{9,8},{10,11... | collective-permute-start | bytes 245768 | tf_op jit(solution)/shard_map/ppermute | solution.py:596
  18.4 1.4 %collective-permute-start.4 = (bf16[5,64,128]{2,1,0:T(8,128)(2,1)S(1)}, bf16[5,64,128]{2,1,0:T(8,128)(2,1)S(1)}, u32[]{:S(2)}, u32[]{:S(2)}) collective-permute-start(bf16[5,64,128]{2,1,0:T(8,128)(2,1)S(1)} %collective-permute-done.1.rest_2_), channel_id=1, source_target_pairs={{0,1},{1,0},{2,3},{3,2},{4,5},{5,4},{6,7},{7,6},{8,9},{9,8},{10,11... | collective-permute-start | bytes 245768 | tf_op jit(solution)/shard_map/ppermute | solution.py:596
  18.9 1.3 %collective-permute-start.5 = (bf16[5,64,128]{2,1,0:T(8,128)(2,1)S(1)}, bf16[5,64,128]{2,1,0:T(8,128)(2,1)S(1)}, u32[]{:S(2)}, u32[]{:S(2)}) collective-permute-start(bf16[5,64,128]{2,1,0:T(8,128)(2,1)S(1)} %collective-permute-done.2.rest_3_), channel_id=1, source_target_pairs={{0,1},{1,0},{2,3},{3,2},{4,5},{5,4},{6,7},{7,6},{8,9},{9,8},{10,11... | collective-permute-start | bytes 245768 | tf_op jit(solution)/shard_map/ppermute | solution.py:596
  23.7 3.7 %collective-permute-start.6 = (f32[2,3,192]{2,1,0:T(4,128)S(1)}, f32[2,3,192]{2,1,0:T(4,128)S(1)}, u32[]{:S(2)}, u32[]{:S(2)}) collective-permute-start(f32[2,3,192]{2,1,0:T(4,128)S(1)} %slice.13), channel_id=1, source_target_pairs={{0,2},{1,3},{2,0},{3,1},{4,6},{5,7},{6,4},{7,5},{8,10},{9,11},{10,... | collective-permute-start | bytes 13832 | tf_op jit(solution)/shard_map/ppermute | solution.py:600
  27.4 1.2 %collective-permute-start.7 = (f32[1,3,192]{2,1,0:T(4,128)S(1)}, f32[1,3,192]{2,1,0:T(4,128)S(1)}, u32[]{:S(2)}, u32[]{:S(2)}) collective-permute-start(f32[1,3,192]{2,1,0:T(4,128)S(1)} %slice.17), channel_id=1, source_target_pairs={{0,1},{1,0},{2,3},{3,2},{4,5},{5,4},{6,7},{7,6},{8,9},{9,8},{10,11... | collective-permute-start | bytes 6920 | tf_op jit(solution)/shard_map/ppermute | solution.py:600
  28.6 3.6 %collective-permute-start.8 = (f32[3,192]{1,0:T(4,128)S(1)}, f32[3,192]{1,0:T(4,128)S(1)}, u32[]{:S(2)}, u32[]{:S(2)}) collective-permute-start(f32[3,192]{1,0:T(4,128)S(1)} %fusion), channel_id=1, source_target_pairs={{0,4},{4,0},{8,12},{12,8},{1,5},{5,1},{9,13},{13,9},{2,6},{6,2},{1... | collective-permute-start | bytes 6920 | tf_op jit(solution)/shard_map/ppermute | solution.py:600
  32.2 4.5 %collective-permute-start.9 = (f32[3,192]{1,0:T(4,128)S(1)}, f32[3,192]{1,0:T(4,128)S(1)}, u32[]{:S(2)}, u32[]{:S(2)}) collective-permute-start(f32[3,192]{1,0:T(4,128)S(1)} %add.14), channel_id=1, source_target_pairs={{0,8},{4,12},{8,0},{12,4},{1,9},{5,13},{9,1},{13,5},{2,10},{6,14},... | collective-permute-start | bytes 6920 | tf_op jit(solution)/shard_map/ppermute | solution.py:600

commit v5 on v3

--- a/solution.py
+++ b/solution.py
@@ -330,36 +330,12 @@
     )(region, pattern, basis, tiles)
 
 
-def prepare_kernel(
-    region,
-    pattern,
-    basis,
-    field,
-    basis_grad,
-    weights,
-    weight_grad,
-    fn_atom,
-    batch_atom,
-    basis_out,
-    field_out,
-    moments,
-    hot,
-    grad_columns,
-    basis_in,
-    field_in,
-    grad_in,
-    wide,
-    turned,
-    grad_wide,
-    sems,
-    *,
-    points,
-    blocks,
-    step,
+def reorder_kernel(
+    pattern, basis, field, basis_grad, weights, basis_out, field_out, turned, grad_wide, basis_in, field_in, grad_in, wide, sems
 ):
-    batches, _, size = basis.shape
-    groups = batches // step
-    me = lax.axis_index("grid")
+    batches, blocks, points, size = basis_out.shape
+    groups = sems.shape[0]
+    step = batches // groups
 
     def copies(group):
         here = pl.ds(group * step, step)
@@ -372,16 +348,6 @@
     for group in range(groups):
         for copy in copies(group):
             copy.start()
-
-    atoms = lax.broadcasted_iota(jnp.int32, (hot.shape[0], size), 0)
-    for position in range(blocks):
-        ids = fn_atom[pl.ds(region[me, position], 1), :]
-        hot[:, position * size : (position + 1) * size] = jnp.where(atoms == ids, 1.0, 0.0).astype(BF16)
-    ids = jnp.concatenate([batch_atom[...], jnp.full((1, size - batches), -1, jnp.int32)], axis=1)
-    hot[:, blocks * size :] = jnp.where(atoms == ids, 1.0, 0.0).astype(BF16)
-    for c in range(PARTS):
-        rows = jnp.concatenate([weight_grad[c], jnp.zeros((size - batches, points), F32)], axis=0)
-        grad_columns[c] = rows.T
 
     @pl.loop(0, groups)
     def _(group):
@@ -405,52 +371,89 @@
                 for c in range(PARTS):
                     grad_wide[c, place, points_here, :] = wide[2 + c, strided, :].astype(BF16)
 
-    for c in range(PARTS):
-        right = jnp.concatenate([grad_wide[c, place] for place in range(blocks)], axis=1)
-        moments[c] = jnp.dot(turned[...], right, preferred_element_type=F32)
-
-
-def prepare(region, pattern, basis, field, basis_grad, weights, weight_grad, fn_atom, batch_atom, atom_total):
+
+def reorder(pattern, basis, field, basis_grad, weights):
     batches, points, blocks, size = basis.shape
     rows = points * blocks
     step = 2 if batches % 2 == 0 else 1
-    smem = pl.BlockSpec(memory_space=pltpu.SMEM)
     hbm = pl.BlockSpec(memory_space=pl.ANY)
     vmem = pl.BlockSpec(memory_space=pltpu.VMEM)
     ordered = jax.ShapeDtypeStruct((batches, blocks, points, size), BF16)
     return pl.pallas_call(
-        functools.partial(prepare_kernel, points=points, blocks=blocks, step=step),
+        reorder_kernel,
         out_shape=(
             ordered,
             ordered,
-            jax.ShapeDtypeStruct((PARTS, blocks * size, blocks * size), F32),
-            jax.ShapeDtypeStruct((atom_total, (blocks + 1) * size), BF16),
-            jax.ShapeDtypeStruct((PARTS, points, size), F32),
-        ),
-        in_specs=[smem, smem, hbm, hbm, hbm, vmem, vmem, vmem, vmem],
-        out_specs=(vmem,) * 5,
+            jax.ShapeDtypeStruct((blocks * size, batches * points), BF16),
+            jax.ShapeDtypeStruct((PARTS, blocks, batches * points, size), BF16),
+        ),
+        in_specs=[pl.BlockSpec(memory_space=pltpu.SMEM), hbm, hbm, hbm, vmem],
+        out_specs=(vmem,) * 4,
         scratch_shapes=[
             pltpu.VMEM((batches, rows, size), BF16),
             pltpu.VMEM((batches, rows, size), BF16),
             pltpu.VMEM((PARTS, batches, rows, size), BF16),
             pltpu.VMEM((2 + PARTS, rows, size), F32),
-            pltpu.VMEM((blocks * size, batches * points), BF16),
-            pltpu.VMEM((PARTS, blocks, batches * points, size), BF16),
             pltpu.SemaphoreType.DMA((batches // step, 3)),
         ],
         compiler_params=pltpu.CompilerParams(vmem_limit_bytes=VMEM_LIMIT),
         cost_estimate=pl.CostEstimate(
-            flops=2 * PARTS * batches * points * (blocks * size) ** 2,
-            bytes_accessed=2 * (2 + PARTS) * batches * rows * size,
-            transcendentals=0,
+            flops=0, bytes_accessed=2 * (2 + PARTS) * batches * rows * size, transcendentals=0
         ),
     )(
-        in_hbm(region),
         in_hbm(pattern.T),
         in_hbm(basis.reshape(batches, rows, size)),
         in_hbm(field.reshape(batches, rows, size)),
         in_hbm(basis_grad.reshape(PARTS, batches, rows, size)),
         in_hbm(weights),
+    )
+
+
+def moment_kernel(region, turned, grad_wide, weight_grad, fn_atom, batch_atom, moments, hot, grad_columns):
+    blocks, _, size = grad_wide.shape[1:]
+    batches = weight_grad.shape[1]
+    me = lax.axis_index("grid")
+    for c in range(PARTS):
+        spans = [(p, min(p + 2, blocks), p, min(p + 2, blocks)) for p in range(0, blocks, 2)]
+        for p in range(2, blocks, 2):
+            spans += [(p - 1, p, p, p + 1), (p, p + 1, p - 1, p)]
+        for top, bottom, first, last in spans:
+            right = jnp.concatenate([grad_wide[c, place] for place in range(first, last)], axis=1)
+            moments[c, top * size : bottom * size, first * size : last * size] = jnp.dot(
+                turned[top * size : bottom * size, :], right, preferred_element_type=F32
+            )
+    atoms = lax.broadcasted_iota(jnp.int32, (size, hot.shape[1]), 1).astype(F32)
+    rows = [fn_atom[pl.ds(region[me, position], 1), :] for position in range(blocks)]
+    rows.append(jnp.concatenate([batch_atom[...], jnp.full((1, size - batches), -1, jnp.int32)], axis=1))
+    for number, row in enumerate(rows):
+        ids = jnp.broadcast_to(row.astype(F32), (size, size)).T[:, 0:1]
+        hot[number * size : (number + 1) * size, :] = jnp.where(atoms == ids, 1.0, 0.0).astype(BF16)
+    for c in range(PARTS):
+        padded = jnp.concatenate([weight_grad[c], jnp.zeros((size - batches, weight_grad.shape[2]), F32)], axis=0)
+        grad_columns[c] = padded.T
+
+
+def moments_and_atoms(region, turned, grad_wide, weight_grad, fn_atom, batch_atom, atom_total):
+    blocks, depth, size = grad_wide.shape[1:]
+    points = weight_grad.shape[2]
+    vmem = pl.BlockSpec(memory_space=pltpu.VMEM)
+    return pl.pallas_call(
+        moment_kernel,
+        out_shape=(
+            jax.ShapeDtypeStruct((PARTS, blocks * size, blocks * size), F32),
+            jax.ShapeDtypeStruct(((blocks + 1) * size, atom_total), BF16),
+            jax.ShapeDtypeStruct((PARTS, points, size), F32),
+        ),
+        in_specs=[pl.BlockSpec(memory_space=pltpu.SMEM)] + [vmem] * 5,
+        out_specs=(vmem,) * 3,
+        compiler_params=pltpu.CompilerParams(vmem_limit_bytes=VMEM_LIMIT),
+        cost_estimate=pl.CostEstimate(
+            flops=2 * PARTS * depth * (blocks * size) ** 2, bytes_accessed=0, transcendentals=0
+        ),
+    )(
+        in_hbm(region),
+        turned,
+        grad_wide,
         in_hbm(weight_grad),
         in_hbm(fn_atom.reshape(-1, size)),
         in_hbm(batch_atom.reshape(1, -1)),
@@ -472,6 +475,9 @@
         owner, slot, count = found[p]
         first = jnp.bitwise_xor(me, owner) * TRAVEL
         for q in range(blocks):
+            if abs(q - p) > half:
+                matrix[p * size : (p + 1) * size, q * size : (q + 1) * size] = jnp.zeros((size, size), BF16)
+                continue
             k = rows[q] - rows[p] + half
             place = jnp.where(
                 k == 0,
@@ -516,14 +522,12 @@
     left = jnp.concatenate(lefts, axis=0)
     high, middle, low = (piece.astype(F32) for piece in split(left))
     left = jnp.concatenate([high, middle, low, jnp.zeros((16 - 3 * PARTS, left.shape[1]), F32)], axis=0).astype(BF16)
+    sums = jnp.dot(left, hot[...], preferred_element_type=F32)
+    value = sums[:PARTS] + sums[PARTS : 2 * PARTS] + sums[2 * PARTS : 3 * PARTS]
     chunk = out.shape[-1]
     for device in range(out.shape[1]):
-        sums = lax.dot_general(
-            left, hot[device * chunk : (device + 1) * chunk, :], NT, preferred_element_type=F32
-        )
-        value = sums[:PARTS] + sums[PARTS : 2 * PARTS] + sums[2 * PARTS : 3 * PARTS]
         for slab in range(slabs):
-            out[slab, device] = value
+            out[slab, device] = value[:, device * chunk : (device + 1) * chunk]
 
 
 def combine(region, prepared, pieces, shapes):
@@ -619,10 +623,10 @@
     shapes = (slabs, atom_devices, atom_total, points, blocks, width, owner_rows)
     own, near = fetch_rows(region, density, slabs, SHARE)
     if region.shape[1] == blocks:
-        ready = prepare(
-            region, pattern, basis, exchange_field, basis_grad, weights, weight_grad, fn_atom, batch_atom, atom_total
-        )
-        near, far, ready = swap_halves(near, ready, atom_devices)
+        ready = reorder(pattern, basis, exchange_field, basis_grad, weights)
+        near, far, (basis_wide, field_wide, turned, grad_wide) = swap_halves(near, ready, atom_devices)
+        built = moments_and_atoms(region, turned, grad_wide, weight_grad, fn_atom, batch_atom, atom_total)
+        ready = (basis_wide, field_wide, *built)
         product, partial_grad = combine(region, ready, [own, *near, *far], shapes)
         gradient = sum_parts(partial_grad)
         contracted = write(pattern, product)

time: 38.5 us -> 37.1 us (0.964)
  waiting for transfers between devices: 5.91 us -> 4.74 us
    ppermute x3, waiting for transfers between devices: 1.2 us -> 0.01 us  [swap_halves(): return (near, [lax.ppermute(piece, 'atoms', swap) for piece in near], ready)]
    pallas_call x1 -> x2, Pallas kernels: 10.2 us -> 10.1 us  [the longest x1 6.62 us: reorder(): pl.pallas_call(reorder_kernel, out_shape=(ordered, ordered, jax.ShapeDtyp...]
  transfers between devices with their start and end apart: 7 -> 7, of which waited for: 4 -> 1; matrix products, arithmetic and copies ran while one was open for 0% -> 0% of each run, Pallas kernels for 32% -> 33%
where the time goes in v5:
time: 37.1 us; the launch traced here: 36.7 us
  Pallas kernels  18.2 us (49%)
  starting transfers between devices  12.4 us (33%)
  waiting for transfers between devices  4.74 us (13%)
  between operations  0.71 us (2%)
  other arithmetic  0.62 us (2%)
    pallas_call x1, Pallas kernels, reorder(): pl.pallas_call(reorder_kernel, out_shape=(ordered, ordered, jax.ShapeDtyp...  6.62 us
    all_to_all x1, starting transfers between devices, sum_parts(): lax.all_to_all(parts, ('grid', 'atoms'), split_axis=0, concat_axis=0, til...  6.18 us
    ppermute x3, starting transfers between devices, fetch_rows(): lax.ppermute(piece, 'grid', [(i, i ^ shift) for i in range(slabs)])  5.59 us
    all_to_all x1, waiting for transfers between devices, sum_parts(): lax.all_to_all(parts, ('grid', 'atoms'), split_axis=0, concat_axis=0, til...  4.71 us
    pallas_call x1, Pallas kernels, combine(): pl.pallas_call(functools.partial(combine_kernel, owner_rows=owner_rows, s...  4.05 us
    pallas_call x1, Pallas kernels, moments_and_atoms(): pl.pallas_call(moment_kernel, out_shape=(jax.ShapeDtypeStruct((PARTS, blo...  3.49 us
    pallas_call x1, Pallas kernels, write(): pl.pallas_call(write_kernel, out_shape=jax.ShapeDtypeStruct(shape, BF16),...  2.18 us
    pallas_call x1, Pallas kernels, rows_to_send(): pl.pallas_call(functools.partial(send_kernel, share=share), out_shape=[ja...  1.87 us
  transfers between devices with their start and end apart: 7, of which 1 were waited for; matrix products, arithmetic and copies ran while one was open for 0% of the time, Pallas kernels for 33%

profile of v5, /device:TPU:0, one launch (start us, length us, event | category | flops | bytes accessed | tf_op | source)
XLA Modules:
  0.0 36.7 jit_solution(3159145479301188009)
XLA Ops:
  0.6 1.9 %shard_map.113 = (bf16[5,128,128]{2,1,0:T(8,128)(2,1)S(1)}, bf16[5,64,128]{2,1,0:T(8,128)(2,1)S(1)}, bf16[5,64,128]{2,1,0:T(8,128)(2,1)S(1)}, bf16[5,64,128]{2,1,0:T(8,128)(2,1)S(1)}) custom-call(s32[4,4]{1,0:T(4,128)} %region.5, bf16[15,3,128,128]{3,2,1,0:T(8,128)(2,1)} %density.1), custom_call_target="tpu_custom_call" | custom-call | tf_op jit(solution)/shard_map/pallas_call | solution.py:84
  2.5 3.0 %collective-permute-start = (bf16[5,64,128]{2,1,0:T(8,128)(2,1)S(1)}, bf16[5,64,128]{2,1,0:T(8,128)(2,1)S(1)}, u32[]{:S(2)}, u32[]{:S(2)}) collective-permute-start(bf16[5,64,128]{2,1,0:T(8,128)(2,1)S(1)} %get-tuple-element.22), channel_id=1, source_target_pairs={{0,4},{4,0},{8,12},{12,8},{1,5},{5,1},{9,13},{13,9},{2,6},{6,2},{1... | collective-permute-start | bytes 245768 | tf_op jit(solution)/shard_map/ppermute | solution.py:98
  5.5 2.6 %collective-permute-start.1 = (bf16[5,64,128]{2,1,0:T(8,128)(2,1)S(1)}, bf16[5,64,128]{2,1,0:T(8,128)(2,1)S(1)}, u32[]{:S(2)}, u32[]{:S(2)}) collective-permute-start(bf16[5,64,128]{2,1,0:T(8,128)(2,1)S(1)} %get-tuple-element.23), channel_id=1, source_target_pairs={{0,8},{4,12},{8,0},{12,4},{1,9},{5,13},{9,1},{13,5},{2,10},{6,14},... | collective-permute-start | bytes 245768 | tf_op jit(solution)/shard_map/ppermute | solution.py:98
  8.1 0.0 collective-permute-start.2
  8.1 6.6 %shard_map.114 = (bf16[16,4,128,128]{3,2,1,0:T(8,128)(2,1)S(1)}, bf16[16,4,128,128]{3,2,1,0:T(8,128)(2,1)S(1)}, bf16[512,2048]{1,0:T(8,128)(2,1)S(1)}, bf16[3,4,2048,128]{3,2,1,0:T(8,128)(2,1)S(1)}) custom-call(s32[4,16]{1,0:T(4,128)} %bitcast.12, bf16[16,512,128]{2,1,0:T(8,128)(2,1)} %bitcast.9, bf16[16,512,128]{2,1,0:T(8,128)(2,1)} %bitcast.10, ...), custom_call_target="tpu_custom_call" | custom-call | bytes 10485760 | tf_op jit(solution)/shard_map/pallas_call | solution.py:382
  14.7 0.0 collective-permute-done.rest_1_
  14.7 0.0 collective-permute-done.1.rest_2_
  14.8 0.0 collective-permute-done.2.rest_3_
  14.8 0.1 collective-permute-start.3
  14.8 0.5 %collective-permute-start.4 = (bf16[5,64,128]{2,1,0:T(8,128)(2,1)S(1)}, bf16[5,64,128]{2,1,0:T(8,128)(2,1)S(1)}, u32[]{:S(2)}, u32[]{:S(2)}) collective-permute-start(bf16[5,64,128]{2,1,0:T(8,128)(2,1)S(1)} %collective-permute-done.1.rest_2_), channel_id=1, source_target_pairs={{0,1},{1,0},{2,3},{3,2},{4,5},{5,4},{6,7},{7,6},{8,9},{9,8},{10,11... | collective-permute-start | bytes 245768 | tf_op jit(solution)/shard_map/ppermute | solution.py:597
  15.3 0.1 collective-permute-start.5
  15.4 3.5 %shard_map.115 = (f32[3,512,512]{2,1,0:T(8,128)S(1)}, bf16[640,768]{1,0:T(8,128)(2,1)S(1)}, f32[3,128,128]{2,1,0:T(8,128)S(1)}) custom-call(s32[4,4]{1,0:T(4,128)} %region.5, bf16[512,2048]{1,0:T(8,128)(2,1)S(1)} %get-tuple-element.31.turned, bf16[3,4,2048,128]{3,2,1,0:T(8,128)(2,1)S(1)} %get-tuple-element.32.grad_wide, f32[3,16,128]{2,1,0:T(8,128)} %weight_grad.1, ...), custom_call_target="tpu_custom_call" | custom-call | flops 3221225472 | tf_op jit(solution)/shard_map/pallas_call | solution.py:440
  18.9 0.0 collective-permute-done.3.rest_4_
  18.9 0.0 collective-permute-done.4.rest_5_
  18.9 0.0 collective-permute-done.5.rest_6_
  18.9 4.1 %shard_map.116 = (bf16[16,4,128,128]{3,2,1,0:T(8,128)(2,1)S(1)}, f32[4,4,3,192]{3,2,1,0:T(4,128)}) custom-call(s32[4,4]{1,0:T(4,128)} %region.5, bf16[16,4,128,128]{3,2,1,0:T(8,128)(2,1)S(1)} %get-tuple-element.29.basis, bf16[16,4,128,128]{3,2,1,0:T(8,128)(2,1)S(1)} %get-tuple-element.30.field, f32[3,512,512]{2,1,0:T(8,128)S(1)} %get-tuple-element.33.moments, ...), custom_call_target="tpu_custom_call" | custom-call | tf_op jit(solution)/shard_map/pallas_call | solution.py:539
  23.0 6.2 %all-to-all-start = ((f32[16,3,192]{2,1,0:T(4,128)}), f32[16,3,192]{2,1,0:T(4,128)S(1)}, u32[]{:S(2)}, u32[]{:S(2)}) async-start(f32[16,3,192]{2,1,0:T(4,128)} %bitcast.7), calls=%async_computation | async-start | bytes 131072 | tf_op jit(solution)/shard_map/all_to_all | solution.py:602
  29.2 2.2 %shard_map.117 = bf16[16,512,128]{2,1,0:T(8,128)(2,1)} custom-call(s32[4,16]{1,0:T(4,128)} %bitcast.13, bf16[16,4,128,128]{3,2,1,0:T(8,128)(2,1)S(1)} %get-tuple-element.40.product), custom_call_target="tpu_custom_call" | custom-call | bytes 4194304 | tf_op jit(solution)/shard_map/pallas_call | solution.py:579
  31.4 4.7 %all-to-all-done = f32[16,3,192]{2,1,0:T(4,128)S(1)} async-done(((f32[16,3,192]{2,1,0:T(4,128)}), f32[16,3,192]{2,1,0:T(4,128)S(1)}, u32[]{:S(2)}, u32[]{:S(2)}) %all-to-all-start) | async-done | bytes 36896 | tf_op jit(solution)/shard_map/all_to_all | solution.py:602
  36.1 0.6 %reduce_sum.9 = f32[3,192]{1,0:T(4,128)} reduce(f32[16,3,192]{2,1,0:T(4,128)S(1)} %all-to-all-done, f32[]{:T(128)} %constant.0.clone.1), dimensions={0}, to_apply=%region_0.0 | reduce | flops 8640 | bytes 39172 | tf_op jit(solution)/shard_map/reduce_sum | solution.py:603
Async XLA Ops:
  2.5 12.2 %collective-permute-start = (bf16[5,64,128]{2,1,0:T(8,128)(2,1)S(1)}, bf16[5,64,128]{2,1,0:T(8,128)(2,1)S(1)}, u32[]{:S(2)}, u32[]{:S(2)}) collective-permute-start(bf16[5,64,128]{2,1,0:T(8,128)(2,1)S(1)} %get-tuple-element.22), channel_id=1, source_target_pairs={{0,4},{4,0},{8,12},{12,8},{1,5},{5,1},{9,13},{13,9},{2,6},{6,2},{1... | collective-permute-start | bytes 245768 | tf_op jit(solution)/shard_map/ppermute | solution.py:98
  5.5 9.2 %collective-permute-start.1 = (bf16[5,64,128]{2,1,0:T(8,128)(2,1)S(1)}, bf16[5,64,128]{2,1,0:T(8,128)(2,1)S(1)}, u32[]{:S(2)}, u32[]{:S(2)}) collective-permute-start(bf16[5,64,128]{2,1,0:T(8,128)(2,1)S(1)} %get-tuple-element.23), channel_id=1, source_target_pairs={{0,8},{4,12},{8,0},{12,4},{1,9},{5,13},{9,1},{13,5},{2,10},{6,14},... | collective-permute-start | bytes 245768 | tf_op jit(solution)/shard_map/ppermute | solution.py:98
  8.1 6.7 %collective-permute-start.2 = (bf16[5,64,128]{2,1,0:T(8,128)(2,1)S(1)}, bf16[5,64,128]{2,1,0:T(8,128)(2,1)S(1)}, u32[]{:S(2)}, u32[]{:S(2)}) collective-permute-start(bf16[5,64,128]{2,1,0:T(8,128)(2,1)S(1)} %get-tuple-element.24), channel_id=1, source_target_pairs={{0,12},{4,8},{8,4},{12,0},{1,13},{5,9},{9,5},{13,1},{2,14},{6,10},... | collective-permute-start | bytes 245768 | tf_op jit(solution)/shard_map/ppermute | solution.py:98
  14.8 4.2 %collective-permute-start.3 = (bf16[5,64,128]{2,1,0:T(8,128)(2,1)S(1)}, bf16[5,64,128]{2,1,0:T(8,128)(2,1)S(1)}, u32[]{:S(2)}, u32[]{:S(2)}) collective-permute-start(bf16[5,64,128]{2,1,0:T(8,128)(2,1)S(1)} %collective-permute-done.rest_1_), channel_id=1, source_target_pairs={{0,1},{1,0},{2,3},{3,2},{4,5},{5,4},{6,7},{7,6},{8,9},{9,8},{10,11... | collective-permute-start | bytes 245768 | tf_op jit(solution)/shard_map/ppermute | solution.py:597
  14.8 4.1 %collective-permute-start.4 = (bf16[5,64,128]{2,1,0:T(8,128)(2,1)S(1)}, bf16[5,64,128]{2,1,0:T(8,128)(2,1)S(1)}, u32[]{:S(2)}, u32[]{:S(2)}) collective-permute-start(bf16[5,64,128]{2,1,0:T(8,128)(2,1)S(1)} %collective-permute-done.1.rest_2_), channel_id=1, source_target_pairs={{0,1},{1,0},{2,3},{3,2},{4,5},{5,4},{6,7},{7,6},{8,9},{9,8},{10,11... | collective-permute-start | bytes 245768 | tf_op jit(solution)/shard_map/ppermute | solution.py:597
  15.3 3.6 %collective-permute-start.5 = (bf16[5,64,128]{2,1,0:T(8,128)(2,1)S(1)}, bf16[5,64,128]{2,1,0:T(8,128)(2,1)S(1)}, u32[]{:S(2)}, u32[]{:S(2)}) collective-permute-start(bf16[5,64,128]{2,1,0:T(8,128)(2,1)S(1)} %collective-permute-done.2.rest_3_), channel_id=1, source_target_pairs={{0,1},{1,0},{2,3},{3,2},{4,5},{5,4},{6,7},{7,6},{8,9},{9,8},{10,11... | collective-permute-start | bytes 245768 | tf_op jit(solution)/shard_map/ppermute | solution.py:597
  23.0 13.1 %all-to-all-start = ((f32[16,3,192]{2,1,0:T(4,128)}), f32[16,3,192]{2,1,0:T(4,128)S(1)}, u32[]{:S(2)}, u32[]{:S(2)}) async-start(f32[16,3,192]{2,1,0:T(4,128)} %bitcast.7), calls=%async_computation | async-start | bytes 131072 | tf_op jit(solution)/shard_map/all_to_all | solution.py:602

commit v6 on v5

--- a/solution.py
+++ b/solution.py
@@ -93,10 +93,10 @@
 
 def fetch_rows(region, density, slabs, share):
     own, *outgoing = rows_to_send(region, density, slabs, share)
-    near = []
-    for shift, piece in enumerate(outgoing, 1):
-        near.append(lax.ppermute(piece, "grid", [(i, i ^ shift) for i in range(slabs)]))
-    return own, near
+    near = {}
+    for shift in reversed(range(1, slabs)):
+        near[shift] = lax.ppermute(outgoing[shift - 1], "grid", [(i, i ^ shift) for i in range(slabs)])
+    return own, [near[shift] for shift in range(1, slabs)]
 
 
 def stage_rows(stage, own, near, far, share):
@@ -330,12 +330,41 @@
     )(region, pattern, basis, tiles)
 
 
+def add_moments(moments, turned, grads, fresh):
+    blocks, _, size = grads.shape[1:]
+    for c in range(PARTS):
+        for p in range(0, blocks, 2):
+            rows = slice(max(p - 1, 0) * size, min(p + 3, blocks) * size)
+            columns = slice(p * size, min(p + 2, blocks) * size)
+            right = jnp.concatenate([grads[c, place] for place in range(p, min(p + 2, blocks))], axis=1)
+            value = jnp.dot(turned[rows, :], right, preferred_element_type=F32)
+            moments[c, rows, columns] = value if fresh else moments[c, rows, columns] + value
+
+
 def reorder_kernel(
-    pattern, basis, field, basis_grad, weights, basis_out, field_out, turned, grad_wide, basis_in, field_in, grad_in, wide, sems
+    pattern,
+    basis,
+    field,
+    basis_grad,
+    weights,
+    basis_out,
+    field_out,
+    moments,
+    last_turned,
+    last_grads,
+    basis_in,
+    field_in,
+    grad_in,
+    wide,
+    turned,
+    grads,
+    sems,
 ):
     batches, blocks, points, size = basis_out.shape
     groups = sems.shape[0]
     step = batches // groups
+    turned = [last_turned if (groups - 1 - group) % 2 == 0 else turned for group in range(groups)]
+    grads = [last_grads if (groups - 1 - group) % 2 == 0 else grads for group in range(groups)]
 
     def copies(group):
         here = pl.ds(group * step, step)
@@ -349,15 +378,14 @@
         for copy in copies(group):
             copy.start()
 
-    @pl.loop(0, groups)
-    def _(group):
+    for group in range(groups):
         for copy in copies(group):
             copy.wait()
         for inner in range(step):
             batch = group * step + inner
-            points_here = pl.ds(pl.multiple_of(batch * points, points), points)
+            points_here = slice(inner * points, (inner + 1) * points)
             places = [pattern[s, batch] for s in range(blocks)]
-            weight = weights[pl.ds(batch, 1), :]
+            weight = weights[batch : batch + 1, :]
             wide[0] = field_in[batch].astype(F32)
             wide[1] = basis_in[batch].astype(F32)
             for c in range(PARTS):
@@ -366,39 +394,51 @@
                 strided = pl.ds(s, points, stride=blocks)
                 values = wide[0, strided, :]
                 field_out[batch, place] = values.astype(BF16)
-                turned[pl.ds(pl.multiple_of(place * size, size), size), points_here] = (values.T * weight).astype(BF16)
+                rows = pl.ds(pl.multiple_of(place * size, size), size)
+                turned[group][rows, points_here] = (values.T * weight).astype(BF16)
                 basis_out[batch, place] = wide[1, strided, :].astype(BF16)
                 for c in range(PARTS):
-                    grad_wide[c, place, points_here, :] = wide[2 + c, strided, :].astype(BF16)
+                    grads[group][c, place, points_here, :] = wide[2 + c, strided, :].astype(BF16)
+        if group > 0:
+            add_moments(moments, turned[group - 1], grads[group - 1], group == 1)
+    if groups == 1:
+        moments[...] = jnp.zeros_like(moments)
 
 
 def reorder(pattern, basis, field, basis_grad, weights):
     batches, points, blocks, size = basis.shape
     rows = points * blocks
-    step = 2 if batches % 2 == 0 else 1
+    step = 4 if batches % 4 == 0 else 1
     hbm = pl.BlockSpec(memory_space=pl.ANY)
     vmem = pl.BlockSpec(memory_space=pltpu.VMEM)
     ordered = jax.ShapeDtypeStruct((batches, blocks, points, size), BF16)
+    turned = (blocks * size, step * points)
+    grads = (PARTS, blocks, step * points, size)
     return pl.pallas_call(
         reorder_kernel,
         out_shape=(
             ordered,
             ordered,
-            jax.ShapeDtypeStruct((blocks * size, batches * points), BF16),
-            jax.ShapeDtypeStruct((PARTS, blocks, batches * points, size), BF16),
+            jax.ShapeDtypeStruct((PARTS, blocks * size, blocks * size), F32),
+            jax.ShapeDtypeStruct(turned, BF16),
+            jax.ShapeDtypeStruct(grads, BF16),
         ),
         in_specs=[pl.BlockSpec(memory_space=pltpu.SMEM), hbm, hbm, hbm, vmem],
-        out_specs=(vmem,) * 4,
+        out_specs=(vmem,) * 5,
         scratch_shapes=[
             pltpu.VMEM((batches, rows, size), BF16),
             pltpu.VMEM((batches, rows, size), BF16),
             pltpu.VMEM((PARTS, batches, rows, size), BF16),
             pltpu.VMEM((2 + PARTS, rows, size), F32),
+            pltpu.VMEM(turned, BF16),
+            pltpu.VMEM(grads, BF16),
             pltpu.SemaphoreType.DMA((batches // step, 3)),
         ],
         compiler_params=pltpu.CompilerParams(vmem_limit_bytes=VMEM_LIMIT),
         cost_estimate=pl.CostEstimate(
-            flops=0, bytes_accessed=2 * (2 + PARTS) * batches * rows * size, transcendentals=0
+            flops=2 * PARTS * batches * points * (blocks * size) ** 2,
+            bytes_accessed=2 * (2 + PARTS) * batches * rows * size,
+            transcendentals=0,
         ),
     )(
         in_hbm(pattern.T),
@@ -409,51 +449,46 @@
     )
 
 
-def moment_kernel(region, turned, grad_wide, weight_grad, fn_atom, batch_atom, moments, hot, grad_columns):
-    blocks, _, size = grad_wide.shape[1:]
+def moment_kernel(
+    region, before, turned, grads, weight_grad, fn_atom, batch_atom, moments, hot, grad_columns
+):
+    blocks, _, size = grads.shape[1:]
     batches = weight_grad.shape[1]
     me = lax.axis_index("grid")
-    for c in range(PARTS):
-        spans = [(p, min(p + 2, blocks), p, min(p + 2, blocks)) for p in range(0, blocks, 2)]
-        for p in range(2, blocks, 2):
-            spans += [(p - 1, p, p, p + 1), (p, p + 1, p - 1, p)]
-        for top, bottom, first, last in spans:
-            right = jnp.concatenate([grad_wide[c, place] for place in range(first, last)], axis=1)
-            moments[c, top * size : bottom * size, first * size : last * size] = jnp.dot(
-                turned[top * size : bottom * size, :], right, preferred_element_type=F32
-            )
-    atoms = lax.broadcasted_iota(jnp.int32, (size, hot.shape[1]), 1).astype(F32)
+    atoms = lax.broadcasted_iota(jnp.int32, (hot.shape[0], size), 0)
     rows = [fn_atom[pl.ds(region[me, position], 1), :] for position in range(blocks)]
     rows.append(jnp.concatenate([batch_atom[...], jnp.full((1, size - batches), -1, jnp.int32)], axis=1))
-    for number, row in enumerate(rows):
-        ids = jnp.broadcast_to(row.astype(F32), (size, size)).T[:, 0:1]
-        hot[number * size : (number + 1) * size, :] = jnp.where(atoms == ids, 1.0, 0.0).astype(BF16)
+    for number, ids in enumerate(rows):
+        hot[:, number * size : (number + 1) * size] = jnp.where(atoms == ids, 1.0, 0.0).astype(BF16)
     for c in range(PARTS):
         padded = jnp.concatenate([weight_grad[c], jnp.zeros((size - batches, weight_grad.shape[2]), F32)], axis=0)
         grad_columns[c] = padded.T
-
-
-def moments_and_atoms(region, turned, grad_wide, weight_grad, fn_atom, batch_atom, atom_total):
-    blocks, depth, size = grad_wide.shape[1:]
+    add_moments(moments, turned, grads, False)
+
+
+def moments_and_atoms(region, before, turned, grads, weight_grad, fn_atom, batch_atom, atom_total):
+    blocks, depth, size = grads.shape[1:]
     points = weight_grad.shape[2]
     vmem = pl.BlockSpec(memory_space=pltpu.VMEM)
     return pl.pallas_call(
         moment_kernel,
         out_shape=(
-            jax.ShapeDtypeStruct((PARTS, blocks * size, blocks * size), F32),
-            jax.ShapeDtypeStruct(((blocks + 1) * size, atom_total), BF16),
+            jax.ShapeDtypeStruct(before.shape, F32),
+            jax.ShapeDtypeStruct((atom_total, (blocks + 1) * size), BF16),
             jax.ShapeDtypeStruct((PARTS, points, size), F32),
         ),
-        in_specs=[pl.BlockSpec(memory_space=pltpu.SMEM)] + [vmem] * 5,
+        in_specs=[pl.BlockSpec(memory_space=pltpu.SMEM)] + [vmem] * 6,
         out_specs=(vmem,) * 3,
+        input_output_aliases={1: 0},
         compiler_params=pltpu.CompilerParams(vmem_limit_bytes=VMEM_LIMIT),
         cost_estimate=pl.CostEstimate(
             flops=2 * PARTS * depth * (blocks * size) ** 2, bytes_accessed=0, transcendentals=0
         ),
     )(
         in_hbm(region),
+        before,
         turned,
-        grad_wide,
+        grads,
         in_hbm(weight_grad),
         in_hbm(fn_atom.reshape(-1, size)),
         in_hbm(batch_atom.reshape(1, -1)),
@@ -522,12 +557,14 @@
     left = jnp.concatenate(lefts, axis=0)
     high, middle, low = (piece.astype(F32) for piece in split(left))
     left = jnp.concatenate([high, middle, low, jnp.zeros((16 - 3 * PARTS, left.shape[1]), F32)], axis=0).astype(BF16)
-    sums = jnp.dot(left, hot[...], preferred_element_type=F32)
-    value = sums[:PARTS] + sums[PARTS : 2 * PARTS] + sums[2 * PARTS : 3 * PARTS]
     chunk = out.shape[-1]
     for device in range(out.shape[1]):
+        sums = lax.dot_general(
+            left, hot[device * chunk : (device + 1) * chunk, :], NT, preferred_element_type=F32
+        )
+        value = sums[:PARTS] + sums[PARTS : 2 * PARTS] + sums[2 * PARTS : 3 * PARTS]
         for slab in range(slabs):
-            out[slab, device] = value[:, device * chunk : (device + 1) * chunk]
+            out[slab, device] = value
 
 
 def combine(region, prepared, pieces, shapes):
@@ -624,8 +661,8 @@
     own, near = fetch_rows(region, density, slabs, SHARE)
     if region.shape[1] == blocks:
         ready = reorder(pattern, basis, exchange_field, basis_grad, weights)
-        near, far, (basis_wide, field_wide, turned, grad_wide) = swap_halves(near, ready, atom_devices)
-        built = moments_and_atoms(region, turned, grad_wide, weight_grad, fn_atom, batch_atom, atom_total)
+        near, far, (basis_wide, field_wide, *partial) = swap_halves(near, ready, atom_devices)
+        built = moments_and_atoms(region, *partial, weight_grad, fn_atom, batch_atom, atom_total)
         ready = (basis_wide, field_wide, *built)
         product, partial_grad = combine(region, ready, [own, *near, *far], shapes)
         gradient = sum_parts(partial_grad)

time: 37.1 us -> 37.1 us (level)
    pallas_call x1, Pallas kernels: 3.49 us -> 1.87 us  [moments_and_atoms(): pl.pallas_call(moment_kernel, out_shape=(jax.ShapeDtypeStruct(before.shap...]
    pallas_call x1, Pallas kernels: 6.62 us -> 8.11 us  [reorder(): pl.pallas_call(reorder_kernel, out_shape=(ordered, ordered, jax.ShapeDtyp...]
where the time goes in v6:
time: 37.1 us; the launch traced here: 36.7 us
  Pallas kernels  18.1 us (49%)
  starting transfers between devices  12.6 us (34%)
  waiting for transfers between devices  4.72 us (13%)
  between operations  0.73 us (2%)
  other arithmetic  0.62 us (2%)
    pallas_call x1, Pallas kernels, reorder(): pl.pallas_call(reorder_kernel, out_shape=(ordered, ordered, jax.ShapeDtyp...  8.11 us
    all_to_all x1, starting transfers between devices, sum_parts(): lax.all_to_all(parts, ('grid', 'atoms'), split_axis=0, concat_axis=0, til...  6.18 us
    ppermute x3, starting transfers between devices, fetch_rows(): lax.ppermute(outgoing[shift - 1], 'grid', [(i, i ^ shift) for i in range(...  5.74 us
    all_to_all x1, waiting for transfers between devices, sum_parts(): lax.all_to_all(parts, ('grid', 'atoms'), split_axis=0, concat_axis=0, til...  4.71 us
    pallas_call x1, Pallas kernels, combine(): pl.pallas_call(functools.partial(combine_kernel, owner_rows=owner_rows, s...  4.11 us
    pallas_call x1, Pallas kernels, write(): pl.pallas_call(write_kernel, out_shape=jax.ShapeDtypeStruct(shape, BF16),...  2.18 us
    pallas_call x1, Pallas kernels, moments_and_atoms(): pl.pallas_call(moment_kernel, out_shape=(jax.ShapeDtypeStruct(before.shap...  1.87 us
    pallas_call x1, Pallas kernels, rows_to_send(): pl.pallas_call(functools.partial(send_kernel, share=share), out_shape=[ja...  1.78 us
  transfers between devices with their start and end apart: 7, of which 1 were waited for; matrix products, arithmetic and copies ran while one was open for 0% of the time, Pallas kernels for 33%

profile of v6, /device:TPU:0, one launch (start us, length us, event | category | flops | bytes accessed | tf_op | source)
XLA Modules:
  0.0 36.7 jit_solution(75984964411064442)
XLA Ops:
  0.6 1.8 %shard_map.113 = (bf16[5,128,128]{2,1,0:T(8,128)(2,1)S(1)}, bf16[5,64,128]{2,1,0:T(8,128)(2,1)S(1)}, bf16[5,64,128]{2,1,0:T(8,128)(2,1)S(1)}, bf16[5,64,128]{2,1,0:T(8,128)(2,1)S(1)}) custom-call(s32[4,4]{1,0:T(4,128)} %region.5, bf16[15,3,128,128]{3,2,1,0:T(8,128)(2,1)} %density.1), custom_call_target="tpu_custom_call" | custom-call | tf_op jit(solution)/shard_map/pallas_call | solution.py:84
  2.4 3.1 %collective-permute-start = (bf16[5,64,128]{2,1,0:T(8,128)(2,1)S(1)}, bf16[5,64,128]{2,1,0:T(8,128)(2,1)S(1)}, u32[]{:S(2)}, u32[]{:S(2)}) collective-permute-start(bf16[5,64,128]{2,1,0:T(8,128)(2,1)S(1)} %get-tuple-element.24), channel_id=1, source_target_pairs={{0,4},{4,0},{8,12},{12,8},{1,5},{5,1},{9,13},{13,9},{2,6},{6,2},{1... | collective-permute-start | bytes 245768 | tf_op jit(solution)/shard_map/ppermute | solution.py:98
  5.5 2.6 %collective-permute-start.1 = (bf16[5,64,128]{2,1,0:T(8,128)(2,1)S(1)}, bf16[5,64,128]{2,1,0:T(8,128)(2,1)S(1)}, u32[]{:S(2)}, u32[]{:S(2)}) collective-permute-start(bf16[5,64,128]{2,1,0:T(8,128)(2,1)S(1)} %get-tuple-element.25), channel_id=1, source_target_pairs={{0,8},{4,12},{8,0},{12,4},{1,9},{5,13},{9,1},{13,5},{2,10},{6,14},... | collective-permute-start | bytes 245768 | tf_op jit(solution)/shard_map/ppermute | solution.py:98
  8.2 0.0 collective-permute-start.2
  8.2 8.1 %shard_map.114 = (bf16[16,4,128,128]{3,2,1,0:T(8,128)(2,1)S(1)}, bf16[16,4,128,128]{3,2,1,0:T(8,128)(2,1)S(1)}, f32[3,512,512]{2,1,0:T(8,128)S(1)}, bf16[512,512...) custom-call(s32[4,16]{1,0:T(4,128)} %bitcast.10, bf16[16,512,128]{2,1,0:T(8,128)(2,1)} %bitcast.14, ...), custom_call_target="tpu_custom_call" | custom-call | flops 3221225472 | bytes 10485760 | tf_op jit(solution)/shard_map/pallas_call | solution.py:417
  16.3 0.0 collective-permute-done.rest_1_
  16.3 0.0 collective-permute-done.1.rest_2_
  16.3 0.0 collective-permute-done.2.rest_3_
  16.3 0.1 collective-permute-start.3
  16.4 0.5 %collective-permute-start.4 = (bf16[5,64,128]{2,1,0:T(8,128)(2,1)S(1)}, bf16[5,64,128]{2,1,0:T(8,128)(2,1)S(1)}, u32[]{:S(2)}, u32[]{:S(2)}) collective-permute-start(bf16[5,64,128]{2,1,0:T(8,128)(2,1)S(1)} %collective-permute-done.1.rest_2_), channel_id=1, source_target_pairs={{0,1},{1,0},{2,3},{3,2},{4,5},{5,4},{6,7},{7,6},{8,9},{9,8},{10,11... | collective-permute-start | bytes 245768 | tf_op jit(solution)/shard_map/ppermute | solution.py:634
  16.9 0.1 collective-permute-start.5
  17.0 1.9 %shard_map.115 = (f32[3,512,512]{2,1,0:T(8,128)S(1)}, bf16[768,640]{1,0:T(8,128)(2,1)S(1)}, f32[3,128,128]{2,1,0:T(8,128)S(1)}) custom-call(s32[4,4]{1,0:T(4,128)} %region.5, f32[3,512,512]{2,1,0:T(8,128)S(1)} %get-tuple-element.34.before, bf16[512,512]{1,0:T(8,128)(2,1)S(1)} %get-tuple-element.35.turned, ...), custom_call_target="tpu_custom_call", output_to_operand_aliasing={{0}: (1, {})} | custom-call | flops 805306368 | tf_op jit(solution)/shard_map/pallas_call | solution.py:473
  18.8 0.0 collective-permute-done.3.rest_4_
  18.9 0.0 collective-permute-done.4.rest_5_
  18.9 0.0 collective-permute-done.5.rest_6_
  18.9 4.1 %shard_map.116 = (bf16[16,4,128,128]{3,2,1,0:T(8,128)(2,1)S(1)}, f32[4,4,3,192]{3,2,1,0:T(4,128)}) custom-call(s32[4,4]{1,0:T(4,128)} %region.5, bf16[16,4,128,128]{3,2,1,0:T(8,128)(2,1)S(1)} %get-tuple-element.32.basis, bf16[16,4,128,128]{3,2,1,0:T(8,128)(2,1)S(1)} %get-tuple-element.33.field, f32[3,512,512]{2,1,0:T(8,128)S(1)} %get-tuple-element.37.moments, ...), custom_call_target="tpu_custom_call" | custom-call | tf_op jit(solution)/shard_map/pallas_call | solution.py:576
  23.0 6.2 %all-to-all-start = ((f32[16,3,192]{2,1,0:T(4,128)}), f32[16,3,192]{2,1,0:T(4,128)S(1)}, u32[]{:S(2)}, u32[]{:S(2)}) async-start(f32[16,3,192]{2,1,0:T(4,128)} %bitcast.7), calls=%async_computation | async-start | bytes 131072 | tf_op jit(solution)/shard_map/all_to_all | solution.py:639
  29.2 2.2 %shard_map.117 = bf16[16,512,128]{2,1,0:T(8,128)(2,1)} custom-call(s32[4,16]{1,0:T(4,128)} %bitcast.11, bf16[16,4,128,128]{3,2,1,0:T(8,128)(2,1)S(1)} %get-tuple-element.44.product), custom_call_target="tpu_custom_call" | custom-call | bytes 4194304 | tf_op jit(solution)/shard_map/pallas_call | solution.py:616
  31.4 4.7 %all-to-all-done = f32[16,3,192]{2,1,0:T(4,128)S(1)} async-done(((f32[16,3,192]{2,1,0:T(4,128)}), f32[16,3,192]{2,1,0:T(4,128)S(1)}, u32[]{:S(2)}, u32[]{:S(2)}) %all-to-all-start) | async-done | bytes 36896 | tf_op jit(solution)/shard_map/all_to_all | solution.py:639
  36.1 0.6 %reduce_sum.9 = f32[3,192]{1,0:T(4,128)} reduce(f32[16,3,192]{2,1,0:T(4,128)S(1)} %all-to-all-done, f32[]{:T(128)} %constant.0.clone.1), dimensions={0}, to_apply=%region_0.0 | reduce | flops 8640 | bytes 39172 | tf_op jit(solution)/shard_map/reduce_sum | solution.py:640
Async XLA Ops:
  2.4 13.9 %collective-permute-start = (bf16[5,64,128]{2,1,0:T(8,128)(2,1)S(1)}, bf16[5,64,128]{2,1,0:T(8,128)(2,1)S(1)}, u32[]{:S(2)}, u32[]{:S(2)}) collective-permute-start(bf16[5,64,128]{2,1,0:T(8,128)(2,1)S(1)} %get-tuple-element.24), channel_id=1, source_target_pairs={{0,4},{4,0},{8,12},{12,8},{1,5},{5,1},{9,13},{13,9},{2,6},{6,2},{1... | collective-permute-start | bytes 245768 | tf_op jit(solution)/shard_map/ppermute | solution.py:98
  5.5 10.8 %collective-permute-start.1 = (bf16[5,64,128]{2,1,0:T(8,128)(2,1)S(1)}, bf16[5,64,128]{2,1,0:T(8,128)(2,1)S(1)}, u32[]{:S(2)}, u32[]{:S(2)}) collective-permute-start(bf16[5,64,128]{2,1,0:T(8,128)(2,1)S(1)} %get-tuple-element.25), channel_id=1, source_target_pairs={{0,8},{4,12},{8,0},{12,4},{1,9},{5,13},{9,1},{13,5},{2,10},{6,14},... | collective-permute-start | bytes 245768 | tf_op jit(solution)/shard_map/ppermute | solution.py:98
  8.2 8.1 %collective-permute-start.2 = (bf16[5,64,128]{2,1,0:T(8,128)(2,1)S(1)}, bf16[5,64,128]{2,1,0:T(8,128)(2,1)S(1)}, u32[]{:S(2)}, u32[]{:S(2)}) collective-permute-start(bf16[5,64,128]{2,1,0:T(8,128)(2,1)S(1)} %get-tuple-element.26), channel_id=1, source_target_pairs={{0,12},{4,8},{8,4},{12,0},{1,13},{5,9},{9,5},{13,1},{2,14},{6,10},... | collective-permute-start | bytes 245768 | tf_op jit(solution)/shard_map/ppermute | solution.py:98
  16.3 2.5 %collective-permute-start.3 = (bf16[5,64,128]{2,1,0:T(8,128)(2,1)S(1)}, bf16[5,64,128]{2,1,0:T(8,128)(2,1)S(1)}, u32[]{:S(2)}, u32[]{:S(2)}) collective-permute-start(bf16[5,64,128]{2,1,0:T(8,128)(2,1)S(1)} %collective-permute-done.rest_1_), channel_id=1, source_target_pairs={{0,1},{1,0},{2,3},{3,2},{4,5},{5,4},{6,7},{7,6},{8,9},{9,8},{10,11... | collective-permute-start | bytes 245768 | tf_op jit(solution)/shard_map/ppermute | solution.py:634
  16.4 2.5 %collective-permute-start.4 = (bf16[5,64,128]{2,1,0:T(8,128)(2,1)S(1)}, bf16[5,64,128]{2,1,0:T(8,128)(2,1)S(1)}, u32[]{:S(2)}, u32[]{:S(2)}) collective-permute-start(bf16[5,64,128]{2,1,0:T(8,128)(2,1)S(1)} %collective-permute-done.1.rest_2_), channel_id=1, source_target_pairs={{0,1},{1,0},{2,3},{3,2},{4,5},{5,4},{6,7},{7,6},{8,9},{9,8},{10,11... | collective-permute-start | bytes 245768 | tf_op jit(solution)/shard_map/ppermute | solution.py:634
  16.9 2.0 %collective-permute-start.5 = (bf16[5,64,128]{2,1,0:T(8,128)(2,1)S(1)}, bf16[5,64,128]{2,1,0:T(8,128)(2,1)S(1)}, u32[]{:S(2)}, u32[]{:S(2)}) collective-permute-start(bf16[5,64,128]{2,1,0:T(8,128)(2,1)S(1)} %collective-permute-done.2.rest_3_), channel_id=1, source_target_pairs={{0,1},{1,0},{2,3},{3,2},{4,5},{5,4},{6,7},{7,6},{8,9},{9,8},{10,11... | collective-permute-start | bytes 245768 | tf_op jit(solution)/shard_map/ppermute | solution.py:634
  23.0 13.1 %all-to-all-start = ((f32[16,3,192]{2,1,0:T(4,128)}), f32[16,3,192]{2,1,0:T(4,128)S(1)}, u32[]{:S(2)}, u32[]{:S(2)}) async-start(f32[16,3,192]{2,1,0:T(4,128)} %bitcast.7), calls=%async_computation | async-start | bytes 131072 | tf_op jit(solution)/shard_map/all_to_all | solution.py:639

commit v7 on v6

--- a/solution.py
+++ b/solution.py
@@ -45,7 +45,7 @@
     owner_rows = density.shape[0]
     rows = density.shape[-2]
     copies = []
-    for shift, out in enumerate(outs):
+    for shift, out in zip((0, *reversed(range(1, len(outs)))), outs):
         slab = jnp.bitwise_xor(me, shift)
         base = jnp.int32(owner_rows)
         count = jnp.int32(0)
@@ -95,7 +95,7 @@
     own, *outgoing = rows_to_send(region, density, slabs, share)
     near = {}
     for shift in reversed(range(1, slabs)):
-        near[shift] = lax.ppermute(outgoing[shift - 1], "grid", [(i, i ^ shift) for i in range(slabs)])
+        near[shift] = lax.ppermute(outgoing[slabs - 1 - shift], "grid", [(i, i ^ shift) for i in range(slabs)])
     return own, [near[shift] for shift in range(1, slabs)]
 
 
@@ -184,6 +184,7 @@
     batch = pl.program_id(0)
     batches = pl.num_programs(0)
     me = lax.axis_index("grid")
+    me_atoms = lax.axis_index("atoms")
     size = tiles.shape[-1]
     region_size = region.shape[1]
 
@@ -239,7 +240,7 @@
         left = jnp.concatenate(lefts, axis=1).astype(BF16)
         chunk = out.shape[-1]
         scale = [jnp.sum(energy_sums[c], axis=1, keepdims=True) for c in range(PARTS)]
-        for device in range(out.shape[1]):
+        for device in range(out.shape[0]):
             atoms = lax.broadcasted_iota(jnp.int32, (chunk, size), 0) + device * chunk
             hot = [
                 jnp.where(atoms == fn_atom[pl.ds(region[me, position], 1), :], 1.0, 0.0).astype(BF16)
@@ -251,8 +252,7 @@
             for c in range(PARTS):
                 value = found[c : c + 1] + found[PARTS + c : PARTS + c + 1] + found[2 * PARTS + c : 2 * PARTS + c + 1]
                 value = value + jnp.sum(jnp.where(mine, scale[c], 0.0), axis=0, keepdims=True)
-                for slab in range(slabs):
-                    out[slab, device, c : c + 1, :] = value
+                out[jnp.bitwise_xor(me_atoms, device), c : c + 1, :] = value
 
 
 def partial_gradient(
@@ -268,7 +268,7 @@
     block = pl.BlockSpec((1, points, columns), lambda b, *_: (b, 0, 0))
     whole = pl.BlockSpec(memory_space=pltpu.VMEM)
     tile_shape = (region_size * width + 1, size, size)
-    out_shape = (slabs, atom_devices, PARTS, atom_total // atom_devices)
+    out_shape = (atom_devices, PARTS, atom_total // atom_devices)
     return pl.pallas_call(
         functools.partial(
             gradient_kernel, points=points, blocks=blocks, width=width, owner_rows=owner_rows, slabs=slabs
@@ -330,28 +330,33 @@
     )(region, pattern, basis, tiles)
 
 
-def add_moments(moments, turned, grads, fresh):
+def moment_terms(blocks):
+    return [(c, p) for c in range(PARTS) for p in range(0, blocks, 2)]
+
+
+def add_moments(moments, turned, grads, fresh, term):
+    c, p = term
     blocks, _, size = grads.shape[1:]
-    for c in range(PARTS):
-        for p in range(0, blocks, 2):
-            rows = slice(max(p - 1, 0) * size, min(p + 3, blocks) * size)
-            columns = slice(p * size, min(p + 2, blocks) * size)
-            right = jnp.concatenate([grads[c, place] for place in range(p, min(p + 2, blocks))], axis=1)
-            value = jnp.dot(turned[rows, :], right, preferred_element_type=F32)
-            moments[c, rows, columns] = value if fresh else moments[c, rows, columns] + value
+    rows = slice(max(p - 1, 0) * size, min(p + 3, blocks) * size)
+    columns = slice(p * size, min(p + 2, blocks) * size)
+    right = jnp.concatenate([grads[c, place] for place in range(p, min(p + 2, blocks))], axis=1)
+    value = jnp.dot(turned[rows, :], right, preferred_element_type=F32)
+    moments[c, rows, columns] = value if fresh else moments[c, rows, columns] + value
 
 
 def reorder_kernel(
-    pattern,
+    pattern_hbm,
     basis,
     field,
     basis_grad,
-    weights,
+    weights_hbm,
     basis_out,
     field_out,
     moments,
     last_turned,
     last_grads,
+    pattern,
+    weights,
     basis_in,
     field_in,
     grad_in,
@@ -359,6 +364,7 @@
     turned,
     grads,
     sems,
+    small_sems,
 ):
     batches, blocks, points, size = basis_out.shape
     groups = sems.shape[0]
@@ -374,33 +380,48 @@
             pltpu.make_async_copy(basis.at[here], basis_in.at[here], sems.at[group, 2]),
         )
 
-    for group in range(groups):
+    for copy in copies(0):
+        copy.start()
+    small = (
+        pltpu.make_async_copy(pattern_hbm, pattern, small_sems.at[0]),
+        pltpu.make_async_copy(weights_hbm, weights, small_sems.at[1]),
+    )
+    for copy in small:
+        copy.start()
+    for group in range(1, groups):
         for copy in copies(group):
             copy.start()
+    for copy in small:
+        copy.wait()
+
+    def put_in_order(group, inner, array):
+        batch = group * step + inner
+        points_here = slice(inner * points, (inner + 1) * points)
+        source = (field_in, basis_in)[array].at[batch] if array < 2 else grad_in.at[array - 2, batch]
+        wide[array] = source[...].astype(F32)
+        for s in range(blocks):
+            place = pattern[s, batch]
+            values = wide[array, pl.ds(s, points, stride=blocks), :]
+            if array == 0:
+                field_out[batch, place] = values.astype(BF16)
+                rows = pl.ds(pl.multiple_of(place * size, size), size)
+                turned[group][rows, points_here] = (values.T * weights[batch : batch + 1, :]).astype(BF16)
+            elif array == 1:
+                basis_out[batch, place] = values.astype(BF16)
+            else:
+                grads[group][array - 2, place, points_here, :] = values.astype(BF16)
 
     for group in range(groups):
         for copy in copies(group):
             copy.wait()
-        for inner in range(step):
-            batch = group * step + inner
-            points_here = slice(inner * points, (inner + 1) * points)
-            places = [pattern[s, batch] for s in range(blocks)]
-            weight = weights[batch : batch + 1, :]
-            wide[0] = field_in[batch].astype(F32)
-            wide[1] = basis_in[batch].astype(F32)
-            for c in range(PARTS):
-                wide[2 + c] = grad_in[c, batch].astype(F32)
-            for s, place in enumerate(places):
-                strided = pl.ds(s, points, stride=blocks)
-                values = wide[0, strided, :]
-                field_out[batch, place] = values.astype(BF16)
-                rows = pl.ds(pl.multiple_of(place * size, size), size)
-                turned[group][rows, points_here] = (values.T * weight).astype(BF16)
-                basis_out[batch, place] = wide[1, strided, :].astype(BF16)
-                for c in range(PARTS):
-                    grads[group][c, place, points_here, :] = wide[2 + c, strided, :].astype(BF16)
-        if group > 0:
-            add_moments(moments, turned[group - 1], grads[group - 1], group == 1)
+        products = moment_terms(blocks) if group > 0 else []
+        work = [(inner, array) for inner in range(step) for array in range(2 + PARTS)]
+        done = 0
+        for number, (inner, array) in enumerate(work):
+            put_in_order(group, inner, array)
+            while done < len(products) and done * len(work) < (number + 1) * len(products):
+                add_moments(moments, turned[group - 1], grads[group - 1], group == 1, products[done])
+                done += 1
     if groups == 1:
         moments[...] = jnp.zeros_like(moments)
 
@@ -423,9 +444,11 @@
             jax.ShapeDtypeStruct(turned, BF16),
             jax.ShapeDtypeStruct(grads, BF16),
         ),
-        in_specs=[pl.BlockSpec(memory_space=pltpu.SMEM), hbm, hbm, hbm, vmem],
+        in_specs=[hbm] * 5,
         out_specs=(vmem,) * 5,
         scratch_shapes=[
+            pltpu.SMEM((blocks, batches), jnp.int32),
+            pltpu.VMEM(weights.shape, F32),
             pltpu.VMEM((batches, rows, size), BF16),
             pltpu.VMEM((batches, rows, size), BF16),
             pltpu.VMEM((PARTS, batches, rows, size), BF16),
@@ -433,6 +456,7 @@
             pltpu.VMEM(turned, BF16),
             pltpu.VMEM(grads, BF16),
             pltpu.SemaphoreType.DMA((batches // step, 3)),
+            pltpu.SemaphoreType.DMA((2,)),
         ],
         compiler_params=pltpu.CompilerParams(vmem_limit_bytes=VMEM_LIMIT),
         cost_estimate=pl.CostEstimate(
@@ -463,7 +487,8 @@
     for c in range(PARTS):
         padded = jnp.concatenate([weight_grad[c], jnp.zeros((size - batches, weight_grad.shape[2]), F32)], axis=0)
         grad_columns[c] = padded.T
-    add_moments(moments, turned, grads, False)
+    for term in moment_terms(blocks):
+        add_moments(moments, turned, grads, False, term)
 
 
 def moments_and_atoms(region, before, turned, grads, weight_grad, fn_atom, batch_atom, atom_total):
@@ -484,15 +509,7 @@
         cost_estimate=pl.CostEstimate(
             flops=2 * PARTS * depth * (blocks * size) ** 2, bytes_accessed=0, transcendentals=0
         ),
-    )(
-        in_hbm(region),
-        before,
-        turned,
-        grads,
-        in_hbm(weight_grad),
-        in_hbm(fn_atom.reshape(-1, size)),
-        in_hbm(batch_atom.reshape(1, -1)),
-    )
+    )(region, before, turned, grads, weight_grad, fn_atom.reshape(-1, size), batch_atom.reshape(1, -1))
 
 
 def combine_kernel(
@@ -501,6 +518,7 @@
     *pieces, product_out, out, stage, matrix, energies = rest
     batches, blocks, points, size = basis.shape
     me = lax.axis_index("grid")
+    me_atoms = lax.axis_index("atoms")
     half = (width - 1) // 2
     stage_rows(stage, pieces[0], pieces[1:slabs], pieces[slabs:], SHARE)
     rows = [region[me, position] for position in range(blocks)]
@@ -558,13 +576,12 @@
     high, middle, low = (piece.astype(F32) for piece in split(left))
     left = jnp.concatenate([high, middle, low, jnp.zeros((16 - 3 * PARTS, left.shape[1]), F32)], axis=0).astype(BF16)
     chunk = out.shape[-1]
-    for device in range(out.shape[1]):
+    for device in range(out.shape[0]):
         sums = lax.dot_general(
             left, hot[device * chunk : (device + 1) * chunk, :], NT, preferred_element_type=F32
         )
         value = sums[:PARTS] + sums[PARTS : 2 * PARTS] + sums[2 * PARTS : 3 * PARTS]
-        for slab in range(slabs):
-            out[slab, device] = value
+        out[jnp.bitwise_xor(me_atoms, device)] = value
 
 
 def combine(region, prepared, pieces, shapes):
@@ -577,7 +594,7 @@
         functools.partial(combine_kernel, owner_rows=owner_rows, slabs=slabs, width=width, step=step),
         out_shape=(
             jax.ShapeDtypeStruct(basis.shape, BF16),
-            jax.ShapeDtypeStruct((slabs, atom_devices, PARTS, atom_total // atom_devices), F32),
+            jax.ShapeDtypeStruct((atom_devices, PARTS, atom_total // atom_devices), F32),
         ),
         in_specs=[pl.BlockSpec(memory_space=pltpu.SMEM)] + [vmem] * (5 + len(pieces)),
         out_specs=(vmem, vmem),
@@ -587,7 +604,7 @@
             pltpu.VMEM((points, size), F32),
         ],
         compiler_params=pltpu.CompilerParams(vmem_limit_bytes=VMEM_LIMIT),
-    )(in_hbm(region), basis, field, moments, hot, grad_columns, *pieces)
+    )(region, basis, field, moments, hot, grad_columns, *pieces)
 
 
 def write_kernel(pattern, product, out, wide, staged, sems):
@@ -625,7 +642,7 @@
         ],
         compiler_params=pltpu.CompilerParams(vmem_limit_bytes=VMEM_LIMIT),
         cost_estimate=pl.CostEstimate(flops=0, bytes_accessed=4 * math.prod(shape), transcendentals=0),
-    )(in_hbm(pattern.T), product)
+    )(pattern.T, product)
 
 
 def swap_halves(near, ready, atom_devices):
@@ -634,10 +651,22 @@
     return near, [lax.ppermute(piece, "atoms", swap) for piece in near], ready
 
 
-def sum_parts(partial_grad):
-    parts = partial_grad.reshape((-1,) + partial_grad.shape[2:])
-    parts = lax.all_to_all(parts, ("grid", "atoms"), split_axis=0, concat_axis=0, tiled=True)
-    return jnp.sum(parts, axis=0)
+def tree_sum(values):
+    if len(values) == 1:
+        return values[0]
+    half = len(values) // 2
+    return tree_sum(values[:half]) + tree_sum(values[half:])
+
+
+def exchange_all(parts, axis, count):
+    moved = {d: lax.ppermute(parts[d], axis, [(i, i ^ d) for i in range(count)]) for d in range(1, count)}
+    return [parts[0]] + [moved[d] for d in range(1, count)]
+
+
+def sum_parts(partial_grad, product, slabs, atom_devices):
+    total = tree_sum(exchange_all([partial_grad[d] for d in range(atom_devices)], "atoms", atom_devices))
+    total, product = lax.optimization_barrier((total, product))
+    return tree_sum(exchange_all([total] * slabs, "grid", slabs)), product
 
 
 def local(
@@ -665,7 +694,7 @@
         built = moments_and_atoms(region, *partial, weight_grad, fn_atom, batch_atom, atom_total)
         ready = (basis_wide, field_wide, *built)
         product, partial_grad = combine(region, ready, [own, *near, *far], shapes)
-        gradient = sum_parts(partial_grad)
+        gradient, product = sum_parts(partial_grad, product, slabs, atom_devices)
         contracted = write(pattern, product)
         return contracted.reshape(basis.shape), gradient
     ready = relayout(
@@ -688,7 +717,7 @@
         [own, *near, *far],
         shapes,
     )
-    gradient = sum_parts(partial_grad)
+    gradient, basis_wide = sum_parts(partial_grad, basis_wide, slabs, atom_devices)
     contracted = contract(region, pattern, basis_wide, tiles, points, blocks, width)
     return contracted.reshape(basis.shape), gradient
 

time: 37.1 us -> 36.1 us (0.973)
  waiting for transfers between devices: 4.72 us -> 4.1 us
  Pallas kernels: 18.1 us -> 17.7 us
    ppermute x3 -> x9, starting transfers between devices: 5.74 us -> 12.1 us  [the longest x6 6.38 us: exchange_all(): lax.ppermute(parts[d], axis, [(i, i ^ d) for i in range(count)])]
    all_to_all x1 -> x0, starting transfers between devices: 6.18 us -> none  [sum_parts(): lax.all_to_all(parts, ('grid', 'atoms'), split_axis=0, concat_axis=0, til...]
    all_to_all x1 -> x0, waiting for transfers between devices: 4.71 us -> none  [sum_parts(): lax.all_to_all(parts, ('grid', 'atoms'), split_axis=0, concat_axis=0, til...]
    ppermute x3 -> x9, waiting for transfers between devices: 0.01 us -> 4.09 us  [the longest x6 4.09 us: exchange_all(): lax.ppermute(parts[d], axis, [(i, i ^ d) for i in range(count)])]
    pallas_call x1, Pallas kernels: 4.11 us -> 3.36 us  [combine(): pl.pallas_call(functools.partial(combine_kernel, owner_rows=owner_rows, s...]
    pallas_call x1, Pallas kernels: 8.11 us -> 8.75 us  [reorder(): pl.pallas_call(reorder_kernel, out_shape=(ordered, ordered, jax.ShapeDtyp...]
    reduce_sum x1 -> x0, other arithmetic: 0.62 us -> none  [sum_parts(): return jnp.sum(parts, axis=0)]
    add x0 -> x2, other arithmetic: none -> 0.6 us  [tree_sum(): return tree_sum(values[:half]) + tree_sum(values[half:])]
  transfers between devices with their start and end apart: 7 -> 12, of which waited for: 1 -> 4; matrix products, arithmetic and copies ran while one was open for 0% -> 0% of each run, Pallas kernels for 33% -> 35%
where the time goes in v7:
time: 36.1 us; the launch traced here: 35.9 us
  Pallas kernels  17.7 us (49%)
  starting transfers between devices  12.7 us (35%)
  waiting for transfers between devices  4.1 us (11%)
  between operations  0.77 us (2%)
  other arithmetic  0.6 us (2%)
    pallas_call x1, Pallas kernels, reorder(): pl.pallas_call(reorder_kernel, out_shape=(ordered, ordered, jax.ShapeDtyp...  8.75 us
    ppermute x6, starting transfers between devices, exchange_all(): lax.ppermute(parts[d], axis, [(i, i ^ d) for i in range(count)])  6.38 us
    ppermute x3, starting transfers between devices, fetch_rows(): lax.ppermute(outgoing[slabs - 1 - shift], 'grid', [(i, i ^ shift) for i i...  5.7 us
    ppermute x6, waiting for transfers between devices, exchange_all(): lax.ppermute(parts[d], axis, [(i, i ^ d) for i in range(count)])  4.09 us
    pallas_call x1, Pallas kernels, combine(): pl.pallas_call(functools.partial(combine_kernel, owner_rows=owner_rows, s...  3.36 us
    pallas_call x1, Pallas kernels, write(): pl.pallas_call(write_kernel, out_shape=jax.ShapeDtypeStruct(shape, BF16),...  2.06 us
    pallas_call x1, Pallas kernels, rows_to_send(): pl.pallas_call(functools.partial(send_kernel, share=share), out_shape=[ja...  1.85 us
    pallas_call x1, Pallas kernels, moments_and_atoms(): pl.pallas_call(moment_kernel, out_shape=(jax.ShapeDtypeStruct(before.shap...  1.66 us
  transfers between devices with their start and end apart: 12, of which 4 were waited for; matrix products, arithmetic and copies ran while one was open for 0% of the time, Pallas kernels for 35%

profile of v7, /device:TPU:0, one launch (start us, length us, event | category | flops | bytes accessed | tf_op | source)
XLA Modules:
  0.0 35.9 jit_solution(17290586955241857890)
XLA Ops:
  0.6 1.9 %shard_map.113 = (bf16[5,128,128]{2,1,0:T(8,128)(2,1)S(1)}, bf16[5,64,128]{2,1,0:T(8,128)(2,1)S(1)}, bf16[5,64,128]{2,1,0:T(8,128)(2,1)S(1)}, bf16[5,64,128]{2,1,0:T(8,128)(2,1)S(1)}) custom-call(s32[4,4]{1,0:T(4,128)} %region.5, bf16[15,3,128,128]{3,2,1,0:T(8,128)(2,1)} %density.1), custom_call_target="tpu_custom_call" | custom-call | tf_op jit(solution)/shard_map/pallas_call | solution.py:84
  2.5 3.1 %collective-permute-start = (bf16[5,64,128]{2,1,0:T(8,128)(2,1)S(1)}, bf16[5,64,128]{2,1,0:T(8,128)(2,1)S(1)}, u32[]{:S(2)}, u32[]{:S(2)}) collective-permute-start(bf16[5,64,128]{2,1,0:T(8,128)(2,1)S(1)} %get-tuple-element.26), channel_id=1, source_target_pairs={{0,4},{4,0},{8,12},{12,8},{1,5},{5,1},{9,13},{13,9},{2,6},{6,2},{1... | collective-permute-start | bytes 245768 | tf_op jit(solution)/shard_map/ppermute | solution.py:98
  5.6 2.6 %collective-permute-start.1 = (bf16[5,64,128]{2,1,0:T(8,128)(2,1)S(1)}, bf16[5,64,128]{2,1,0:T(8,128)(2,1)S(1)}, u32[]{:S(2)}, u32[]{:S(2)}) collective-permute-start(bf16[5,64,128]{2,1,0:T(8,128)(2,1)S(1)} %get-tuple-element.27), channel_id=1, source_target_pairs={{0,8},{4,12},{8,0},{12,4},{1,9},{5,13},{9,1},{13,5},{2,10},{6,14},... | collective-permute-start | bytes 245768 | tf_op jit(solution)/shard_map/ppermute | solution.py:98
  8.2 0.0 collective-permute-start.2
  8.2 0.0 copy-start
  8.2 0.0 copy-start.1
  8.2 0.0 copy-start.2
  8.2 0.0 copy-start.4
  8.2 8.8 %shard_map.114 = (bf16[16,4,128,128]{3,2,1,0:T(8,128)(2,1)S(1)}, bf16[16,4,128,128]{3,2,1,0:T(8,128)(2,1)S(1)}, f32[3,512,512]{2,1,0:T(8,128)S(1)}, bf16[512,512...) custom-call(s32[4,16]{1,0:T(4,128)} %bitcast.18, bf16[16,512,128]{2,1,0:T(8,128)(2,1)} %bitcast.23, ...), custom_call_target="tpu_custom_call" | custom-call | flops 3221225472 | bytes 10485760 | tf_op jit(solution)/shard_map/pallas_call | solution.py:438
  17.0 0.0 collective-permute-done.rest_1_
  17.0 0.0 collective-permute-done.1.rest_2_
  17.0 0.0 collective-permute-done.2.rest_3_
  17.0 0.1 collective-permute-start.3
  17.1 0.5 %collective-permute-start.4 = (bf16[5,64,128]{2,1,0:T(8,128)(2,1)S(1)}, bf16[5,64,128]{2,1,0:T(8,128)(2,1)S(1)}, u32[]{:S(2)}, u32[]{:S(2)}) collective-permute-start(bf16[5,64,128]{2,1,0:T(8,128)(2,1)S(1)} %collective-permute-done.1.rest_2_), channel_id=1, source_target_pairs={{0,1},{1,0},{2,3},{3,2},{4,5},{5,4},{6,7},{7,6},{8,9},{9,8},{10,11... | collective-permute-start | bytes 245768 | tf_op jit(solution)/shard_map/ppermute | solution.py:651
  17.6 0.1 collective-permute-start.5
  17.7 0.0 copy-done
  17.7 0.0 copy-done.1
  17.7 0.0 copy-done.2
  17.7 0.0 copy-done.4
  17.7 1.7 %shard_map.115 = (f32[3,512,512]{2,1,0:T(8,128)S(1)}, bf16[768,640]{1,0:T(8,128)(2,1)S(1)}, f32[3,128,128]{2,1,0:T(8,128)S(1)}) custom-call(s32[4,4]{1,0:T(4,128)S(1)} %copy-done.2, f32[3,512,512]{2,1,0:T(8,128)S(1)} %get-tuple-element.36.before, bf16[512,512]{1,0:T(8,128)(2,1)S(1)} %get-tuple-element.37.turned, ...), custom_call_target="tpu_custom_call", output_to_operand_aliasing={{0}: (1, {})} | custom-call | flops 805306368 | tf_op jit(solution)/shard_map/pallas_call | solution.py:498
  19.3 0.0 collective-permute-done.3.rest_4_
  19.4 0.0 collective-permute-done.4.rest_5_
  19.4 0.0 collective-permute-done.5.rest_6_
  19.4 0.0 copy-start.3
  19.4 3.4 %shard_map.116 = (bf16[16,4,128,128]{3,2,1,0:T(8,128)(2,1)S(1)}, f32[4,3,192]{2,1,0:T(4,128)S(1)}) custom-call(s32[4,4]{1,0:T(4,128)S(1)} %copy-done.2, bf16[16,4,128,128]{3,2,1,0:T(8,128)(2,1)S(1)} %get-tuple-element.34.basis, bf16[16,4,128,128]{3,2,1,0:T(8,128)(2,1)S(1)} %get-tuple-element.35.field, f32[3,512,512]{2,1,0:T(8,128)S(1)} %get-tuple-element.39.moments, ...), custom_call_target="tpu_custom_call" | custom-call | tf_op jit(solution)/shard_map/pallas_call | solution.py:593
  22.8 0.5 %collective-permute-start.6 = (f32[3,192]{1,0:T(4,128)S(1)}, f32[3,192]{1,0:T(4,128)S(1)}, u32[]{:S(2)}, u32[]{:S(2)}) collective-permute-start(f32[3,192]{1,0:T(4,128)S(1)} %get-tuple-element.52), channel_id=1, source_target_pairs={{0,1},{1,0},{2,3},{3,2},{4,5},{5,4},{6,7},{7,6},{8,9},{9,8},{10,11... | collective-permute-start | bytes 6920 | tf_op jit(solution)/shard_map/ppermute | solution.py:662
  23.3 1.7 %collective-permute-start.7 = (f32[3,192]{1,0:T(4,128)S(1)}, f32[3,192]{1,0:T(4,128)S(1)}, u32[]{:S(2)}, u32[]{:S(2)}) collective-permute-start(f32[3,192]{1,0:T(4,128)S(1)} %get-tuple-element.51), channel_id=1, source_target_pairs={{0,2},{1,3},{2,0},{3,1},{4,6},{5,7},{6,4},{7,5},{8,10},{9,11},{10,... | collective-permute-start | bytes 6920 | tf_op jit(solution)/shard_map/ppermute | solution.py:662
  24.9 0.0 collective-permute-start.8
  24.9 0.0 collective-permute-done.6
  25.0 1.9 %collective-permute-done.7 = f32[3,192]{1,0:T(4,128)S(1)} collective-permute-done((f32[3,192]{1,0:T(4,128)S(1)}, f32[3,192]{1,0:T(4,128)S(1)}, u32[]{:S(2)}, u32[]{:S(2)}) %collective-permute-start.7) | collective-permute-done | bytes 2336 | tf_op jit(solution)/shard_map/ppermute | solution.py:662
  26.9 1.1 %collective-permute-done.8 = f32[3,192]{1,0:T(4,128)S(1)} collective-permute-done((f32[3,192]{1,0:T(4,128)S(1)}, f32[3,192]{1,0:T(4,128)S(1)}, u32[]{:S(2)}, u32[]{:S(2)}) %collective-permute-start.8) | collective-permute-done | bytes 2336 | tf_op jit(solution)/shard_map/ppermute | solution.py:662
  28.0 1.6 %collective-permute-start.10 = (f32[3,192]{1,0:T(4,128)S(1)}, f32[3,192]{1,0:T(4,128)S(1)}, u32[]{:S(2)}, u32[]{:S(2)}) collective-permute-start(f32[3,192]{1,0:T(4,128)S(1)} %fusion), channel_id=1, source_target_pairs={{0,8},{4,12},{8,0},{12,4},{1,9},{5,13},{9,1},{13,5},{2,10},{6,14},... | collective-permute-start | bytes 6920 | tf_op jit(solution)/shard_map/ppermute | solution.py:662
  29.6 2.1 %collective-permute-start.11 = (f32[3,192]{1,0:T(4,128)S(1)}, f32[3,192]{1,0:T(4,128)S(1)}, u32[]{:S(2)}, u32[]{:S(2)}) collective-permute-start(f32[3,192]{1,0:T(4,128)S(1)} %fusion), channel_id=1, source_target_pairs={{0,12},{4,8},{8,4},{12,0},{1,13},{5,9},{9,5},{13,1},{2,14},{6,10},... | collective-permute-start | bytes 6920 | tf_op jit(solution)/shard_map/ppermute | solution.py:662
  31.7 0.5 %collective-permute-start.9 = (f32[3,192]{1,0:T(4,128)S(1)}, f32[3,192]{1,0:T(4,128)S(1)}, u32[]{:S(2)}, u32[]{:S(2)}) collective-permute-start(f32[3,192]{1,0:T(4,128)S(1)} %fusion), channel_id=1, source_target_pairs={{0,4},{4,0},{8,12},{12,8},{1,5},{5,1},{9,13},{13,9},{2,6},{6,2},{1... | collective-permute-start | bytes 6920 | tf_op jit(solution)/shard_map/ppermute | solution.py:662
  32.2 0.0 copy-done.3
  32.2 2.1 %shard_map.117 = bf16[16,512,128]{2,1,0:T(8,128)(2,1)} custom-call(s32[4,16]{1,0:T(4,128)S(1)} %bitcast.19, bf16[16,4,128,128]{3,2,1,0:T(8,128)(2,1)S(1)} %get-tuple-element.48.product), custom_call_target="tpu_custom_call" | custom-call | bytes 4194304 | tf_op jit(solution)/shard_map/pallas_call | solution.py:633
  34.3 0.0 collective-permute-done.10
  34.3 0.8 %collective-permute-done.11 = f32[3,192]{1,0:T(4,128)S(1)} collective-permute-done((f32[3,192]{1,0:T(4,128)S(1)}, f32[3,192]{1,0:T(4,128)S(1)}, u32[]{:S(2)}, u32[]{:S(2)}) %collective-permute-start.11) | collective-permute-done | bytes 2336 | tf_op jit(solution)/shard_map/ppermute | solution.py:662
  35.0 0.3 collective-permute-done.9
  35.3 0.6 %add_add_fusion = f32[3,192]{1,0:T(4,128)} fusion(f32[3,192]{1,0:T(4,128)S(1)} %collective-permute-done.10, f32[3,192]{1,0:T(4,128)S(1)} %collective-permute-done.11, f32[3,192]{1,0:T(4,128)S(1)} %fusion, f32[3,192]{1,0:T(4,128)S(1)} %collective-permute-done.9), kind=kLoop, calls=%fused_computation.2 | loop fusion | flops 1728 | bytes 11520 | tf_op jit(solution)/shard_map/add | solution.py:658
  (2 shorter events, 0.0 us)
Async XLA Ops:
  2.5 14.5 %collective-permute-start = (bf16[5,64,128]{2,1,0:T(8,128)(2,1)S(1)}, bf16[5,64,128]{2,1,0:T(8,128)(2,1)S(1)}, u32[]{:S(2)}, u32[]{:S(2)}) collective-permute-start(bf16[5,64,128]{2,1,0:T(8,128)(2,1)S(1)} %get-tuple-element.26), channel_id=1, source_target_pairs={{0,4},{4,0},{8,12},{12,8},{1,5},{5,1},{9,13},{13,9},{2,6},{6,2},{1... | collective-permute-start | bytes 245768 | tf_op jit(solution)/shard_map/ppermute | solution.py:98
  5.6 11.4 %collective-permute-start.1 = (bf16[5,64,128]{2,1,0:T(8,128)(2,1)S(1)}, bf16[5,64,128]{2,1,0:T(8,128)(2,1)S(1)}, u32[]{:S(2)}, u32[]{:S(2)}) collective-permute-start(bf16[5,64,128]{2,1,0:T(8,128)(2,1)S(1)} %get-tuple-element.27), channel_id=1, source_target_pairs={{0,8},{4,12},{8,0},{12,4},{1,9},{5,13},{9,1},{13,5},{2,10},{6,14},... | collective-permute-start | bytes 245768 | tf_op jit(solution)/shard_map/ppermute | solution.py:98
  8.2 8.8 %collective-permute-start.2 = (bf16[5,64,128]{2,1,0:T(8,128)(2,1)S(1)}, bf16[5,64,128]{2,1,0:T(8,128)(2,1)S(1)}, u32[]{:S(2)}, u32[]{:S(2)}) collective-permute-start(bf16[5,64,128]{2,1,0:T(8,128)(2,1)S(1)} %get-tuple-element.28), channel_id=1, source_target_pairs={{0,12},{4,8},{8,4},{12,0},{1,13},{5,9},{9,5},{13,1},{2,14},{6,10},... | collective-permute-start | bytes 245768 | tf_op jit(solution)/shard_map/ppermute | solution.py:98
  8.2 9.5 %copy-start = (s32[7680]{0:T(1024)S(1)}, s32[7680]{0:T(1024)}, u32[]{:S(2)}) copy-start(s32[7680]{0:T(1024)} %param.18) | copy-start | bytes 92164
  8.2 9.5 %copy-start.1 = (f32[3,16,128]{2,1,0:T(8,128)S(1)}, f32[3,16,128]{2,1,0:T(8,128)}, u32[]{:S(2)}) copy-start(f32[3,16,128]{2,1,0:T(8,128)} %weight_grad.1) | copy-start | bytes 73732
  8.2 9.5 %copy-start.2 = (s32[4,4]{1,0:T(4,128)S(1)}, s32[4,4]{1,0:T(4,128)}, u32[]{:S(2)}) copy-start(s32[4,4]{1,0:T(4,128)} %region.5) | copy-start | bytes 196
  8.2 9.5 %copy-start.4 = (s32[16]{0:T(128)S(1)}, s32[16]{0:T(128)}, u32[]{:S(2)}) copy-start(s32[16]{0:T(128)} %param.19) | copy-start | bytes 196
  17.0 2.3 %collective-permute-start.3 = (bf16[5,64,128]{2,1,0:T(8,128)(2,1)S(1)}, bf16[5,64,128]{2,1,0:T(8,128)(2,1)S(1)}, u32[]{:S(2)}, u32[]{:S(2)}) collective-permute-start(bf16[5,64,128]{2,1,0:T(8,128)(2,1)S(1)} %collective-permute-done.rest_1_), channel_id=1, source_target_pairs={{0,1},{1,0},{2,3},{3,2},{4,5},{5,4},{6,7},{7,6},{8,9},{9,8},{10,11... | collective-permute-start | bytes 245768 | tf_op jit(solution)/shard_map/ppermute | solution.py:651
  17.1 2.3 %collective-permute-start.4 = (bf16[5,64,128]{2,1,0:T(8,128)(2,1)S(1)}, bf16[5,64,128]{2,1,0:T(8,128)(2,1)S(1)}, u32[]{:S(2)}, u32[]{:S(2)}) collective-permute-start(bf16[5,64,128]{2,1,0:T(8,128)(2,1)S(1)} %collective-permute-done.1.rest_2_), channel_id=1, source_target_pairs={{0,1},{1,0},{2,3},{3,2},{4,5},{5,4},{6,7},{7,6},{8,9},{9,8},{10,11... | collective-permute-start | bytes 245768 | tf_op jit(solution)/shard_map/ppermute | solution.py:651
  17.6 1.8 %collective-permute-start.5 = (bf16[5,64,128]{2,1,0:T(8,128)(2,1)S(1)}, bf16[5,64,128]{2,1,0:T(8,128)(2,1)S(1)}, u32[]{:S(2)}, u32[]{:S(2)}) collective-permute-start(bf16[5,64,128]{2,1,0:T(8,128)(2,1)S(1)} %collective-permute-done.2.rest_3_), channel_id=1, source_target_pairs={{0,1},{1,0},{2,3},{3,2},{4,5},{5,4},{6,7},{7,6},{8,9},{9,8},{10,11... | collective-permute-start | bytes 245768 | tf_op jit(solution)/shard_map/ppermute | solution.py:651
  19.4 12.8 %copy-start.3 = (s32[16,4]{0,1:T(4,128)S(1)}, s32[16,4]{0,1:T(4,128)}, u32[]{:S(2)}) copy-start(s32[16,4]{0,1:T(4,128)} %param.17) | copy-start | bytes 772
  22.8 2.2 %collective-permute-start.6 = (f32[3,192]{1,0:T(4,128)S(1)}, f32[3,192]{1,0:T(4,128)S(1)}, u32[]{:S(2)}, u32[]{:S(2)}) collective-permute-start(f32[3,192]{1,0:T(4,128)S(1)} %get-tuple-element.52), channel_id=1, source_target_pairs={{0,1},{1,0},{2,3},{3,2},{4,5},{5,4},{6,7},{7,6},{8,9},{9,8},{10,11... | collective-permute-start | bytes 6920 | tf_op jit(solution)/shard_map/ppermute | solution.py:662
  23.3 3.6 %collective-permute-start.7 = (f32[3,192]{1,0:T(4,128)S(1)}, f32[3,192]{1,0:T(4,128)S(1)}, u32[]{:S(2)}, u32[]{:S(2)}) collective-permute-start(f32[3,192]{1,0:T(4,128)S(1)} %get-tuple-element.51), channel_id=1, source_target_pairs={{0,2},{1,3},{2,0},{3,1},{4,6},{5,7},{6,4},{7,5},{8,10},{9,11},{10,... | collective-permute-start | bytes 6920 | tf_op jit(solution)/shard_map/ppermute | solution.py:662
  24.9 3.1 %collective-permute-start.8 = (f32[3,192]{1,0:T(4,128)S(1)}, f32[3,192]{1,0:T(4,128)S(1)}, u32[]{:S(2)}, u32[]{:S(2)}) collective-permute-start(f32[3,192]{1,0:T(4,128)S(1)} %get-tuple-element.50), channel_id=1, source_target_pairs={{0,3},{1,2},{2,1},{3,0},{4,7},{5,6},{6,5},{7,4},{8,11},{9,10},{10,... | collective-permute-start | bytes 6920 | tf_op jit(solution)/shard_map/ppermute | solution.py:662
  28.0 6.3 %collective-permute-start.10 = (f32[3,192]{1,0:T(4,128)S(1)}, f32[3,192]{1,0:T(4,128)S(1)}, u32[]{:S(2)}, u32[]{:S(2)}) collective-permute-start(f32[3,192]{1,0:T(4,128)S(1)} %fusion), channel_id=1, source_target_pairs={{0,8},{4,12},{8,0},{12,4},{1,9},{5,13},{9,1},{13,5},{2,10},{6,14},... | collective-permute-start | bytes 6920 | tf_op jit(solution)/shard_map/ppermute | solution.py:662
  29.6 5.4 %collective-permute-start.11 = (f32[3,192]{1,0:T(4,128)S(1)}, f32[3,192]{1,0:T(4,128)S(1)}, u32[]{:S(2)}, u32[]{:S(2)}) collective-permute-start(f32[3,192]{1,0:T(4,128)S(1)} %fusion), channel_id=1, source_target_pairs={{0,12},{4,8},{8,4},{12,0},{1,13},{5,9},{9,5},{13,1},{2,14},{6,10},... | collective-permute-start | bytes 6920 | tf_op jit(solution)/shard_map/ppermute | solution.py:662
  31.7 3.6 %collective-permute-start.9 = (f32[3,192]{1,0:T(4,128)S(1)}, f32[3,192]{1,0:T(4,128)S(1)}, u32[]{:S(2)}, u32[]{:S(2)}) collective-permute-start(f32[3,192]{1,0:T(4,128)S(1)} %fusion), channel_id=1, source_target_pairs={{0,4},{4,0},{8,12},{12,8},{1,5},{5,1},{9,13},{13,9},{2,6},{6,2},{1... | collective-permute-start | bytes 6920 | tf_op jit(solution)/shard_map/ppermute | solution.py:662

commit v8 on v7

--- a/solution.py
+++ b/solution.py
@@ -10,6 +10,7 @@
 
 TRAVEL = 5
 SHARE = 2
+CHUNK = 2
 PARTS = 3
 F32 = jnp.float32
 BF16 = jnp.bfloat16
@@ -37,8 +38,17 @@
     return jnp.where(jnp.logical_and(slot == 0, count == 2), 1, 4)
 
 
-def send_kernel(region, density, *rest, share):
-    *outs, sems = rest
+def send_kernel(region_hbm, density, basis, field, basis_grad, *rest, share):
+    *outs, first_basis, first_field, first_grad, region, sems, small_sems = rest
+    fetches = (
+        pltpu.make_async_copy(region_hbm, region, small_sems.at[0]),
+        pltpu.make_async_copy(field.at[pl.ds(0, first_field.shape[0])], first_field, small_sems.at[1]),
+        pltpu.make_async_copy(basis_grad.at[:, pl.ds(0, first_grad.shape[1])], first_grad, small_sems.at[2]),
+        pltpu.make_async_copy(basis.at[pl.ds(0, first_basis.shape[0])], first_basis, small_sems.at[3]),
+    )
+    for copy in fetches:
+        copy.start()
+    fetches[0].wait()
     me = lax.axis_index("grid")
     part = lax.rem(lax.axis_index("atoms"), share)
     size = region.shape[1]
@@ -70,7 +80,7 @@
             copies.append(pltpu.make_async_copy(source, target, sems.at[shift, number]))
     for copy in copies:
         copy.start()
-    for copy in copies:
+    for copy in (*copies, *fetches[1:]):
         copy.wait()
 
 
@@ -78,25 +88,38 @@
     return pltpu.with_memory_space_constraint(array, pltpu.HBM)
 
 
-def rows_to_send(region, density, slabs, share):
+def rows_to_send(region, density, basis, field, basis_grad, slabs, share):
     size = density.shape[-1]
     kept = [size] + [size // share] * (slabs - 1)
+    first = jax.ShapeDtypeStruct((CHUNK, *basis.shape[1:]), BF16)
+    first_grad = jax.ShapeDtypeStruct((PARTS, CHUNK, *basis.shape[1:]), BF16)
+    hbm = pl.BlockSpec(memory_space=pl.ANY)
     return pl.pallas_call(
         functools.partial(send_kernel, share=share),
-        out_shape=[jax.ShapeDtypeStruct((TRAVEL, rows, size), density.dtype) for rows in kept],
-        in_specs=[pl.BlockSpec(memory_space=pltpu.SMEM), pl.BlockSpec(memory_space=pl.ANY)],
-        out_specs=[pl.BlockSpec(memory_space=pltpu.VMEM)] * slabs,
-        scratch_shapes=[pltpu.SemaphoreType.DMA((slabs, 3))],
+        out_shape=[
+            *(jax.ShapeDtypeStruct((TRAVEL, rows, size), density.dtype) for rows in kept),
+            first,
+            first,
+            first_grad,
+        ],
+        in_specs=[hbm] * 5,
+        out_specs=[pl.BlockSpec(memory_space=pltpu.VMEM)] * (slabs + 3),
+        scratch_shapes=[
+            pltpu.SMEM(region.shape, jnp.int32),
+            pltpu.SemaphoreType.DMA((slabs, 3)),
+            pltpu.SemaphoreType.DMA((4,)),
+        ],
         compiler_params=pltpu.CompilerParams(vmem_limit_bytes=VMEM_LIMIT),
-    )(in_hbm(region), in_hbm(density))
-
-
-def fetch_rows(region, density, slabs, share):
-    own, *outgoing = rows_to_send(region, density, slabs, share)
+    )(in_hbm(region), in_hbm(density), in_hbm(basis), in_hbm(field), in_hbm(basis_grad))
+
+
+def fetch_rows(region, density, basis, field, basis_grad, slabs, share):
+    own, *rest = rows_to_send(region, density, basis, field, basis_grad, slabs, share)
+    outgoing, first = rest[: slabs - 1], rest[slabs - 1 :]
     near = {}
     for shift in reversed(range(1, slabs)):
         near[shift] = lax.ppermute(outgoing[slabs - 1 - shift], "grid", [(i, i ^ shift) for i in range(slabs)])
-    return own, [near[shift] for shift in range(1, slabs)]
+    return own, [near[shift] for shift in range(1, slabs)], first
 
 
 def stage_rows(stage, own, near, far, share):
@@ -350,6 +373,9 @@
     field,
     basis_grad,
     weights_hbm,
+    first_basis,
+    first_field,
+    first_grad,
     basis_out,
     field_out,
     moments,
@@ -367,69 +393,71 @@
     small_sems,
 ):
     batches, blocks, points, size = basis_out.shape
-    groups = sems.shape[0]
-    step = batches // groups
+    step = last_turned.shape[1] // points
+    groups = batches // step
     turned = [last_turned if (groups - 1 - group) % 2 == 0 else turned for group in range(groups)]
     grads = [last_grads if (groups - 1 - group) % 2 == 0 else grads for group in range(groups)]
 
-    def copies(group):
-        here = pl.ds(group * step, step)
-        return (
-            pltpu.make_async_copy(field.at[here], field_in.at[here], sems.at[group, 0]),
-            pltpu.make_async_copy(basis_grad.at[:, here], grad_in.at[:, here], sems.at[group, 1]),
-            pltpu.make_async_copy(basis.at[here], basis_in.at[here], sems.at[group, 2]),
-        )
-
-    for copy in copies(0):
-        copy.start()
+    def copies(chunk):
+        here = pl.ds(chunk * CHUNK, CHUNK)
+        pairs = [(field.at[here], field_in.at[here]), (basis.at[here], basis_in.at[here])]
+        pairs += [(basis_grad.at[c, here], grad_in.at[c, here]) for c in range(PARTS)]
+        return [
+            pltpu.make_async_copy(source, target, sems.at[chunk, number])
+            for number, (source, target) in enumerate(pairs)
+        ]
+
     small = (
         pltpu.make_async_copy(pattern_hbm, pattern, small_sems.at[0]),
         pltpu.make_async_copy(weights_hbm, weights, small_sems.at[1]),
     )
     for copy in small:
         copy.start()
-    for group in range(1, groups):
-        for copy in copies(group):
+    for chunk in range(1, batches // CHUNK):
+        for copy in copies(chunk):
             copy.start()
     for copy in small:
         copy.wait()
-
-    def put_in_order(group, inner, array):
-        batch = group * step + inner
-        points_here = slice(inner * points, (inner + 1) * points)
-        source = (field_in, basis_in)[array].at[batch] if array < 2 else grad_in.at[array - 2, batch]
-        wide[array] = source[...].astype(F32)
-        for s in range(blocks):
-            place = pattern[s, batch]
-            values = wide[array, pl.ds(s, points, stride=blocks), :]
-            if array == 0:
-                field_out[batch, place] = values.astype(BF16)
+    diagonal = lax.broadcasted_iota(jnp.int32, (size, size), 0) == lax.broadcasted_iota(jnp.int32, (size, size), 1)
+    identity = jnp.where(diagonal, 1.0, 0.0).astype(BF16)
+
+    for group in range(groups):
+        for inner in range(step):
+            batch = group * step + inner
+            if batch >= CHUNK and batch % CHUNK == 0:
+                for copy in copies(batch // CHUNK):
+                    copy.wait()
+            if batch < CHUNK:
+                sources = [first_field.at[batch], first_basis.at[batch]] + [first_grad.at[c, batch] for c in range(PARTS)]
+            else:
+                sources = [field_in.at[batch], basis_in.at[batch]] + [grad_in.at[c, batch] for c in range(PARTS)]
+            points_here = slice(inner * points, (inner + 1) * points)
+            places = [pattern[s, batch] for s in range(blocks)]
+            weight = weights[batch : batch + 1, :]
+            for array, source in enumerate(sources):
+                wide[array] = source[...].astype(F32)
+            values = [
+                [wide[array, pl.ds(s, points, stride=blocks), :].astype(BF16) for s in range(blocks)]
+                for array in range(2 + PARTS)
+            ]
+            across = lax.dot_general(identity, jnp.concatenate(values[0], axis=0), NT, preferred_element_type=F32)
+            for s, place in enumerate(places):
+                field_out[batch, place] = values[0][s]
                 rows = pl.ds(pl.multiple_of(place * size, size), size)
-                turned[group][rows, points_here] = (values.T * weights[batch : batch + 1, :]).astype(BF16)
-            elif array == 1:
-                basis_out[batch, place] = values.astype(BF16)
-            else:
-                grads[group][array - 2, place, points_here, :] = values.astype(BF16)
-
-    for group in range(groups):
-        for copy in copies(group):
-            copy.wait()
-        products = moment_terms(blocks) if group > 0 else []
-        work = [(inner, array) for inner in range(step) for array in range(2 + PARTS)]
-        done = 0
-        for number, (inner, array) in enumerate(work):
-            put_in_order(group, inner, array)
-            while done < len(products) and done * len(work) < (number + 1) * len(products):
-                add_moments(moments, turned[group - 1], grads[group - 1], group == 1, products[done])
-                done += 1
+                turned[group][rows, points_here] = (across[:, s * points : (s + 1) * points] * weight).astype(BF16)
+                basis_out[batch, place] = values[1][s]
+                for c in range(PARTS):
+                    grads[group][c, place, points_here, :] = values[2 + c][s]
+        if group > 0:
+            for term in moment_terms(blocks):
+                add_moments(moments, turned[group - 1], grads[group - 1], group == 1, term)
     if groups == 1:
         moments[...] = jnp.zeros_like(moments)
 
 
-def reorder(pattern, basis, field, basis_grad, weights):
-    batches, points, blocks, size = basis.shape
-    rows = points * blocks
-    step = 4 if batches % 4 == 0 else 1
+def reorder(pattern, basis, field, basis_grad, weights, first, points, blocks):
+    batches, rows, size = basis.shape
+    step = 4 if batches % 4 == 0 else CHUNK
     hbm = pl.BlockSpec(memory_space=pl.ANY)
     vmem = pl.BlockSpec(memory_space=pltpu.VMEM)
     ordered = jax.ShapeDtypeStruct((batches, blocks, points, size), BF16)
@@ -444,7 +472,7 @@
             jax.ShapeDtypeStruct(turned, BF16),
             jax.ShapeDtypeStruct(grads, BF16),
         ),
-        in_specs=[hbm] * 5,
+        in_specs=[hbm] * 5 + [vmem] * 3,
         out_specs=(vmem,) * 5,
         scratch_shapes=[
             pltpu.SMEM((blocks, batches), jnp.int32),
@@ -455,7 +483,7 @@
             pltpu.VMEM((2 + PARTS, rows, size), F32),
             pltpu.VMEM(turned, BF16),
             pltpu.VMEM(grads, BF16),
-            pltpu.SemaphoreType.DMA((batches // step, 3)),
+            pltpu.SemaphoreType.DMA((batches // CHUNK, 2 + PARTS)),
             pltpu.SemaphoreType.DMA((2,)),
         ],
         compiler_params=pltpu.CompilerParams(vmem_limit_bytes=VMEM_LIMIT),
@@ -464,13 +492,7 @@
             bytes_accessed=2 * (2 + PARTS) * batches * rows * size,
             transcendentals=0,
         ),
-    )(
-        in_hbm(pattern.T),
-        in_hbm(basis.reshape(batches, rows, size)),
-        in_hbm(field.reshape(batches, rows, size)),
-        in_hbm(basis_grad.reshape(PARTS, batches, rows, size)),
-        in_hbm(weights),
-    )
+    )(in_hbm(pattern.T), in_hbm(basis), in_hbm(field), in_hbm(basis_grad), in_hbm(weights), *first)
 
 
 def moment_kernel(
@@ -687,9 +709,12 @@
     atom_devices = lax.axis_size("atoms")
     atom_total = fn_atom.shape[0] // (10 * slabs * atom_devices) * slabs * atom_devices
     shapes = (slabs, atom_devices, atom_total, points, blocks, width, owner_rows)
-    own, near = fetch_rows(region, density, slabs, SHARE)
+    flat_basis = basis.reshape(batches, points * blocks, size)
+    flat_field = exchange_field.reshape(batches, points * blocks, size)
+    flat_grad = basis_grad.reshape(PARTS, batches, points * blocks, size)
+    own, near, first = fetch_rows(region, density, flat_basis, flat_field, flat_grad, slabs, SHARE)
     if region.shape[1] == blocks:
-        ready = reorder(pattern, basis, exchange_field, basis_grad, weights)
+        ready = reorder(pattern, flat_basis, flat_field, flat_grad, weights, first, points, blocks)
         near, far, (basis_wide, field_wide, *partial) = swap_halves(near, ready, atom_devices)
         built = moments_and_atoms(region, *partial, weight_grad, fn_atom, batch_atom, atom_total)
         ready = (basis_wide, field_wide, *built)
@@ -697,19 +722,14 @@
         gradient, product = sum_parts(partial_grad, product, slabs, atom_devices)
         contracted = write(pattern, product)
         return contracted.reshape(basis.shape), gradient
-    ready = relayout(
-        in_hbm(basis.reshape(batches, points * blocks, size)),
-        in_hbm(exchange_field.reshape(batches, points * blocks, size)),
-        points,
-        blocks,
-    )
+    ready = relayout(in_hbm(flat_basis), in_hbm(flat_field), points, blocks)
     near, far, (basis_wide, field_wide) = swap_halves(near, ready, atom_devices)
     tiles, partial_grad = partial_gradient(
         region,
         pattern,
         basis_wide,
         field_wide,
-        in_hbm(basis_grad.reshape(PARTS, batches, points * blocks, size)),
+        in_hbm(flat_grad),
         weights,
         weight_grad,
         fn_atom,

time: 36.1 us -> 37.2 us (1.030)
  Pallas kernels: 17.7 us -> 18.8 us
    pallas_call x1, Pallas kernels: 8.75 us -> 9.79 us  [reorder(): pl.pallas_call(reorder_kernel, out_shape=(ordered, ordered, jax.ShapeDtyp...]
  transfers between devices with their start and end apart: 12 -> 12, of which waited for: 4 -> 4; matrix products, arithmetic and copies ran while one was open for 0% -> 0% of each run, Pallas kernels for 35% -> 37%
where the time goes in v8:
time: 37.2 us; the launch traced here: 36.9 us
  Pallas kernels  18.8 us (51%)
  starting transfers between devices  12.6 us (34%)
  waiting for transfers between devices  4.1 us (11%)
  between operations  0.77 us (2%)
  other arithmetic  0.6 us (2%)
    pallas_call x1, Pallas kernels, reorder(): pl.pallas_call(reorder_kernel, out_shape=(ordered, ordered, jax.ShapeDtyp...  9.79 us
    ppermute x6, starting transfers between devices, exchange_all(): lax.ppermute(parts[d], axis, [(i, i ^ d) for i in range(count)])  6.36 us
    ppermute x3, starting transfers between devices, fetch_rows(): lax.ppermute(outgoing[slabs - 1 - shift], 'grid', [(i, i ^ shift) for i i...  5.62 us
    ppermute x6, waiting for transfers between devices, exchange_all(): lax.ppermute(parts[d], axis, [(i, i ^ d) for i in range(count)])  4.09 us
    pallas_call x1, Pallas kernels, combine(): pl.pallas_call(functools.partial(combine_kernel, owner_rows=owner_rows, s...  3.34 us
    pallas_call x1, Pallas kernels, write(): pl.pallas_call(write_kernel, out_shape=jax.ShapeDtypeStruct(shape, BF16),...  2.06 us
    pallas_call x1, Pallas kernels, rows_to_send(): pl.pallas_call(functools.partial(send_kernel, share=share), out_shape=[*(...  1.95 us
    pallas_call x1, Pallas kernels, moments_and_atoms(): pl.pallas_call(moment_kernel, out_shape=(jax.ShapeDtypeStruct(before.shap...  1.67 us
  transfers between devices with their start and end apart: 12, of which 4 were waited for; matrix products, arithmetic and copies ran while one was open for 0% of the time, Pallas kernels for 37%

profile of v8, /device:TPU:0, one launch (start us, length us, event | category | flops | bytes accessed | tf_op | source)
XLA Modules:
  0.0 36.9 jit_solution(10246902118937305197)
XLA Ops:
  0.6 2.0 %shard_map.113 = (bf16[5,128,128]{2,1,0:T(8,128)(2,1)S(1)}, bf16[5,64,128]{2,1,0:T(8,128)(2,1)S(1)}, bf16[5,64,128]{2,1,0:T(8,128)(2,1)S(1)}, bf16[5,64,128]{2,1...) custom-call(s32[4,4]{1,0:T(4,128)} %region.3, ...), custom_call_target="tpu_custom_call" | custom-call | tf_op jit(solution)/shard_map/pallas_call | solution.py:97
  2.6 3.0 %collective-permute-start = (bf16[5,64,128]{2,1,0:T(8,128)(2,1)S(1)}, bf16[5,64,128]{2,1,0:T(8,128)(2,1)S(1)}, u32[]{:S(2)}, u32[]{:S(2)}) collective-permute-start(bf16[5,64,128]{2,1,0:T(8,128)(2,1)S(1)} %get-tuple-element.29), channel_id=1, source_target_pairs={{0,4},{4,0},{8,12},{12,8},{1,5},{5,1},{9,13},{13,9},{2,6},{6,2},{1... | collective-permute-start | bytes 245768 | tf_op jit(solution)/shard_map/ppermute | solution.py:121
  5.6 2.6 %collective-permute-start.1 = (bf16[5,64,128]{2,1,0:T(8,128)(2,1)S(1)}, bf16[5,64,128]{2,1,0:T(8,128)(2,1)S(1)}, u32[]{:S(2)}, u32[]{:S(2)}) collective-permute-start(bf16[5,64,128]{2,1,0:T(8,128)(2,1)S(1)} %get-tuple-element.30), channel_id=1, source_target_pairs={{0,8},{4,12},{8,0},{12,4},{1,9},{5,13},{9,1},{13,5},{2,10},{6,14},... | collective-permute-start | bytes 245768 | tf_op jit(solution)/shard_map/ppermute | solution.py:121
  8.2 0.0 collective-permute-start.2
  8.2 0.0 copy-start
  8.2 0.0 copy-start.1
  8.2 0.0 copy-start.2
  8.2 0.0 copy-start.4
  8.2 9.8 %shard_map.114 = (bf16[16,4,128,128]{3,2,1,0:T(8,128)(2,1)S(1)}, bf16[16,4,128,128]{3,2,1,0:T(8,128)(2,1)S(1)}, f32[3,512,512]{2,1,0:T(8,128)S(1)}, bf16[512,512...) custom-call(s32[4,16]{1,0:T(4,128)} %bitcast.18, bf16[16,512,128]{2,1,0:T(8,128)(2,1)} %bitcast.24, ...), custom_call_target="tpu_custom_call" | custom-call | flops 3221225472 | bytes 10485760 | tf_op jit(solution)/shard_map/pallas_call | solution.py:466
  18.0 0.0 collective-permute-done.rest_1_
  18.0 0.0 collective-permute-done.1.rest_2_
  18.1 0.0 collective-permute-done.2.rest_3_
  18.1 0.1 collective-permute-start.3
  18.1 0.5 %collective-permute-start.4 = (bf16[5,64,128]{2,1,0:T(8,128)(2,1)S(1)}, bf16[5,64,128]{2,1,0:T(8,128)(2,1)S(1)}, u32[]{:S(2)}, u32[]{:S(2)}) collective-permute-start(bf16[5,64,128]{2,1,0:T(8,128)(2,1)S(1)} %collective-permute-done.1.rest_2_), channel_id=1, source_target_pairs={{0,1},{1,0},{2,3},{3,2},{4,5},{5,4},{6,7},{7,6},{8,9},{9,8},{10,11... | collective-permute-start | bytes 245768 | tf_op jit(solution)/shard_map/ppermute | solution.py:673
  18.6 0.1 collective-permute-start.5
  18.7 0.0 copy-done
  18.7 0.0 copy-done.1
  18.7 0.0 copy-done.2
  18.7 0.0 copy-done.4
  18.7 1.7 %shard_map.115 = (f32[3,512,512]{2,1,0:T(8,128)S(1)}, bf16[768,640]{1,0:T(8,128)(2,1)S(1)}, f32[3,128,128]{2,1,0:T(8,128)S(1)}) custom-call(s32[4,4]{1,0:T(4,128)S(1)} %copy-done.2, f32[3,512,512]{2,1,0:T(8,128)S(1)} %get-tuple-element.42.before, bf16[512,512]{1,0:T(8,128)(2,1)S(1)} %get-tuple-element.43.turned, ...), custom_call_target="tpu_custom_call", output_to_operand_aliasing={{0}: (1, {})} | custom-call | flops 805306368 | tf_op jit(solution)/shard_map/pallas_call | solution.py:520
  20.4 0.0 collective-permute-done.3.rest_4_
  20.4 0.0 collective-permute-done.4.rest_5_
  20.4 0.0 collective-permute-done.5.rest_6_
  20.4 0.0 copy-start.3
  20.5 3.3 %shard_map.116 = (bf16[16,4,128,128]{3,2,1,0:T(8,128)(2,1)S(1)}, f32[4,3,192]{2,1,0:T(4,128)S(1)}) custom-call(s32[4,4]{1,0:T(4,128)S(1)} %copy-done.2, bf16[16,4,128,128]{3,2,1,0:T(8,128)(2,1)S(1)} %get-tuple-element.40.basis, bf16[16,4,128,128]{3,2,1,0:T(8,128)(2,1)S(1)} %get-tuple-element.41.field, f32[3,512,512]{2,1,0:T(8,128)S(1)} %get-tuple-element.45.moments, ...), custom_call_target="tpu_custom_call" | custom-call | tf_op jit(solution)/shard_map/pallas_call | solution.py:615
  23.8 0.5 %collective-permute-start.6 = (f32[3,192]{1,0:T(4,128)S(1)}, f32[3,192]{1,0:T(4,128)S(1)}, u32[]{:S(2)}, u32[]{:S(2)}) collective-permute-start(f32[3,192]{1,0:T(4,128)S(1)} %get-tuple-element.58), channel_id=1, source_target_pairs={{0,1},{1,0},{2,3},{3,2},{4,5},{5,4},{6,7},{7,6},{8,9},{9,8},{10,11... | collective-permute-start | bytes 6920 | tf_op jit(solution)/shard_map/ppermute | solution.py:684
  24.3 1.7 %collective-permute-start.7 = (f32[3,192]{1,0:T(4,128)S(1)}, f32[3,192]{1,0:T(4,128)S(1)}, u32[]{:S(2)}, u32[]{:S(2)}) collective-permute-start(f32[3,192]{1,0:T(4,128)S(1)} %get-tuple-element.57), channel_id=1, source_target_pairs={{0,2},{1,3},{2,0},{3,1},{4,6},{5,7},{6,4},{7,5},{8,10},{9,11},{10,... | collective-permute-start | bytes 6920 | tf_op jit(solution)/shard_map/ppermute | solution.py:684
  26.1 0.0 collective-permute-start.8
  26.1 0.0 collective-permute-done.6
  26.1 1.9 %collective-permute-done.7 = f32[3,192]{1,0:T(4,128)S(1)} collective-permute-done((f32[3,192]{1,0:T(4,128)S(1)}, f32[3,192]{1,0:T(4,128)S(1)}, u32[]{:S(2)}, u32[]{:S(2)}) %collective-permute-start.7) | collective-permute-done | bytes 2336 | tf_op jit(solution)/shard_map/ppermute | solution.py:684
  27.9 1.2 %collective-permute-done.8 = f32[3,192]{1,0:T(4,128)S(1)} collective-permute-done((f32[3,192]{1,0:T(4,128)S(1)}, f32[3,192]{1,0:T(4,128)S(1)}, u32[]{:S(2)}, u32[]{:S(2)}) %collective-permute-start.8) | collective-permute-done | bytes 2336 | tf_op jit(solution)/shard_map/ppermute | solution.py:684
  29.1 1.6 %collective-permute-start.10 = (f32[3,192]{1,0:T(4,128)S(1)}, f32[3,192]{1,0:T(4,128)S(1)}, u32[]{:S(2)}, u32[]{:S(2)}) collective-permute-start(f32[3,192]{1,0:T(4,128)S(1)} %fusion), channel_id=1, source_target_pairs={{0,8},{4,12},{8,0},{12,4},{1,9},{5,13},{9,1},{13,5},{2,10},{6,14},... | collective-permute-start | bytes 6920 | tf_op jit(solution)/shard_map/ppermute | solution.py:684
  30.7 2.0 %collective-permute-start.11 = (f32[3,192]{1,0:T(4,128)S(1)}, f32[3,192]{1,0:T(4,128)S(1)}, u32[]{:S(2)}, u32[]{:S(2)}) collective-permute-start(f32[3,192]{1,0:T(4,128)S(1)} %fusion), channel_id=1, source_target_pairs={{0,12},{4,8},{8,4},{12,0},{1,13},{5,9},{9,5},{13,1},{2,14},{6,10},... | collective-permute-start | bytes 6920 | tf_op jit(solution)/shard_map/ppermute | solution.py:684
  32.7 0.5 %collective-permute-start.9 = (f32[3,192]{1,0:T(4,128)S(1)}, f32[3,192]{1,0:T(4,128)S(1)}, u32[]{:S(2)}, u32[]{:S(2)}) collective-permute-start(f32[3,192]{1,0:T(4,128)S(1)} %fusion), channel_id=1, source_target_pairs={{0,4},{4,0},{8,12},{12,8},{1,5},{5,1},{9,13},{13,9},{2,6},{6,2},{1... | collective-permute-start | bytes 6920 | tf_op jit(solution)/shard_map/ppermute | solution.py:684
  33.2 0.0 copy-done.3
  33.2 2.1 %shard_map.117 = bf16[16,512,128]{2,1,0:T(8,128)(2,1)} custom-call(s32[4,16]{1,0:T(4,128)S(1)} %bitcast.19, bf16[16,4,128,128]{3,2,1,0:T(8,128)(2,1)S(1)} %get-tuple-element.54.product), custom_call_target="tpu_custom_call" | custom-call | bytes 4194304 | tf_op jit(solution)/shard_map/pallas_call | solution.py:655
  35.3 0.0 collective-permute-done.10
  35.3 0.8 %collective-permute-done.11 = f32[3,192]{1,0:T(4,128)S(1)} collective-permute-done((f32[3,192]{1,0:T(4,128)S(1)}, f32[3,192]{1,0:T(4,128)S(1)}, u32[]{:S(2)}, u32[]{:S(2)}) %collective-permute-start.11) | collective-permute-done | bytes 2336 | tf_op jit(solution)/shard_map/ppermute | solution.py:684
  36.2 0.2 collective-permute-done.9
  36.3 0.6 %add_add_fusion = f32[3,192]{1,0:T(4,128)} fusion(f32[3,192]{1,0:T(4,128)S(1)} %collective-permute-done.10, f32[3,192]{1,0:T(4,128)S(1)} %collective-permute-done.11, f32[3,192]{1,0:T(4,128)S(1)} %fusion, f32[3,192]{1,0:T(4,128)S(1)} %collective-permute-done.9), kind=kLoop, calls=%fused_computation.2 | loop fusion | flops 1728 | bytes 11520 | tf_op jit(solution)/shard_map/add | solution.py:680
  (2 shorter events, 0.0 us)
Async XLA Ops:
  2.6 15.4 %collective-permute-start = (bf16[5,64,128]{2,1,0:T(8,128)(2,1)S(1)}, bf16[5,64,128]{2,1,0:T(8,128)(2,1)S(1)}, u32[]{:S(2)}, u32[]{:S(2)}) collective-permute-start(bf16[5,64,128]{2,1,0:T(8,128)(2,1)S(1)} %get-tuple-element.29), channel_id=1, source_target_pairs={{0,4},{4,0},{8,12},{12,8},{1,5},{5,1},{9,13},{13,9},{2,6},{6,2},{1... | collective-permute-start | bytes 245768 | tf_op jit(solution)/shard_map/ppermute | solution.py:121
  5.6 12.4 %collective-permute-start.1 = (bf16[5,64,128]{2,1,0:T(8,128)(2,1)S(1)}, bf16[5,64,128]{2,1,0:T(8,128)(2,1)S(1)}, u32[]{:S(2)}, u32[]{:S(2)}) collective-permute-start(bf16[5,64,128]{2,1,0:T(8,128)(2,1)S(1)} %get-tuple-element.30), channel_id=1, source_target_pairs={{0,8},{4,12},{8,0},{12,4},{1,9},{5,13},{9,1},{13,5},{2,10},{6,14},... | collective-permute-start | bytes 245768 | tf_op jit(solution)/shard_map/ppermute | solution.py:121
  8.2 9.8 %collective-permute-start.2 = (bf16[5,64,128]{2,1,0:T(8,128)(2,1)S(1)}, bf16[5,64,128]{2,1,0:T(8,128)(2,1)S(1)}, u32[]{:S(2)}, u32[]{:S(2)}) collective-permute-start(bf16[5,64,128]{2,1,0:T(8,128)(2,1)S(1)} %get-tuple-element.31), channel_id=1, source_target_pairs={{0,12},{4,8},{8,4},{12,0},{1,13},{5,9},{9,5},{13,1},{2,14},{6,10},... | collective-permute-start | bytes 245768 | tf_op jit(solution)/shard_map/ppermute | solution.py:121
  8.2 10.5 %copy-start = (s32[7680]{0:T(1024)S(1)}, s32[7680]{0:T(1024)}, u32[]{:S(2)}) copy-start(s32[7680]{0:T(1024)} %param.18) | copy-start | bytes 92164
  8.2 10.5 %copy-start.1 = (f32[3,16,128]{2,1,0:T(8,128)S(1)}, f32[3,16,128]{2,1,0:T(8,128)}, u32[]{:S(2)}) copy-start(f32[3,16,128]{2,1,0:T(8,128)} %weight_grad.1) | copy-start | bytes 73732
  8.2 10.5 %copy-start.2 = (s32[4,4]{1,0:T(4,128)S(1)}, s32[4,4]{1,0:T(4,128)}, u32[]{:S(2)}) copy-start(s32[4,4]{1,0:T(4,128)} %region.3) | copy-start | bytes 196
  8.2 10.5 %copy-start.4 = (s32[16]{0:T(128)S(1)}, s32[16]{0:T(128)}, u32[]{:S(2)}) copy-start(s32[16]{0:T(128)} %param.19) | copy-start | bytes 196
  18.1 2.3 %collective-permute-start.3 = (bf16[5,64,128]{2,1,0:T(8,128)(2,1)S(1)}, bf16[5,64,128]{2,1,0:T(8,128)(2,1)S(1)}, u32[]{:S(2)}, u32[]{:S(2)}) collective-permute-start(bf16[5,64,128]{2,1,0:T(8,128)(2,1)S(1)} %collective-permute-done.rest_1_), channel_id=1, source_target_pairs={{0,1},{1,0},{2,3},{3,2},{4,5},{5,4},{6,7},{7,6},{8,9},{9,8},{10,11... | collective-permute-start | bytes 245768 | tf_op jit(solution)/shard_map/ppermute | solution.py:673
  18.1 2.3 %collective-permute-start.4 = (bf16[5,64,128]{2,1,0:T(8,128)(2,1)S(1)}, bf16[5,64,128]{2,1,0:T(8,128)(2,1)S(1)}, u32[]{:S(2)}, u32[]{:S(2)}) collective-permute-start(bf16[5,64,128]{2,1,0:T(8,128)(2,1)S(1)} %collective-permute-done.1.rest_2_), channel_id=1, source_target_pairs={{0,1},{1,0},{2,3},{3,2},{4,5},{5,4},{6,7},{7,6},{8,9},{9,8},{10,11... | collective-permute-start | bytes 245768 | tf_op jit(solution)/shard_map/ppermute | solution.py:673
  18.6 1.8 %collective-permute-start.5 = (bf16[5,64,128]{2,1,0:T(8,128)(2,1)S(1)}, bf16[5,64,128]{2,1,0:T(8,128)(2,1)S(1)}, u32[]{:S(2)}, u32[]{:S(2)}) collective-permute-start(bf16[5,64,128]{2,1,0:T(8,128)(2,1)S(1)} %collective-permute-done.2.rest_3_), channel_id=1, source_target_pairs={{0,1},{1,0},{2,3},{3,2},{4,5},{5,4},{6,7},{7,6},{8,9},{9,8},{10,11... | collective-permute-start | bytes 245768 | tf_op jit(solution)/shard_map/ppermute | solution.py:673
  20.4 12.8 %copy-start.3 = (s32[16,4]{0,1:T(4,128)S(1)}, s32[16,4]{0,1:T(4,128)}, u32[]{:S(2)}) copy-start(s32[16,4]{0,1:T(4,128)} %param.17) | copy-start | bytes 772
  23.8 2.2 %collective-permute-start.6 = (f32[3,192]{1,0:T(4,128)S(1)}, f32[3,192]{1,0:T(4,128)S(1)}, u32[]{:S(2)}, u32[]{:S(2)}) collective-permute-start(f32[3,192]{1,0:T(4,128)S(1)} %get-tuple-element.58), channel_id=1, source_target_pairs={{0,1},{1,0},{2,3},{3,2},{4,5},{5,4},{6,7},{7,6},{8,9},{9,8},{10,11... | collective-permute-start | bytes 6920 | tf_op jit(solution)/shard_map/ppermute | solution.py:684
  24.3 3.6 %collective-permute-start.7 = (f32[3,192]{1,0:T(4,128)S(1)}, f32[3,192]{1,0:T(4,128)S(1)}, u32[]{:S(2)}, u32[]{:S(2)}) collective-permute-start(f32[3,192]{1,0:T(4,128)S(1)} %get-tuple-element.57), channel_id=1, source_target_pairs={{0,2},{1,3},{2,0},{3,1},{4,6},{5,7},{6,4},{7,5},{8,10},{9,11},{10,... | collective-permute-start | bytes 6920 | tf_op jit(solution)/shard_map/ppermute | solution.py:684
  26.1 3.1 %collective-permute-start.8 = (f32[3,192]{1,0:T(4,128)S(1)}, f32[3,192]{1,0:T(4,128)S(1)}, u32[]{:S(2)}, u32[]{:S(2)}) collective-permute-start(f32[3,192]{1,0:T(4,128)S(1)} %get-tuple-element.56), channel_id=1, source_target_pairs={{0,3},{1,2},{2,1},{3,0},{4,7},{5,6},{6,5},{7,4},{8,11},{9,10},{10,... | collective-permute-start | bytes 6920 | tf_op jit(solution)/shard_map/ppermute | solution.py:684
  29.1 6.2 %collective-permute-start.10 = (f32[3,192]{1,0:T(4,128)S(1)}, f32[3,192]{1,0:T(4,128)S(1)}, u32[]{:S(2)}, u32[]{:S(2)}) collective-permute-start(f32[3,192]{1,0:T(4,128)S(1)} %fusion), channel_id=1, source_target_pairs={{0,8},{4,12},{8,0},{12,4},{1,9},{5,13},{9,1},{13,5},{2,10},{6,14},... | collective-permute-start | bytes 6920 | tf_op jit(solution)/shard_map/ppermute | solution.py:684
  30.7 5.4 %collective-permute-start.11 = (f32[3,192]{1,0:T(4,128)S(1)}, f32[3,192]{1,0:T(4,128)S(1)}, u32[]{:S(2)}, u32[]{:S(2)}) collective-permute-start(f32[3,192]{1,0:T(4,128)S(1)} %fusion), channel_id=1, source_target_pairs={{0,12},{4,8},{8,4},{12,0},{1,13},{5,9},{9,5},{13,1},{2,14},{6,10},... | collective-permute-start | bytes 6920 | tf_op jit(solution)/shard_map/ppermute | solution.py:684
  32.7 3.6 %collective-permute-start.9 = (f32[3,192]{1,0:T(4,128)S(1)}, f32[3,192]{1,0:T(4,128)S(1)}, u32[]{:S(2)}, u32[]{:S(2)}) collective-permute-start(f32[3,192]{1,0:T(4,128)S(1)} %fusion), channel_id=1, source_target_pairs={{0,4},{4,0},{8,12},{12,8},{1,5},{5,1},{9,13},{13,9},{2,6},{6,2},{1... | collective-permute-start | bytes 6920 | tf_op jit(solution)/shard_map/ppermute | solution.py:684

commit v9 on v8

--- a/solution.py
+++ b/solution.py
@@ -418,39 +418,44 @@
             copy.start()
     for copy in small:
         copy.wait()
-    diagonal = lax.broadcasted_iota(jnp.int32, (size, size), 0) == lax.broadcasted_iota(jnp.int32, (size, size), 1)
-    identity = jnp.where(diagonal, 1.0, 0.0).astype(BF16)
+
+    def put_in_order(group, inner, array, starts):
+        batch = group * step + inner
+        points_here = slice(inner * points, (inner + 1) * points)
+        if array < 2:
+            source = ((first_field, first_basis) if batch < CHUNK else (field_in, basis_in))[array].at[batch]
+        else:
+            source = (first_grad if batch < CHUNK else grad_in).at[array - 2, batch]
+        wide[array] = source[...].astype(F32)
+        for place in range(blocks):
+            values = wide[array, pl.ds(starts[place], points, stride=blocks), :].astype(BF16)
+            if array == 0:
+                field_out[batch, place] = values
+                across = values.T.astype(F32) * weights[batch : batch + 1, :]
+                turned[group][place * size : (place + 1) * size, points_here] = across.astype(BF16)
+            elif array == 1:
+                basis_out[batch, place] = values
+            else:
+                grads[group][array - 2, place, points_here, :] = values
 
     for group in range(groups):
-        for inner in range(step):
+        products = moment_terms(blocks) if group > 0 else []
+        work = step * (2 + PARTS)
+        done = 0
+        for number in range(work):
+            inner, array = divmod(number, 2 + PARTS)
             batch = group * step + inner
-            if batch >= CHUNK and batch % CHUNK == 0:
-                for copy in copies(batch // CHUNK):
-                    copy.wait()
-            if batch < CHUNK:
-                sources = [first_field.at[batch], first_basis.at[batch]] + [first_grad.at[c, batch] for c in range(PARTS)]
-            else:
-                sources = [field_in.at[batch], basis_in.at[batch]] + [grad_in.at[c, batch] for c in range(PARTS)]
-            points_here = slice(inner * points, (inner + 1) * points)
-            places = [pattern[s, batch] for s in range(blocks)]
-            weight = weights[batch : batch + 1, :]
-            for array, source in enumerate(sources):
-                wide[array] = source[...].astype(F32)
-            values = [
-                [wide[array, pl.ds(s, points, stride=blocks), :].astype(BF16) for s in range(blocks)]
-                for array in range(2 + PARTS)
-            ]
-            across = lax.dot_general(identity, jnp.concatenate(values[0], axis=0), NT, preferred_element_type=F32)
-            for s, place in enumerate(places):
-                field_out[batch, place] = values[0][s]
-                rows = pl.ds(pl.multiple_of(place * size, size), size)
-                turned[group][rows, points_here] = (across[:, s * points : (s + 1) * points] * weight).astype(BF16)
-                basis_out[batch, place] = values[1][s]
-                for c in range(PARTS):
-                    grads[group][c, place, points_here, :] = values[2 + c][s]
-        if group > 0:
-            for term in moment_terms(blocks):
-                add_moments(moments, turned[group - 1], grads[group - 1], group == 1, term)
+            if array == 0:
+                if batch >= CHUNK and batch % CHUNK == 0:
+                    for copy in copies(batch // CHUNK):
+                        copy.wait()
+                starts = [
+                    sum(jnp.where(pattern[s, batch] == place, s, 0) for s in range(blocks)) for place in range(blocks)
+                ]
+            put_in_order(group, inner, array, starts)
+            while done < len(products) and done * work < (number + 1) * len(products):
+                add_moments(moments, turned[group - 1], grads[group - 1], group == 1, products[done])
+                done += 1
     if groups == 1:
         moments[...] = jnp.zeros_like(moments)
 

time: 37.2 us -> 38.3 us (1.030)
  Pallas kernels: 18.8 us -> 19.9 us
    pallas_call x1, Pallas kernels: 9.79 us -> 10.9 us  [reorder(): pl.pallas_call(reorder_kernel, out_shape=(ordered, ordered, jax.ShapeDtyp...]
  transfers between devices with their start and end apart: 12 -> 12, of which waited for: 4 -> 4; matrix products, arithmetic and copies ran while one was open for 0% -> 0% of each run, Pallas kernels for 37% -> 39%
where the time goes in v9:
time: 38.3 us; the launch traced here: 38.1 us
  Pallas kernels  19.9 us (52%)
  starting transfers between devices  12.7 us (33%)
  waiting for transfers between devices  4.1 us (11%)
  between operations  0.77 us (2%)
  other arithmetic  0.6 us (2%)
    pallas_call x1, Pallas kernels, reorder(): pl.pallas_call(reorder_kernel, out_shape=(ordered, ordered, jax.ShapeDtyp...  10.9 us
    ppermute x6, starting transfers between devices, exchange_all(): lax.ppermute(parts[d], axis, [(i, i ^ d) for i in range(count)])  6.38 us
    ppermute x3, starting transfers between devices, fetch_rows(): lax.ppermute(outgoing[slabs - 1 - shift], 'grid', [(i, i ^ shift) for i i...  5.68 us
    ppermute x6, waiting for transfers between devices, exchange_all(): lax.ppermute(parts[d], axis, [(i, i ^ d) for i in range(count)])  4.09 us
    pallas_call x1, Pallas kernels, combine(): pl.pallas_call(functools.partial(combine_kernel, owner_rows=owner_rows, s...  3.34 us
    pallas_call x1, Pallas kernels, write(): pl.pallas_call(write_kernel, out_shape=jax.ShapeDtypeStruct(shape, BF16),...  2.06 us
    pallas_call x1, Pallas kernels, rows_to_send(): pl.pallas_call(functools.partial(send_kernel, share=share), out_shape=[*(...  1.89 us
    pallas_call x1, Pallas kernels, moments_and_atoms(): pl.pallas_call(moment_kernel, out_shape=(jax.ShapeDtypeStruct(before.shap...  1.67 us
  transfers between devices with their start and end apart: 12, of which 4 were waited for; matrix products, arithmetic and copies ran while one was open for 0% of the time, Pallas kernels for 39%

profile of v9, /device:TPU:0, one launch (start us, length us, event | category | flops | bytes accessed | tf_op | source)
XLA Modules:
  0.0 38.1 jit_solution(984729699985009051)
XLA Ops:
  0.6 1.9 %shard_map.113 = (bf16[5,128,128]{2,1,0:T(8,128)(2,1)S(1)}, bf16[5,64,128]{2,1,0:T(8,128)(2,1)S(1)}, bf16[5,64,128]{2,1,0:T(8,128)(2,1)S(1)}, bf16[5,64,128]{2,1...) custom-call(s32[4,4]{1,0:T(4,128)} %region.3, ...), custom_call_target="tpu_custom_call" | custom-call | tf_op jit(solution)/shard_map/pallas_call | solution.py:97
  2.5 3.1 %collective-permute-start = (bf16[5,64,128]{2,1,0:T(8,128)(2,1)S(1)}, bf16[5,64,128]{2,1,0:T(8,128)(2,1)S(1)}, u32[]{:S(2)}, u32[]{:S(2)}) collective-permute-start(bf16[5,64,128]{2,1,0:T(8,128)(2,1)S(1)} %get-tuple-element.29), channel_id=1, source_target_pairs={{0,4},{4,0},{8,12},{12,8},{1,5},{5,1},{9,13},{13,9},{2,6},{6,2},{1... | collective-permute-start | bytes 245768 | tf_op jit(solution)/shard_map/ppermute | solution.py:121
  5.6 2.6 %collective-permute-start.1 = (bf16[5,64,128]{2,1,0:T(8,128)(2,1)S(1)}, bf16[5,64,128]{2,1,0:T(8,128)(2,1)S(1)}, u32[]{:S(2)}, u32[]{:S(2)}) collective-permute-start(bf16[5,64,128]{2,1,0:T(8,128)(2,1)S(1)} %get-tuple-element.30), channel_id=1, source_target_pairs={{0,8},{4,12},{8,0},{12,4},{1,9},{5,13},{9,1},{13,5},{2,10},{6,14},... | collective-permute-start | bytes 245768 | tf_op jit(solution)/shard_map/ppermute | solution.py:121
  8.2 0.0 collective-permute-start.2
  8.2 0.0 copy-start
  8.2 0.0 copy-start.1
  8.2 0.0 copy-start.2
  8.2 0.0 copy-start.4
  8.2 10.9 %shard_map.114 = (bf16[16,4,128,128]{3,2,1,0:T(8,128)(2,1)S(1)}, bf16[16,4,128,128]{3,2,1,0:T(8,128)(2,1)S(1)}, f32[3,512,512]{2,1,0:T(8,128)S(1)}, bf16[512,512...) custom-call(s32[4,16]{1,0:T(4,128)} %bitcast.18, bf16[16,512,128]{2,1,0:T(8,128)(2,1)} %bitcast.24, ...), custom_call_target="tpu_custom_call" | custom-call | flops 3221225472 | bytes 10485760 | tf_op jit(solution)/shard_map/pallas_call | solution.py:471
  19.2 0.0 collective-permute-done.rest_1_
  19.2 0.0 collective-permute-done.1.rest_2_
  19.2 0.0 collective-permute-done.2.rest_3_
  19.2 0.1 collective-permute-start.3
  19.3 0.5 %collective-permute-start.4 = (bf16[5,64,128]{2,1,0:T(8,128)(2,1)S(1)}, bf16[5,64,128]{2,1,0:T(8,128)(2,1)S(1)}, u32[]{:S(2)}, u32[]{:S(2)}) collective-permute-start(bf16[5,64,128]{2,1,0:T(8,128)(2,1)S(1)} %collective-permute-done.1.rest_2_), channel_id=1, source_target_pairs={{0,1},{1,0},{2,3},{3,2},{4,5},{5,4},{6,7},{7,6},{8,9},{9,8},{10,11... | collective-permute-start | bytes 245768 | tf_op jit(solution)/shard_map/ppermute | solution.py:678
  19.8 0.1 collective-permute-start.5
  19.9 0.0 copy-done
  19.9 0.0 copy-done.1
  19.9 0.0 copy-done.2
  19.9 0.0 copy-done.4
  19.9 1.7 %shard_map.115 = (f32[3,512,512]{2,1,0:T(8,128)S(1)}, bf16[768,640]{1,0:T(8,128)(2,1)S(1)}, f32[3,128,128]{2,1,0:T(8,128)S(1)}) custom-call(s32[4,4]{1,0:T(4,128)S(1)} %copy-done.2, f32[3,512,512]{2,1,0:T(8,128)S(1)} %get-tuple-element.42.before, bf16[512,512]{1,0:T(8,128)(2,1)S(1)} %get-tuple-element.43.turned, ...), custom_call_target="tpu_custom_call", output_to_operand_aliasing={{0}: (1, {})} | custom-call | flops 805306368 | tf_op jit(solution)/shard_map/pallas_call | solution.py:525
  21.6 0.0 collective-permute-done.3.rest_4_
  21.6 0.0 collective-permute-done.4.rest_5_
  21.6 0.0 collective-permute-done.5.rest_6_
  21.6 0.0 copy-start.3
  21.6 3.3 %shard_map.116 = (bf16[16,4,128,128]{3,2,1,0:T(8,128)(2,1)S(1)}, f32[4,3,192]{2,1,0:T(4,128)S(1)}) custom-call(s32[4,4]{1,0:T(4,128)S(1)} %copy-done.2, bf16[16,4,128,128]{3,2,1,0:T(8,128)(2,1)S(1)} %get-tuple-element.40.basis, bf16[16,4,128,128]{3,2,1,0:T(8,128)(2,1)S(1)} %get-tuple-element.41.field, f32[3,512,512]{2,1,0:T(8,128)S(1)} %get-tuple-element.45.moments, ...), custom_call_target="tpu_custom_call" | custom-call | tf_op jit(solution)/shard_map/pallas_call | solution.py:620
  25.0 0.5 %collective-permute-start.6 = (f32[3,192]{1,0:T(4,128)S(1)}, f32[3,192]{1,0:T(4,128)S(1)}, u32[]{:S(2)}, u32[]{:S(2)}) collective-permute-start(f32[3,192]{1,0:T(4,128)S(1)} %get-tuple-element.58), channel_id=1, source_target_pairs={{0,1},{1,0},{2,3},{3,2},{4,5},{5,4},{6,7},{7,6},{8,9},{9,8},{10,11... | collective-permute-start | bytes 6920 | tf_op jit(solution)/shard_map/ppermute | solution.py:689
  25.5 1.7 %collective-permute-start.7 = (f32[3,192]{1,0:T(4,128)S(1)}, f32[3,192]{1,0:T(4,128)S(1)}, u32[]{:S(2)}, u32[]{:S(2)}) collective-permute-start(f32[3,192]{1,0:T(4,128)S(1)} %get-tuple-element.57), channel_id=1, source_target_pairs={{0,2},{1,3},{2,0},{3,1},{4,6},{5,7},{6,4},{7,5},{8,10},{9,11},{10,... | collective-permute-start | bytes 6920 | tf_op jit(solution)/shard_map/ppermute | solution.py:689
  27.2 0.0 collective-permute-start.8
  27.2 0.0 collective-permute-done.6
  27.2 1.9 %collective-permute-done.7 = f32[3,192]{1,0:T(4,128)S(1)} collective-permute-done((f32[3,192]{1,0:T(4,128)S(1)}, f32[3,192]{1,0:T(4,128)S(1)}, u32[]{:S(2)}, u32[]{:S(2)}) %collective-permute-start.7) | collective-permute-done | bytes 2336 | tf_op jit(solution)/shard_map/ppermute | solution.py:689
  29.1 1.2 %collective-permute-done.8 = f32[3,192]{1,0:T(4,128)S(1)} collective-permute-done((f32[3,192]{1,0:T(4,128)S(1)}, f32[3,192]{1,0:T(4,128)S(1)}, u32[]{:S(2)}, u32[]{:S(2)}) %collective-permute-start.8) | collective-permute-done | bytes 2336 | tf_op jit(solution)/shard_map/ppermute | solution.py:689
  30.2 1.7 %collective-permute-start.10 = (f32[3,192]{1,0:T(4,128)S(1)}, f32[3,192]{1,0:T(4,128)S(1)}, u32[]{:S(2)}, u32[]{:S(2)}) collective-permute-start(f32[3,192]{1,0:T(4,128)S(1)} %fusion), channel_id=1, source_target_pairs={{0,8},{4,12},{8,0},{12,4},{1,9},{5,13},{9,1},{13,5},{2,10},{6,14},... | collective-permute-start | bytes 6920 | tf_op jit(solution)/shard_map/ppermute | solution.py:689
  31.9 2.0 %collective-permute-start.11 = (f32[3,192]{1,0:T(4,128)S(1)}, f32[3,192]{1,0:T(4,128)S(1)}, u32[]{:S(2)}, u32[]{:S(2)}) collective-permute-start(f32[3,192]{1,0:T(4,128)S(1)} %fusion), channel_id=1, source_target_pairs={{0,12},{4,8},{8,4},{12,0},{1,13},{5,9},{9,5},{13,1},{2,14},{6,10},... | collective-permute-start | bytes 6920 | tf_op jit(solution)/shard_map/ppermute | solution.py:689
  33.9 0.5 %collective-permute-start.9 = (f32[3,192]{1,0:T(4,128)S(1)}, f32[3,192]{1,0:T(4,128)S(1)}, u32[]{:S(2)}, u32[]{:S(2)}) collective-permute-start(f32[3,192]{1,0:T(4,128)S(1)} %fusion), channel_id=1, source_target_pairs={{0,4},{4,0},{8,12},{12,8},{1,5},{5,1},{9,13},{13,9},{2,6},{6,2},{1... | collective-permute-start | bytes 6920 | tf_op jit(solution)/shard_map/ppermute | solution.py:689
  34.4 0.0 copy-done.3
  34.4 2.1 %shard_map.117 = bf16[16,512,128]{2,1,0:T(8,128)(2,1)} custom-call(s32[4,16]{1,0:T(4,128)S(1)} %bitcast.19, bf16[16,4,128,128]{3,2,1,0:T(8,128)(2,1)S(1)} %get-tuple-element.54.product), custom_call_target="tpu_custom_call" | custom-call | bytes 4194304 | tf_op jit(solution)/shard_map/pallas_call | solution.py:660
  36.5 0.0 collective-permute-done.10
  36.5 0.8 %collective-permute-done.11 = f32[3,192]{1,0:T(4,128)S(1)} collective-permute-done((f32[3,192]{1,0:T(4,128)S(1)}, f32[3,192]{1,0:T(4,128)S(1)}, u32[]{:S(2)}, u32[]{:S(2)}) %collective-permute-start.11) | collective-permute-done | bytes 2336 | tf_op jit(solution)/shard_map/ppermute | solution.py:689
  37.3 0.2 collective-permute-done.9
  37.5 0.6 %add_add_fusion = f32[3,192]{1,0:T(4,128)} fusion(f32[3,192]{1,0:T(4,128)S(1)} %collective-permute-done.10, f32[3,192]{1,0:T(4,128)S(1)} %collective-permute-done.11, f32[3,192]{1,0:T(4,128)S(1)} %fusion, f32[3,192]{1,0:T(4,128)S(1)} %collective-permute-done.9), kind=kLoop, calls=%fused_computation.2 | loop fusion | flops 1728 | bytes 11520 | tf_op jit(solution)/shard_map/add | solution.py:685
  (2 shorter events, 0.0 us)
Async XLA Ops:
  2.5 16.7 %collective-permute-start = (bf16[5,64,128]{2,1,0:T(8,128)(2,1)S(1)}, bf16[5,64,128]{2,1,0:T(8,128)(2,1)S(1)}, u32[]{:S(2)}, u32[]{:S(2)}) collective-permute-start(bf16[5,64,128]{2,1,0:T(8,128)(2,1)S(1)} %get-tuple-element.29), channel_id=1, source_target_pairs={{0,4},{4,0},{8,12},{12,8},{1,5},{5,1},{9,13},{13,9},{2,6},{6,2},{1... | collective-permute-start | bytes 245768 | tf_op jit(solution)/shard_map/ppermute | solution.py:121
  5.6 13.6 %collective-permute-start.1 = (bf16[5,64,128]{2,1,0:T(8,128)(2,1)S(1)}, bf16[5,64,128]{2,1,0:T(8,128)(2,1)S(1)}, u32[]{:S(2)}, u32[]{:S(2)}) collective-permute-start(bf16[5,64,128]{2,1,0:T(8,128)(2,1)S(1)} %get-tuple-element.30), channel_id=1, source_target_pairs={{0,8},{4,12},{8,0},{12,4},{1,9},{5,13},{9,1},{13,5},{2,10},{6,14},... | collective-permute-start | bytes 245768 | tf_op jit(solution)/shard_map/ppermute | solution.py:121
  8.2 11.0 %collective-permute-start.2 = (bf16[5,64,128]{2,1,0:T(8,128)(2,1)S(1)}, bf16[5,64,128]{2,1,0:T(8,128)(2,1)S(1)}, u32[]{:S(2)}, u32[]{:S(2)}) collective-permute-start(bf16[5,64,128]{2,1,0:T(8,128)(2,1)S(1)} %get-tuple-element.31), channel_id=1, source_target_pairs={{0,12},{4,8},{8,4},{12,0},{1,13},{5,9},{9,5},{13,1},{2,14},{6,10},... | collective-permute-start | bytes 245768 | tf_op jit(solution)/shard_map/ppermute | solution.py:121
  8.2 11.7 %copy-start = (s32[7680]{0:T(1024)S(1)}, s32[7680]{0:T(1024)}, u32[]{:S(2)}) copy-start(s32[7680]{0:T(1024)} %param.18) | copy-start | bytes 92164
  8.2 11.7 %copy-start.1 = (f32[3,16,128]{2,1,0:T(8,128)S(1)}, f32[3,16,128]{2,1,0:T(8,128)}, u32[]{:S(2)}) copy-start(f32[3,16,128]{2,1,0:T(8,128)} %weight_grad.1) | copy-start | bytes 73732
  8.2 11.7 %copy-start.2 = (s32[4,4]{1,0:T(4,128)S(1)}, s32[4,4]{1,0:T(4,128)}, u32[]{:S(2)}) copy-start(s32[4,4]{1,0:T(4,128)} %region.3) | copy-start | bytes 196
  8.2 11.7 %copy-start.4 = (s32[16]{0:T(128)S(1)}, s32[16]{0:T(128)}, u32[]{:S(2)}) copy-start(s32[16]{0:T(128)} %param.19) | copy-start | bytes 196
  19.2 2.3 %collective-permute-start.3 = (bf16[5,64,128]{2,1,0:T(8,128)(2,1)S(1)}, bf16[5,64,128]{2,1,0:T(8,128)(2,1)S(1)}, u32[]{:S(2)}, u32[]{:S(2)}) collective-permute-start(bf16[5,64,128]{2,1,0:T(8,128)(2,1)S(1)} %collective-permute-done.rest_1_), channel_id=1, source_target_pairs={{0,1},{1,0},{2,3},{3,2},{4,5},{5,4},{6,7},{7,6},{8,9},{9,8},{10,11... | collective-permute-start | bytes 245768 | tf_op jit(solution)/shard_map/ppermute | solution.py:678
  19.3 2.3 %collective-permute-start.4 = (bf16[5,64,128]{2,1,0:T(8,128)(2,1)S(1)}, bf16[5,64,128]{2,1,0:T(8,128)(2,1)S(1)}, u32[]{:S(2)}, u32[]{:S(2)}) collective-permute-start(bf16[5,64,128]{2,1,0:T(8,128)(2,1)S(1)} %collective-permute-done.1.rest_2_), channel_id=1, source_target_pairs={{0,1},{1,0},{2,3},{3,2},{4,5},{5,4},{6,7},{7,6},{8,9},{9,8},{10,11... | collective-permute-start | bytes 245768 | tf_op jit(solution)/shard_map/ppermute | solution.py:678
  19.8 1.8 %collective-permute-start.5 = (bf16[5,64,128]{2,1,0:T(8,128)(2,1)S(1)}, bf16[5,64,128]{2,1,0:T(8,128)(2,1)S(1)}, u32[]{:S(2)}, u32[]{:S(2)}) collective-permute-start(bf16[5,64,128]{2,1,0:T(8,128)(2,1)S(1)} %collective-permute-done.2.rest_3_), channel_id=1, source_target_pairs={{0,1},{1,0},{2,3},{3,2},{4,5},{5,4},{6,7},{7,6},{8,9},{9,8},{10,11... | collective-permute-start | bytes 245768 | tf_op jit(solution)/shard_map/ppermute | solution.py:678
  21.6 12.8 %copy-start.3 = (s32[16,4]{0,1:T(4,128)S(1)}, s32[16,4]{0,1:T(4,128)}, u32[]{:S(2)}) copy-start(s32[16,4]{0,1:T(4,128)} %param.17) | copy-start | bytes 772
  25.0 2.2 %collective-permute-start.6 = (f32[3,192]{1,0:T(4,128)S(1)}, f32[3,192]{1,0:T(4,128)S(1)}, u32[]{:S(2)}, u32[]{:S(2)}) collective-permute-start(f32[3,192]{1,0:T(4,128)S(1)} %get-tuple-element.58), channel_id=1, source_target_pairs={{0,1},{1,0},{2,3},{3,2},{4,5},{5,4},{6,7},{7,6},{8,9},{9,8},{10,11... | collective-permute-start | bytes 6920 | tf_op jit(solution)/shard_map/ppermute | solution.py:689
  25.5 3.6 %collective-permute-start.7 = (f32[3,192]{1,0:T(4,128)S(1)}, f32[3,192]{1,0:T(4,128)S(1)}, u32[]{:S(2)}, u32[]{:S(2)}) collective-permute-start(f32[3,192]{1,0:T(4,128)S(1)} %get-tuple-element.57), channel_id=1, source_target_pairs={{0,2},{1,3},{2,0},{3,1},{4,6},{5,7},{6,4},{7,5},{8,10},{9,11},{10,... | collective-permute-start | bytes 6920 | tf_op jit(solution)/shard_map/ppermute | solution.py:689
  27.2 3.1 %collective-permute-start.8 = (f32[3,192]{1,0:T(4,128)S(1)}, f32[3,192]{1,0:T(4,128)S(1)}, u32[]{:S(2)}, u32[]{:S(2)}) collective-permute-start(f32[3,192]{1,0:T(4,128)S(1)} %get-tuple-element.56), channel_id=1, source_target_pairs={{0,3},{1,2},{2,1},{3,0},{4,7},{5,6},{6,5},{7,4},{8,11},{9,10},{10,... | collective-permute-start | bytes 6920 | tf_op jit(solution)/shard_map/ppermute | solution.py:689
  30.2 6.2 %collective-permute-start.10 = (f32[3,192]{1,0:T(4,128)S(1)}, f32[3,192]{1,0:T(4,128)S(1)}, u32[]{:S(2)}, u32[]{:S(2)}) collective-permute-start(f32[3,192]{1,0:T(4,128)S(1)} %fusion), channel_id=1, source_target_pairs={{0,8},{4,12},{8,0},{12,4},{1,9},{5,13},{9,1},{13,5},{2,10},{6,14},... | collective-permute-start | bytes 6920 | tf_op jit(solution)/shard_map/ppermute | solution.py:689
  31.9 5.4 %collective-permute-start.11 = (f32[3,192]{1,0:T(4,128)S(1)}, f32[3,192]{1,0:T(4,128)S(1)}, u32[]{:S(2)}, u32[]{:S(2)}) collective-permute-start(f32[3,192]{1,0:T(4,128)S(1)} %fusion), channel_id=1, source_target_pairs={{0,12},{4,8},{8,4},{12,0},{1,13},{5,9},{9,5},{13,1},{2,14},{6,10},... | collective-permute-start | bytes 6920 | tf_op jit(solution)/shard_map/ppermute | solution.py:689
  33.9 3.6 %collective-permute-start.9 = (f32[3,192]{1,0:T(4,128)S(1)}, f32[3,192]{1,0:T(4,128)S(1)}, u32[]{:S(2)}, u32[]{:S(2)}) collective-permute-start(f32[3,192]{1,0:T(4,128)S(1)} %fusion), channel_id=1, source_target_pairs={{0,4},{4,0},{8,12},{12,8},{1,5},{5,1},{9,13},{13,9},{2,6},{6,2},{1... | collective-permute-start | bytes 6920 | tf_op jit(solution)/shard_map/ppermute | solution.py:689

commit v10 on v7

--- a/solution.py
+++ b/solution.py
@@ -24,8 +24,7 @@
     for other in range(region.shape[1]):
         same = jnp.where(lax.div(region[slab, other], owner_rows) == owner, 1, 0)
         count = count + same
-        if other < position:
-            slot = slot + same
+        slot = slot + jnp.where(other < position, same, 0)
     return owner, slot, count
 
 
@@ -330,20 +329,6 @@
     )(region, pattern, basis, tiles)
 
 
-def moment_terms(blocks):
-    return [(c, p) for c in range(PARTS) for p in range(0, blocks, 2)]
-
-
-def add_moments(moments, turned, grads, fresh, term):
-    c, p = term
-    blocks, _, size = grads.shape[1:]
-    rows = slice(max(p - 1, 0) * size, min(p + 3, blocks) * size)
-    columns = slice(p * size, min(p + 2, blocks) * size)
-    right = jnp.concatenate([grads[c, place] for place in range(p, min(p + 2, blocks))], axis=1)
-    value = jnp.dot(turned[rows, :], right, preferred_element_type=F32)
-    moments[c, rows, columns] = value if fresh else moments[c, rows, columns] + value
-
-
 def reorder_kernel(
     pattern_hbm,
     basis,
@@ -352,100 +337,78 @@
     weights_hbm,
     basis_out,
     field_out,
-    moments,
-    last_turned,
-    last_grads,
+    turned,
+    grads,
     pattern,
     weights,
     basis_in,
     field_in,
     grad_in,
     wide,
-    turned,
-    grads,
     sems,
     small_sems,
 ):
     batches, blocks, points, size = basis_out.shape
-    groups = sems.shape[0]
-    step = batches // groups
-    turned = [last_turned if (groups - 1 - group) % 2 == 0 else turned for group in range(groups)]
-    grads = [last_grads if (groups - 1 - group) % 2 == 0 else grads for group in range(groups)]
-
-    def copies(group):
-        here = pl.ds(group * step, step)
+
+    def copies(batch):
         return (
-            pltpu.make_async_copy(field.at[here], field_in.at[here], sems.at[group, 0]),
-            pltpu.make_async_copy(basis_grad.at[:, here], grad_in.at[:, here], sems.at[group, 1]),
-            pltpu.make_async_copy(basis.at[here], basis_in.at[here], sems.at[group, 2]),
+            pltpu.make_async_copy(field.at[batch], field_in.at[batch], sems.at[batch, 0]),
+            pltpu.make_async_copy(basis.at[batch], basis_in.at[batch], sems.at[batch, 1]),
+            pltpu.make_async_copy(basis_grad.at[:, batch], grad_in.at[:, batch], sems.at[batch, 2]),
         )
 
-    for copy in copies(0):
-        copy.start()
     small = (
         pltpu.make_async_copy(pattern_hbm, pattern, small_sems.at[0]),
         pltpu.make_async_copy(weights_hbm, weights, small_sems.at[1]),
     )
     for copy in small:
         copy.start()
-    for group in range(1, groups):
-        for copy in copies(group):
+
+    @pl.loop(0, batches)
+    def _(batch):
+        for copy in copies(batch):
             copy.start()
+
     for copy in small:
         copy.wait()
 
-    def put_in_order(group, inner, array):
-        batch = group * step + inner
-        points_here = slice(inner * points, (inner + 1) * points)
-        source = (field_in, basis_in)[array].at[batch] if array < 2 else grad_in.at[array - 2, batch]
-        wide[array] = source[...].astype(F32)
-        for s in range(blocks):
-            place = pattern[s, batch]
-            values = wide[array, pl.ds(s, points, stride=blocks), :]
-            if array == 0:
-                field_out[batch, place] = values.astype(BF16)
-                rows = pl.ds(pl.multiple_of(place * size, size), size)
-                turned[group][rows, points_here] = (values.T * weights[batch : batch + 1, :]).astype(BF16)
-            elif array == 1:
-                basis_out[batch, place] = values.astype(BF16)
-            else:
-                grads[group][array - 2, place, points_here, :] = values.astype(BF16)
-
-    for group in range(groups):
-        for copy in copies(group):
+    @pl.loop(0, batches)
+    def _(batch):
+        for copy in copies(batch):
             copy.wait()
-        products = moment_terms(blocks) if group > 0 else []
-        work = [(inner, array) for inner in range(step) for array in range(2 + PARTS)]
-        done = 0
-        for number, (inner, array) in enumerate(work):
-            put_in_order(group, inner, array)
-            while done < len(products) and done * len(work) < (number + 1) * len(products):
-                add_moments(moments, turned[group - 1], grads[group - 1], group == 1, products[done])
-                done += 1
-    if groups == 1:
-        moments[...] = jnp.zeros_like(moments)
+        points_here = pl.ds(pl.multiple_of(batch * points, points), points)
+        places = [pattern[s, batch] for s in range(blocks)]
+        weight = weights[pl.ds(batch, 1), :]
+        wide[0] = field_in[batch].astype(F32)
+        wide[1] = basis_in[batch].astype(F32)
+        for c in range(PARTS):
+            wide[2 + c] = grad_in[c, batch].astype(F32)
+        for s, place in enumerate(places):
+            strided = pl.ds(s, points, stride=blocks)
+            values = wide[0, strided, :]
+            field_out[batch, place] = values.astype(BF16)
+            turned[pl.ds(pl.multiple_of(place * size, size), size), points_here] = (values.T * weight).astype(BF16)
+            basis_out[batch, place] = wide[1, strided, :].astype(BF16)
+            for c in range(PARTS):
+                grads[c, place, points_here, :] = wide[2 + c, strided, :].astype(BF16)
 
 
 def reorder(pattern, basis, field, basis_grad, weights):
     batches, points, blocks, size = basis.shape
     rows = points * blocks
-    step = 4 if batches % 4 == 0 else 1
     hbm = pl.BlockSpec(memory_space=pl.ANY)
     vmem = pl.BlockSpec(memory_space=pltpu.VMEM)
     ordered = jax.ShapeDtypeStruct((batches, blocks, points, size), BF16)
-    turned = (blocks * size, step * points)
-    grads = (PARTS, blocks, step * points, size)
     return pl.pallas_call(
         reorder_kernel,
         out_shape=(
             ordered,
             ordered,
-            jax.ShapeDtypeStruct((PARTS, blocks * size, blocks * size), F32),
-            jax.ShapeDtypeStruct(turned, BF16),
-            jax.ShapeDtypeStruct(grads, BF16),
+            jax.ShapeDtypeStruct((blocks * size, batches * points), BF16),
+            jax.ShapeDtypeStruct((PARTS, blocks, batches * points, size), BF16),
         ),
         in_specs=[hbm] * 5,
-        out_specs=(vmem,) * 5,
+        out_specs=(vmem,) * 4,
         scratch_shapes=[
             pltpu.SMEM((blocks, batches), jnp.int32),
             pltpu.VMEM(weights.shape, F32),
@@ -453,16 +416,12 @@
             pltpu.VMEM((batches, rows, size), BF16),
             pltpu.VMEM((PARTS, batches, rows, size), BF16),
             pltpu.VMEM((2 + PARTS, rows, size), F32),
-            pltpu.VMEM(turned, BF16),
-            pltpu.VMEM(grads, BF16),
-            pltpu.SemaphoreType.DMA((batches // step, 3)),
+            pltpu.SemaphoreType.DMA((batches, 3)),
             pltpu.SemaphoreType.DMA((2,)),
         ],
         compiler_params=pltpu.CompilerParams(vmem_limit_bytes=VMEM_LIMIT),
         cost_estimate=pl.CostEstimate(
-            flops=2 * PARTS * batches * points * (blocks * size) ** 2,
-            bytes_accessed=2 * (2 + PARTS) * batches * rows * size,
-            transcendentals=0,
+            flops=0, bytes_accessed=2 * (2 + PARTS) * batches * rows * size, transcendentals=0
         ),
     )(
         in_hbm(pattern.T),
@@ -473,81 +432,92 @@
     )
 
 
-def moment_kernel(
-    region, before, turned, grads, weight_grad, fn_atom, batch_atom, moments, hot, grad_columns
-):
+def moment_kernel(region, turned, grads, weight_grad, fn_atom, batch_atom, moments, hot, grad_columns):
     blocks, _, size = grads.shape[1:]
     batches = weight_grad.shape[1]
     me = lax.axis_index("grid")
+    taken = min(3, blocks) * size
+
+    @pl.loop(0, PARTS * (blocks // 2))
+    def _(number):
+        c = lax.div(number, blocks // 2)
+        p = lax.rem(number, blocks // 2) * 2
+        start = jnp.minimum(jnp.maximum(p - 1, 0), blocks - min(3, blocks)) * size
+        rows = pl.ds(pl.multiple_of(start, size), taken)
+        right = jnp.concatenate([grads[c, p], grads[c, p + 1]], axis=1)
+        columns = pl.ds(pl.multiple_of(p * size, size), 2 * size)
+        moments[c, rows, columns] = jnp.dot(turned[rows, :], right, preferred_element_type=F32)
+
     atoms = lax.broadcasted_iota(jnp.int32, (hot.shape[0], size), 0)
-    rows = [fn_atom[pl.ds(region[me, position], 1), :] for position in range(blocks)]
-    rows.append(jnp.concatenate([batch_atom[...], jnp.full((1, size - batches), -1, jnp.int32)], axis=1))
-    for number, ids in enumerate(rows):
-        hot[:, number * size : (number + 1) * size] = jnp.where(atoms == ids, 1.0, 0.0).astype(BF16)
+    ids = jnp.concatenate([batch_atom[...], jnp.full((1, size - batches), -1, jnp.int32)], axis=1)
+    hot[:, blocks * size :] = jnp.where(atoms == ids, 1.0, 0.0).astype(BF16)
+
+    @pl.loop(0, blocks)
+    def _(position):
+        ids = fn_atom[pl.ds(region[me, position], 1), :]
+        columns = pl.ds(pl.multiple_of(position * size, size), size)
+        hot[:, columns] = jnp.where(atoms == ids, 1.0, 0.0).astype(BF16)
+
     for c in range(PARTS):
         padded = jnp.concatenate([weight_grad[c], jnp.zeros((size - batches, weight_grad.shape[2]), F32)], axis=0)
         grad_columns[c] = padded.T
-    for term in moment_terms(blocks):
-        add_moments(moments, turned, grads, False, term)
-
-
-def moments_and_atoms(region, before, turned, grads, weight_grad, fn_atom, batch_atom, atom_total):
+
+
+def moments_and_atoms(region, turned, grads, weight_grad, fn_atom, batch_atom, atom_total):
     blocks, depth, size = grads.shape[1:]
     points = weight_grad.shape[2]
     vmem = pl.BlockSpec(memory_space=pltpu.VMEM)
     return pl.pallas_call(
         moment_kernel,
         out_shape=(
-            jax.ShapeDtypeStruct(before.shape, F32),
+            jax.ShapeDtypeStruct((PARTS, blocks * size, blocks * size), F32),
             jax.ShapeDtypeStruct((atom_total, (blocks + 1) * size), BF16),
             jax.ShapeDtypeStruct((PARTS, points, size), F32),
         ),
-        in_specs=[pl.BlockSpec(memory_space=pltpu.SMEM)] + [vmem] * 6,
+        in_specs=[pl.BlockSpec(memory_space=pltpu.SMEM)] + [vmem] * 5,
         out_specs=(vmem,) * 3,
-        input_output_aliases={1: 0},
         compiler_params=pltpu.CompilerParams(vmem_limit_bytes=VMEM_LIMIT),
         cost_estimate=pl.CostEstimate(
             flops=2 * PARTS * depth * (blocks * size) ** 2, bytes_accessed=0, transcendentals=0
         ),
-    )(region, before, turned, grads, weight_grad, fn_atom.reshape(-1, size), batch_atom.reshape(1, -1))
+    )(region, turned, grads, weight_grad, fn_atom.reshape(-1, size), batch_atom.reshape(1, -1))
 
 
 def combine_kernel(
     region, basis, field, moments, hot, grad_columns, *rest, owner_rows, slabs, width, step
 ):
-    *pieces, product_out, out, stage, matrix, energies = rest
+    *pieces, product_out, out, stage, matrix, energies, derivative = rest
     batches, blocks, points, size = basis.shape
     me = lax.axis_index("grid")
     me_atoms = lax.axis_index("atoms")
     half = (width - 1) // 2
     stage_rows(stage, pieces[0], pieces[1:slabs], pieces[slabs:], SHARE)
-    rows = [region[me, position] for position in range(blocks)]
-    found = [owner_and_slot(region, me, position, owner_rows) for position in range(blocks)]
-    totals = [[jnp.zeros((8, size), F32) for _ in range(blocks)] for _ in range(PARTS)]
-    for p in range(blocks):
-        owner, slot, count = found[p]
+    matrix[...] = jnp.zeros_like(matrix)
+
+    @pl.loop(0, blocks)
+    def _(p):
+        row = region[me, p]
+        owner, slot, count = owner_and_slot(region, me, p, owner_rows)
         first = jnp.bitwise_xor(me, owner) * TRAVEL
-        for q in range(blocks):
-            if abs(q - p) > half:
-                matrix[p * size : (p + 1) * size, q * size : (q + 1) * size] = jnp.zeros((size, size), BF16)
-                continue
-            k = rows[q] - rows[p] + half
-            place = jnp.where(
-                k == 0,
-                travel_place(slot, count, 0),
-                jnp.where(k == 1, travel_place(slot, count, 1), travel_place(slot, count, 2)),
-            )
-            inside = jnp.logical_and(k >= 0, k < width)
-            tile = stage[first + place].astype(F32)
+        here = pl.ds(pl.multiple_of(p * size, size), size)
+        totals = [jnp.zeros((8, size), F32) for _ in range(PARTS)]
+        for k in range(width):
+            q = jnp.minimum(jnp.maximum(p + k - half, 0), blocks - 1)
+            inside = jnp.logical_and(q == p + k - half, region[me, q] == row + k - half)
+            tile = stage[first + travel_place(slot, count, k)].astype(F32)
             tile = jnp.where(inside, tile, 0.0)
-            matrix[p * size : (p + 1) * size, q * size : (q + 1) * size] = tile.astype(BF16)
+            there = pl.ds(pl.multiple_of(q * size, size), size)
             turned = tile.T
             for c in range(PARTS):
-                terms = turned * moments[c, q * size : (q + 1) * size, p * size : (p + 1) * size]
-                totals[c][p] = totals[c][p] + jnp.sum(terms.reshape(-1, 8, size), axis=0)
-    derivative = [
-        jnp.concatenate([jnp.sum(total, axis=0, keepdims=True) for total in totals[c]], axis=1) for c in range(PARTS)
-    ]
+                terms = turned * moments[c, there, here]
+                totals[c] = totals[c] + jnp.sum(terms.reshape(-1, 8, size), axis=0)
+
+            @pl.when(inside)
+            def _():
+                matrix[here, there] = tile.astype(BF16)
+
+        for c in range(PARTS):
+            derivative[c : c + 1, here] = -2.0 * jnp.sum(totals[c], axis=0, keepdims=True)
 
     energies[...] = jnp.zeros_like(energies)
     lanes = lax.broadcasted_iota(jnp.int32, (points, size), 1)
@@ -571,24 +541,24 @@
     lefts = []
     for c in range(PARTS):
         term = jnp.sum(energies[...] * grad_columns[c], axis=0, keepdims=True)
-        lefts.append(jnp.concatenate([-2.0 * derivative[c], term], axis=1))
+        lefts.append(jnp.concatenate([derivative[c : c + 1, :], term], axis=1))
     left = jnp.concatenate(lefts, axis=0)
     high, middle, low = (piece.astype(F32) for piece in split(left))
     left = jnp.concatenate([high, middle, low, jnp.zeros((16 - 3 * PARTS, left.shape[1]), F32)], axis=0).astype(BF16)
     chunk = out.shape[-1]
-    for device in range(out.shape[0]):
-        sums = lax.dot_general(
-            left, hot[device * chunk : (device + 1) * chunk, :], NT, preferred_element_type=F32
-        )
-        value = sums[:PARTS] + sums[PARTS : 2 * PARTS] + sums[2 * PARTS : 3 * PARTS]
-        out[jnp.bitwise_xor(me_atoms, device)] = value
+
+    @pl.loop(0, out.shape[0])
+    def _(device):
+        atoms = pl.ds(pl.multiple_of(device * chunk, 16), chunk)
+        sums = lax.dot_general(left, hot[atoms, :], NT, preferred_element_type=F32)
+        out[jnp.bitwise_xor(me_atoms, device)] = sums[:PARTS] + sums[PARTS : 2 * PARTS] + sums[2 * PARTS : 3 * PARTS]
 
 
 def combine(region, prepared, pieces, shapes):
     basis, field, moments, hot, grad_columns = prepared
     slabs, atom_devices, atom_total, points, blocks, width, owner_rows = shapes
     batches, _, _, size = basis.shape
-    step = 4 if batches % 4 == 0 else 1
+    step = 2 if batches % 2 == 0 else 1
     vmem = pl.BlockSpec(memory_space=pltpu.VMEM)
     return pl.pallas_call(
         functools.partial(combine_kernel, owner_rows=owner_rows, slabs=slabs, width=width, step=step),
@@ -602,6 +572,7 @@
             pltpu.VMEM((slabs * TRAVEL, size, size), BF16),
             pltpu.VMEM((blocks * size, blocks * size), BF16),
             pltpu.VMEM((points, size), F32),
+            pltpu.VMEM((PARTS, blocks * size), F32),
         ],
         compiler_params=pltpu.CompilerParams(vmem_limit_bytes=VMEM_LIMIT),
     )(region, basis, field, moments, hot, grad_columns, *pieces)

time: 36.1 us -> 39.7 us (1.100)
  Pallas kernels: 17.7 us -> 20.6 us
  waiting for transfers between devices: 4.1 us -> 5.21 us
  starting transfers between devices: 12.7 us -> 12.3 us
    pallas_call x1, Pallas kernels: 1.66 us -> 4.4 us  [moments_and_atoms(): pl.pallas_call(moment_kernel, out_shape=(jax.ShapeDtypeStruct((PARTS, blo...]
    pallas_call x1, Pallas kernels: 3.36 us -> 6 us  [combine(): pl.pallas_call(functools.partial(combine_kernel, owner_rows=owner_rows, s...]
    pallas_call x1, Pallas kernels: 8.75 us -> 6.31 us  [reorder(): pl.pallas_call(reorder_kernel, out_shape=(ordered, ordered, jax.ShapeDtyp...]
    ppermute x6, waiting for transfers between devices: 4.09 us -> 4.77 us  [exchange_all(): lax.ppermute(parts[d], axis, [(i, i ^ d) for i in range(count)])]
    ppermute x3, waiting for transfers between devices: 0.01 us -> 0.43 us  [fetch_rows(): lax.ppermute(outgoing[slabs - 1 - shift], 'grid', [(i, i ^ shift) for i i...]
  transfers between devices with their start and end apart: 12 -> 12, of which waited for: 4 -> 4; matrix products, arithmetic and copies ran while one was open for 0% -> 0% of each run, Pallas kernels for 35% -> 32%
where the time goes in v10:
time: 39.7 us; the launch traced here: 39.5 us
  Pallas kernels  20.6 us (52%)
  starting transfers between devices  12.3 us (31%)
  waiting for transfers between devices  5.21 us (13%)
  between operations  0.75 us (2%)
  other arithmetic  0.6 us (2%)
    pallas_call x1, Pallas kernels, reorder(): pl.pallas_call(reorder_kernel, out_shape=(ordered, ordered, jax.ShapeDtyp...  6.31 us
    ppermute x6, starting transfers between devices, exchange_all(): lax.ppermute(parts[d], axis, [(i, i ^ d) for i in range(count)])  6.09 us
    pallas_call x1, Pallas kernels, combine(): pl.pallas_call(functools.partial(combine_kernel, owner_rows=owner_rows, s...  6 us
    ppermute x3, starting transfers between devices, fetch_rows(): lax.ppermute(outgoing[slabs - 1 - shift], 'grid', [(i, i ^ shift) for i i...  5.67 us
    ppermute x6, waiting for transfers between devices, exchange_all(): lax.ppermute(parts[d], axis, [(i, i ^ d) for i in range(count)])  4.77 us
    pallas_call x1, Pallas kernels, moments_and_atoms(): pl.pallas_call(moment_kernel, out_shape=(jax.ShapeDtypeStruct((PARTS, blo...  4.4 us
    pallas_call x1, Pallas kernels, write(): pl.pallas_call(write_kernel, out_shape=jax.ShapeDtypeStruct(shape, BF16),...  2.06 us
    pallas_call x1, Pallas kernels, rows_to_send(): pl.pallas_call(functools.partial(send_kernel, share=share), out_shape=[ja...  1.79 us
  transfers between devices with their start and end apart: 12, of which 4 were waited for; matrix products, arithmetic and copies ran while one was open for 0% of the time, Pallas kernels for 32%

profile of v10, /device:TPU:0, one launch (start us, length us, event | category | flops | bytes accessed | tf_op | source)
XLA Modules:
  0.0 39.5 jit_solution(18312721776667394743)
XLA Ops:
  0.6 1.8 %shard_map.113 = (bf16[5,128,128]{2,1,0:T(8,128)(2,1)S(1)}, bf16[5,64,128]{2,1,0:T(8,128)(2,1)S(1)}, bf16[5,64,128]{2,1,0:T(8,128)(2,1)S(1)}, bf16[5,64,128]{2,1,0:T(8,128)(2,1)S(1)}) custom-call(s32[4,4]{1,0:T(4,128)} %region.5, bf16[15,3,128,128]{3,2,1,0:T(8,128)(2,1)} %density.1), custom_call_target="tpu_custom_call" | custom-call | tf_op jit(solution)/shard_map/pallas_call | solution.py:83
  2.4 3.1 %collective-permute-start = (bf16[5,64,128]{2,1,0:T(8,128)(2,1)S(1)}, bf16[5,64,128]{2,1,0:T(8,128)(2,1)S(1)}, u32[]{:S(2)}, u32[]{:S(2)}) collective-permute-start(bf16[5,64,128]{2,1,0:T(8,128)(2,1)S(1)} %get-tuple-element.24), channel_id=1, source_target_pairs={{0,4},{4,0},{8,12},{12,8},{1,5},{5,1},{9,13},{13,9},{2,6},{6,2},{1... | collective-permute-start | bytes 245768 | tf_op jit(solution)/shard_map/ppermute | solution.py:97
  5.5 2.5 %collective-permute-start.1 = (bf16[5,64,128]{2,1,0:T(8,128)(2,1)S(1)}, bf16[5,64,128]{2,1,0:T(8,128)(2,1)S(1)}, u32[]{:S(2)}, u32[]{:S(2)}) collective-permute-start(bf16[5,64,128]{2,1,0:T(8,128)(2,1)S(1)} %get-tuple-element.25), channel_id=1, source_target_pairs={{0,8},{4,12},{8,0},{12,4},{1,9},{5,13},{9,1},{13,5},{2,10},{6,14},... | collective-permute-start | bytes 245768 | tf_op jit(solution)/shard_map/ppermute | solution.py:97
  8.1 0.0 collective-permute-start.2
  8.1 0.0 copy-start
  8.1 0.0 copy-start.2
  8.1 0.0 copy-start.3
  8.1 0.0 copy-start.4
  8.1 6.3 %shard_map.114 = (bf16[16,4,128,128]{3,2,1,0:T(8,128)(2,1)S(1)}, bf16[16,4,128,128]{3,2,1,0:T(8,128)(2,1)S(1)}, bf16[512,2048]{1,0:T(8,128)(2,1)S(1)}, bf16[3,4,2048,128]{3,2,1,0:T(8,128)(2,1)S(1)}) custom-call(s32[4,16]{1,0:T(4,128)} %bitcast.17, bf16[16,512,128]{2,1,0:T(8,128)(2,1)} %bitcast.22, bf16[16,512,128]{2,1,0:T(8,128)(2,1)} %bitcast.23, ...), custom_call_target="tpu_custom_call" | custom-call | bytes 10485760 | tf_op jit(solution)/shard_map/pallas_call | solution.py:402
  14.4 0.0 collective-permute-done.rest_1_
  14.4 0.4 %collective-permute-done.1.rest_2_ = bf16[5,64,128]{2,1,0:T(8,128)(2,1)S(1)} collective-permute-done((bf16[5,64,128]{2,1,0:T(8,128)(2,1)S(1)}, bf16[5,64,128]{2,1,0:T(8,128)(2,1)S(1)}, u32[]{:S(2)}, u32[]{:S(2)}) %collective-permute-start.1) | collective-permute-done | bytes 81952 | tf_op jit(solution)/shard_map/ppermute | solution.py:97
  14.9 0.0 collective-permute-done.2.rest_3_
  14.9 0.0 collective-permute-start.3
  14.9 0.5 %collective-permute-start.4 = (bf16[5,64,128]{2,1,0:T(8,128)(2,1)S(1)}, bf16[5,64,128]{2,1,0:T(8,128)(2,1)S(1)}, u32[]{:S(2)}, u32[]{:S(2)}) collective-permute-start(bf16[5,64,128]{2,1,0:T(8,128)(2,1)S(1)} %collective-permute-done.1.rest_2_), channel_id=1, source_target_pairs={{0,1},{1,0},{2,3},{3,2},{4,5},{5,4},{6,7},{7,6},{8,9},{9,8},{10,11... | collective-permute-start | bytes 245768 | tf_op jit(solution)/shard_map/ppermute | solution.py:622
  15.4 0.0 collective-permute-start.5
  15.4 0.0 copy-done
  15.4 0.0 copy-done.2
  15.4 0.0 copy-done.3
  15.4 0.0 copy-done.4
  15.4 4.4 %shard_map.115 = (f32[3,512,512]{2,1,0:T(8,128)S(1)}, bf16[768,640]{1,0:T(8,128)(2,1)S(1)}, f32[3,128,128]{2,1,0:T(8,128)S(1)}) custom-call(s32[4,4]{1,0:T(4,128)S(1)} %copy-done, bf16[512,2048]{1,0:T(8,128)(2,1)S(1)} %get-tuple-element.33.turned, bf16[3,4,2048,128]{3,2,1,0:T(8,128)(2,1)S(1)} %get-tuple-element.34.grads, f32[3,16,128]{2,1,0:T(8,128)S(1)} %copy-done.3, ...), custom_call_target="tpu_custom_call" | custom-call | flops 3221225472 | tf_op jit(solution)/shard_map/pallas_call | solution.py:470
  19.8 0.0 collective-permute-done.3.rest_4_
  19.8 0.0 collective-permute-done.4.rest_5_
  19.8 0.0 collective-permute-done.5.rest_6_
  19.9 0.0 copy-start.1
  19.9 6.0 %shard_map.116 = (bf16[16,4,128,128]{3,2,1,0:T(8,128)(2,1)S(1)}, f32[4,3,192]{2,1,0:T(4,128)S(1)}) custom-call(s32[4,4]{1,0:T(4,128)S(1)} %copy-done, bf16[16,4,128,128]{3,2,1,0:T(8,128)(2,1)S(1)} %get-tuple-element.31.basis, bf16[16,4,128,128]{3,2,1,0:T(8,128)(2,1)S(1)} %get-tuple-element.32.field, f32[3,512,512]{2,1,0:T(8,128)S(1)} %get-tuple-element.35.moments, ...), custom_call_target="tpu_custom_call" | custom-call | tf_op jit(solution)/shard_map/pallas_call | solution.py:563
  25.9 0.1 slice_bitcast_fusion
  26.0 0.6 %collective-permute-start.6 = (f32[3,192]{1,0:T(4,128)S(1)}, f32[3,192]{1,0:T(4,128)S(1)}, u32[]{:S(2)}, u32[]{:S(2)}) collective-permute-start(f32[3,192]{1,0:T(4,128)S(1)} %get-tuple-element.48), channel_id=1, source_target_pairs={{0,1},{1,0},{2,3},{3,2},{4,5},{5,4},{6,7},{7,6},{8,9},{9,8},{10,11... | collective-permute-start | bytes 6920 | tf_op jit(solution)/shard_map/ppermute | solution.py:633
  26.5 1.5 %collective-permute-start.7 = (f32[3,192]{1,0:T(4,128)S(1)}, f32[3,192]{1,0:T(4,128)S(1)}, u32[]{:S(2)}, u32[]{:S(2)}) collective-permute-start(f32[3,192]{1,0:T(4,128)S(1)} %get-tuple-element.47), channel_id=1, source_target_pairs={{0,2},{1,3},{2,0},{3,1},{4,6},{5,7},{6,4},{7,5},{8,10},{9,11},{10,... | collective-permute-start | bytes 6920 | tf_op jit(solution)/shard_map/ppermute | solution.py:633
  28.0 0.0 collective-permute-start.8
  28.0 0.0 collective-permute-done.6
  28.0 2.1 %collective-permute-done.7 = f32[3,192]{1,0:T(4,128)S(1)} collective-permute-done((f32[3,192]{1,0:T(4,128)S(1)}, f32[3,192]{1,0:T(4,128)S(1)}, u32[]{:S(2)}, u32[]{:S(2)}) %collective-permute-start.7) | collective-permute-done | bytes 2336 | tf_op jit(solution)/shard_map/ppermute | solution.py:633
  30.1 0.9 %collective-permute-done.8 = f32[3,192]{1,0:T(4,128)S(1)} collective-permute-done((f32[3,192]{1,0:T(4,128)S(1)}, f32[3,192]{1,0:T(4,128)S(1)}, u32[]{:S(2)}, u32[]{:S(2)}) %collective-permute-start.8) | collective-permute-done | bytes 2336 | tf_op jit(solution)/shard_map/ppermute | solution.py:633
  31.1 2.4 %collective-permute-start.10 = (f32[3,192]{1,0:T(4,128)S(1)}, f32[3,192]{1,0:T(4,128)S(1)}, u32[]{:S(2)}, u32[]{:S(2)}) collective-permute-start(f32[3,192]{1,0:T(4,128)S(1)} %fusion), channel_id=1, source_target_pairs={{0,8},{4,12},{8,0},{12,4},{1,9},{5,13},{9,1},{13,5},{2,10},{6,14},... | collective-permute-start | bytes 6920 | tf_op jit(solution)/shard_map/ppermute | solution.py:633
  33.5 1.4 %collective-permute-start.11 = (f32[3,192]{1,0:T(4,128)S(1)}, f32[3,192]{1,0:T(4,128)S(1)}, u32[]{:S(2)}, u32[]{:S(2)}) collective-permute-start(f32[3,192]{1,0:T(4,128)S(1)} %fusion), channel_id=1, source_target_pairs={{0,12},{4,8},{8,4},{12,0},{1,13},{5,9},{9,5},{13,1},{2,14},{6,10},... | collective-permute-start | bytes 6920 | tf_op jit(solution)/shard_map/ppermute | solution.py:633
  34.9 0.2 collective-permute-start.9
  35.1 0.0 copy-done.1
  35.1 2.1 %shard_map.117 = bf16[16,512,128]{2,1,0:T(8,128)(2,1)} custom-call(s32[4,16]{1,0:T(4,128)S(1)} %bitcast.18, bf16[16,4,128,128]{3,2,1,0:T(8,128)(2,1)S(1)} %get-tuple-element.44.product), custom_call_target="tpu_custom_call" | custom-call | bytes 4194304 | tf_op jit(solution)/shard_map/pallas_call | solution.py:604
  37.2 0.0 collective-permute-done.10
  37.2 1.7 %collective-permute-done.11 = f32[3,192]{1,0:T(4,128)S(1)} collective-permute-done((f32[3,192]{1,0:T(4,128)S(1)}, f32[3,192]{1,0:T(4,128)S(1)}, u32[]{:S(2)}, u32[]{:S(2)}) %collective-permute-start.11) | collective-permute-done | bytes 2336 | tf_op jit(solution)/shard_map/ppermute | solution.py:633
  38.9 0.0 collective-permute-done.9
  38.9 0.6 %add_add_fusion = f32[3,192]{1,0:T(4,128)} fusion(f32[3,192]{1,0:T(4,128)S(1)} %collective-permute-done.10, f32[3,192]{1,0:T(4,128)S(1)} %collective-permute-done.11, f32[3,192]{1,0:T(4,128)S(1)} %fusion, f32[3,192]{1,0:T(4,128)S(1)} %collective-permute-done.9), kind=kLoop, calls=%fused_computation.2 | loop fusion | flops 1728 | bytes 11520 | tf_op jit(solution)/shard_map/add | solution.py:629
  (1 shorter events, 0.0 us)
Async XLA Ops:
  2.4 12.0 %collective-permute-start = (bf16[5,64,128]{2,1,0:T(8,128)(2,1)S(1)}, bf16[5,64,128]{2,1,0:T(8,128)(2,1)S(1)}, u32[]{:S(2)}, u32[]{:S(2)}) collective-permute-start(bf16[5,64,128]{2,1,0:T(8,128)(2,1)S(1)} %get-tuple-element.24), channel_id=1, source_target_pairs={{0,4},{4,0},{8,12},{12,8},{1,5},{5,1},{9,13},{13,9},{2,6},{6,2},{1... | collective-permute-start | bytes 245768 | tf_op jit(solution)/shard_map/ppermute | solution.py:97
  5.5 9.3 %collective-permute-start.1 = (bf16[5,64,128]{2,1,0:T(8,128)(2,1)S(1)}, bf16[5,64,128]{2,1,0:T(8,128)(2,1)S(1)}, u32[]{:S(2)}, u32[]{:S(2)}) collective-permute-start(bf16[5,64,128]{2,1,0:T(8,128)(2,1)S(1)} %get-tuple-element.25), channel_id=1, source_target_pairs={{0,8},{4,12},{8,0},{12,4},{1,9},{5,13},{9,1},{13,5},{2,10},{6,14},... | collective-permute-start | bytes 245768 | tf_op jit(solution)/shard_map/ppermute | solution.py:97
  8.1 6.8 %collective-permute-start.2 = (bf16[5,64,128]{2,1,0:T(8,128)(2,1)S(1)}, bf16[5,64,128]{2,1,0:T(8,128)(2,1)S(1)}, u32[]{:S(2)}, u32[]{:S(2)}) collective-permute-start(bf16[5,64,128]{2,1,0:T(8,128)(2,1)S(1)} %get-tuple-element.26), channel_id=1, source_target_pairs={{0,12},{4,8},{8,4},{12,0},{1,13},{5,9},{9,5},{13,1},{2,14},{6,10},... | collective-permute-start | bytes 245768 | tf_op jit(solution)/shard_map/ppermute | solution.py:97
  8.1 7.3 %copy-start = (s32[4,4]{1,0:T(4,128)S(1)}, s32[4,4]{1,0:T(4,128)}, u32[]{:S(2)}) copy-start(s32[4,4]{1,0:T(4,128)} %region.5) | copy-start | bytes 196
  8.1 7.3 %copy-start.2 = (s32[7680]{0:T(1024)S(1)}, s32[7680]{0:T(1024)}, u32[]{:S(2)}) copy-start(s32[7680]{0:T(1024)} %param.18) | copy-start | bytes 92164
  8.1 7.3 %copy-start.3 = (f32[3,16,128]{2,1,0:T(8,128)S(1)}, f32[3,16,128]{2,1,0:T(8,128)}, u32[]{:S(2)}) copy-start(f32[3,16,128]{2,1,0:T(8,128)} %weight_grad.1) | copy-start | bytes 73732
  8.1 7.3 %copy-start.4 = (s32[16]{0:T(128)S(1)}, s32[16]{0:T(128)}, u32[]{:S(2)}) copy-start(s32[16]{0:T(128)} %param.19) | copy-start | bytes 196
  14.9 5.0 %collective-permute-start.3 = (bf16[5,64,128]{2,1,0:T(8,128)(2,1)S(1)}, bf16[5,64,128]{2,1,0:T(8,128)(2,1)S(1)}, u32[]{:S(2)}, u32[]{:S(2)}) collective-permute-start(bf16[5,64,128]{2,1,0:T(8,128)(2,1)S(1)} %collective-permute-done.rest_1_), channel_id=1, source_target_pairs={{0,1},{1,0},{2,3},{3,2},{4,5},{5,4},{6,7},{7,6},{8,9},{9,8},{10,11... | collective-permute-start | bytes 245768 | tf_op jit(solution)/shard_map/ppermute | solution.py:622
  14.9 5.0 %collective-permute-start.4 = (bf16[5,64,128]{2,1,0:T(8,128)(2,1)S(1)}, bf16[5,64,128]{2,1,0:T(8,128)(2,1)S(1)}, u32[]{:S(2)}, u32[]{:S(2)}) collective-permute-start(bf16[5,64,128]{2,1,0:T(8,128)(2,1)S(1)} %collective-permute-done.1.rest_2_), channel_id=1, source_target_pairs={{0,1},{1,0},{2,3},{3,2},{4,5},{5,4},{6,7},{7,6},{8,9},{9,8},{10,11... | collective-permute-start | bytes 245768 | tf_op jit(solution)/shard_map/ppermute | solution.py:622
  15.4 4.5 %collective-permute-start.5 = (bf16[5,64,128]{2,1,0:T(8,128)(2,1)S(1)}, bf16[5,64,128]{2,1,0:T(8,128)(2,1)S(1)}, u32[]{:S(2)}, u32[]{:S(2)}) collective-permute-start(bf16[5,64,128]{2,1,0:T(8,128)(2,1)S(1)} %collective-permute-done.2.rest_3_), channel_id=1, source_target_pairs={{0,1},{1,0},{2,3},{3,2},{4,5},{5,4},{6,7},{7,6},{8,9},{9,8},{10,11... | collective-permute-start | bytes 245768 | tf_op jit(solution)/shard_map/ppermute | solution.py:622
  19.9 15.2 %copy-start.1 = (s32[16,4]{0,1:T(4,128)S(1)}, s32[16,4]{0,1:T(4,128)}, u32[]{:S(2)}) copy-start(s32[16,4]{0,1:T(4,128)} %param.17) | copy-start | bytes 772
  26.0 2.1 %collective-permute-start.6 = (f32[3,192]{1,0:T(4,128)S(1)}, f32[3,192]{1,0:T(4,128)S(1)}, u32[]{:S(2)}, u32[]{:S(2)}) collective-permute-start(f32[3,192]{1,0:T(4,128)S(1)} %get-tuple-element.48), channel_id=1, source_target_pairs={{0,1},{1,0},{2,3},{3,2},{4,5},{5,4},{6,7},{7,6},{8,9},{9,8},{10,11... | collective-permute-start | bytes 6920 | tf_op jit(solution)/shard_map/ppermute | solution.py:633
  26.5 3.6 %collective-permute-start.7 = (f32[3,192]{1,0:T(4,128)S(1)}, f32[3,192]{1,0:T(4,128)S(1)}, u32[]{:S(2)}, u32[]{:S(2)}) collective-permute-start(f32[3,192]{1,0:T(4,128)S(1)} %get-tuple-element.47), channel_id=1, source_target_pairs={{0,2},{1,3},{2,0},{3,1},{4,6},{5,7},{6,4},{7,5},{8,10},{9,11},{10,... | collective-permute-start | bytes 6920 | tf_op jit(solution)/shard_map/ppermute | solution.py:633
  28.0 3.1 %collective-permute-start.8 = (f32[3,192]{1,0:T(4,128)S(1)}, f32[3,192]{1,0:T(4,128)S(1)}, u32[]{:S(2)}, u32[]{:S(2)}) collective-permute-start(f32[3,192]{1,0:T(4,128)S(1)} %get-tuple-element.46), channel_id=1, source_target_pairs={{0,3},{1,2},{2,1},{3,0},{4,7},{5,6},{6,5},{7,4},{8,11},{9,10},{10,... | collective-permute-start | bytes 6920 | tf_op jit(solution)/shard_map/ppermute | solution.py:633
  31.1 6.1 %collective-permute-start.10 = (f32[3,192]{1,0:T(4,128)S(1)}, f32[3,192]{1,0:T(4,128)S(1)}, u32[]{:S(2)}, u32[]{:S(2)}) collective-permute-start(f32[3,192]{1,0:T(4,128)S(1)} %fusion), channel_id=1, source_target_pairs={{0,8},{4,12},{8,0},{12,4},{1,9},{5,13},{9,1},{13,5},{2,10},{6,14},... | collective-permute-start | bytes 6920 | tf_op jit(solution)/shard_map/ppermute | solution.py:633
  33.5 5.4 %collective-permute-start.11 = (f32[3,192]{1,0:T(4,128)S(1)}, f32[3,192]{1,0:T(4,128)S(1)}, u32[]{:S(2)}, u32[]{:S(2)}) collective-permute-start(f32[3,192]{1,0:T(4,128)S(1)} %fusion), channel_id=1, source_target_pairs={{0,12},{4,8},{8,4},{12,0},{1,13},{5,9},{9,5},{13,1},{2,14},{6,10},... | collective-permute-start | bytes 6920 | tf_op jit(solution)/shard_map/ppermute | solution.py:633
  34.9 4.0 %collective-permute-start.9 = (f32[3,192]{1,0:T(4,128)S(1)}, f32[3,192]{1,0:T(4,128)S(1)}, u32[]{:S(2)}, u32[]{:S(2)}) collective-permute-start(f32[3,192]{1,0:T(4,128)S(1)} %fusion), channel_id=1, source_target_pairs={{0,4},{4,0},{8,12},{12,8},{1,5},{5,1},{9,13},{13,9},{2,6},{6,2},{1... | collective-permute-start | bytes 6920 | tf_op jit(solution)/shard_map/ppermute | solution.py:633

commit v11 on v10

--- a/solution.py
+++ b/solution.py
@@ -10,6 +10,7 @@
 
 TRAVEL = 5
 SHARE = 2
+CHUNK = 2
 PARTS = 3
 F32 = jnp.float32
 BF16 = jnp.bfloat16
@@ -36,8 +37,25 @@
     return jnp.where(jnp.logical_and(slot == 0, count == 2), 1, 4)
 
 
-def send_kernel(region, density, *rest, share):
-    *outs, sems = rest
+def send_kernel(
+    region_hbm, density, basis, field, basis_grad, fn_atom_hbm, batch_atom_hbm, weight_grad_hbm, *rest, share
+):
+    *outs, first_basis, first_field, first_grad, hot, grad_columns = rest[:-7]
+    region, fn_atom, batch_atom, weight_grad, sems, small_sems, first_sems = rest[-7:]
+    small = (
+        pltpu.make_async_copy(region_hbm, region, small_sems.at[0]),
+        pltpu.make_async_copy(fn_atom_hbm, fn_atom, small_sems.at[1]),
+        pltpu.make_async_copy(batch_atom_hbm, batch_atom, small_sems.at[2]),
+        pltpu.make_async_copy(weight_grad_hbm, weight_grad, small_sems.at[3]),
+    )
+    firsts = (
+        pltpu.make_async_copy(field.at[pl.ds(0, first_field.shape[0])], first_field, first_sems.at[0]),
+        pltpu.make_async_copy(basis_grad.at[:, pl.ds(0, first_grad.shape[1])], first_grad, first_sems.at[1]),
+        pltpu.make_async_copy(basis.at[pl.ds(0, first_basis.shape[0])], first_basis, first_sems.at[2]),
+    )
+    for copy in small:
+        copy.start()
+    small[0].wait()
     me = lax.axis_index("grid")
     part = lax.rem(lax.axis_index("atoms"), share)
     size = region.shape[1]
@@ -67,9 +85,28 @@
         )
         for number, (source, target) in enumerate(pairs):
             copies.append(pltpu.make_async_copy(source, target, sems.at[shift, number]))
-    for copy in copies:
+    for copy in (*copies, *firsts):
         copy.start()
-    for copy in copies:
+    for copy in small[1:]:
+        copy.wait()
+    length = density.shape[-1]
+    batches = weight_grad.shape[1]
+    atoms = lax.broadcasted_iota(jnp.int32, (hot.shape[0], length), 0)
+    fill = jnp.full((1, length - batches), -1, jnp.int32)
+    hot[:, size * length :] = jnp.where(
+        atoms == jnp.concatenate([batch_atom[...], fill], axis=1), 1.0, 0.0
+    ).astype(BF16)
+
+    @pl.loop(0, size)
+    def _(position):
+        ids = fn_atom[pl.ds(region[me, position], 1), :]
+        columns = pl.ds(pl.multiple_of(position * length, length), length)
+        hot[:, columns] = jnp.where(atoms == ids, 1.0, 0.0).astype(BF16)
+
+    for c in range(PARTS):
+        padding = jnp.zeros((length - batches, weight_grad.shape[2]), F32)
+        grad_columns[c] = jnp.concatenate([weight_grad[c], padding], axis=0).T
+    for copy in (*copies, *firsts):
         copy.wait()
 
 
@@ -77,25 +114,42 @@
     return pltpu.with_memory_space_constraint(array, pltpu.HBM)
 
 
-def rows_to_send(region, density, slabs, share):
+def send(region, density, basis, field, basis_grad, fn_atom, batch_atom, weight_grad, slabs, share, atom_total):
     size = density.shape[-1]
     kept = [size] + [size // share] * (slabs - 1)
+    first = jax.ShapeDtypeStruct((CHUNK, *basis.shape[1:]), BF16)
+    hbm = pl.BlockSpec(memory_space=pl.ANY)
+    operands = (region, density, basis, field, basis_grad, fn_atom, batch_atom, weight_grad)
     return pl.pallas_call(
         functools.partial(send_kernel, share=share),
-        out_shape=[jax.ShapeDtypeStruct((TRAVEL, rows, size), density.dtype) for rows in kept],
-        in_specs=[pl.BlockSpec(memory_space=pltpu.SMEM), pl.BlockSpec(memory_space=pl.ANY)],
-        out_specs=[pl.BlockSpec(memory_space=pltpu.VMEM)] * slabs,
-        scratch_shapes=[pltpu.SemaphoreType.DMA((slabs, 3))],
+        out_shape=[
+            *(jax.ShapeDtypeStruct((TRAVEL, rows, size), density.dtype) for rows in kept),
+            first,
+            first,
+            jax.ShapeDtypeStruct((PARTS, CHUNK, *basis.shape[1:]), BF16),
+            jax.ShapeDtypeStruct((atom_total, (region.shape[1] + 1) * size), BF16),
+            jax.ShapeDtypeStruct((PARTS, weight_grad.shape[2], size), F32),
+        ],
+        in_specs=[hbm] * len(operands),
+        out_specs=[pl.BlockSpec(memory_space=pltpu.VMEM)] * (slabs + 5),
+        scratch_shapes=[
+            pltpu.SMEM(region.shape, jnp.int32),
+            pltpu.VMEM(fn_atom.shape, jnp.int32),
+            pltpu.VMEM(batch_atom.shape, jnp.int32),
+            pltpu.VMEM(weight_grad.shape, F32),
+            pltpu.SemaphoreType.DMA((slabs, 3)),
+            pltpu.SemaphoreType.DMA((4,)),
+            pltpu.SemaphoreType.DMA((3,)),
+        ],
         compiler_params=pltpu.CompilerParams(vmem_limit_bytes=VMEM_LIMIT),
-    )(in_hbm(region), in_hbm(density))
-
-
-def fetch_rows(region, density, slabs, share):
-    own, *outgoing = rows_to_send(region, density, slabs, share)
+    )(*(in_hbm(operand) for operand in operands))
+
+
+def travel(outgoing, slabs):
     near = {}
     for shift in reversed(range(1, slabs)):
         near[shift] = lax.ppermute(outgoing[slabs - 1 - shift], "grid", [(i, i ^ shift) for i in range(slabs)])
-    return own, [near[shift] for shift in range(1, slabs)]
+    return [near[shift] for shift in range(1, slabs)]
 
 
 def stage_rows(stage, own, near, far, share):
@@ -335,6 +389,9 @@
     field,
     basis_grad,
     weights_hbm,
+    first_basis,
+    first_field,
+    first_grad,
     basis_out,
     field_out,
     turned,
@@ -363,8 +420,12 @@
     )
     for copy in small:
         copy.start()
-
-    @pl.loop(0, batches)
+    for batch in range(CHUNK):
+        pltpu.make_async_copy(first_field.at[batch], field_in.at[batch], sems.at[batch, 0]).start()
+        pltpu.make_async_copy(first_basis.at[batch], basis_in.at[batch], sems.at[batch, 1]).start()
+        pltpu.make_async_copy(first_grad.at[:, batch], grad_in.at[:, batch], sems.at[batch, 2]).start()
+
+    @pl.loop(CHUNK, batches)
     def _(batch):
         for copy in copies(batch):
             copy.start()
@@ -393,9 +454,8 @@
                 grads[c, place, points_here, :] = wide[2 + c, strided, :].astype(BF16)
 
 
-def reorder(pattern, basis, field, basis_grad, weights):
-    batches, points, blocks, size = basis.shape
-    rows = points * blocks
+def reorder(pattern, basis, field, basis_grad, weights, first, points, blocks):
+    batches, rows, size = basis.shape
     hbm = pl.BlockSpec(memory_space=pl.ANY)
     vmem = pl.BlockSpec(memory_space=pltpu.VMEM)
     ordered = jax.ShapeDtypeStruct((batches, blocks, points, size), BF16)
@@ -407,7 +467,7 @@
             jax.ShapeDtypeStruct((blocks * size, batches * points), BF16),
             jax.ShapeDtypeStruct((PARTS, blocks, batches * points, size), BF16),
         ),
-        in_specs=[hbm] * 5,
+        in_specs=[hbm] * 5 + [vmem] * 3,
         out_specs=(vmem,) * 4,
         scratch_shapes=[
             pltpu.SMEM((blocks, batches), jnp.int32),
@@ -423,101 +483,71 @@
         cost_estimate=pl.CostEstimate(
             flops=0, bytes_accessed=2 * (2 + PARTS) * batches * rows * size, transcendentals=0
         ),
-    )(
-        in_hbm(pattern.T),
-        in_hbm(basis.reshape(batches, rows, size)),
-        in_hbm(field.reshape(batches, rows, size)),
-        in_hbm(basis_grad.reshape(PARTS, batches, rows, size)),
-        in_hbm(weights),
-    )
-
-
-def moment_kernel(region, turned, grads, weight_grad, fn_atom, batch_atom, moments, hot, grad_columns):
+    )(in_hbm(pattern.T), in_hbm(basis), in_hbm(field), in_hbm(basis_grad), in_hbm(weights), *first)
+
+
+def moment_kernel(turned, grads, moments):
     blocks, _, size = grads.shape[1:]
-    batches = weight_grad.shape[1]
-    me = lax.axis_index("grid")
-    taken = min(3, blocks) * size
-
-    @pl.loop(0, PARTS * (blocks // 2))
-    def _(number):
-        c = lax.div(number, blocks // 2)
-        p = lax.rem(number, blocks // 2) * 2
-        start = jnp.minimum(jnp.maximum(p - 1, 0), blocks - min(3, blocks)) * size
-        rows = pl.ds(pl.multiple_of(start, size), taken)
-        right = jnp.concatenate([grads[c, p], grads[c, p + 1]], axis=1)
-        columns = pl.ds(pl.multiple_of(p * size, size), 2 * size)
-        moments[c, rows, columns] = jnp.dot(turned[rows, :], right, preferred_element_type=F32)
-
-    atoms = lax.broadcasted_iota(jnp.int32, (hot.shape[0], size), 0)
-    ids = jnp.concatenate([batch_atom[...], jnp.full((1, size - batches), -1, jnp.int32)], axis=1)
-    hot[:, blocks * size :] = jnp.where(atoms == ids, 1.0, 0.0).astype(BF16)
-
-    @pl.loop(0, blocks)
-    def _(position):
-        ids = fn_atom[pl.ds(region[me, position], 1), :]
-        columns = pl.ds(pl.multiple_of(position * size, size), size)
-        hot[:, columns] = jnp.where(atoms == ids, 1.0, 0.0).astype(BF16)
-
     for c in range(PARTS):
-        padded = jnp.concatenate([weight_grad[c], jnp.zeros((size - batches, weight_grad.shape[2]), F32)], axis=0)
-        grad_columns[c] = padded.T
-
-
-def moments_and_atoms(region, turned, grads, weight_grad, fn_atom, batch_atom, atom_total):
+        for p in range(0, blocks, 2):
+            rows = slice(max(p - 1, 0) * size, min(p + 3, blocks) * size)
+            right = jnp.concatenate([grads[c, p], grads[c, p + 1]], axis=1)
+            moments[c, rows, p * size : (p + 2) * size] = jnp.dot(
+                turned[rows, :], right, preferred_element_type=F32
+            )
+
+
+def build_moments(turned, grads):
     blocks, depth, size = grads.shape[1:]
-    points = weight_grad.shape[2]
     vmem = pl.BlockSpec(memory_space=pltpu.VMEM)
     return pl.pallas_call(
         moment_kernel,
-        out_shape=(
-            jax.ShapeDtypeStruct((PARTS, blocks * size, blocks * size), F32),
-            jax.ShapeDtypeStruct((atom_total, (blocks + 1) * size), BF16),
-            jax.ShapeDtypeStruct((PARTS, points, size), F32),
-        ),
-        in_specs=[pl.BlockSpec(memory_space=pltpu.SMEM)] + [vmem] * 5,
-        out_specs=(vmem,) * 3,
+        out_shape=jax.ShapeDtypeStruct((PARTS, blocks * size, blocks * size), F32),
+        in_specs=[vmem, vmem],
+        out_specs=vmem,
         compiler_params=pltpu.CompilerParams(vmem_limit_bytes=VMEM_LIMIT),
         cost_estimate=pl.CostEstimate(
             flops=2 * PARTS * depth * (blocks * size) ** 2, bytes_accessed=0, transcendentals=0
         ),
-    )(region, turned, grads, weight_grad, fn_atom.reshape(-1, size), batch_atom.reshape(1, -1))
+    )(turned, grads)
 
 
 def combine_kernel(
     region, basis, field, moments, hot, grad_columns, *rest, owner_rows, slabs, width, step
 ):
-    *pieces, product_out, out, stage, matrix, energies, derivative = rest
+    *pieces, product_out, out, stage, matrix, energies = rest
     batches, blocks, points, size = basis.shape
     me = lax.axis_index("grid")
     me_atoms = lax.axis_index("atoms")
     half = (width - 1) // 2
     stage_rows(stage, pieces[0], pieces[1:slabs], pieces[slabs:], SHARE)
-    matrix[...] = jnp.zeros_like(matrix)
-
-    @pl.loop(0, blocks)
-    def _(p):
-        row = region[me, p]
-        owner, slot, count = owner_and_slot(region, me, p, owner_rows)
+    rows = [region[me, position] for position in range(blocks)]
+    found = [owner_and_slot(region, me, position, owner_rows) for position in range(blocks)]
+    totals = [[jnp.zeros((8, size), F32) for _ in range(blocks)] for _ in range(PARTS)]
+    for p in range(blocks):
+        owner, slot, count = found[p]
         first = jnp.bitwise_xor(me, owner) * TRAVEL
-        here = pl.ds(pl.multiple_of(p * size, size), size)
-        totals = [jnp.zeros((8, size), F32) for _ in range(PARTS)]
-        for k in range(width):
-            q = jnp.minimum(jnp.maximum(p + k - half, 0), blocks - 1)
-            inside = jnp.logical_and(q == p + k - half, region[me, q] == row + k - half)
-            tile = stage[first + travel_place(slot, count, k)].astype(F32)
+        for q in range(blocks):
+            if abs(q - p) > half:
+                matrix[p * size : (p + 1) * size, q * size : (q + 1) * size] = jnp.zeros((size, size), BF16)
+                continue
+            k = rows[q] - rows[p] + half
+            place = jnp.where(
+                k == 0,
+                travel_place(slot, count, 0),
+                jnp.where(k == 1, travel_place(slot, count, 1), travel_place(slot, count, 2)),
+            )
+            inside = jnp.logical_and(k >= 0, k < width)
+            tile = stage[first + place].astype(F32)
             tile = jnp.where(inside, tile, 0.0)
-            there = pl.ds(pl.multiple_of(q * size, size), size)
+            matrix[p * size : (p + 1) * size, q * size : (q + 1) * size] = tile.astype(BF16)
             turned = tile.T
             for c in range(PARTS):
-                terms = turned * moments[c, there, here]
-                totals[c] = totals[c] + jnp.sum(terms.reshape(-1, 8, size), axis=0)
-
-            @pl.when(inside)
-            def _():
-                matrix[here, there] = tile.astype(BF16)
-
-        for c in range(PARTS):
-            derivative[c : c + 1, here] = -2.0 * jnp.sum(totals[c], axis=0, keepdims=True)
+                terms = turned * moments[c, q * size : (q + 1) * size, p * size : (p + 1) * size]
+                totals[c][p] = totals[c][p] + jnp.sum(terms.reshape(-1, 8, size), axis=0)
+    derivative = [
+        jnp.concatenate([jnp.sum(total, axis=0, keepdims=True) for total in totals[c]], axis=1) for c in range(PARTS)
+    ]
 
     energies[...] = jnp.zeros_like(energies)
     lanes = lax.broadcasted_iota(jnp.int32, (points, size), 1)
@@ -527,38 +557,41 @@
         left = [
             jnp.concatenate([basis[group * step + inner, p] for p in range(blocks)], axis=1) for inner in range(step)
         ]
-        product = jnp.dot(jnp.concatenate(left, axis=0), matrix[...], preferred_element_type=F32)
+        left = jnp.concatenate(left, axis=0)
+        energy = [jnp.zeros((points, size), F32) for _ in range(step)]
+        for q in range(0, blocks, 2):
+            product = jnp.dot(left, matrix[:, q * size : (q + 2) * size], preferred_element_type=F32)
+            for inner in range(step):
+                batch = group * step + inner
+                for column in range(2):
+                    part = product[inner * points : (inner + 1) * points, column * size : (column + 1) * size]
+                    product_out[batch, q + column] = part.astype(BF16)
+                    energy[inner] = energy[inner] + part * field[batch, q + column].astype(F32)
         for inner in range(step):
-            batch = group * step + inner
-            energy = jnp.zeros((points, size), F32)
-            for q in range(blocks):
-                part = product[inner * points : (inner + 1) * points, q * size : (q + 1) * size]
-                product_out[batch, q] = part.astype(BF16)
-                energy = energy + part * field[batch, q].astype(F32)
-            energy = jnp.sum(energy, axis=1, keepdims=True)
-            energies[...] = jnp.where(lanes == batch, energy, energies[...])
+            total = jnp.sum(energy[inner], axis=1, keepdims=True)
+            energies[...] = jnp.where(lanes == group * step + inner, total, energies[...])
 
     lefts = []
     for c in range(PARTS):
         term = jnp.sum(energies[...] * grad_columns[c], axis=0, keepdims=True)
-        lefts.append(jnp.concatenate([derivative[c : c + 1, :], term], axis=1))
+        lefts.append(jnp.concatenate([-2.0 * derivative[c], term], axis=1))
     left = jnp.concatenate(lefts, axis=0)
     high, middle, low = (piece.astype(F32) for piece in split(left))
     left = jnp.concatenate([high, middle, low, jnp.zeros((16 - 3 * PARTS, left.shape[1]), F32)], axis=0).astype(BF16)
     chunk = out.shape[-1]
-
-    @pl.loop(0, out.shape[0])
-    def _(device):
-        atoms = pl.ds(pl.multiple_of(device * chunk, 16), chunk)
-        sums = lax.dot_general(left, hot[atoms, :], NT, preferred_element_type=F32)
-        out[jnp.bitwise_xor(me_atoms, device)] = sums[:PARTS] + sums[PARTS : 2 * PARTS] + sums[2 * PARTS : 3 * PARTS]
+    for device in range(out.shape[0]):
+        sums = lax.dot_general(
+            left, hot[device * chunk : (device + 1) * chunk, :], NT, preferred_element_type=F32
+        )
+        value = sums[:PARTS] + sums[PARTS : 2 * PARTS] + sums[2 * PARTS : 3 * PARTS]
+        out[jnp.bitwise_xor(me_atoms, device)] = value
 
 
 def combine(region, prepared, pieces, shapes):
     basis, field, moments, hot, grad_columns = prepared
     slabs, atom_devices, atom_total, points, blocks, width, owner_rows = shapes
     batches, _, _, size = basis.shape
-    step = 2 if batches % 2 == 0 else 1
+    step = 4 if batches % 4 == 0 else 1
     vmem = pl.BlockSpec(memory_space=pltpu.VMEM)
     return pl.pallas_call(
         functools.partial(combine_kernel, owner_rows=owner_rows, slabs=slabs, width=width, step=step),
@@ -572,7 +605,6 @@
             pltpu.VMEM((slabs * TRAVEL, size, size), BF16),
             pltpu.VMEM((blocks * size, blocks * size), BF16),
             pltpu.VMEM((points, size), F32),
-            pltpu.VMEM((PARTS, blocks * size), F32),
         ],
         compiler_params=pltpu.CompilerParams(vmem_limit_bytes=VMEM_LIMIT),
     )(region, basis, field, moments, hot, grad_columns, *pieces)
@@ -658,29 +690,40 @@
     atom_devices = lax.axis_size("atoms")
     atom_total = fn_atom.shape[0] // (10 * slabs * atom_devices) * slabs * atom_devices
     shapes = (slabs, atom_devices, atom_total, points, blocks, width, owner_rows)
-    own, near = fetch_rows(region, density, slabs, SHARE)
+    flat_basis = basis.reshape(batches, points * blocks, size)
+    flat_field = exchange_field.reshape(batches, points * blocks, size)
+    flat_grad = basis_grad.reshape(PARTS, batches, points * blocks, size)
+    own, *sent = send(
+        region,
+        density,
+        flat_basis,
+        flat_field,
+        flat_grad,
+        fn_atom.reshape(-1, size),
+        batch_atom.reshape(1, -1),
+        weight_grad,
+        slabs,
+        SHARE,
+        atom_total,
+    )
+    near = travel(sent[: slabs - 1], slabs)
+    *first, hot, grad_columns = sent[slabs - 1 :]
     if region.shape[1] == blocks:
-        ready = reorder(pattern, basis, exchange_field, basis_grad, weights)
-        near, far, (basis_wide, field_wide, *partial) = swap_halves(near, ready, atom_devices)
-        built = moments_and_atoms(region, *partial, weight_grad, fn_atom, batch_atom, atom_total)
-        ready = (basis_wide, field_wide, *built)
+        ready = reorder(pattern, flat_basis, flat_field, flat_grad, weights, first, points, blocks)
+        near, far, (basis_wide, field_wide, turned, grads) = swap_halves(near, ready, atom_devices)
+        ready = (basis_wide, field_wide, build_moments(turned, grads), hot, grad_columns)
         product, partial_grad = combine(region, ready, [own, *near, *far], shapes)
         gradient, product = sum_parts(partial_grad, product, slabs, atom_devices)
         contracted = write(pattern, product)
         return contracted.reshape(basis.shape), gradient
-    ready = relayout(
-        in_hbm(basis.reshape(batches, points * blocks, size)),
-        in_hbm(exchange_field.reshape(batches, points * blocks, size)),
-        points,
-        blocks,
-    )
+    ready = relayout(in_hbm(flat_basis), in_hbm(flat_field), points, blocks)
     near, far, (basis_wide, field_wide) = swap_halves(near, ready, atom_devices)
     tiles, partial_grad = partial_gradient(
         region,
         pattern,
         basis_wide,
         field_wide,
-        in_hbm(basis_grad.reshape(PARTS, batches, points * blocks, size)),
+        in_hbm(flat_grad),
         weights,
         weight_grad,
         fn_atom,

time: 39.7 us -> 35.7 us (0.90)
  Pallas kernels: 20.6 us -> 16.8 us
  waiting for transfers between devices: 5.21 us -> 4.62 us
    pallas_call x1, Pallas kernels: 6 us -> 3.34 us  [combine(): pl.pallas_call(functools.partial(combine_kernel, owner_rows=owner_rows, s...]
    pallas_call x2, Pallas kernels: 6.19 us -> 4.98 us  [the longest x1 2.59 us: build_moments(): pl.pallas_call(moment_kernel, out_shape=jax.ShapeDtypeStruct((PARTS, bloc...]
  transfers between devices with their start and end apart: 12 -> 12, of which waited for: 4 -> 4; matrix products, arithmetic and copies ran while one was open for 0% -> 0% of each run, Pallas kernels for 32% -> 31%
where the time goes in v11:
time: 35.7 us; the launch traced here: 35.4 us
  Pallas kernels  16.8 us (47%)
  starting transfers between devices  12.6 us (35%)
  waiting for transfers between devices  4.62 us (13%)
  between operations  0.74 us (2%)
  other arithmetic  0.6 us (2%)
    pallas_call x1, Pallas kernels, reorder(): pl.pallas_call(reorder_kernel, out_shape=(ordered, ordered, jax.ShapeDtyp...  6.46 us
    ppermute x6, starting transfers between devices, exchange_all(): lax.ppermute(parts[d], axis, [(i, i ^ d) for i in range(count)])  6.34 us
    ppermute x3, starting transfers between devices, travel(): lax.ppermute(outgoing[slabs - 1 - shift], 'grid', [(i, i ^ shift) for i i...  5.68 us
    ppermute x6, waiting for transfers between devices, exchange_all(): lax.ppermute(parts[d], axis, [(i, i ^ d) for i in range(count)])  4.49 us
    pallas_call x1, Pallas kernels, combine(): pl.pallas_call(functools.partial(combine_kernel, owner_rows=owner_rows, s...  3.34 us
    pallas_call x1, Pallas kernels, build_moments(): pl.pallas_call(moment_kernel, out_shape=jax.ShapeDtypeStruct((PARTS, bloc...  2.59 us
    pallas_call x1, Pallas kernels, send(): pl.pallas_call(functools.partial(send_kernel, share=share), out_shape=[*(...  2.39 us
    pallas_call x1, Pallas kernels, write(): pl.pallas_call(write_kernel, out_shape=jax.ShapeDtypeStruct(shape, BF16),...  2.06 us
  transfers between devices with their start and end apart: 12, of which 4 were waited for; matrix products, arithmetic and copies ran while one was open for 0% of the time, Pallas kernels for 31%

profile of v11, /device:TPU:0, one launch (start us, length us, event | category | flops | bytes accessed | tf_op | source)
XLA Modules:
  0.0 35.4 jit_solution(10935275766099433672)
XLA Ops:
  0.6 2.4 %shard_map.113 = (bf16[5,128,128]{2,1,0:T(8,128)(2,1)S(1)}, bf16[5,64,128]{2,1,0:T(8,128)(2,1)S(1)}, bf16[5,64,128]{2,1,0:T(8,128)(2,1)S(1)}, bf16[5,64,128]{2,1...) custom-call(s32[4,4]{1,0:T(4,128)} %region.1, ...), custom_call_target="tpu_custom_call" | custom-call | tf_op jit(solution)/shard_map/pallas_call | solution.py:123
  3.0 3.1 %collective-permute-start = (bf16[5,64,128]{2,1,0:T(8,128)(2,1)S(1)}, bf16[5,64,128]{2,1,0:T(8,128)(2,1)S(1)}, u32[]{:S(2)}, u32[]{:S(2)}) collective-permute-start(bf16[5,64,128]{2,1,0:T(8,128)(2,1)S(1)} %get-tuple-element.26), channel_id=1, source_target_pairs={{0,4},{4,0},{8,12},{12,8},{1,5},{5,1},{9,13},{13,9},{2,6},{6,2},{1... | collective-permute-start | bytes 245768 | tf_op jit(solution)/shard_map/ppermute | solution.py:151
  6.1 2.6 %collective-permute-start.1 = (bf16[5,64,128]{2,1,0:T(8,128)(2,1)S(1)}, bf16[5,64,128]{2,1,0:T(8,128)(2,1)S(1)}, u32[]{:S(2)}, u32[]{:S(2)}) collective-permute-start(bf16[5,64,128]{2,1,0:T(8,128)(2,1)S(1)} %get-tuple-element.27), channel_id=1, source_target_pairs={{0,8},{4,12},{8,0},{12,4},{1,9},{5,13},{9,1},{13,5},{2,10},{6,14},... | collective-permute-start | bytes 245768 | tf_op jit(solution)/shard_map/ppermute | solution.py:151
  8.7 0.0 collective-permute-start.2
  8.7 6.5 %shard_map.114 = (bf16[16,4,128,128]{3,2,1,0:T(8,128)(2,1)S(1)}, bf16[16,4,128,128]{3,2,1,0:T(8,128)(2,1)S(1)}, bf16[512,2048]{1,0:T(8,128)(2,1)S(1)}, bf16[3,4,2048,128]{3,2,1,0:T(8,128)(2,1)S(1)}) custom-call(s32[4,16]{1,0:T(4,128)} %bitcast.17, bf16[16,512,128]{2,1,0:T(8,128)(2,1)} %bitcast.22, bf16[16,512,128]{2,1,0:T(8,128)(2,1)} %bitcast.24, ...), custom_call_target="tpu_custom_call" | custom-call | bytes 10485760 | tf_op jit(solution)/shard_map/pallas_call | solution.py:462
  15.2 0.0 collective-permute-done.rest_1_
  15.2 0.1 collective-permute-done.1.rest_2_
  15.3 0.0 collective-permute-done.2.rest_3_
  15.3 0.0 copy-start
  15.3 0.0 collective-permute-start.3
  15.3 0.5 %collective-permute-start.4 = (bf16[5,64,128]{2,1,0:T(8,128)(2,1)S(1)}, bf16[5,64,128]{2,1,0:T(8,128)(2,1)S(1)}, u32[]{:S(2)}, u32[]{:S(2)}) collective-permute-start(bf16[5,64,128]{2,1,0:T(8,128)(2,1)S(1)} %collective-permute-done.1.rest_2_), channel_id=1, source_target_pairs={{0,1},{1,0},{2,3},{3,2},{4,5},{5,4},{6,7},{7,6},{8,9},{9,8},{10,11... | collective-permute-start | bytes 245768 | tf_op jit(solution)/shard_map/ppermute | solution.py:654
  15.8 0.1 collective-permute-start.5
  15.9 2.6 %shard_map.115.moments = f32[3,512,512]{2,1,0:T(8,128)S(1)} custom-call(bf16[512,2048]{1,0:T(8,128)(2,1)S(1)} %get-tuple-element.38.turned, bf16[3,4,2048,128]{3,2,1,0:T(8,128)(2,1)S(1)} %get-tuple-element.39.grads), custom_call_target="tpu_custom_call" | custom-call | flops 3221225472 | tf_op jit(solution)/shard_map/pallas_call | solution.py:503
  18.5 0.0 collective-permute-done.3.rest_4_
  18.5 0.0 collective-permute-done.4.rest_5_
  18.5 0.0 collective-permute-done.5.rest_6_
  18.5 0.0 copy-done
  18.5 0.0 copy-start.1
  18.5 3.3 %shard_map.116 = (bf16[16,4,128,128]{3,2,1,0:T(8,128)(2,1)S(1)}, f32[4,3,192]{2,1,0:T(4,128)S(1)}) custom-call(s32[4,4]{1,0:T(4,128)S(1)} %copy-done, bf16[16,4,128,128]{3,2,1,0:T(8,128)(2,1)S(1)} %get-tuple-element.36.basis, bf16[16,4,128,128]{3,2,1,0:T(8,128)(2,1)S(1)} %get-tuple-element.37.field, f32[3,512,512]{2,1,0:T(8,128)S(1)} %shard_map.115.moments, ...), custom_call_target="tpu_custom_call" | custom-call | tf_op jit(solution)/shard_map/pallas_call | solution.py:596
  21.9 0.5 %collective-permute-start.6 = (f32[3,192]{1,0:T(4,128)S(1)}, f32[3,192]{1,0:T(4,128)S(1)}, u32[]{:S(2)}, u32[]{:S(2)}) collective-permute-start(f32[3,192]{1,0:T(4,128)S(1)} %get-tuple-element.52), channel_id=1, source_target_pairs={{0,1},{1,0},{2,3},{3,2},{4,5},{5,4},{6,7},{7,6},{8,9},{9,8},{10,11... | collective-permute-start | bytes 6920 | tf_op jit(solution)/shard_map/ppermute | solution.py:665
  22.4 1.7 %collective-permute-start.7 = (f32[3,192]{1,0:T(4,128)S(1)}, f32[3,192]{1,0:T(4,128)S(1)}, u32[]{:S(2)}, u32[]{:S(2)}) collective-permute-start(f32[3,192]{1,0:T(4,128)S(1)} %get-tuple-element.51), channel_id=1, source_target_pairs={{0,2},{1,3},{2,0},{3,1},{4,6},{5,7},{6,4},{7,5},{8,10},{9,11},{10,... | collective-permute-start | bytes 6920 | tf_op jit(solution)/shard_map/ppermute | solution.py:665
  24.1 0.0 collective-permute-start.8
  24.1 0.0 collective-permute-done.6
  24.1 1.9 %collective-permute-done.7 = f32[3,192]{1,0:T(4,128)S(1)} collective-permute-done((f32[3,192]{1,0:T(4,128)S(1)}, f32[3,192]{1,0:T(4,128)S(1)}, u32[]{:S(2)}, u32[]{:S(2)}) %collective-permute-start.7) | collective-permute-done | bytes 2336 | tf_op jit(solution)/shard_map/ppermute | solution.py:665
  26.0 1.1 %collective-permute-done.8 = f32[3,192]{1,0:T(4,128)S(1)} collective-permute-done((f32[3,192]{1,0:T(4,128)S(1)}, f32[3,192]{1,0:T(4,128)S(1)}, u32[]{:S(2)}, u32[]{:S(2)}) %collective-permute-start.8) | collective-permute-done | bytes 2336 | tf_op jit(solution)/shard_map/ppermute | solution.py:665
  27.1 2.3 %collective-permute-start.10 = (f32[3,192]{1,0:T(4,128)S(1)}, f32[3,192]{1,0:T(4,128)S(1)}, u32[]{:S(2)}, u32[]{:S(2)}) collective-permute-start(f32[3,192]{1,0:T(4,128)S(1)} %fusion), channel_id=1, source_target_pairs={{0,8},{4,12},{8,0},{12,4},{1,9},{5,13},{9,1},{13,5},{2,10},{6,14},... | collective-permute-start | bytes 6920 | tf_op jit(solution)/shard_map/ppermute | solution.py:665
  29.4 1.4 %collective-permute-start.11 = (f32[3,192]{1,0:T(4,128)S(1)}, f32[3,192]{1,0:T(4,128)S(1)}, u32[]{:S(2)}, u32[]{:S(2)}) collective-permute-start(f32[3,192]{1,0:T(4,128)S(1)} %fusion), channel_id=1, source_target_pairs={{0,12},{4,8},{8,4},{12,0},{1,13},{5,9},{9,5},{13,1},{2,14},{6,10},... | collective-permute-start | bytes 6920 | tf_op jit(solution)/shard_map/ppermute | solution.py:665
  30.8 0.5 %collective-permute-start.9 = (f32[3,192]{1,0:T(4,128)S(1)}, f32[3,192]{1,0:T(4,128)S(1)}, u32[]{:S(2)}, u32[]{:S(2)}) collective-permute-start(f32[3,192]{1,0:T(4,128)S(1)} %fusion), channel_id=1, source_target_pairs={{0,4},{4,0},{8,12},{12,8},{1,5},{5,1},{9,13},{13,9},{2,6},{6,2},{1... | collective-permute-start | bytes 6920 | tf_op jit(solution)/shard_map/ppermute | solution.py:665
  31.3 0.0 copy-done.1
  31.3 2.1 %shard_map.117 = bf16[16,512,128]{2,1,0:T(8,128)(2,1)} custom-call(s32[4,16]{1,0:T(4,128)S(1)} %bitcast.18, bf16[16,4,128,128]{3,2,1,0:T(8,128)(2,1)S(1)} %get-tuple-element.48.product), custom_call_target="tpu_custom_call" | custom-call | bytes 4194304 | tf_op jit(solution)/shard_map/pallas_call | solution.py:636
  33.4 0.0 collective-permute-done.10
  33.4 1.4 %collective-permute-done.11 = f32[3,192]{1,0:T(4,128)S(1)} collective-permute-done((f32[3,192]{1,0:T(4,128)S(1)}, f32[3,192]{1,0:T(4,128)S(1)}, u32[]{:S(2)}, u32[]{:S(2)}) %collective-permute-start.11) | collective-permute-done | bytes 2336 | tf_op jit(solution)/shard_map/ppermute | solution.py:665
  34.8 0.0 collective-permute-done.9
  34.8 0.6 %add_add_fusion = f32[3,192]{1,0:T(4,128)} fusion(f32[3,192]{1,0:T(4,128)S(1)} %collective-permute-done.10, f32[3,192]{1,0:T(4,128)S(1)} %collective-permute-done.11, f32[3,192]{1,0:T(4,128)S(1)} %fusion, f32[3,192]{1,0:T(4,128)S(1)} %collective-permute-done.9), kind=kLoop, calls=%fused_computation.2 | loop fusion | flops 1728 | bytes 11520 | tf_op jit(solution)/shard_map/add | solution.py:661
  (2 shorter events, 0.0 us)
Async XLA Ops:
  3.0 12.1 %collective-permute-start = (bf16[5,64,128]{2,1,0:T(8,128)(2,1)S(1)}, bf16[5,64,128]{2,1,0:T(8,128)(2,1)S(1)}, u32[]{:S(2)}, u32[]{:S(2)}) collective-permute-start(bf16[5,64,128]{2,1,0:T(8,128)(2,1)S(1)} %get-tuple-element.26), channel_id=1, source_target_pairs={{0,4},{4,0},{8,12},{12,8},{1,5},{5,1},{9,13},{13,9},{2,6},{6,2},{1... | collective-permute-start | bytes 245768 | tf_op jit(solution)/shard_map/ppermute | solution.py:151
  6.1 9.2 %collective-permute-start.1 = (bf16[5,64,128]{2,1,0:T(8,128)(2,1)S(1)}, bf16[5,64,128]{2,1,0:T(8,128)(2,1)S(1)}, u32[]{:S(2)}, u32[]{:S(2)}) collective-permute-start(bf16[5,64,128]{2,1,0:T(8,128)(2,1)S(1)} %get-tuple-element.27), channel_id=1, source_target_pairs={{0,8},{4,12},{8,0},{12,4},{1,9},{5,13},{9,1},{13,5},{2,10},{6,14},... | collective-permute-start | bytes 245768 | tf_op jit(solution)/shard_map/ppermute | solution.py:151
  8.7 6.6 %collective-permute-start.2 = (bf16[5,64,128]{2,1,0:T(8,128)(2,1)S(1)}, bf16[5,64,128]{2,1,0:T(8,128)(2,1)S(1)}, u32[]{:S(2)}, u32[]{:S(2)}) collective-permute-start(bf16[5,64,128]{2,1,0:T(8,128)(2,1)S(1)} %get-tuple-element.28), channel_id=1, source_target_pairs={{0,12},{4,8},{8,4},{12,0},{1,13},{5,9},{9,5},{13,1},{2,14},{6,10},... | collective-permute-start | bytes 245768 | tf_op jit(solution)/shard_map/ppermute | solution.py:151
  15.3 3.2 %copy-start = (s32[4,4]{1,0:T(4,128)S(1)}, s32[4,4]{1,0:T(4,128)}, u32[]{:S(2)}) copy-start(s32[4,4]{1,0:T(4,128)} %region.1) | copy-start | bytes 196
  15.3 3.2 %collective-permute-start.3 = (bf16[5,64,128]{2,1,0:T(8,128)(2,1)S(1)}, bf16[5,64,128]{2,1,0:T(8,128)(2,1)S(1)}, u32[]{:S(2)}, u32[]{:S(2)}) collective-permute-start(bf16[5,64,128]{2,1,0:T(8,128)(2,1)S(1)} %collective-permute-done.rest_1_), channel_id=1, source_target_pairs={{0,1},{1,0},{2,3},{3,2},{4,5},{5,4},{6,7},{7,6},{8,9},{9,8},{10,11... | collective-permute-start | bytes 245768 | tf_op jit(solution)/shard_map/ppermute | solution.py:654
  15.3 3.2 %collective-permute-start.4 = (bf16[5,64,128]{2,1,0:T(8,128)(2,1)S(1)}, bf16[5,64,128]{2,1,0:T(8,128)(2,1)S(1)}, u32[]{:S(2)}, u32[]{:S(2)}) collective-permute-start(bf16[5,64,128]{2,1,0:T(8,128)(2,1)S(1)} %collective-permute-done.1.rest_2_), channel_id=1, source_target_pairs={{0,1},{1,0},{2,3},{3,2},{4,5},{5,4},{6,7},{7,6},{8,9},{9,8},{10,11... | collective-permute-start | bytes 245768 | tf_op jit(solution)/shard_map/ppermute | solution.py:654
  15.8 2.7 %collective-permute-start.5 = (bf16[5,64,128]{2,1,0:T(8,128)(2,1)S(1)}, bf16[5,64,128]{2,1,0:T(8,128)(2,1)S(1)}, u32[]{:S(2)}, u32[]{:S(2)}) collective-permute-start(bf16[5,64,128]{2,1,0:T(8,128)(2,1)S(1)} %collective-permute-done.2.rest_3_), channel_id=1, source_target_pairs={{0,1},{1,0},{2,3},{3,2},{4,5},{5,4},{6,7},{7,6},{8,9},{9,8},{10,11... | collective-permute-start | bytes 245768 | tf_op jit(solution)/shard_map/ppermute | solution.py:654
  18.5 12.8 %copy-start.1 = (s32[16,4]{0,1:T(4,128)S(1)}, s32[16,4]{0,1:T(4,128)}, u32[]{:S(2)}) copy-start(s32[16,4]{0,1:T(4,128)} %param.17) | copy-start | bytes 772
  21.9 2.2 %collective-permute-start.6 = (f32[3,192]{1,0:T(4,128)S(1)}, f32[3,192]{1,0:T(4,128)S(1)}, u32[]{:S(2)}, u32[]{:S(2)}) collective-permute-start(f32[3,192]{1,0:T(4,128)S(1)} %get-tuple-element.52), channel_id=1, source_target_pairs={{0,1},{1,0},{2,3},{3,2},{4,5},{5,4},{6,7},{7,6},{8,9},{9,8},{10,11... | collective-permute-start | bytes 6920 | tf_op jit(solution)/shard_map/ppermute | solution.py:665
  22.4 3.6 %collective-permute-start.7 = (f32[3,192]{1,0:T(4,128)S(1)}, f32[3,192]{1,0:T(4,128)S(1)}, u32[]{:S(2)}, u32[]{:S(2)}) collective-permute-start(f32[3,192]{1,0:T(4,128)S(1)} %get-tuple-element.51), channel_id=1, source_target_pairs={{0,2},{1,3},{2,0},{3,1},{4,6},{5,7},{6,4},{7,5},{8,10},{9,11},{10,... | collective-permute-start | bytes 6920 | tf_op jit(solution)/shard_map/ppermute | solution.py:665
  24.1 3.1 %collective-permute-start.8 = (f32[3,192]{1,0:T(4,128)S(1)}, f32[3,192]{1,0:T(4,128)S(1)}, u32[]{:S(2)}, u32[]{:S(2)}) collective-permute-start(f32[3,192]{1,0:T(4,128)S(1)} %get-tuple-element.50), channel_id=1, source_target_pairs={{0,3},{1,2},{2,1},{3,0},{4,7},{5,6},{6,5},{7,4},{8,11},{9,10},{10,... | collective-permute-start | bytes 6920 | tf_op jit(solution)/shard_map/ppermute | solution.py:665
  27.1 6.2 %collective-permute-start.10 = (f32[3,192]{1,0:T(4,128)S(1)}, f32[3,192]{1,0:T(4,128)S(1)}, u32[]{:S(2)}, u32[]{:S(2)}) collective-permute-start(f32[3,192]{1,0:T(4,128)S(1)} %fusion), channel_id=1, source_target_pairs={{0,8},{4,12},{8,0},{12,4},{1,9},{5,13},{9,1},{13,5},{2,10},{6,14},... | collective-permute-start | bytes 6920 | tf_op jit(solution)/shard_map/ppermute | solution.py:665
  29.4 5.4 %collective-permute-start.11 = (f32[3,192]{1,0:T(4,128)S(1)}, f32[3,192]{1,0:T(4,128)S(1)}, u32[]{:S(2)}, u32[]{:S(2)}) collective-permute-start(f32[3,192]{1,0:T(4,128)S(1)} %fusion), channel_id=1, source_target_pairs={{0,12},{4,8},{8,4},{12,0},{1,13},{5,9},{9,5},{13,1},{2,14},{6,10},... | collective-permute-start | bytes 6920 | tf_op jit(solution)/shard_map/ppermute | solution.py:665
  30.8 4.0 %collective-permute-start.9 = (f32[3,192]{1,0:T(4,128)S(1)}, f32[3,192]{1,0:T(4,128)S(1)}, u32[]{:S(2)}, u32[]{:S(2)}) collective-permute-start(f32[3,192]{1,0:T(4,128)S(1)} %fusion), channel_id=1, source_target_pairs={{0,4},{4,0},{8,12},{12,8},{1,5},{5,1},{9,13},{13,9},{2,6},{6,2},{1... | collective-permute-start | bytes 6920 | tf_op jit(solution)/shard_map/ppermute | solution.py:665

commit v12 on v11

--- a/solution.py
+++ b/solution.py
@@ -10,7 +10,6 @@
 
 TRAVEL = 5
 SHARE = 2
-CHUNK = 2
 PARTS = 3
 F32 = jnp.float32
 BF16 = jnp.bfloat16
@@ -37,25 +36,8 @@
     return jnp.where(jnp.logical_and(slot == 0, count == 2), 1, 4)
 
 
-def send_kernel(
-    region_hbm, density, basis, field, basis_grad, fn_atom_hbm, batch_atom_hbm, weight_grad_hbm, *rest, share
-):
-    *outs, first_basis, first_field, first_grad, hot, grad_columns = rest[:-7]
-    region, fn_atom, batch_atom, weight_grad, sems, small_sems, first_sems = rest[-7:]
-    small = (
-        pltpu.make_async_copy(region_hbm, region, small_sems.at[0]),
-        pltpu.make_async_copy(fn_atom_hbm, fn_atom, small_sems.at[1]),
-        pltpu.make_async_copy(batch_atom_hbm, batch_atom, small_sems.at[2]),
-        pltpu.make_async_copy(weight_grad_hbm, weight_grad, small_sems.at[3]),
-    )
-    firsts = (
-        pltpu.make_async_copy(field.at[pl.ds(0, first_field.shape[0])], first_field, first_sems.at[0]),
-        pltpu.make_async_copy(basis_grad.at[:, pl.ds(0, first_grad.shape[1])], first_grad, first_sems.at[1]),
-        pltpu.make_async_copy(basis.at[pl.ds(0, first_basis.shape[0])], first_basis, first_sems.at[2]),
-    )
-    for copy in small:
-        copy.start()
-    small[0].wait()
+def send_kernel(region, density, *rest, share):
+    *outs, sems = rest
     me = lax.axis_index("grid")
     part = lax.rem(lax.axis_index("atoms"), share)
     size = region.shape[1]
@@ -85,28 +67,9 @@
         )
         for number, (source, target) in enumerate(pairs):
             copies.append(pltpu.make_async_copy(source, target, sems.at[shift, number]))
-    for copy in (*copies, *firsts):
+    for copy in copies:
         copy.start()
-    for copy in small[1:]:
-        copy.wait()
-    length = density.shape[-1]
-    batches = weight_grad.shape[1]
-    atoms = lax.broadcasted_iota(jnp.int32, (hot.shape[0], length), 0)
-    fill = jnp.full((1, length - batches), -1, jnp.int32)
-    hot[:, size * length :] = jnp.where(
-        atoms == jnp.concatenate([batch_atom[...], fill], axis=1), 1.0, 0.0
-    ).astype(BF16)
-
-    @pl.loop(0, size)
-    def _(position):
-        ids = fn_atom[pl.ds(region[me, position], 1), :]
-        columns = pl.ds(pl.multiple_of(position * length, length), length)
-        hot[:, columns] = jnp.where(atoms == ids, 1.0, 0.0).astype(BF16)
-
-    for c in range(PARTS):
-        padding = jnp.zeros((length - batches, weight_grad.shape[2]), F32)
-        grad_columns[c] = jnp.concatenate([weight_grad[c], padding], axis=0).T
-    for copy in (*copies, *firsts):
+    for copy in copies:
         copy.wait()
 
 
@@ -114,42 +77,25 @@
     return pltpu.with_memory_space_constraint(array, pltpu.HBM)
 
 
-def send(region, density, basis, field, basis_grad, fn_atom, batch_atom, weight_grad, slabs, share, atom_total):
+def rows_to_send(region, density, slabs, share):
     size = density.shape[-1]
     kept = [size] + [size // share] * (slabs - 1)
-    first = jax.ShapeDtypeStruct((CHUNK, *basis.shape[1:]), BF16)
-    hbm = pl.BlockSpec(memory_space=pl.ANY)
-    operands = (region, density, basis, field, basis_grad, fn_atom, batch_atom, weight_grad)
     return pl.pallas_call(
         functools.partial(send_kernel, share=share),
-        out_shape=[
-            *(jax.ShapeDtypeStruct((TRAVEL, rows, size), density.dtype) for rows in kept),
-            first,
-            first,
-            jax.ShapeDtypeStruct((PARTS, CHUNK, *basis.shape[1:]), BF16),
-            jax.ShapeDtypeStruct((atom_total, (region.shape[1] + 1) * size), BF16),
-            jax.ShapeDtypeStruct((PARTS, weight_grad.shape[2], size), F32),
-        ],
-        in_specs=[hbm] * len(operands),
-        out_specs=[pl.BlockSpec(memory_space=pltpu.VMEM)] * (slabs + 5),
-        scratch_shapes=[
-            pltpu.SMEM(region.shape, jnp.int32),
-            pltpu.VMEM(fn_atom.shape, jnp.int32),
-            pltpu.VMEM(batch_atom.shape, jnp.int32),
-            pltpu.VMEM(weight_grad.shape, F32),
-            pltpu.SemaphoreType.DMA((slabs, 3)),
-            pltpu.SemaphoreType.DMA((4,)),
-            pltpu.SemaphoreType.DMA((3,)),
-        ],
-        compiler_params=pltpu.CompilerParams(vmem_limit_bytes=VMEM_LIMIT),
-    )(*(in_hbm(operand) for operand in operands))
-
-
-def travel(outgoing, slabs):
+        out_shape=[jax.ShapeDtypeStruct((TRAVEL, rows, size), density.dtype) for rows in kept],
+        in_specs=[pl.BlockSpec(memory_space=pltpu.SMEM), pl.BlockSpec(memory_space=pl.ANY)],
+        out_specs=[pl.BlockSpec(memory_space=pltpu.VMEM)] * slabs,
+        scratch_shapes=[pltpu.SemaphoreType.DMA((slabs, 3))],
+        compiler_params=pltpu.CompilerParams(vmem_limit_bytes=VMEM_LIMIT),
+    )(in_hbm(region), in_hbm(density))
+
+
+def fetch_rows(region, density, slabs, share):
+    own, *outgoing = rows_to_send(region, density, slabs, share)
     near = {}
     for shift in reversed(range(1, slabs)):
         near[shift] = lax.ppermute(outgoing[slabs - 1 - shift], "grid", [(i, i ^ shift) for i in range(slabs)])
-    return [near[shift] for shift in range(1, slabs)]
+    return own, [near[shift] for shift in range(1, slabs)]
 
 
 def stage_rows(stage, own, near, far, share):
@@ -389,9 +335,6 @@
     field,
     basis_grad,
     weights_hbm,
-    first_basis,
-    first_field,
-    first_grad,
     basis_out,
     field_out,
     turned,
@@ -420,12 +363,8 @@
     )
     for copy in small:
         copy.start()
-    for batch in range(CHUNK):
-        pltpu.make_async_copy(first_field.at[batch], field_in.at[batch], sems.at[batch, 0]).start()
-        pltpu.make_async_copy(first_basis.at[batch], basis_in.at[batch], sems.at[batch, 1]).start()
-        pltpu.make_async_copy(first_grad.at[:, batch], grad_in.at[:, batch], sems.at[batch, 2]).start()
-
-    @pl.loop(CHUNK, batches)
+
+    @pl.loop(0, batches)
     def _(batch):
         for copy in copies(batch):
             copy.start()
@@ -446,15 +385,16 @@
             wide[2 + c] = grad_in[c, batch].astype(F32)
         for s, place in enumerate(places):
             strided = pl.ds(s, points, stride=blocks)
-            values = wide[0, strided, :]
-            field_out[batch, place] = values.astype(BF16)
-            turned[pl.ds(pl.multiple_of(place * size, size), size), points_here] = (values.T * weight).astype(BF16)
+            values = wide[0, strided, :].astype(BF16)
+            field_out[batch, place] = values
+            rows = pl.ds(pl.multiple_of(place * size, size), size)
+            turned[rows, points_here] = (values.T.astype(F32) * weight).astype(BF16)
             basis_out[batch, place] = wide[1, strided, :].astype(BF16)
             for c in range(PARTS):
                 grads[c, place, points_here, :] = wide[2 + c, strided, :].astype(BF16)
 
 
-def reorder(pattern, basis, field, basis_grad, weights, first, points, blocks):
+def reorder(pattern, basis, field, basis_grad, weights, points, blocks):
     batches, rows, size = basis.shape
     hbm = pl.BlockSpec(memory_space=pl.ANY)
     vmem = pl.BlockSpec(memory_space=pltpu.VMEM)
@@ -467,7 +407,7 @@
             jax.ShapeDtypeStruct((blocks * size, batches * points), BF16),
             jax.ShapeDtypeStruct((PARTS, blocks, batches * points, size), BF16),
         ),
-        in_specs=[hbm] * 5 + [vmem] * 3,
+        in_specs=[hbm] * 5,
         out_specs=(vmem,) * 4,
         scratch_shapes=[
             pltpu.SMEM((blocks, batches), jnp.int32),
@@ -483,7 +423,7 @@
         cost_estimate=pl.CostEstimate(
             flops=0, bytes_accessed=2 * (2 + PARTS) * batches * rows * size, transcendentals=0
         ),
-    )(in_hbm(pattern.T), in_hbm(basis), in_hbm(field), in_hbm(basis_grad), in_hbm(weights), *first)
+    )(in_hbm(pattern.T), in_hbm(basis), in_hbm(field), in_hbm(basis_grad), in_hbm(weights))
 
 
 def moment_kernel(turned, grads, moments):
@@ -510,6 +450,41 @@
             flops=2 * PARTS * depth * (blocks * size) ** 2, bytes_accessed=0, transcendentals=0
         ),
     )(turned, grads)
+
+
+def atom_kernel(region, fn_atom, batch_atom, weight_grad, hot, grad_columns):
+    batches, points = weight_grad.shape[1:]
+    size = fn_atom.shape[1]
+    blocks = region.shape[1]
+    me = lax.axis_index("grid")
+    atoms = lax.broadcasted_iota(jnp.int32, (hot.shape[0], size), 0)
+    ids = jnp.concatenate([batch_atom[...], jnp.full((1, size - batches), -1, jnp.int32)], axis=1)
+    hot[:, blocks * size :] = jnp.where(atoms == ids, 1.0, 0.0).astype(BF16)
+
+    @pl.loop(0, blocks)
+    def _(position):
+        ids = fn_atom[pl.ds(region[me, position], 1), :]
+        columns = pl.ds(pl.multiple_of(position * size, size), size)
+        hot[:, columns] = jnp.where(atoms == ids, 1.0, 0.0).astype(BF16)
+
+    for c in range(PARTS):
+        padding = jnp.zeros((size - batches, points), F32)
+        grad_columns[c] = jnp.concatenate([weight_grad[c], padding], axis=0).T
+
+
+def atom_matrix(region, fn_atom, batch_atom, weight_grad, blocks, size, atom_total):
+    vmem = pl.BlockSpec(memory_space=pltpu.VMEM)
+    return pl.pallas_call(
+        atom_kernel,
+        out_shape=(
+            jax.ShapeDtypeStruct((atom_total, (blocks + 1) * size), BF16),
+            jax.ShapeDtypeStruct((PARTS, weight_grad.shape[2], size), F32),
+        ),
+        in_specs=[pl.BlockSpec(memory_space=pltpu.SMEM)] + [vmem] * 3,
+        out_specs=(vmem, vmem),
+        compiler_params=pltpu.CompilerParams(vmem_limit_bytes=VMEM_LIMIT),
+        cost_estimate=pl.CostEstimate(flops=1000000000, bytes_accessed=2 * atom_total * size, transcendentals=0),
+    )(region, fn_atom.reshape(-1, size), batch_atom.reshape(1, -1), weight_grad)
 
 
 def combine_kernel(
@@ -591,7 +566,7 @@
     basis, field, moments, hot, grad_columns = prepared
     slabs, atom_devices, atom_total, points, blocks, width, owner_rows = shapes
     batches, _, _, size = basis.shape
-    step = 4 if batches % 4 == 0 else 1
+    step = 8 if batches % 8 == 0 else 1
     vmem = pl.BlockSpec(memory_space=pltpu.VMEM)
     return pl.pallas_call(
         functools.partial(combine_kernel, owner_rows=owner_rows, slabs=slabs, width=width, step=step),
@@ -693,25 +668,15 @@
     flat_basis = basis.reshape(batches, points * blocks, size)
     flat_field = exchange_field.reshape(batches, points * blocks, size)
     flat_grad = basis_grad.reshape(PARTS, batches, points * blocks, size)
-    own, *sent = send(
-        region,
-        density,
-        flat_basis,
-        flat_field,
-        flat_grad,
-        fn_atom.reshape(-1, size),
-        batch_atom.reshape(1, -1),
-        weight_grad,
-        slabs,
-        SHARE,
-        atom_total,
-    )
-    near = travel(sent[: slabs - 1], slabs)
-    *first, hot, grad_columns = sent[slabs - 1 :]
+    own, near = fetch_rows(region, density, slabs, SHARE)
     if region.shape[1] == blocks:
-        ready = reorder(pattern, flat_basis, flat_field, flat_grad, weights, first, points, blocks)
-        near, far, (basis_wide, field_wide, turned, grads) = swap_halves(near, ready, atom_devices)
-        ready = (basis_wide, field_wide, build_moments(turned, grads), hot, grad_columns)
+        basis_wide, field_wide, turned, grads = reorder(
+            pattern, flat_basis, flat_field, flat_grad, weights, points, blocks
+        )
+        ready = (basis_wide, field_wide, build_moments(turned, grads), batch_atom)
+        near, far, (basis_wide, field_wide, moments, batch_atom) = swap_halves(near, ready, atom_devices)
+        hot, grad_columns = atom_matrix(region, fn_atom, batch_atom, weight_grad, blocks, size, atom_total)
+        ready = (basis_wide, field_wide, moments, hot, grad_columns)
         product, partial_grad = combine(region, ready, [own, *near, *far], shapes)
         gradient, product = sum_parts(partial_grad, product, slabs, atom_devices)
         contracted = write(pattern, product)

time: 35.7 us -> 34.4 us (0.964)
  Pallas kernels: 16.8 us -> 15.8 us
    pallas_call x1, Pallas kernels: 6.46 us -> 5.59 us  [reorder(): pl.pallas_call(reorder_kernel, out_shape=(ordered, ordered, jax.ShapeDtyp...]
    pallas_call x1, Pallas kernels: 3.34 us -> 2.87 us  [combine(): pl.pallas_call(functools.partial(combine_kernel, owner_rows=owner_rows, s...]
    ppermute x6, waiting for transfers between devices: 4.49 us -> 4.06 us  [exchange_all(): lax.ppermute(parts[d], axis, [(i, i ^ d) for i in range(count)])]
    pallas_call x1 -> x2, Pallas kernels: 2.39 us -> 2.74 us  [the longest x1 1.78 us: rows_to_send(): pl.pallas_call(functools.partial(send_kernel, share=share), out_shape=[ja...]
  transfers between devices with their start and end apart: 12 -> 12, of which waited for: 4 -> 5; matrix products, arithmetic and copies ran while one was open for 0% -> 0% of each run, Pallas kernels for 31% -> 33%
where the time goes in v12:
time: 34.4 us; the launch traced here: 34.1 us
  Pallas kernels  15.8 us (46%)
  starting transfers between devices  12.5 us (36%)
  waiting for transfers between devices  4.27 us (12%)
  between operations  0.77 us (2%)
  other arithmetic  0.6 us (2%)
    ppermute x6, starting transfers between devices, exchange_all(): lax.ppermute(parts[d], axis, [(i, i ^ d) for i in range(count)])  6.21 us
    ppermute x3, starting transfers between devices, fetch_rows(): lax.ppermute(outgoing[slabs - 1 - shift], 'grid', [(i, i ^ shift) for i i...  5.68 us
    pallas_call x1, Pallas kernels, reorder(): pl.pallas_call(reorder_kernel, out_shape=(ordered, ordered, jax.ShapeDtyp...  5.59 us
    ppermute x6, waiting for transfers between devices, exchange_all(): lax.ppermute(parts[d], axis, [(i, i ^ d) for i in range(count)])  4.06 us
    pallas_call x1, Pallas kernels, combine(): pl.pallas_call(functools.partial(combine_kernel, owner_rows=owner_rows, s...  2.87 us
    pallas_call x1, Pallas kernels, build_moments(): pl.pallas_call(moment_kernel, out_shape=jax.ShapeDtypeStruct((PARTS, bloc...  2.59 us
    pallas_call x1, Pallas kernels, write(): pl.pallas_call(write_kernel, out_shape=jax.ShapeDtypeStruct(shape, BF16),...  2.06 us
    pallas_call x1, Pallas kernels, rows_to_send(): pl.pallas_call(functools.partial(send_kernel, share=share), out_shape=[ja...  1.78 us
  transfers between devices with their start and end apart: 12, of which 5 were waited for; matrix products, arithmetic and copies ran while one was open for 0% of the time, Pallas kernels for 33%

profile of v12, /device:TPU:0, one launch (start us, length us, event | category | flops | bytes accessed | tf_op | source)
XLA Modules:
  0.0 34.1 jit_solution(870321922784738246)
XLA Ops:
  0.6 1.8 %shard_map.113 = (bf16[5,128,128]{2,1,0:T(8,128)(2,1)S(1)}, bf16[5,64,128]{2,1,0:T(8,128)(2,1)S(1)}, bf16[5,64,128]{2,1,0:T(8,128)(2,1)S(1)}, bf16[5,64,128]{2,1,0:T(8,128)(2,1)S(1)}) custom-call(s32[4,4]{1,0:T(4,128)} %region.5, bf16[15,3,128,128]{3,2,1,0:T(8,128)(2,1)} %density.1), custom_call_target="tpu_custom_call" | custom-call | tf_op jit(solution)/shard_map/pallas_call | solution.py:83
  2.4 3.1 %collective-permute-start = (bf16[5,64,128]{2,1,0:T(8,128)(2,1)S(1)}, bf16[5,64,128]{2,1,0:T(8,128)(2,1)S(1)}, u32[]{:S(2)}, u32[]{:S(2)}) collective-permute-start(bf16[5,64,128]{2,1,0:T(8,128)(2,1)S(1)} %get-tuple-element.23), channel_id=1, source_target_pairs={{0,4},{4,0},{8,12},{12,8},{1,5},{5,1},{9,13},{13,9},{2,6},{6,2},{1... | collective-permute-start | bytes 245768 | tf_op jit(solution)/shard_map/ppermute | solution.py:97
  5.5 2.6 %collective-permute-start.1 = (bf16[5,64,128]{2,1,0:T(8,128)(2,1)S(1)}, bf16[5,64,128]{2,1,0:T(8,128)(2,1)S(1)}, u32[]{:S(2)}, u32[]{:S(2)}) collective-permute-start(bf16[5,64,128]{2,1,0:T(8,128)(2,1)S(1)} %get-tuple-element.24), channel_id=1, source_target_pairs={{0,8},{4,12},{8,0},{12,4},{1,9},{5,13},{9,1},{13,5},{2,10},{6,14},... | collective-permute-start | bytes 245768 | tf_op jit(solution)/shard_map/ppermute | solution.py:97
  8.1 0.0 collective-permute-start.2
  8.1 5.6 %shard_map.114 = (bf16[16,4,128,128]{3,2,1,0:T(8,128)(2,1)S(1)}, bf16[16,4,128,128]{3,2,1,0:T(8,128)(2,1)S(1)}, bf16[512,2048]{1,0:T(8,128)(2,1)S(1)}, bf16[3,4,2048,128]{3,2,1,0:T(8,128)(2,1)S(1)}) custom-call(s32[4,16]{1,0:T(4,128)} %bitcast.17, bf16[16,512,128]{2,1,0:T(8,128)(2,1)} %bitcast.22, bf16[16,512,128]{2,1,0:T(8,128)(2,1)} %bitcast.23, ...), custom_call_target="tpu_custom_call" | custom-call | bytes 10485760 | tf_op jit(solution)/shard_map/pallas_call | solution.py:402
  13.7 0.0 copy-start
  13.7 0.0 copy-start.2
  13.7 0.0 copy-start.3
  13.7 0.0 copy-start.4
  13.7 2.6 %shard_map.115.moments = f32[3,512,512]{2,1,0:T(8,128)S(1)} custom-call(bf16[512,2048]{1,0:T(8,128)(2,1)S(1)} %get-tuple-element.28.turned, bf16[3,4,2048,128]{3,2,1,0:T(8,128)(2,1)S(1)} %get-tuple-element.29.grads), custom_call_target="tpu_custom_call" | custom-call | flops 3221225472 | tf_op jit(solution)/shard_map/pallas_call | solution.py:443
  16.3 0.0 collective-permute-done.rest_1_
  16.4 0.0 collective-permute-done.1.rest_2_
  16.4 0.0 collective-permute-done.2.rest_3_
  16.4 0.1 collective-permute-start.3
  16.5 0.5 %collective-permute-start.4 = (bf16[5,64,128]{2,1,0:T(8,128)(2,1)S(1)}, bf16[5,64,128]{2,1,0:T(8,128)(2,1)S(1)}, u32[]{:S(2)}, u32[]{:S(2)}) collective-permute-start(bf16[5,64,128]{2,1,0:T(8,128)(2,1)S(1)} %collective-permute-done.1.rest_2_), channel_id=1, source_target_pairs={{0,1},{1,0},{2,3},{3,2},{4,5},{5,4},{6,7},{7,6},{8,9},{9,8},{10,11... | collective-permute-start | bytes 245768 | tf_op jit(solution)/shard_map/ppermute | solution.py:629
  17.0 0.1 collective-permute-start.5
  17.0 0.0 copy-done
  17.0 0.0 copy-done.2
  17.0 0.0 copy-done.3
  17.0 0.0 copy-done.4
  17.0 1.0 %shard_map.116 = (bf16[768,640]{1,0:T(8,128)(2,1)S(1)}, f32[3,128,128]{2,1,0:T(8,128)S(1)}) custom-call(s32[4,4]{1,0:T(4,128)S(1)} %copy-done, s32[60,128]{1,0:T(8,128)S(1)} %bitcast.19, s32[1,16]{1,0:T(1,128)S(1)} %bitcast.20, f32[3,16,128]{2,1,0:T(8,128)S(1)} %copy-done.3), custom_call_target="tpu_custom_call" | custom-call | flops 1000000000 | bytes 196608 | tf_op jit(solution)/shard_map/pallas_call | solution.py:477
  18.0 0.0 collective-permute-done.3.rest_4_
  18.0 0.0 collective-permute-done.4.rest_5_
  18.0 0.2 collective-permute-done.5.rest_6_
  18.2 0.0 copy-start.1
  18.2 2.9 %shard_map.117 = (bf16[16,4,128,128]{3,2,1,0:T(8,128)(2,1)S(1)}, f32[4,3,192]{2,1,0:T(4,128)S(1)}) custom-call(s32[4,4]{1,0:T(4,128)S(1)} %copy-done, bf16[16,4,128,128]{3,2,1,0:T(8,128)(2,1)S(1)} %get-tuple-element.30.basis, bf16[16,4,128,128]{3,2,1,0:T(8,128)(2,1)S(1)} %get-tuple-element.31.field, f32[3,512,512]{2,1,0:T(8,128)S(1)} %shard_map.115.moments, ...), custom_call_target="tpu_custom_call" | custom-call | tf_op jit(solution)/shard_map/pallas_call | solution.py:571
  21.1 0.3 collective-permute-start.6
  21.5 1.7 %collective-permute-start.7 = (f32[3,192]{1,0:T(4,128)S(1)}, f32[3,192]{1,0:T(4,128)S(1)}, u32[]{:S(2)}, u32[]{:S(2)}) collective-permute-start(f32[3,192]{1,0:T(4,128)S(1)} %get-tuple-element.45), channel_id=1, source_target_pairs={{0,2},{1,3},{2,0},{3,1},{4,6},{5,7},{6,4},{7,5},{8,10},{9,11},{10,... | collective-permute-start | bytes 6920 | tf_op jit(solution)/shard_map/ppermute | solution.py:640
  23.2 0.0 collective-permute-start.8
  23.2 0.0 collective-permute-done.6
  23.2 1.9 %collective-permute-done.7 = f32[3,192]{1,0:T(4,128)S(1)} collective-permute-done((f32[3,192]{1,0:T(4,128)S(1)}, f32[3,192]{1,0:T(4,128)S(1)}, u32[]{:S(2)}, u32[]{:S(2)}) %collective-permute-start.7) | collective-permute-done | bytes 2336 | tf_op jit(solution)/shard_map/ppermute | solution.py:640
  25.1 1.1 %collective-permute-done.8 = f32[3,192]{1,0:T(4,128)S(1)} collective-permute-done((f32[3,192]{1,0:T(4,128)S(1)}, f32[3,192]{1,0:T(4,128)S(1)}, u32[]{:S(2)}, u32[]{:S(2)}) %collective-permute-start.8) | collective-permute-done | bytes 2336 | tf_op jit(solution)/shard_map/ppermute | solution.py:640
  26.2 1.8 %collective-permute-start.10 = (f32[3,192]{1,0:T(4,128)S(1)}, f32[3,192]{1,0:T(4,128)S(1)}, u32[]{:S(2)}, u32[]{:S(2)}) collective-permute-start(f32[3,192]{1,0:T(4,128)S(1)} %fusion), channel_id=1, source_target_pairs={{0,8},{4,12},{8,0},{12,4},{1,9},{5,13},{9,1},{13,5},{2,10},{6,14},... | collective-permute-start | bytes 6920 | tf_op jit(solution)/shard_map/ppermute | solution.py:640
  28.0 1.9 %collective-permute-start.11 = (f32[3,192]{1,0:T(4,128)S(1)}, f32[3,192]{1,0:T(4,128)S(1)}, u32[]{:S(2)}, u32[]{:S(2)}) collective-permute-start(f32[3,192]{1,0:T(4,128)S(1)} %fusion), channel_id=1, source_target_pairs={{0,12},{4,8},{8,4},{12,0},{1,13},{5,9},{9,5},{13,1},{2,14},{6,10},... | collective-permute-start | bytes 6920 | tf_op jit(solution)/shard_map/ppermute | solution.py:640
  29.9 0.5 %collective-permute-start.9 = (f32[3,192]{1,0:T(4,128)S(1)}, f32[3,192]{1,0:T(4,128)S(1)}, u32[]{:S(2)}, u32[]{:S(2)}) collective-permute-start(f32[3,192]{1,0:T(4,128)S(1)} %fusion), channel_id=1, source_target_pairs={{0,4},{4,0},{8,12},{12,8},{1,5},{5,1},{9,13},{13,9},{2,6},{6,2},{1... | collective-permute-start | bytes 6920 | tf_op jit(solution)/shard_map/ppermute | solution.py:640
  30.4 0.0 copy-done.1
  30.4 2.1 %shard_map.118 = bf16[16,512,128]{2,1,0:T(8,128)(2,1)} custom-call(s32[4,16]{1,0:T(4,128)S(1)} %bitcast.18, bf16[16,4,128,128]{3,2,1,0:T(8,128)(2,1)S(1)} %get-tuple-element.42.product), custom_call_target="tpu_custom_call" | custom-call | bytes 4194304 | tf_op jit(solution)/shard_map/pallas_call | solution.py:611
  32.4 0.0 collective-permute-done.10
  32.4 0.9 %collective-permute-done.11 = f32[3,192]{1,0:T(4,128)S(1)} collective-permute-done((f32[3,192]{1,0:T(4,128)S(1)}, f32[3,192]{1,0:T(4,128)S(1)}, u32[]{:S(2)}, u32[]{:S(2)}) %collective-permute-start.11) | collective-permute-done | bytes 2336 | tf_op jit(solution)/shard_map/ppermute | solution.py:640
  33.4 0.1 collective-permute-done.9
  33.5 0.6 %add_add_fusion = f32[3,192]{1,0:T(4,128)} fusion(f32[3,192]{1,0:T(4,128)S(1)} %collective-permute-done.10, f32[3,192]{1,0:T(4,128)S(1)} %collective-permute-done.11, f32[3,192]{1,0:T(4,128)S(1)} %fusion, f32[3,192]{1,0:T(4,128)S(1)} %collective-permute-done.9), kind=kLoop, calls=%fused_computation.2 | loop fusion | flops 1728 | bytes 11520 | tf_op jit(solution)/shard_map/add | solution.py:636
  (2 shorter events, 0.0 us)
Async XLA Ops:
  2.4 13.9 %collective-permute-start = (bf16[5,64,128]{2,1,0:T(8,128)(2,1)S(1)}, bf16[5,64,128]{2,1,0:T(8,128)(2,1)S(1)}, u32[]{:S(2)}, u32[]{:S(2)}) collective-permute-start(bf16[5,64,128]{2,1,0:T(8,128)(2,1)S(1)} %get-tuple-element.23), channel_id=1, source_target_pairs={{0,4},{4,0},{8,12},{12,8},{1,5},{5,1},{9,13},{13,9},{2,6},{6,2},{1... | collective-permute-start | bytes 245768 | tf_op jit(solution)/shard_map/ppermute | solution.py:97
  5.5 10.9 %collective-permute-start.1 = (bf16[5,64,128]{2,1,0:T(8,128)(2,1)S(1)}, bf16[5,64,128]{2,1,0:T(8,128)(2,1)S(1)}, u32[]{:S(2)}, u32[]{:S(2)}) collective-permute-start(bf16[5,64,128]{2,1,0:T(8,128)(2,1)S(1)} %get-tuple-element.24), channel_id=1, source_target_pairs={{0,8},{4,12},{8,0},{12,4},{1,9},{5,13},{9,1},{13,5},{2,10},{6,14},... | collective-permute-start | bytes 245768 | tf_op jit(solution)/shard_map/ppermute | solution.py:97
  8.1 8.3 %collective-permute-start.2 = (bf16[5,64,128]{2,1,0:T(8,128)(2,1)S(1)}, bf16[5,64,128]{2,1,0:T(8,128)(2,1)S(1)}, u32[]{:S(2)}, u32[]{:S(2)}) collective-permute-start(bf16[5,64,128]{2,1,0:T(8,128)(2,1)S(1)} %get-tuple-element.25), channel_id=1, source_target_pairs={{0,12},{4,8},{8,4},{12,0},{1,13},{5,9},{9,5},{13,1},{2,14},{6,10},... | collective-permute-start | bytes 245768 | tf_op jit(solution)/shard_map/ppermute | solution.py:97
  13.7 3.3 %copy-start = (s32[4,4]{1,0:T(4,128)S(1)}, s32[4,4]{1,0:T(4,128)}, u32[]{:S(2)}) copy-start(s32[4,4]{1,0:T(4,128)} %region.5) | copy-start | bytes 196
  13.7 3.3 %copy-start.2 = (s32[7680]{0:T(1024)S(1)}, s32[7680]{0:T(1024)}, u32[]{:S(2)}) copy-start(s32[7680]{0:T(1024)} %param.18) | copy-start | bytes 92164
  13.7 3.3 %copy-start.3 = (f32[3,16,128]{2,1,0:T(8,128)S(1)}, f32[3,16,128]{2,1,0:T(8,128)}, u32[]{:S(2)}) copy-start(f32[3,16,128]{2,1,0:T(8,128)} %weight_grad.1) | copy-start | bytes 73732
  13.7 3.3 %copy-start.4 = (s32[16]{0:T(128)S(1)}, s32[16]{0:T(128)}, u32[]{:S(2)}) copy-start(s32[16]{0:T(128)} %param.19) | copy-start | bytes 196
  16.4 1.6 %collective-permute-start.3 = (bf16[5,64,128]{2,1,0:T(8,128)(2,1)S(1)}, bf16[5,64,128]{2,1,0:T(8,128)(2,1)S(1)}, u32[]{:S(2)}, u32[]{:S(2)}) collective-permute-start(bf16[5,64,128]{2,1,0:T(8,128)(2,1)S(1)} %collective-permute-done.rest_1_), channel_id=1, source_target_pairs={{0,1},{1,0},{2,3},{3,2},{4,5},{5,4},{6,7},{7,6},{8,9},{9,8},{10,11... | collective-permute-start | bytes 245768 | tf_op jit(solution)/shard_map/ppermute | solution.py:629
  16.5 1.6 %collective-permute-start.4 = (bf16[5,64,128]{2,1,0:T(8,128)(2,1)S(1)}, bf16[5,64,128]{2,1,0:T(8,128)(2,1)S(1)}, u32[]{:S(2)}, u32[]{:S(2)}) collective-permute-start(bf16[5,64,128]{2,1,0:T(8,128)(2,1)S(1)} %collective-permute-done.1.rest_2_), channel_id=1, source_target_pairs={{0,1},{1,0},{2,3},{3,2},{4,5},{5,4},{6,7},{7,6},{8,9},{9,8},{10,11... | collective-permute-start | bytes 245768 | tf_op jit(solution)/shard_map/ppermute | solution.py:629
  17.0 1.3 %collective-permute-start.5 = (bf16[5,64,128]{2,1,0:T(8,128)(2,1)S(1)}, bf16[5,64,128]{2,1,0:T(8,128)(2,1)S(1)}, u32[]{:S(2)}, u32[]{:S(2)}) collective-permute-start(bf16[5,64,128]{2,1,0:T(8,128)(2,1)S(1)} %collective-permute-done.2.rest_3_), channel_id=1, source_target_pairs={{0,1},{1,0},{2,3},{3,2},{4,5},{5,4},{6,7},{7,6},{8,9},{9,8},{10,11... | collective-permute-start | bytes 245768 | tf_op jit(solution)/shard_map/ppermute | solution.py:629
  18.2 12.1 %copy-start.1 = (s32[16,4]{0,1:T(4,128)S(1)}, s32[16,4]{0,1:T(4,128)}, u32[]{:S(2)}) copy-start(s32[16,4]{0,1:T(4,128)} %param.17) | copy-start | bytes 772
  21.1 2.0 %collective-permute-start.6 = (f32[3,192]{1,0:T(4,128)S(1)}, f32[3,192]{1,0:T(4,128)S(1)}, u32[]{:S(2)}, u32[]{:S(2)}) collective-permute-start(f32[3,192]{1,0:T(4,128)S(1)} %get-tuple-element.46), channel_id=1, source_target_pairs={{0,1},{1,0},{2,3},{3,2},{4,5},{5,4},{6,7},{7,6},{8,9},{9,8},{10,11... | collective-permute-start | bytes 6920 | tf_op jit(solution)/shard_map/ppermute | solution.py:640
  21.5 3.6 %collective-permute-start.7 = (f32[3,192]{1,0:T(4,128)S(1)}, f32[3,192]{1,0:T(4,128)S(1)}, u32[]{:S(2)}, u32[]{:S(2)}) collective-permute-start(f32[3,192]{1,0:T(4,128)S(1)} %get-tuple-element.45), channel_id=1, source_target_pairs={{0,2},{1,3},{2,0},{3,1},{4,6},{5,7},{6,4},{7,5},{8,10},{9,11},{10,... | collective-permute-start | bytes 6920 | tf_op jit(solution)/shard_map/ppermute | solution.py:640
  23.2 3.0 %collective-permute-start.8 = (f32[3,192]{1,0:T(4,128)S(1)}, f32[3,192]{1,0:T(4,128)S(1)}, u32[]{:S(2)}, u32[]{:S(2)}) collective-permute-start(f32[3,192]{1,0:T(4,128)S(1)} %get-tuple-element.44), channel_id=1, source_target_pairs={{0,3},{1,2},{2,1},{3,0},{4,7},{5,6},{6,5},{7,4},{8,11},{9,10},{10,... | collective-permute-start | bytes 6920 | tf_op jit(solution)/shard_map/ppermute | solution.py:640
  26.2 6.2 %collective-permute-start.10 = (f32[3,192]{1,0:T(4,128)S(1)}, f32[3,192]{1,0:T(4,128)S(1)}, u32[]{:S(2)}, u32[]{:S(2)}) collective-permute-start(f32[3,192]{1,0:T(4,128)S(1)} %fusion), channel_id=1, source_target_pairs={{0,8},{4,12},{8,0},{12,4},{1,9},{5,13},{9,1},{13,5},{2,10},{6,14},... | collective-permute-start | bytes 6920 | tf_op jit(solution)/shard_map/ppermute | solution.py:640
  28.0 5.4 %collective-permute-start.11 = (f32[3,192]{1,0:T(4,128)S(1)}, f32[3,192]{1,0:T(4,128)S(1)}, u32[]{:S(2)}, u32[]{:S(2)}) collective-permute-start(f32[3,192]{1,0:T(4,128)S(1)} %fusion), channel_id=1, source_target_pairs={{0,12},{4,8},{8,4},{12,0},{1,13},{5,9},{9,5},{13,1},{2,14},{6,10},... | collective-permute-start | bytes 6920 | tf_op jit(solution)/shard_map/ppermute | solution.py:640
  29.9 3.6 %collective-permute-start.9 = (f32[3,192]{1,0:T(4,128)S(1)}, f32[3,192]{1,0:T(4,128)S(1)}, u32[]{:S(2)}, u32[]{:S(2)}) collective-permute-start(f32[3,192]{1,0:T(4,128)S(1)} %fusion), channel_id=1, source_target_pairs={{0,4},{4,0},{8,12},{12,8},{1,5},{5,1},{9,13},{13,9},{2,6},{6,2},{1... | collective-permute-start | bytes 6920 | tf_op jit(solution)/shard_map/ppermute | solution.py:640

commit v13 on v12

--- a/solution.py
+++ b/solution.py
@@ -9,7 +9,6 @@
 from jax.sharding import PartitionSpec as P
 
 TRAVEL = 5
-SHARE = 2
 PARTS = 3
 F32 = jnp.float32
 BF16 = jnp.bfloat16
@@ -36,16 +35,25 @@
     return jnp.where(jnp.logical_and(slot == 0, count == 2), 1, 4)
 
 
-def send_kernel(region, density, *rest, share):
-    *outs, sems = rest
+def partners(slabs):
+    shifts = list(reversed(range(1, slabs)))
+    pairs = [(shifts[i], shifts[i + 1]) for i in range(0, slabs - 2, 2)]
+    return pairs + [(shifts[-1],) * 2]
+
+
+def send_kernel(region_hbm, density, *rest):
+    *outs, region, sems, region_sem = rest
+    fetch = pltpu.make_async_copy(region_hbm, region, region_sem)
+    fetch.start()
+    fetch.wait()
     me = lax.axis_index("grid")
-    part = lax.rem(lax.axis_index("atoms"), share)
-    size = region.shape[1]
+    core = lax.rem(lax.axis_index("atoms"), 2)
+    slabs, size = region.shape
     owner_rows = density.shape[0]
     rows = density.shape[-2]
     copies = []
-    for shift, out in zip((0, *reversed(range(1, len(outs)))), outs):
-        slab = jnp.bitwise_xor(me, shift)
+    for number, ((low, high), out) in enumerate(zip([(0, 0)] + partners(slabs), outs)):
+        slab = jnp.bitwise_xor(me, jnp.where(core == 0, low, high))
         base = jnp.int32(owner_rows)
         count = jnp.int32(0)
         for position in range(size):
@@ -58,15 +66,15 @@
         lower = base == 0
         edge = jnp.where(jnp.logical_and(count == 2, jnp.logical_not(lower)), after, base)
         kept = out.shape[1]
-        first = 0 if kept == rows else pl.multiple_of(part * kept, kept)
+        first = 0 if kept == rows else pl.multiple_of(core * kept, kept)
         here = pl.ds(first, kept)
         pairs = (
             (density.at[base, pl.ds(1, 2), here, :], out.at[pl.ds(0, 2)]),
             (density.at[after, pl.ds(0, 2), here, :], out.at[pl.ds(2, 2)]),
             (density.at[edge, jnp.where(lower, 0, 2), here, :], out.at[4]),
         )
-        for number, (source, target) in enumerate(pairs):
-            copies.append(pltpu.make_async_copy(source, target, sems.at[shift, number]))
+        for part, (source, target) in enumerate(pairs):
+            copies.append(pltpu.make_async_copy(source, target, sems.at[number, part]))
     for copy in copies:
         copy.start()
     for copy in copies:
@@ -77,35 +85,51 @@
     return pltpu.with_memory_space_constraint(array, pltpu.HBM)
 
 
-def rows_to_send(region, density, slabs, share):
+def rows_to_send(region, density, slabs):
     size = density.shape[-1]
-    kept = [size] + [size // share] * (slabs - 1)
-    return pl.pallas_call(
-        functools.partial(send_kernel, share=share),
+    exchanges = partners(slabs)
+    kept = [size] + [size if low != high else size // 2 for low, high in exchanges]
+    hbm = pl.BlockSpec(memory_space=pl.ANY)
+    return pl.pallas_call(
+        send_kernel,
         out_shape=[jax.ShapeDtypeStruct((TRAVEL, rows, size), density.dtype) for rows in kept],
-        in_specs=[pl.BlockSpec(memory_space=pltpu.SMEM), pl.BlockSpec(memory_space=pl.ANY)],
-        out_specs=[pl.BlockSpec(memory_space=pltpu.VMEM)] * slabs,
-        scratch_shapes=[pltpu.SemaphoreType.DMA((slabs, 3))],
+        in_specs=[hbm, hbm],
+        out_specs=[pl.BlockSpec(memory_space=pltpu.VMEM)] * len(kept),
+        scratch_shapes=[
+            pltpu.SMEM(region.shape, jnp.int32),
+            pltpu.SemaphoreType.DMA((len(kept), 3)),
+            pltpu.SemaphoreType.DMA,
+        ],
         compiler_params=pltpu.CompilerParams(vmem_limit_bytes=VMEM_LIMIT),
     )(in_hbm(region), in_hbm(density))
 
 
-def fetch_rows(region, density, slabs, share):
-    own, *outgoing = rows_to_send(region, density, slabs, share)
-    near = {}
-    for shift in reversed(range(1, slabs)):
-        near[shift] = lax.ppermute(outgoing[slabs - 1 - shift], "grid", [(i, i ^ shift) for i in range(slabs)])
-    return own, [near[shift] for shift in range(1, slabs)]
-
-
-def stage_rows(stage, own, near, far, share):
-    part = lax.rem(lax.axis_index("atoms"), share)
-    kept = near[0].shape[1]
+def fetch_rows(region, density, slabs, atom_devices):
+    own, *outgoing = rows_to_send(region, density, slabs)
+    near = []
+    for shifts, piece in zip(partners(slabs), outgoing):
+        moves = [
+            (z * atom_devices + a, (z ^ shifts[a % 2]) * atom_devices + a) for z in range(slabs) for a in range(atom_devices)
+        ]
+        near.append(lax.ppermute(piece, ("grid", "atoms"), moves))
+    return own, near
+
+
+def stage_rows(stage, own, near, far, slabs):
+    core = lax.rem(lax.axis_index("atoms"), 2)
     for place in range(TRAVEL):
         stage[place] = own[place]
-        for shift, (here, there) in enumerate(zip(near, far), 1):
-            stage[shift * TRAVEL + place, pl.ds(pl.multiple_of(part * kept, kept), kept), :] = here[place]
-            stage[shift * TRAVEL + place, pl.ds(pl.multiple_of((1 - part) * kept, kept), kept), :] = there[place]
+    for (low, high), here, there in zip(partners(slabs), near, far):
+        kept = here.shape[1]
+        mine = jnp.where(core == 0, low, high) * TRAVEL
+        other = jnp.where(core == 0, high, low) * TRAVEL
+        for place in range(TRAVEL):
+            if low != high:
+                stage[mine + place] = here[place]
+                stage[other + place] = there[place]
+            else:
+                stage[mine + place, pl.ds(pl.multiple_of(core * kept, kept), kept), :] = here[place]
+                stage[mine + place, pl.ds(pl.multiple_of((1 - core) * kept, kept), kept), :] = there[place]
 
 
 def block_major(x_ref, wide, points, blocks):
@@ -190,7 +214,7 @@
     @pl.when(batch == 0)
     def _():
         tiles[region_size * width] = jnp.zeros((size, size), BF16)
-        stage_rows(stage, pieces[0], pieces[1:slabs], pieces[slabs:], SHARE)
+        stage_rows(stage, pieces[0], pieces[1 : 1 + slabs // 2], pieces[1 + slabs // 2 :], slabs)
         for position in range(region_size):
             owner, slot, count = owner_and_slot(region, me, position, owner_rows)
             shift = jnp.bitwise_xor(me, owner)
@@ -495,7 +519,7 @@
     me = lax.axis_index("grid")
     me_atoms = lax.axis_index("atoms")
     half = (width - 1) // 2
-    stage_rows(stage, pieces[0], pieces[1:slabs], pieces[slabs:], SHARE)
+    stage_rows(stage, pieces[0], pieces[1 : 1 + slabs // 2], pieces[1 + slabs // 2 :], slabs)
     rows = [region[me, position] for position in range(blocks)]
     found = [owner_and_slot(region, me, position, owner_rows) for position in range(blocks)]
     totals = [[jnp.zeros((8, size), F32) for _ in range(blocks)] for _ in range(PARTS)]
@@ -566,7 +590,7 @@
     basis, field, moments, hot, grad_columns = prepared
     slabs, atom_devices, atom_total, points, blocks, width, owner_rows = shapes
     batches, _, _, size = basis.shape
-    step = 8 if batches % 8 == 0 else 1
+    step = 16 if batches % 16 == 0 else 1
     vmem = pl.BlockSpec(memory_space=pltpu.VMEM)
     return pl.pallas_call(
         functools.partial(combine_kernel, owner_rows=owner_rows, slabs=slabs, width=width, step=step),
@@ -668,7 +692,7 @@
     flat_basis = basis.reshape(batches, points * blocks, size)
     flat_field = exchange_field.reshape(batches, points * blocks, size)
     flat_grad = basis_grad.reshape(PARTS, batches, points * blocks, size)
-    own, near = fetch_rows(region, density, slabs, SHARE)
+    own, near = fetch_rows(region, density, slabs, atom_devices)
     if region.shape[1] == blocks:
         basis_wide, field_wide, turned, grads = reorder(
             pattern, flat_basis, flat_field, flat_grad, weights, points, blocks

time: 34.4 us -> 33.2 us (0.965)
  waiting for transfers between devices: 4.27 us -> 3.85 us
  starting transfers between devices: 12.5 us -> 12.1 us
    ppermute x3 -> x2, starting transfers between devices: 5.68 us -> 5.15 us  [fetch_rows(): near.append(lax.ppermute(piece, ('grid', 'atoms'), moves))]
  transfers between devices with their start and end apart: 12 -> 10, of which waited for: 5 -> 3; matrix products, arithmetic and copies ran while one was open for 0% -> 0% of each run, Pallas kernels for 33% -> 34%
where the time goes in v13:
time: 33.2 us; the launch traced here: 32.9 us
  Pallas kernels  15.6 us (47%)
  starting transfers between devices  12.1 us (36%)
  waiting for transfers between devices  3.85 us (12%)
  between operations  0.76 us (2%)
  other arithmetic  0.6 us (2%)
    ppermute x6, starting transfers between devices, exchange_all(): lax.ppermute(parts[d], axis, [(i, i ^ d) for i in range(count)])  6.38 us
    pallas_call x1, Pallas kernels, reorder(): pl.pallas_call(reorder_kernel, out_shape=(ordered, ordered, jax.ShapeDtyp...  5.59 us
    ppermute x2, starting transfers between devices, fetch_rows(): near.append(lax.ppermute(piece, ('grid', 'atoms'), moves))  5.15 us
    ppermute x6, waiting for transfers between devices, exchange_all(): lax.ppermute(parts[d], axis, [(i, i ^ d) for i in range(count)])  3.82 us
    pallas_call x1, Pallas kernels, build_moments(): pl.pallas_call(moment_kernel, out_shape=jax.ShapeDtypeStruct((PARTS, bloc...  2.59 us
    pallas_call x1, Pallas kernels, combine(): pl.pallas_call(functools.partial(combine_kernel, owner_rows=owner_rows, s...  2.59 us
    pallas_call x1, Pallas kernels, write(): pl.pallas_call(write_kernel, out_shape=jax.ShapeDtypeStruct(shape, BF16),...  2.06 us
    pallas_call x1, Pallas kernels, rows_to_send(): pl.pallas_call(send_kernel, out_shape=[jax.ShapeDtypeStruct((TRAVEL, rows...  1.77 us
  transfers between devices with their start and end apart: 10, of which 3 were waited for; matrix products, arithmetic and copies ran while one was open for 0% of the time, Pallas kernels for 34%

profile of v13, /device:TPU:0, one launch (start us, length us, event | category | flops | bytes accessed | tf_op | source)
XLA Modules:
  0.0 32.9 jit_solution(11420151432695442514)
XLA Ops:
  0.6 1.8 %shard_map.113 = (bf16[5,128,128]{2,1,0:T(8,128)(2,1)S(1)}, bf16[5,128,128]{2,1,0:T(8,128)(2,1)S(1)}, bf16[5,64,128]{2,1,0:T(8,128)(2,1)S(1)}) custom-call(s32[4,4]{1,0:T(4,128)} %region.3, bf16[15,3,128,128]{3,2,1,0:T(8,128)(2,1)} %density.1), custom_call_target="tpu_custom_call" | custom-call | tf_op jit(solution)/shard_map/pallas_call | solution.py:93
  2.4 5.1 %collective-permute-start = (bf16[5,128,128]{2,1,0:T(8,128)(2,1)S(1)}, bf16[5,128,128]{2,1,0:T(8,128)(2,1)S(1)}, u32[]{:S(2)}, u32[]{:S(2)}) collective-permute-start(bf16[5,128,128]{2,1,0:T(8,128)(2,1)S(1)} %get-tuple-element.21), channel_id=1, source_target_pairs={{0,12},{1,9},{2,14},{3,11},{4,8},{5,13},{6,10},{7,15},{8,4},{9,1},... | collective-permute-start | bytes 491528 | tf_op jit(solution)/shard_map/ppermute | solution.py:114
  7.6 0.0 collective-permute-start.1
  7.6 5.6 %shard_map.114 = (bf16[16,4,128,128]{3,2,1,0:T(8,128)(2,1)S(1)}, bf16[16,4,128,128]{3,2,1,0:T(8,128)(2,1)S(1)}, bf16[512,2048]{1,0:T(8,128)(2,1)S(1)}, bf16[3,4,2048,128]{3,2,1,0:T(8,128)(2,1)S(1)}) custom-call(s32[4,16]{1,0:T(4,128)} %bitcast.17, bf16[16,512,128]{2,1,0:T(8,128)(2,1)} %bitcast.22, bf16[16,512,128]{2,1,0:T(8,128)(2,1)} %bitcast.23, ...), custom_call_target="tpu_custom_call" | custom-call | bytes 10485760 | tf_op jit(solution)/shard_map/pallas_call | solution.py:426
  13.2 0.0 copy-start
  13.2 0.0 copy-start.2
  13.2 0.0 copy-start.3
  13.2 0.0 copy-start.4
  13.2 2.6 %shard_map.115.moments = f32[3,512,512]{2,1,0:T(8,128)S(1)} custom-call(bf16[512,2048]{1,0:T(8,128)(2,1)S(1)} %get-tuple-element.25.turned, bf16[3,4,2048,128]{3,2,1,0:T(8,128)(2,1)S(1)} %get-tuple-element.26.grads), custom_call_target="tpu_custom_call" | custom-call | flops 3221225472 | tf_op jit(solution)/shard_map/pallas_call | solution.py:467
  15.8 0.0 collective-permute-done.1.rest_2_
  15.8 0.0 collective-permute-done.rest_1_
  15.8 0.1 collective-permute-start.2
  15.9 0.5 %collective-permute-start.3 = (bf16[5,64,128]{2,1,0:T(8,128)(2,1)S(1)}, bf16[5,64,128]{2,1,0:T(8,128)(2,1)S(1)}, u32[]{:S(2)}, u32[]{:S(2)}) collective-permute-start(bf16[5,64,128]{2,1,0:T(8,128)(2,1)S(1)} %collective-permute-done.1.rest_2_), channel_id=1, source_target_pairs={{0,1},{1,0},{2,3},{3,2},{4,5},{5,4},{6,7},{7,6},{8,9},{9,8},{10,11... | collective-permute-start | bytes 245768 | tf_op jit(solution)/shard_map/ppermute | solution.py:653
  16.4 0.0 copy-done
  16.4 0.0 copy-done.2
  16.4 0.0 copy-done.3
  16.4 0.0 copy-done.4
  16.4 1.0 %shard_map.116 = (bf16[768,640]{1,0:T(8,128)(2,1)S(1)}, f32[3,128,128]{2,1,0:T(8,128)S(1)}) custom-call(s32[4,4]{1,0:T(4,128)S(1)} %copy-done, s32[60,128]{1,0:T(8,128)S(1)} %bitcast.19, s32[1,16]{1,0:T(1,128)S(1)} %bitcast.20, f32[3,16,128]{2,1,0:T(8,128)S(1)} %copy-done.3), custom_call_target="tpu_custom_call" | custom-call | flops 1000000000 | bytes 196608 | tf_op jit(solution)/shard_map/pallas_call | solution.py:501
  17.4 0.0 collective-permute-done.3.rest_4_
  17.4 0.0 collective-permute-done.2.rest_3_
  17.4 0.0 copy-start.1
  17.4 2.6 %shard_map.117 = (bf16[16,4,128,128]{3,2,1,0:T(8,128)(2,1)S(1)}, f32[4,3,192]{2,1,0:T(4,128)S(1)}) custom-call(s32[4,4]{1,0:T(4,128)S(1)} %copy-done, bf16[16,4,128,128]{3,2,1,0:T(8,128)(2,1)S(1)} %get-tuple-element.27.basis, bf16[16,4,128,128]{3,2,1,0:T(8,128)(2,1)S(1)} %get-tuple-element.28.field, f32[3,512,512]{2,1,0:T(8,128)S(1)} %shard_map.115.moments, ...), custom_call_target="tpu_custom_call" | custom-call | tf_op jit(solution)/shard_map/pallas_call | solution.py:595
  20.0 0.3 %collective-permute-start.4 = (f32[3,192]{1,0:T(4,128)S(1)}, f32[3,192]{1,0:T(4,128)S(1)}, u32[]{:S(2)}, u32[]{:S(2)}) collective-permute-start(f32[3,192]{1,0:T(4,128)S(1)} %get-tuple-element.42), channel_id=1, source_target_pairs={{0,1},{1,0},{2,3},{3,2},{4,5},{5,4},{6,7},{7,6},{8,9},{9,8},{10,11... | collective-permute-start | bytes 6920 | tf_op jit(solution)/shard_map/ppermute | solution.py:664
  20.4 1.5 %collective-permute-start.5 = (f32[3,192]{1,0:T(4,128)S(1)}, f32[3,192]{1,0:T(4,128)S(1)}, u32[]{:S(2)}, u32[]{:S(2)}) collective-permute-start(f32[3,192]{1,0:T(4,128)S(1)} %get-tuple-element.41), channel_id=1, source_target_pairs={{0,2},{1,3},{2,0},{3,1},{4,6},{5,7},{6,4},{7,5},{8,10},{9,11},{10,... | collective-permute-start | bytes 6920 | tf_op jit(solution)/shard_map/ppermute | solution.py:664
  21.9 0.1 collective-permute-start.6
  22.0 0.0 collective-permute-done.4
  22.0 2.0 %collective-permute-done.5 = f32[3,192]{1,0:T(4,128)S(1)} collective-permute-done((f32[3,192]{1,0:T(4,128)S(1)}, f32[3,192]{1,0:T(4,128)S(1)}, u32[]{:S(2)}, u32[]{:S(2)}) %collective-permute-start.5) | collective-permute-done | bytes 2336 | tf_op jit(solution)/shard_map/ppermute | solution.py:664
  24.0 0.9 %collective-permute-done.6 = f32[3,192]{1,0:T(4,128)S(1)} collective-permute-done((f32[3,192]{1,0:T(4,128)S(1)}, f32[3,192]{1,0:T(4,128)S(1)}, u32[]{:S(2)}, u32[]{:S(2)}) %collective-permute-start.6) | collective-permute-done | bytes 2336 | tf_op jit(solution)/shard_map/ppermute | solution.py:664
  24.9 2.0 %collective-permute-start.7 = (f32[3,192]{1,0:T(4,128)S(1)}, f32[3,192]{1,0:T(4,128)S(1)}, u32[]{:S(2)}, u32[]{:S(2)}) collective-permute-start(f32[3,192]{1,0:T(4,128)S(1)} %fusion), channel_id=1, source_target_pairs={{0,4},{4,0},{8,12},{12,8},{1,5},{5,1},{9,13},{13,9},{2,6},{6,2},{1... | collective-permute-start | bytes 6920 | tf_op jit(solution)/shard_map/ppermute | solution.py:664
  26.9 0.0 collective-permute-start.8
  26.9 2.4 %collective-permute-start.9 = (f32[3,192]{1,0:T(4,128)S(1)}, f32[3,192]{1,0:T(4,128)S(1)}, u32[]{:S(2)}, u32[]{:S(2)}) collective-permute-start(f32[3,192]{1,0:T(4,128)S(1)} %fusion), channel_id=1, source_target_pairs={{0,12},{4,8},{8,4},{12,0},{1,13},{5,9},{9,5},{13,1},{2,14},{6,10},... | collective-permute-start | bytes 6920 | tf_op jit(solution)/shard_map/ppermute | solution.py:664
  29.4 0.0 copy-done.1
  29.4 2.1 %shard_map.118 = bf16[16,512,128]{2,1,0:T(8,128)(2,1)} custom-call(s32[4,16]{1,0:T(4,128)S(1)} %bitcast.18, bf16[16,4,128,128]{3,2,1,0:T(8,128)(2,1)S(1)} %get-tuple-element.38.product), custom_call_target="tpu_custom_call" | custom-call | bytes 4194304 | tf_op jit(solution)/shard_map/pallas_call | solution.py:635
  31.4 0.0 collective-permute-done.7
  31.4 0.0 collective-permute-done.8
  31.4 0.9 %collective-permute-done.9 = f32[3,192]{1,0:T(4,128)S(1)} collective-permute-done((f32[3,192]{1,0:T(4,128)S(1)}, f32[3,192]{1,0:T(4,128)S(1)}, u32[]{:S(2)}, u32[]{:S(2)}) %collective-permute-start.9) | collective-permute-done | bytes 2336 | tf_op jit(solution)/shard_map/ppermute | solution.py:664
  32.3 0.6 %add_add_fusion = f32[3,192]{1,0:T(4,128)} fusion(f32[3,192]{1,0:T(4,128)S(1)} %collective-permute-done.8, f32[3,192]{1,0:T(4,128)S(1)} %collective-permute-done.9, f32[3,192]{1,0:T(4,128)S(1)} %fusion, f32[3,192]{1,0:T(4,128)S(1)} %collective-permute-done.7), kind=kLoop, calls=%fused_computation.2 | loop fusion | flops 1728 | bytes 11520 | tf_op jit(solution)/shard_map/add | solution.py:660
  (2 shorter events, 0.0 us)
Async XLA Ops:
  2.4 13.4 %collective-permute-start = (bf16[5,128,128]{2,1,0:T(8,128)(2,1)S(1)}, bf16[5,128,128]{2,1,0:T(8,128)(2,1)S(1)}, u32[]{:S(2)}, u32[]{:S(2)}) collective-permute-start(bf16[5,128,128]{2,1,0:T(8,128)(2,1)S(1)} %get-tuple-element.21), channel_id=1, source_target_pairs={{0,12},{1,9},{2,14},{3,11},{4,8},{5,13},{6,10},{7,15},{8,4},{9,1},... | collective-permute-start | bytes 491528 | tf_op jit(solution)/shard_map/ppermute | solution.py:114
  7.6 8.3 %collective-permute-start.1 = (bf16[5,64,128]{2,1,0:T(8,128)(2,1)S(1)}, bf16[5,64,128]{2,1,0:T(8,128)(2,1)S(1)}, u32[]{:S(2)}, u32[]{:S(2)}) collective-permute-start(bf16[5,64,128]{2,1,0:T(8,128)(2,1)S(1)} %get-tuple-element.22), channel_id=1, source_target_pairs={{0,4},{1,5},{2,6},{3,7},{4,0},{5,1},{6,2},{7,3},{8,12},{9,13},{10,... | collective-permute-start | bytes 245768 | tf_op jit(solution)/shard_map/ppermute | solution.py:114
  13.2 3.2 %copy-start = (s32[4,4]{1,0:T(4,128)S(1)}, s32[4,4]{1,0:T(4,128)}, u32[]{:S(2)}) copy-start(s32[4,4]{1,0:T(4,128)} %region.3) | copy-start | bytes 196
  13.2 3.2 %copy-start.2 = (s32[7680]{0:T(1024)S(1)}, s32[7680]{0:T(1024)}, u32[]{:S(2)}) copy-start(s32[7680]{0:T(1024)} %param.18) | copy-start | bytes 92164
  13.2 3.2 %copy-start.3 = (f32[3,16,128]{2,1,0:T(8,128)S(1)}, f32[3,16,128]{2,1,0:T(8,128)}, u32[]{:S(2)}) copy-start(f32[3,16,128]{2,1,0:T(8,128)} %weight_grad.1) | copy-start | bytes 73732
  13.2 3.2 %copy-start.4 = (s32[16]{0:T(128)S(1)}, s32[16]{0:T(128)}, u32[]{:S(2)}) copy-start(s32[16]{0:T(128)} %param.19) | copy-start | bytes 196
  15.8 1.6 %collective-permute-start.2 = (bf16[5,128,128]{2,1,0:T(8,128)(2,1)S(1)}, bf16[5,128,128]{2,1,0:T(8,128)(2,1)S(1)}, u32[]{:S(2)}, u32[]{:S(2)}) collective-permute-start(bf16[5,128,128]{2,1,0:T(8,128)(2,1)S(1)} %collective-permute-done.rest_1_), channel_id=1, source_target_pairs={{0,1},{1,0},{2,3},{3,2},{4,5},{5,4},{6,7},{7,6},{8,9},{9,8},{10,11... | collective-permute-start | bytes 491528 | tf_op jit(solution)/shard_map/ppermute | solution.py:653
  15.9 1.5 %collective-permute-start.3 = (bf16[5,64,128]{2,1,0:T(8,128)(2,1)S(1)}, bf16[5,64,128]{2,1,0:T(8,128)(2,1)S(1)}, u32[]{:S(2)}, u32[]{:S(2)}) collective-permute-start(bf16[5,64,128]{2,1,0:T(8,128)(2,1)S(1)} %collective-permute-done.1.rest_2_), channel_id=1, source_target_pairs={{0,1},{1,0},{2,3},{3,2},{4,5},{5,4},{6,7},{7,6},{8,9},{9,8},{10,11... | collective-permute-start | bytes 245768 | tf_op jit(solution)/shard_map/ppermute | solution.py:653
  17.4 11.9 %copy-start.1 = (s32[16,4]{0,1:T(4,128)S(1)}, s32[16,4]{0,1:T(4,128)}, u32[]{:S(2)}) copy-start(s32[16,4]{0,1:T(4,128)} %param.17) | copy-start | bytes 772
  20.0 1.9 %collective-permute-start.4 = (f32[3,192]{1,0:T(4,128)S(1)}, f32[3,192]{1,0:T(4,128)S(1)}, u32[]{:S(2)}, u32[]{:S(2)}) collective-permute-start(f32[3,192]{1,0:T(4,128)S(1)} %get-tuple-element.42), channel_id=1, source_target_pairs={{0,1},{1,0},{2,3},{3,2},{4,5},{5,4},{6,7},{7,6},{8,9},{9,8},{10,11... | collective-permute-start | bytes 6920 | tf_op jit(solution)/shard_map/ppermute | solution.py:664
  20.4 3.6 %collective-permute-start.5 = (f32[3,192]{1,0:T(4,128)S(1)}, f32[3,192]{1,0:T(4,128)S(1)}, u32[]{:S(2)}, u32[]{:S(2)}) collective-permute-start(f32[3,192]{1,0:T(4,128)S(1)} %get-tuple-element.41), channel_id=1, source_target_pairs={{0,2},{1,3},{2,0},{3,1},{4,6},{5,7},{6,4},{7,5},{8,10},{9,11},{10,... | collective-permute-start | bytes 6920 | tf_op jit(solution)/shard_map/ppermute | solution.py:664
  21.9 3.0 %collective-permute-start.6 = (f32[3,192]{1,0:T(4,128)S(1)}, f32[3,192]{1,0:T(4,128)S(1)}, u32[]{:S(2)}, u32[]{:S(2)}) collective-permute-start(f32[3,192]{1,0:T(4,128)S(1)} %get-tuple-element.40), channel_id=1, source_target_pairs={{0,3},{1,2},{2,1},{3,0},{4,7},{5,6},{6,5},{7,4},{8,11},{9,10},{10,... | collective-permute-start | bytes 6920 | tf_op jit(solution)/shard_map/ppermute | solution.py:664
  24.9 6.5 %collective-permute-start.7 = (f32[3,192]{1,0:T(4,128)S(1)}, f32[3,192]{1,0:T(4,128)S(1)}, u32[]{:S(2)}, u32[]{:S(2)}) collective-permute-start(f32[3,192]{1,0:T(4,128)S(1)} %fusion), channel_id=1, source_target_pairs={{0,4},{4,0},{8,12},{12,8},{1,5},{5,1},{9,13},{13,9},{2,6},{6,2},{1... | collective-permute-start | bytes 6920 | tf_op jit(solution)/shard_map/ppermute | solution.py:664
  26.9 4.5 %collective-permute-start.8 = (f32[3,192]{1,0:T(4,128)S(1)}, f32[3,192]{1,0:T(4,128)S(1)}, u32[]{:S(2)}, u32[]{:S(2)}) collective-permute-start(f32[3,192]{1,0:T(4,128)S(1)} %fusion), channel_id=1, source_target_pairs={{0,8},{4,12},{8,0},{12,4},{1,9},{5,13},{9,1},{13,5},{2,10},{6,14},... | collective-permute-start | bytes 6920 | tf_op jit(solution)/shard_map/ppermute | solution.py:664
  26.9 5.4 %collective-permute-start.9 = (f32[3,192]{1,0:T(4,128)S(1)}, f32[3,192]{1,0:T(4,128)S(1)}, u32[]{:S(2)}, u32[]{:S(2)}) collective-permute-start(f32[3,192]{1,0:T(4,128)S(1)} %fusion), channel_id=1, source_target_pairs={{0,12},{4,8},{8,4},{12,0},{1,13},{5,9},{9,5},{13,1},{2,14},{6,10},... | collective-permute-start | bytes 6920 | tf_op jit(solution)/shard_map/ppermute | solution.py:664

commit v14 on v13

--- a/solution.py
+++ b/solution.py
@@ -9,6 +9,7 @@
 from jax.sharding import PartitionSpec as P
 
 TRAVEL = 5
+AHEAD = 2
 PARTS = 3
 F32 = jnp.float32
 BF16 = jnp.bfloat16
@@ -36,15 +37,21 @@
 
 
 def partners(slabs):
-    shifts = list(reversed(range(1, slabs)))
-    pairs = [(shifts[i], shifts[i + 1]) for i in range(0, slabs - 2, 2)]
-    return pairs + [(shifts[-1],) * 2]
-
-
-def send_kernel(region_hbm, density, *rest):
-    *outs, region, sems, region_sem = rest
-    fetch = pltpu.make_async_copy(region_hbm, region, region_sem)
+    return [(1, 1)] + [(shift + 1, shift) for shift in range(2, slabs, 2)]
+
+
+def send_kernel(region_hbm, density, pattern, weights, basis, field, basis_grad, *rest):
+    *outs, first_pattern, first_weights, first_basis, first_field, first_grad, region, sems, other_sems = rest
+    ahead = first_basis.shape[0]
+    fetch = pltpu.make_async_copy(region_hbm, region, other_sems.at[0])
     fetch.start()
+    others = (
+        pltpu.make_async_copy(pattern, first_pattern, other_sems.at[1]),
+        pltpu.make_async_copy(weights, first_weights, other_sems.at[2]),
+        pltpu.make_async_copy(field.at[pl.ds(0, ahead)], first_field, other_sems.at[3]),
+        pltpu.make_async_copy(basis.at[pl.ds(0, ahead)], first_basis, other_sems.at[4]),
+        pltpu.make_async_copy(basis_grad.at[:, pl.ds(0, ahead)], first_grad, other_sems.at[5]),
+    )
     fetch.wait()
     me = lax.axis_index("grid")
     core = lax.rem(lax.axis_index("atoms"), 2)
@@ -75,9 +82,9 @@
         )
         for part, (source, target) in enumerate(pairs):
             copies.append(pltpu.make_async_copy(source, target, sems.at[number, part]))
-    for copy in copies:
+    for copy in (*copies, *others):
         copy.start()
-    for copy in copies:
+    for copy in (*copies, *others):
         copy.wait()
 
 
@@ -85,34 +92,43 @@
     return pltpu.with_memory_space_constraint(array, pltpu.HBM)
 
 
-def rows_to_send(region, density, slabs):
+def rows_to_send(region, density, pattern, weights, basis, field, basis_grad, slabs):
     size = density.shape[-1]
     exchanges = partners(slabs)
     kept = [size] + [size if low != high else size // 2 for low, high in exchanges]
-    hbm = pl.BlockSpec(memory_space=pl.ANY)
+    ahead = jax.ShapeDtypeStruct((AHEAD, *basis.shape[1:]), BF16)
+    operands = (region, density, pattern.T, weights, basis, field, basis_grad)
     return pl.pallas_call(
         send_kernel,
-        out_shape=[jax.ShapeDtypeStruct((TRAVEL, rows, size), density.dtype) for rows in kept],
-        in_specs=[hbm, hbm],
-        out_specs=[pl.BlockSpec(memory_space=pltpu.VMEM)] * len(kept),
+        out_shape=[
+            *(jax.ShapeDtypeStruct((TRAVEL, rows, size), density.dtype) for rows in kept),
+            jax.ShapeDtypeStruct(pattern.T.shape, jnp.int32),
+            jax.ShapeDtypeStruct(weights.shape, F32),
+            ahead,
+            ahead,
+            jax.ShapeDtypeStruct((PARTS, AHEAD, *basis.shape[1:]), BF16),
+        ],
+        in_specs=[pl.BlockSpec(memory_space=pl.ANY)] * len(operands),
+        out_specs=[pl.BlockSpec(memory_space=pltpu.VMEM)] * (len(kept) + 5),
         scratch_shapes=[
             pltpu.SMEM(region.shape, jnp.int32),
             pltpu.SemaphoreType.DMA((len(kept), 3)),
-            pltpu.SemaphoreType.DMA,
+            pltpu.SemaphoreType.DMA((6,)),
         ],
         compiler_params=pltpu.CompilerParams(vmem_limit_bytes=VMEM_LIMIT),
-    )(in_hbm(region), in_hbm(density))
-
-
-def fetch_rows(region, density, slabs, atom_devices):
-    own, *outgoing = rows_to_send(region, density, slabs)
+    )(*(in_hbm(operand) for operand in operands))
+
+
+def fetch_rows(region, density, pattern, weights, basis, field, basis_grad, slabs, atom_devices):
+    own, *rest = rows_to_send(region, density, pattern, weights, basis, field, basis_grad, slabs)
+    outgoing, first = rest[: slabs // 2], rest[slabs // 2 :]
     near = []
     for shifts, piece in zip(partners(slabs), outgoing):
         moves = [
             (z * atom_devices + a, (z ^ shifts[a % 2]) * atom_devices + a) for z in range(slabs) for a in range(atom_devices)
         ]
         near.append(lax.ppermute(piece, ("grid", "atoms"), moves))
-    return own, near
+    return own, near, first
 
 
 def stage_rows(stage, own, near, far, slabs):
@@ -354,23 +370,23 @@
 
 
 def reorder_kernel(
-    pattern_hbm,
     basis,
     field,
     basis_grad,
-    weights_hbm,
+    pattern,
+    weights,
+    first_basis,
+    first_field,
+    first_grad,
     basis_out,
     field_out,
     turned,
     grads,
-    pattern,
-    weights,
     basis_in,
     field_in,
     grad_in,
     wide,
     sems,
-    small_sems,
 ):
     batches, blocks, points, size = basis_out.shape
 
@@ -381,32 +397,19 @@
             pltpu.make_async_copy(basis_grad.at[:, batch], grad_in.at[:, batch], sems.at[batch, 2]),
         )
 
-    small = (
-        pltpu.make_async_copy(pattern_hbm, pattern, small_sems.at[0]),
-        pltpu.make_async_copy(weights_hbm, weights, small_sems.at[1]),
-    )
-    for copy in small:
-        copy.start()
-
-    @pl.loop(0, batches)
+    @pl.loop(AHEAD, batches)
     def _(batch):
         for copy in copies(batch):
             copy.start()
 
-    for copy in small:
-        copy.wait()
-
-    @pl.loop(0, batches)
-    def _(batch):
-        for copy in copies(batch):
-            copy.wait()
+    def put_in_order(batch, field_here, basis_here, grads_here):
         points_here = pl.ds(pl.multiple_of(batch * points, points), points)
         places = [pattern[s, batch] for s in range(blocks)]
         weight = weights[pl.ds(batch, 1), :]
-        wide[0] = field_in[batch].astype(F32)
-        wide[1] = basis_in[batch].astype(F32)
+        wide[0] = field_here[...].astype(F32)
+        wide[1] = basis_here[...].astype(F32)
         for c in range(PARTS):
-            wide[2 + c] = grad_in[c, batch].astype(F32)
+            wide[2 + c] = grads_here[c].astype(F32)
         for s, place in enumerate(places):
             strided = pl.ds(s, points, stride=blocks)
             values = wide[0, strided, :].astype(BF16)
@@ -417,8 +420,18 @@
             for c in range(PARTS):
                 grads[c, place, points_here, :] = wide[2 + c, strided, :].astype(BF16)
 
-
-def reorder(pattern, basis, field, basis_grad, weights, points, blocks):
+    @pl.loop(0, AHEAD)
+    def _(batch):
+        put_in_order(batch, first_field.at[batch], first_basis.at[batch], first_grad.at[:, batch])
+
+    @pl.loop(AHEAD, batches)
+    def _(batch):
+        for copy in copies(batch):
+            copy.wait()
+        put_in_order(batch, field_in.at[batch], basis_in.at[batch], grad_in.at[:, batch])
+
+
+def reorder(basis, field, basis_grad, first, points, blocks):
     batches, rows, size = basis.shape
     hbm = pl.BlockSpec(memory_space=pl.ANY)
     vmem = pl.BlockSpec(memory_space=pltpu.VMEM)
@@ -431,23 +444,20 @@
             jax.ShapeDtypeStruct((blocks * size, batches * points), BF16),
             jax.ShapeDtypeStruct((PARTS, blocks, batches * points, size), BF16),
         ),
-        in_specs=[hbm] * 5,
+        in_specs=[hbm] * 3 + [pl.BlockSpec(memory_space=pltpu.SMEM)] + [vmem] * 4,
         out_specs=(vmem,) * 4,
         scratch_shapes=[
-            pltpu.SMEM((blocks, batches), jnp.int32),
-            pltpu.VMEM(weights.shape, F32),
             pltpu.VMEM((batches, rows, size), BF16),
             pltpu.VMEM((batches, rows, size), BF16),
             pltpu.VMEM((PARTS, batches, rows, size), BF16),
             pltpu.VMEM((2 + PARTS, rows, size), F32),
             pltpu.SemaphoreType.DMA((batches, 3)),
-            pltpu.SemaphoreType.DMA((2,)),
         ],
         compiler_params=pltpu.CompilerParams(vmem_limit_bytes=VMEM_LIMIT),
         cost_estimate=pl.CostEstimate(
             flops=0, bytes_accessed=2 * (2 + PARTS) * batches * rows * size, transcendentals=0
         ),
-    )(in_hbm(pattern.T), in_hbm(basis), in_hbm(field), in_hbm(basis_grad), in_hbm(weights))
+    )(in_hbm(basis), in_hbm(field), in_hbm(basis_grad), *first)
 
 
 def moment_kernel(turned, grads, moments):
@@ -537,10 +547,9 @@
                 jnp.where(k == 1, travel_place(slot, count, 1), travel_place(slot, count, 2)),
             )
             inside = jnp.logical_and(k >= 0, k < width)
-            tile = stage[first + place].astype(F32)
-            tile = jnp.where(inside, tile, 0.0)
-            matrix[p * size : (p + 1) * size, q * size : (q + 1) * size] = tile.astype(BF16)
-            turned = tile.T
+            tile = jnp.where(inside, stage[first + place], jnp.zeros((size, size), BF16))
+            matrix[p * size : (p + 1) * size, q * size : (q + 1) * size] = tile
+            turned = tile.T.astype(F32)
             for c in range(PARTS):
                 terms = turned * moments[c, q * size : (q + 1) * size, p * size : (p + 1) * size]
                 totals[c][p] = totals[c][p] + jnp.sum(terms.reshape(-1, 8, size), axis=0)
@@ -661,8 +670,8 @@
 
 
 def exchange_all(parts, axis, count):
-    moved = {d: lax.ppermute(parts[d], axis, [(i, i ^ d) for i in range(count)]) for d in range(1, count)}
-    return [parts[0]] + [moved[d] for d in range(1, count)]
+    farthest_first = range(count - 1, 0, -1)
+    return [parts[0]] + [lax.ppermute(parts[d], axis, [(i, i ^ d) for i in range(count)]) for d in farthest_first]
 
 
 def sum_parts(partial_grad, product, slabs, atom_devices):
@@ -692,11 +701,11 @@
     flat_basis = basis.reshape(batches, points * blocks, size)
     flat_field = exchange_field.reshape(batches, points * blocks, size)
     flat_grad = basis_grad.reshape(PARTS, batches, points * blocks, size)
-    own, near = fetch_rows(region, density, slabs, atom_devices)
+    own, near, first = fetch_rows(
+        region, density, pattern, weights, flat_basis, flat_field, flat_grad, slabs, atom_devices
+    )
     if region.shape[1] == blocks:
-        basis_wide, field_wide, turned, grads = reorder(
-            pattern, flat_basis, flat_field, flat_grad, weights, points, blocks
-        )
+        basis_wide, field_wide, turned, grads = reorder(flat_basis, flat_field, flat_grad, first, points, blocks)
         ready = (basis_wide, field_wide, build_moments(turned, grads), batch_atom)
         near, far, (basis_wide, field_wide, moments, batch_atom) = swap_halves(near, ready, atom_devices)
         hot, grad_columns = atom_matrix(region, fn_atom, batch_atom, weight_grad, blocks, size, atom_total)

time: 33.2 us -> 34.1 us (1.027)
  Pallas kernels: 15.6 us -> 16.2 us
    pallas_call x1, Pallas kernels: 1.77 us -> 2.4 us  [rows_to_send(): pl.pallas_call(send_kernel, out_shape=[*(jax.ShapeDtypeStruct((TRAVEL, ro...]
    ppermute x2, starting transfers between devices: 5.15 us -> 5.56 us  [fetch_rows(): near.append(lax.ppermute(piece, ('grid', 'atoms'), moves))]
  transfers between devices with their start and end apart: 10 -> 10, of which waited for: 3 -> 3; matrix products, arithmetic and copies ran while one was open for 0% -> 0% of each run, Pallas kernels for 34% -> 33%
where the time goes in v14:
time: 34.1 us; the launch traced here: 33.9 us
  Pallas kernels  16.2 us (48%)
  starting transfers between devices  12.4 us (36%)
  waiting for transfers between devices  3.8 us (11%)
  between operations  0.77 us (2%)
  other arithmetic  0.6 us (2%)
    ppermute x6, starting transfers between devices, exchange_all(): lax.ppermute(parts[d], axis, [(i, i ^ d) for i in range(count)])  6.31 us
    pallas_call x1, Pallas kernels, reorder(): pl.pallas_call(reorder_kernel, out_shape=(ordered, ordered, jax.ShapeDtyp...  5.63 us
    ppermute x2, starting transfers between devices, fetch_rows(): near.append(lax.ppermute(piece, ('grid', 'atoms'), moves))  5.56 us
    ppermute x6, waiting for transfers between devices, exchange_all(): lax.ppermute(parts[d], axis, [(i, i ^ d) for i in range(count)])  3.77 us
    pallas_call x1, Pallas kernels, build_moments(): pl.pallas_call(moment_kernel, out_shape=jax.ShapeDtypeStruct((PARTS, bloc...  2.63 us
    pallas_call x1, Pallas kernels, combine(): pl.pallas_call(functools.partial(combine_kernel, owner_rows=owner_rows, s...  2.56 us
    pallas_call x1, Pallas kernels, rows_to_send(): pl.pallas_call(send_kernel, out_shape=[*(jax.ShapeDtypeStruct((TRAVEL, ro...  2.4 us
    pallas_call x1, Pallas kernels, write(): pl.pallas_call(write_kernel, out_shape=jax.ShapeDtypeStruct(shape, BF16),...  2.06 us
  transfers between devices with their start and end apart: 10, of which 3 were waited for; matrix products, arithmetic and copies ran while one was open for 0% of the time, Pallas kernels for 33%

profile of v14, /device:TPU:0, one launch (start us, length us, event | category | flops | bytes accessed | tf_op | source)
XLA Modules:
  0.0 33.9 jit_solution(3106816196871952918)
XLA Ops:
  0.6 2.4 %shard_map.113 = (bf16[5,128,128]{2,1,0:T(8,128)(2,1)S(1)}, bf16[5,64,128]{2,1,0:T(8,128)(2,1)S(1)}, bf16[5,128,128]{2,1,0:T(8,128)(2,1)S(1)}, s32[4,16]{1,0:T(4...) custom-call(s32[4,4]{1,0:T(4,128)} %region.3, ...), custom_call_target="tpu_custom_call" | custom-call | tf_op jit(solution)/shard_map/pallas_call | solution.py:101
  3.0 3.1 %collective-permute-start = (bf16[5,64,128]{2,1,0:T(8,128)(2,1)S(1)}, bf16[5,64,128]{2,1,0:T(8,128)(2,1)S(1)}, u32[]{:S(2)}, u32[]{:S(2)}) collective-permute-start(bf16[5,64,128]{2,1,0:T(8,128)(2,1)S(1)} %get-tuple-element.26), channel_id=1, source_target_pairs={{0,4},{1,5},{2,6},{3,7},{4,0},{5,1},{6,2},{7,3},{8,12},{9,13},{10,... | collective-permute-start | bytes 245768 | tf_op jit(solution)/shard_map/ppermute | solution.py:130
  6.1 2.5 %collective-permute-start.1 = (bf16[5,128,128]{2,1,0:T(8,128)(2,1)S(1)}, bf16[5,128,128]{2,1,0:T(8,128)(2,1)S(1)}, u32[]{:S(2)}, u32[]{:S(2)}) collective-permute-start(bf16[5,128,128]{2,1,0:T(8,128)(2,1)S(1)} %get-tuple-element.27), channel_id=1, source_target_pairs={{0,12},{1,9},{2,14},{3,11},{4,8},{5,13},{6,10},{7,15},{8,4},{9,1},... | collective-permute-start | bytes 491528 | tf_op jit(solution)/shard_map/ppermute | solution.py:130
  8.6 5.6 %shard_map.114 = (bf16[16,4,128,128]{3,2,1,0:T(8,128)(2,1)S(1)}, bf16[16,4,128,128]{3,2,1,0:T(8,128)(2,1)S(1)}, bf16[512,2048]{1,0:T(8,128)(2,1)S(1)}, bf16[3,4,2048,128]{3,2,1,0:T(8,128)(2,1)S(1)}) custom-call(bf16[16,512,128]{2,1,0:T(8,128)(2,1)} %bitcast.24, bf16[16,512,128]{2,1,0:T(8,128)(2,1)} %bitcast.26, bf16[3,16,512,128]{3,2,1,0:T(8,128)(2,1)} %bitcast.22, ...), custom_call_target="tpu_custom_call" | custom-call | bytes 10485760 | tf_op jit(solution)/shard_map/pallas_call | solution.py:439
  14.2 0.0 copy-start
  14.3 0.0 copy-start.2
  14.3 0.0 copy-start.3
  14.3 0.0 copy-start.4
  14.3 2.6 %shard_map.115.moments = f32[3,512,512]{2,1,0:T(8,128)S(1)} custom-call(bf16[512,2048]{1,0:T(8,128)(2,1)S(1)} %get-tuple-element.35.turned, bf16[3,4,2048,128]{3,2,1,0:T(8,128)(2,1)S(1)} %get-tuple-element.36.grads), custom_call_target="tpu_custom_call" | custom-call | flops 3221225472 | tf_op jit(solution)/shard_map/pallas_call | solution.py:477
  16.9 0.0 collective-permute-done.rest_1_
  16.9 0.0 collective-permute-done.1.rest_2_
  17.0 0.1 collective-permute-start.3
  17.0 0.5 %collective-permute-start.2 = (bf16[5,64,128]{2,1,0:T(8,128)(2,1)S(1)}, bf16[5,64,128]{2,1,0:T(8,128)(2,1)S(1)}, u32[]{:S(2)}, u32[]{:S(2)}) collective-permute-start(bf16[5,64,128]{2,1,0:T(8,128)(2,1)S(1)} %collective-permute-done.rest_1_), channel_id=1, source_target_pairs={{0,1},{1,0},{2,3},{3,2},{4,5},{5,4},{6,7},{7,6},{8,9},{9,8},{10,11... | collective-permute-start | bytes 245768 | tf_op jit(solution)/shard_map/ppermute | solution.py:662
  17.5 0.0 copy-done
  17.5 0.0 copy-done.2
  17.5 0.0 copy-done.3
  17.5 0.0 copy-done.4
  17.5 1.0 %shard_map.116 = (bf16[768,640]{1,0:T(8,128)(2,1)S(1)}, f32[3,128,128]{2,1,0:T(8,128)S(1)}) custom-call(s32[4,4]{1,0:T(4,128)S(1)} %copy-done, s32[60,128]{1,0:T(8,128)S(1)} %bitcast.19, s32[1,16]{1,0:T(1,128)S(1)} %bitcast.20, f32[3,16,128]{2,1,0:T(8,128)S(1)} %copy-done.3), custom_call_target="tpu_custom_call" | custom-call | flops 1000000000 | bytes 196608 | tf_op jit(solution)/shard_map/pallas_call | solution.py:511
  18.5 0.0 collective-permute-done.2.rest_3_
  18.5 0.0 collective-permute-done.3.rest_4_
  18.5 0.0 copy-start.1
  18.5 2.6 %shard_map.117 = (bf16[16,4,128,128]{3,2,1,0:T(8,128)(2,1)S(1)}, f32[4,3,192]{2,1,0:T(4,128)S(1)}) custom-call(s32[4,4]{1,0:T(4,128)S(1)} %copy-done, bf16[16,4,128,128]{3,2,1,0:T(8,128)(2,1)S(1)} %get-tuple-element.37.basis, bf16[16,4,128,128]{3,2,1,0:T(8,128)(2,1)S(1)} %get-tuple-element.38.field, f32[3,512,512]{2,1,0:T(8,128)S(1)} %shard_map.115.moments, ...), custom_call_target="tpu_custom_call" | custom-call | tf_op jit(solution)/shard_map/pallas_call | solution.py:604
  21.1 0.3 collective-permute-start.6
  21.5 1.5 %collective-permute-start.5 = (f32[3,192]{1,0:T(4,128)S(1)}, f32[3,192]{1,0:T(4,128)S(1)}, u32[]{:S(2)}, u32[]{:S(2)}) collective-permute-start(f32[3,192]{1,0:T(4,128)S(1)} %get-tuple-element.51), channel_id=1, source_target_pairs={{0,2},{1,3},{2,0},{3,1},{4,6},{5,7},{6,4},{7,5},{8,10},{9,11},{10,... | collective-permute-start | bytes 6920 | tf_op jit(solution)/shard_map/ppermute | solution.py:674
  22.9 0.1 collective-permute-start.4
  23.1 0.0 collective-permute-done.6
  23.1 2.0 %collective-permute-done.5 = f32[3,192]{1,0:T(4,128)S(1)} collective-permute-done((f32[3,192]{1,0:T(4,128)S(1)}, f32[3,192]{1,0:T(4,128)S(1)}, u32[]{:S(2)}, u32[]{:S(2)}) %collective-permute-start.5) | collective-permute-done | bytes 2336 | tf_op jit(solution)/shard_map/ppermute | solution.py:674
  25.1 0.9 %collective-permute-done.4 = f32[3,192]{1,0:T(4,128)S(1)} collective-permute-done((f32[3,192]{1,0:T(4,128)S(1)}, f32[3,192]{1,0:T(4,128)S(1)}, u32[]{:S(2)}, u32[]{:S(2)}) %collective-permute-start.4) | collective-permute-done | bytes 2336 | tf_op jit(solution)/shard_map/ppermute | solution.py:674
  26.0 0.7 %collective-permute-start.9 = (f32[3,192]{1,0:T(4,128)S(1)}, f32[3,192]{1,0:T(4,128)S(1)}, u32[]{:S(2)}, u32[]{:S(2)}) collective-permute-start(f32[3,192]{1,0:T(4,128)S(1)} %fusion), channel_id=1, source_target_pairs={{0,4},{4,0},{8,12},{12,8},{1,5},{5,1},{9,13},{13,9},{2,6},{6,2},{1... | collective-permute-start | bytes 6920 | tf_op jit(solution)/shard_map/ppermute | solution.py:674
  26.7 1.2 %collective-permute-start.8 = (f32[3,192]{1,0:T(4,128)S(1)}, f32[3,192]{1,0:T(4,128)S(1)}, u32[]{:S(2)}, u32[]{:S(2)}) collective-permute-start(f32[3,192]{1,0:T(4,128)S(1)} %fusion), channel_id=1, source_target_pairs={{0,8},{4,12},{8,0},{12,4},{1,9},{5,13},{9,1},{13,5},{2,10},{6,14},... | collective-permute-start | bytes 6920 | tf_op jit(solution)/shard_map/ppermute | solution.py:674
  27.9 2.5 %collective-permute-start.7 = (f32[3,192]{1,0:T(4,128)S(1)}, f32[3,192]{1,0:T(4,128)S(1)}, u32[]{:S(2)}, u32[]{:S(2)}) collective-permute-start(f32[3,192]{1,0:T(4,128)S(1)} %fusion), channel_id=1, source_target_pairs={{0,12},{4,8},{8,4},{12,0},{1,13},{5,9},{9,5},{13,1},{2,14},{6,10},... | collective-permute-start | bytes 6920 | tf_op jit(solution)/shard_map/ppermute | solution.py:674
  30.4 0.0 copy-done.1
  30.4 2.1 %shard_map.118 = bf16[16,512,128]{2,1,0:T(8,128)(2,1)} custom-call(s32[4,16]{1,0:T(4,128)S(1)} %bitcast.18, bf16[16,4,128,128]{3,2,1,0:T(8,128)(2,1)S(1)} %get-tuple-element.48.product), custom_call_target="tpu_custom_call" | custom-call | bytes 4194304 | tf_op jit(solution)/shard_map/pallas_call | solution.py:644
  32.4 0.0 collective-permute-done.9
  32.5 0.0 collective-permute-done.8
  32.5 0.8 %collective-permute-done.7 = f32[3,192]{1,0:T(4,128)S(1)} collective-permute-done((f32[3,192]{1,0:T(4,128)S(1)}, f32[3,192]{1,0:T(4,128)S(1)}, u32[]{:S(2)}, u32[]{:S(2)}) %collective-permute-start.7) | collective-permute-done | bytes 2336 | tf_op jit(solution)/shard_map/ppermute | solution.py:674
  33.3 0.6 %add_add_fusion = f32[3,192]{1,0:T(4,128)} fusion(f32[3,192]{1,0:T(4,128)S(1)} %collective-permute-done.8, f32[3,192]{1,0:T(4,128)S(1)} %collective-permute-done.9, f32[3,192]{1,0:T(4,128)S(1)} %fusion, f32[3,192]{1,0:T(4,128)S(1)} %collective-permute-done.7), kind=kLoop, calls=%fused_computation.2 | loop fusion | flops 1728 | bytes 11520 | tf_op jit(solution)/shard_map/add | solution.py:669
  (2 shorter events, 0.0 us)
Async XLA Ops:
  3.0 13.9 %collective-permute-start = (bf16[5,64,128]{2,1,0:T(8,128)(2,1)S(1)}, bf16[5,64,128]{2,1,0:T(8,128)(2,1)S(1)}, u32[]{:S(2)}, u32[]{:S(2)}) collective-permute-start(bf16[5,64,128]{2,1,0:T(8,128)(2,1)S(1)} %get-tuple-element.26), channel_id=1, source_target_pairs={{0,4},{1,5},{2,6},{3,7},{4,0},{5,1},{6,2},{7,3},{8,12},{9,13},{10,... | collective-permute-start | bytes 245768 | tf_op jit(solution)/shard_map/ppermute | solution.py:130
  6.1 10.8 %collective-permute-start.1 = (bf16[5,128,128]{2,1,0:T(8,128)(2,1)S(1)}, bf16[5,128,128]{2,1,0:T(8,128)(2,1)S(1)}, u32[]{:S(2)}, u32[]{:S(2)}) collective-permute-start(bf16[5,128,128]{2,1,0:T(8,128)(2,1)S(1)} %get-tuple-element.27), channel_id=1, source_target_pairs={{0,12},{1,9},{2,14},{3,11},{4,8},{5,13},{6,10},{7,15},{8,4},{9,1},... | collective-permute-start | bytes 491528 | tf_op jit(solution)/shard_map/ppermute | solution.py:130
  14.2 3.3 %copy-start = (s32[4,4]{1,0:T(4,128)S(1)}, s32[4,4]{1,0:T(4,128)}, u32[]{:S(2)}) copy-start(s32[4,4]{1,0:T(4,128)} %region.3) | copy-start | bytes 196
  14.3 3.3 %copy-start.2 = (s32[7680]{0:T(1024)S(1)}, s32[7680]{0:T(1024)}, u32[]{:S(2)}) copy-start(s32[7680]{0:T(1024)} %param.18) | copy-start | bytes 92164
  14.3 3.3 %copy-start.3 = (f32[3,16,128]{2,1,0:T(8,128)S(1)}, f32[3,16,128]{2,1,0:T(8,128)}, u32[]{:S(2)}) copy-start(f32[3,16,128]{2,1,0:T(8,128)} %weight_grad.1) | copy-start | bytes 73732
  14.3 3.3 %copy-start.4 = (s32[16]{0:T(128)S(1)}, s32[16]{0:T(128)}, u32[]{:S(2)}) copy-start(s32[16]{0:T(128)} %param.19) | copy-start | bytes 196
  17.0 1.6 %collective-permute-start.3 = (bf16[5,128,128]{2,1,0:T(8,128)(2,1)S(1)}, bf16[5,128,128]{2,1,0:T(8,128)(2,1)S(1)}, u32[]{:S(2)}, u32[]{:S(2)}) collective-permute-start(bf16[5,128,128]{2,1,0:T(8,128)(2,1)S(1)} %collective-permute-done.1.rest_2_), channel_id=1, source_target_pairs={{0,1},{1,0},{2,3},{3,2},{4,5},{5,4},{6,7},{7,6},{8,9},{9,8},{10,11... | collective-permute-start | bytes 491528 | tf_op jit(solution)/shard_map/ppermute | solution.py:662
  17.0 1.5 %collective-permute-start.2 = (bf16[5,64,128]{2,1,0:T(8,128)(2,1)S(1)}, bf16[5,64,128]{2,1,0:T(8,128)(2,1)S(1)}, u32[]{:S(2)}, u32[]{:S(2)}) collective-permute-start(bf16[5,64,128]{2,1,0:T(8,128)(2,1)S(1)} %collective-permute-done.rest_1_), channel_id=1, source_target_pairs={{0,1},{1,0},{2,3},{3,2},{4,5},{5,4},{6,7},{7,6},{8,9},{9,8},{10,11... | collective-permute-start | bytes 245768 | tf_op jit(solution)/shard_map/ppermute | solution.py:662
  18.5 11.8 %copy-start.1 = (s32[16,4]{0,1:T(4,128)S(1)}, s32[16,4]{0,1:T(4,128)}, u32[]{:S(2)}) copy-start(s32[16,4]{0,1:T(4,128)} %param.17) | copy-start | bytes 772
  21.1 1.9 %collective-permute-start.6 = (f32[3,192]{1,0:T(4,128)S(1)}, f32[3,192]{1,0:T(4,128)S(1)}, u32[]{:S(2)}, u32[]{:S(2)}) collective-permute-start(f32[3,192]{1,0:T(4,128)S(1)} %get-tuple-element.50), channel_id=1, source_target_pairs={{0,1},{1,0},{2,3},{3,2},{4,5},{5,4},{6,7},{7,6},{8,9},{9,8},{10,11... | collective-permute-start | bytes 6920 | tf_op jit(solution)/shard_map/ppermute | solution.py:674
  21.5 3.6 %collective-permute-start.5 = (f32[3,192]{1,0:T(4,128)S(1)}, f32[3,192]{1,0:T(4,128)S(1)}, u32[]{:S(2)}, u32[]{:S(2)}) collective-permute-start(f32[3,192]{1,0:T(4,128)S(1)} %get-tuple-element.51), channel_id=1, source_target_pairs={{0,2},{1,3},{2,0},{3,1},{4,6},{5,7},{6,4},{7,5},{8,10},{9,11},{10,... | collective-permute-start | bytes 6920 | tf_op jit(solution)/shard_map/ppermute | solution.py:674
  22.9 3.0 %collective-permute-start.4 = (f32[3,192]{1,0:T(4,128)S(1)}, f32[3,192]{1,0:T(4,128)S(1)}, u32[]{:S(2)}, u32[]{:S(2)}) collective-permute-start(f32[3,192]{1,0:T(4,128)S(1)} %get-tuple-element.52), channel_id=1, source_target_pairs={{0,3},{1,2},{2,1},{3,0},{4,7},{5,6},{6,5},{7,4},{8,11},{9,10},{10,... | collective-permute-start | bytes 6920 | tf_op jit(solution)/shard_map/ppermute | solution.py:674
  26.0 6.5 %collective-permute-start.9 = (f32[3,192]{1,0:T(4,128)S(1)}, f32[3,192]{1,0:T(4,128)S(1)}, u32[]{:S(2)}, u32[]{:S(2)}) collective-permute-start(f32[3,192]{1,0:T(4,128)S(1)} %fusion), channel_id=1, source_target_pairs={{0,4},{4,0},{8,12},{12,8},{1,5},{5,1},{9,13},{13,9},{2,6},{6,2},{1... | collective-permute-start | bytes 6920 | tf_op jit(solution)/shard_map/ppermute | solution.py:674
  26.7 5.8 %collective-permute-start.8 = (f32[3,192]{1,0:T(4,128)S(1)}, f32[3,192]{1,0:T(4,128)S(1)}, u32[]{:S(2)}, u32[]{:S(2)}) collective-permute-start(f32[3,192]{1,0:T(4,128)S(1)} %fusion), channel_id=1, source_target_pairs={{0,8},{4,12},{8,0},{12,4},{1,9},{5,13},{9,1},{13,5},{2,10},{6,14},... | collective-permute-start | bytes 6920 | tf_op jit(solution)/shard_map/ppermute | solution.py:674
  27.9 5.4 %collective-permute-start.7 = (f32[3,192]{1,0:T(4,128)S(1)}, f32[3,192]{1,0:T(4,128)S(1)}, u32[]{:S(2)}, u32[]{:S(2)}) collective-permute-start(f32[3,192]{1,0:T(4,128)S(1)} %fusion), channel_id=1, source_target_pairs={{0,12},{4,8},{8,4},{12,0},{1,13},{5,9},{9,5},{13,1},{2,14},{6,10},... | collective-permute-start | bytes 6920 | tf_op jit(solution)/shard_map/ppermute | solution.py:674

commit v15 on v13

--- a/solution.py
+++ b/solution.py
@@ -13,6 +13,7 @@
 F32 = jnp.float32
 BF16 = jnp.bfloat16
 NT = (((1,), (1,)), ((), ()))
+TN = (((0,), (0,)), ((), ()))
 VMEM_LIMIT = 32 * 1024 * 1024
 
 
@@ -36,9 +37,7 @@
 
 
 def partners(slabs):
-    shifts = list(reversed(range(1, slabs)))
-    pairs = [(shifts[i], shifts[i + 1]) for i in range(0, slabs - 2, 2)]
-    return pairs + [(shifts[-1],) * 2]
+    return [(1, 1)] + [(shift + 1, shift) for shift in range(2, slabs, 2)]
 
 
 def send_kernel(region_hbm, density, *rest):
@@ -361,10 +360,11 @@
     weights_hbm,
     basis_out,
     field_out,
-    turned,
+    weighted,
     grads,
     pattern,
     weights,
+    columns,
     basis_in,
     field_in,
     grad_in,
@@ -395,6 +395,9 @@
 
     for copy in small:
         copy.wait()
+    rows = jnp.concatenate([weights[...], jnp.zeros((size - batches, points), F32)], axis=0).T
+    for batch in range(batches):
+        columns[batch] = jnp.broadcast_to(rows[:, batch : batch + 1], (points, size))
 
     @pl.loop(0, batches)
     def _(batch):
@@ -402,17 +405,15 @@
             copy.wait()
         points_here = pl.ds(pl.multiple_of(batch * points, points), points)
         places = [pattern[s, batch] for s in range(blocks)]
-        weight = weights[pl.ds(batch, 1), :]
         wide[0] = field_in[batch].astype(F32)
         wide[1] = basis_in[batch].astype(F32)
         for c in range(PARTS):
             wide[2 + c] = grad_in[c, batch].astype(F32)
         for s, place in enumerate(places):
             strided = pl.ds(s, points, stride=blocks)
-            values = wide[0, strided, :].astype(BF16)
-            field_out[batch, place] = values
-            rows = pl.ds(pl.multiple_of(place * size, size), size)
-            turned[rows, points_here] = (values.T.astype(F32) * weight).astype(BF16)
+            values = wide[0, strided, :]
+            field_out[batch, place] = values.astype(BF16)
+            weighted[place, points_here, :] = (values * columns[batch]).astype(BF16)
             basis_out[batch, place] = wide[1, strided, :].astype(BF16)
             for c in range(PARTS):
                 grads[c, place, points_here, :] = wide[2 + c, strided, :].astype(BF16)
@@ -428,7 +429,7 @@
         out_shape=(
             ordered,
             ordered,
-            jax.ShapeDtypeStruct((blocks * size, batches * points), BF16),
+            jax.ShapeDtypeStruct((blocks, batches * points, size), BF16),
             jax.ShapeDtypeStruct((PARTS, blocks, batches * points, size), BF16),
         ),
         in_specs=[hbm] * 5,
@@ -436,6 +437,7 @@
         scratch_shapes=[
             pltpu.SMEM((blocks, batches), jnp.int32),
             pltpu.VMEM(weights.shape, F32),
+            pltpu.VMEM((batches, points, size), F32),
             pltpu.VMEM((batches, rows, size), BF16),
             pltpu.VMEM((batches, rows, size), BF16),
             pltpu.VMEM((PARTS, batches, rows, size), BF16),
@@ -450,18 +452,19 @@
     )(in_hbm(pattern.T), in_hbm(basis), in_hbm(field), in_hbm(basis_grad), in_hbm(weights))
 
 
-def moment_kernel(turned, grads, moments):
+def moment_kernel(weighted, grads, moments):
     blocks, _, size = grads.shape[1:]
-    for c in range(PARTS):
-        for p in range(0, blocks, 2):
-            rows = slice(max(p - 1, 0) * size, min(p + 3, blocks) * size)
+    for p in range(0, blocks, 2):
+        first, last = max(p - 1, 0), min(p + 3, blocks)
+        left = jnp.concatenate([weighted[place] for place in range(first, last)], axis=1)
+        for c in range(PARTS):
             right = jnp.concatenate([grads[c, p], grads[c, p + 1]], axis=1)
-            moments[c, rows, p * size : (p + 2) * size] = jnp.dot(
-                turned[rows, :], right, preferred_element_type=F32
+            moments[c, first * size : last * size, p * size : (p + 2) * size] = lax.dot_general(
+                left, right, TN, preferred_element_type=F32
             )
 
 
-def build_moments(turned, grads):
+def build_moments(weighted, grads):
     blocks, depth, size = grads.shape[1:]
     vmem = pl.BlockSpec(memory_space=pltpu.VMEM)
     return pl.pallas_call(
@@ -473,7 +476,7 @@
         cost_estimate=pl.CostEstimate(
             flops=2 * PARTS * depth * (blocks * size) ** 2, bytes_accessed=0, transcendentals=0
         ),
-    )(turned, grads)
+    )(weighted, grads)
 
 
 def atom_kernel(region, fn_atom, batch_atom, weight_grad, hot, grad_columns):
@@ -537,10 +540,9 @@
                 jnp.where(k == 1, travel_place(slot, count, 1), travel_place(slot, count, 2)),
             )
             inside = jnp.logical_and(k >= 0, k < width)
-            tile = stage[first + place].astype(F32)
-            tile = jnp.where(inside, tile, 0.0)
-            matrix[p * size : (p + 1) * size, q * size : (q + 1) * size] = tile.astype(BF16)
-            turned = tile.T
+            tile = jnp.where(inside, stage[first + place], jnp.zeros((size, size), BF16))
+            matrix[p * size : (p + 1) * size, q * size : (q + 1) * size] = tile
+            turned = tile.T.astype(F32)
             for c in range(PARTS):
                 terms = turned * moments[c, q * size : (q + 1) * size, p * size : (p + 1) * size]
                 totals[c][p] = totals[c][p] + jnp.sum(terms.reshape(-1, 8, size), axis=0)
@@ -694,10 +696,10 @@
     flat_grad = basis_grad.reshape(PARTS, batches, points * blocks, size)
     own, near = fetch_rows(region, density, slabs, atom_devices)
     if region.shape[1] == blocks:
-        basis_wide, field_wide, turned, grads = reorder(
+        basis_wide, field_wide, weighted, grads = reorder(
             pattern, flat_basis, flat_field, flat_grad, weights, points, blocks
         )
-        ready = (basis_wide, field_wide, build_moments(turned, grads), batch_atom)
+        ready = (basis_wide, field_wide, build_moments(weighted, grads), batch_atom)
         near, far, (basis_wide, field_wide, moments, batch_atom) = swap_halves(near, ready, atom_devices)
         hot, grad_columns = atom_matrix(region, fn_atom, batch_atom, weight_grad, blocks, size, atom_total)
         ready = (basis_wide, field_wide, moments, hot, grad_columns)

time: 33.2 us -> 33.1 us (level)
  Pallas kernels: 15.6 us -> 15 us
  waiting for transfers between devices: 3.85 us -> 4.38 us
    pallas_call x1, Pallas kernels: 5.59 us -> 4.98 us  [reorder(): pl.pallas_call(reorder_kernel, out_shape=(ordered, ordered, jax.ShapeDtyp...]
    ppermute x6, waiting for transfers between devices: 3.82 us -> 4.35 us  [exchange_all(): lax.ppermute(parts[d], axis, [(i, i ^ d) for i in range(count)])]
  transfers between devices with their start and end apart: 10 -> 10, of which waited for: 3 -> 3; matrix products, arithmetic and copies ran while one was open for 0% -> 0% of each run, Pallas kernels for 34% -> 32%
where the time goes in v15:
time: 33.1 us; the launch traced here: 32.9 us
  Pallas kernels  15 us (45%)
  starting transfers between devices  12.1 us (37%)
  waiting for transfers between devices  4.38 us (13%)
  between operations  0.76 us (2%)
  other arithmetic  0.6 us (2%)
    ppermute x6, starting transfers between devices, exchange_all(): lax.ppermute(parts[d], axis, [(i, i ^ d) for i in range(count)])  6.38 us
    ppermute x2, starting transfers between devices, fetch_rows(): near.append(lax.ppermute(piece, ('grid', 'atoms'), moves))  5.12 us
    pallas_call x1, Pallas kernels, reorder(): pl.pallas_call(reorder_kernel, out_shape=(ordered, ordered, jax.ShapeDtyp...  4.98 us
    ppermute x6, waiting for transfers between devices, exchange_all(): lax.ppermute(parts[d], axis, [(i, i ^ d) for i in range(count)])  4.35 us
    pallas_call x1, Pallas kernels, build_moments(): pl.pallas_call(moment_kernel, out_shape=jax.ShapeDtypeStruct((PARTS, bloc...  2.66 us
    pallas_call x1, Pallas kernels, combine(): pl.pallas_call(functools.partial(combine_kernel, owner_rows=owner_rows, s...  2.56 us
    pallas_call x1, Pallas kernels, write(): pl.pallas_call(write_kernel, out_shape=jax.ShapeDtypeStruct(shape, BF16),...  2.06 us
    pallas_call x1, Pallas kernels, rows_to_send(): pl.pallas_call(send_kernel, out_shape=[jax.ShapeDtypeStruct((TRAVEL, rows...  1.83 us
  transfers between devices with their start and end apart: 10, of which 3 were waited for; matrix products, arithmetic and copies ran while one was open for 0% of the time, Pallas kernels for 32%

profile of v15, /device:TPU:0, one launch (start us, length us, event | category | flops | bytes accessed | tf_op | source)
XLA Modules:
  0.0 32.9 jit_solution(14173375114047566732)
XLA Ops:
  0.6 1.8 %shard_map.113 = (bf16[5,128,128]{2,1,0:T(8,128)(2,1)S(1)}, bf16[5,64,128]{2,1,0:T(8,128)(2,1)S(1)}, bf16[5,128,128]{2,1,0:T(8,128)(2,1)S(1)}) custom-call(s32[4,4]{1,0:T(4,128)} %region.3, bf16[15,3,128,128]{3,2,1,0:T(8,128)(2,1)} %density.1), custom_call_target="tpu_custom_call" | custom-call | tf_op jit(solution)/shard_map/pallas_call | solution.py:92
  2.5 5.1 %collective-permute-start.1 = (bf16[5,128,128]{2,1,0:T(8,128)(2,1)S(1)}, bf16[5,128,128]{2,1,0:T(8,128)(2,1)S(1)}, u32[]{:S(2)}, u32[]{:S(2)}) collective-permute-start(bf16[5,128,128]{2,1,0:T(8,128)(2,1)S(1)} %get-tuple-element.22), channel_id=1, source_target_pairs={{0,12},{1,9},{2,14},{3,11},{4,8},{5,13},{6,10},{7,15},{8,4},{9,1},... | collective-permute-start | bytes 491528 | tf_op jit(solution)/shard_map/ppermute | solution.py:113
  7.6 0.0 collective-permute-start
  7.6 5.0 %shard_map.114 = (bf16[16,4,128,128]{3,2,1,0:T(8,128)(2,1)S(1)}, bf16[16,4,128,128]{3,2,1,0:T(8,128)(2,1)S(1)}, bf16[4,2048,128]{2,1,0:T(8,128)(2,1)S(1)}, bf16[3,4,2048,128]{3,2,1,0:T(8,128)(2,1)S(1)}) custom-call(s32[4,16]{1,0:T(4,128)} %bitcast.17, bf16[16,512,128]{2,1,0:T(8,128)(2,1)} %bitcast.22, bf16[16,512,128]{2,1,0:T(8,128)(2,1)} %bitcast.23, ...), custom_call_target="tpu_custom_call" | custom-call | bytes 10485760 | tf_op jit(solution)/shard_map/pallas_call | solution.py:427
  12.6 0.0 copy-start
  12.6 0.0 copy-start.2
  12.6 0.0 copy-start.3
  12.6 0.0 copy-start.4
  12.6 2.7 %shard_map.115.moments = f32[3,512,512]{2,1,0:T(8,128)S(1)} custom-call(bf16[4,2048,128]{2,1,0:T(8,128)(2,1)S(1)} %get-tuple-element.25.weighted, bf16[3,4,2048,128]{3,2,1,0:T(8,128)(2,1)S(1)} %get-tuple-element.26.grads), custom_call_target="tpu_custom_call" | custom-call | flops 3221225472 | tf_op jit(solution)/shard_map/pallas_call | solution.py:470
  15.3 0.0 collective-permute-done.rest_1_
  15.3 0.0 collective-permute-done.1.rest_2_
  15.3 0.1 collective-permute-start.3
  15.4 0.5 %collective-permute-start.2 = (bf16[5,64,128]{2,1,0:T(8,128)(2,1)S(1)}, bf16[5,64,128]{2,1,0:T(8,128)(2,1)S(1)}, u32[]{:S(2)}, u32[]{:S(2)}) collective-permute-start(bf16[5,64,128]{2,1,0:T(8,128)(2,1)S(1)} %collective-permute-done.rest_1_), channel_id=1, source_target_pairs={{0,1},{1,0},{2,3},{3,2},{4,5},{5,4},{6,7},{7,6},{8,9},{9,8},{10,11... | collective-permute-start | bytes 245768 | tf_op jit(solution)/shard_map/ppermute | solution.py:655
  15.9 0.0 copy-done
  15.9 0.0 copy-done.2
  15.9 0.0 copy-done.3
  15.9 0.0 copy-done.4
  15.9 1.0 %shard_map.116 = (bf16[768,640]{1,0:T(8,128)(2,1)S(1)}, f32[3,128,128]{2,1,0:T(8,128)S(1)}) custom-call(s32[4,4]{1,0:T(4,128)S(1)} %copy-done, s32[60,128]{1,0:T(8,128)S(1)} %bitcast.19, s32[1,16]{1,0:T(1,128)S(1)} %bitcast.20, f32[3,16,128]{2,1,0:T(8,128)S(1)} %copy-done.3), custom_call_target="tpu_custom_call" | custom-call | flops 1000000000 | bytes 196608 | tf_op jit(solution)/shard_map/pallas_call | solution.py:504
  16.9 0.0 collective-permute-done.2.rest_3_
  16.9 0.0 collective-permute-done.3.rest_4_
  16.9 0.0 copy-start.1
  16.9 2.6 %shard_map.117 = (bf16[16,4,128,128]{3,2,1,0:T(8,128)(2,1)S(1)}, f32[4,3,192]{2,1,0:T(4,128)S(1)}) custom-call(s32[4,4]{1,0:T(4,128)S(1)} %copy-done, bf16[16,4,128,128]{3,2,1,0:T(8,128)(2,1)S(1)} %get-tuple-element.27.basis, bf16[16,4,128,128]{3,2,1,0:T(8,128)(2,1)S(1)} %get-tuple-element.28.field, f32[3,512,512]{2,1,0:T(8,128)S(1)} %shard_map.115.moments, ...), custom_call_target="tpu_custom_call" | custom-call | tf_op jit(solution)/shard_map/pallas_call | solution.py:597
  19.5 0.3 collective-permute-start.4
  19.8 1.5 %collective-permute-start.5 = (f32[3,192]{1,0:T(4,128)S(1)}, f32[3,192]{1,0:T(4,128)S(1)}, u32[]{:S(2)}, u32[]{:S(2)}) collective-permute-start(f32[3,192]{1,0:T(4,128)S(1)} %get-tuple-element.41), channel_id=1, source_target_pairs={{0,2},{1,3},{2,0},{3,1},{4,6},{5,7},{6,4},{7,5},{8,10},{9,11},{10,... | collective-permute-start | bytes 6920 | tf_op jit(solution)/shard_map/ppermute | solution.py:666
  21.3 0.1 collective-permute-start.6
  21.4 0.0 collective-permute-done.4
  21.4 2.0 %collective-permute-done.5 = f32[3,192]{1,0:T(4,128)S(1)} collective-permute-done((f32[3,192]{1,0:T(4,128)S(1)}, f32[3,192]{1,0:T(4,128)S(1)}, u32[]{:S(2)}, u32[]{:S(2)}) %collective-permute-start.5) | collective-permute-done | bytes 2336 | tf_op jit(solution)/shard_map/ppermute | solution.py:666
  23.4 0.9 %collective-permute-done.6 = f32[3,192]{1,0:T(4,128)S(1)} collective-permute-done((f32[3,192]{1,0:T(4,128)S(1)}, f32[3,192]{1,0:T(4,128)S(1)}, u32[]{:S(2)}, u32[]{:S(2)}) %collective-permute-start.6) | collective-permute-done | bytes 2336 | tf_op jit(solution)/shard_map/ppermute | solution.py:666
  24.3 2.0 %collective-permute-start.7 = (f32[3,192]{1,0:T(4,128)S(1)}, f32[3,192]{1,0:T(4,128)S(1)}, u32[]{:S(2)}, u32[]{:S(2)}) collective-permute-start(f32[3,192]{1,0:T(4,128)S(1)} %fusion), channel_id=1, source_target_pairs={{0,4},{4,0},{8,12},{12,8},{1,5},{5,1},{9,13},{13,9},{2,6},{6,2},{1... | collective-permute-start | bytes 6920 | tf_op jit(solution)/shard_map/ppermute | solution.py:666
  26.4 0.5 %collective-permute-start.8 = (f32[3,192]{1,0:T(4,128)S(1)}, f32[3,192]{1,0:T(4,128)S(1)}, u32[]{:S(2)}, u32[]{:S(2)}) collective-permute-start(f32[3,192]{1,0:T(4,128)S(1)} %fusion), channel_id=1, source_target_pairs={{0,8},{4,12},{8,0},{12,4},{1,9},{5,13},{9,1},{13,5},{2,10},{6,14},... | collective-permute-start | bytes 6920 | tf_op jit(solution)/shard_map/ppermute | solution.py:666
  26.9 1.9 %collective-permute-start.9 = (f32[3,192]{1,0:T(4,128)S(1)}, f32[3,192]{1,0:T(4,128)S(1)}, u32[]{:S(2)}, u32[]{:S(2)}) collective-permute-start(f32[3,192]{1,0:T(4,128)S(1)} %fusion), channel_id=1, source_target_pairs={{0,12},{4,8},{8,4},{12,0},{1,13},{5,9},{9,5},{13,1},{2,14},{6,10},... | collective-permute-start | bytes 6920 | tf_op jit(solution)/shard_map/ppermute | solution.py:666
  28.8 0.0 copy-done.1
  28.8 2.1 %shard_map.118 = bf16[16,512,128]{2,1,0:T(8,128)(2,1)} custom-call(s32[4,16]{1,0:T(4,128)S(1)} %bitcast.18, bf16[16,4,128,128]{3,2,1,0:T(8,128)(2,1)S(1)} %get-tuple-element.38.product), custom_call_target="tpu_custom_call" | custom-call | bytes 4194304 | tf_op jit(solution)/shard_map/pallas_call | solution.py:637
  30.9 0.0 collective-permute-done.7
  30.9 0.0 collective-permute-done.8
  30.9 1.4 %collective-permute-done.9 = f32[3,192]{1,0:T(4,128)S(1)} collective-permute-done((f32[3,192]{1,0:T(4,128)S(1)}, f32[3,192]{1,0:T(4,128)S(1)}, u32[]{:S(2)}, u32[]{:S(2)}) %collective-permute-start.9) | collective-permute-done | bytes 2336 | tf_op jit(solution)/shard_map/ppermute | solution.py:666
  32.3 0.6 %add_add_fusion = f32[3,192]{1,0:T(4,128)} fusion(f32[3,192]{1,0:T(4,128)S(1)} %collective-permute-done.8, f32[3,192]{1,0:T(4,128)S(1)} %collective-permute-done.9, f32[3,192]{1,0:T(4,128)S(1)} %fusion, f32[3,192]{1,0:T(4,128)S(1)} %collective-permute-done.7), kind=kLoop, calls=%fused_computation.2 | loop fusion | flops 1728 | bytes 11520 | tf_op jit(solution)/shard_map/add | solution.py:662
  (2 shorter events, 0.0 us)
Async XLA Ops:
  2.5 12.8 %collective-permute-start.1 = (bf16[5,128,128]{2,1,0:T(8,128)(2,1)S(1)}, bf16[5,128,128]{2,1,0:T(8,128)(2,1)S(1)}, u32[]{:S(2)}, u32[]{:S(2)}) collective-permute-start(bf16[5,128,128]{2,1,0:T(8,128)(2,1)S(1)} %get-tuple-element.22), channel_id=1, source_target_pairs={{0,12},{1,9},{2,14},{3,11},{4,8},{5,13},{6,10},{7,15},{8,4},{9,1},... | collective-permute-start | bytes 491528 | tf_op jit(solution)/shard_map/ppermute | solution.py:113
  7.6 7.7 %collective-permute-start = (bf16[5,64,128]{2,1,0:T(8,128)(2,1)S(1)}, bf16[5,64,128]{2,1,0:T(8,128)(2,1)S(1)}, u32[]{:S(2)}, u32[]{:S(2)}) collective-permute-start(bf16[5,64,128]{2,1,0:T(8,128)(2,1)S(1)} %get-tuple-element.21), channel_id=1, source_target_pairs={{0,4},{1,5},{2,6},{3,7},{4,0},{5,1},{6,2},{7,3},{8,12},{9,13},{10,... | collective-permute-start | bytes 245768 | tf_op jit(solution)/shard_map/ppermute | solution.py:113
  12.6 3.3 %copy-start = (s32[4,4]{1,0:T(4,128)S(1)}, s32[4,4]{1,0:T(4,128)}, u32[]{:S(2)}) copy-start(s32[4,4]{1,0:T(4,128)} %region.3) | copy-start | bytes 196
  12.6 3.3 %copy-start.2 = (s32[7680]{0:T(1024)S(1)}, s32[7680]{0:T(1024)}, u32[]{:S(2)}) copy-start(s32[7680]{0:T(1024)} %param.18) | copy-start | bytes 92164
  12.6 3.3 %copy-start.3 = (f32[3,16,128]{2,1,0:T(8,128)S(1)}, f32[3,16,128]{2,1,0:T(8,128)}, u32[]{:S(2)}) copy-start(f32[3,16,128]{2,1,0:T(8,128)} %weight_grad.1) | copy-start | bytes 73732
  12.6 3.3 %copy-start.4 = (s32[16]{0:T(128)S(1)}, s32[16]{0:T(128)}, u32[]{:S(2)}) copy-start(s32[16]{0:T(128)} %param.19) | copy-start | bytes 196
  15.3 1.6 %collective-permute-start.3 = (bf16[5,128,128]{2,1,0:T(8,128)(2,1)S(1)}, bf16[5,128,128]{2,1,0:T(8,128)(2,1)S(1)}, u32[]{:S(2)}, u32[]{:S(2)}) collective-permute-start(bf16[5,128,128]{2,1,0:T(8,128)(2,1)S(1)} %collective-permute-done.1.rest_2_), channel_id=1, source_target_pairs={{0,1},{1,0},{2,3},{3,2},{4,5},{5,4},{6,7},{7,6},{8,9},{9,8},{10,11... | collective-permute-start | bytes 491528 | tf_op jit(solution)/shard_map/ppermute | solution.py:655
  15.4 1.5 %collective-permute-start.2 = (bf16[5,64,128]{2,1,0:T(8,128)(2,1)S(1)}, bf16[5,64,128]{2,1,0:T(8,128)(2,1)S(1)}, u32[]{:S(2)}, u32[]{:S(2)}) collective-permute-start(bf16[5,64,128]{2,1,0:T(8,128)(2,1)S(1)} %collective-permute-done.rest_1_), channel_id=1, source_target_pairs={{0,1},{1,0},{2,3},{3,2},{4,5},{5,4},{6,7},{7,6},{8,9},{9,8},{10,11... | collective-permute-start | bytes 245768 | tf_op jit(solution)/shard_map/ppermute | solution.py:655
  16.9 11.9 %copy-start.1 = (s32[16,4]{0,1:T(4,128)S(1)}, s32[16,4]{0,1:T(4,128)}, u32[]{:S(2)}) copy-start(s32[16,4]{0,1:T(4,128)} %param.17) | copy-start | bytes 772
  19.5 1.9 %collective-permute-start.4 = (f32[3,192]{1,0:T(4,128)S(1)}, f32[3,192]{1,0:T(4,128)S(1)}, u32[]{:S(2)}, u32[]{:S(2)}) collective-permute-start(f32[3,192]{1,0:T(4,128)S(1)} %get-tuple-element.42), channel_id=1, source_target_pairs={{0,1},{1,0},{2,3},{3,2},{4,5},{5,4},{6,7},{7,6},{8,9},{9,8},{10,11... | collective-permute-start | bytes 6920 | tf_op jit(solution)/shard_map/ppermute | solution.py:666
  19.8 3.6 %collective-permute-start.5 = (f32[3,192]{1,0:T(4,128)S(1)}, f32[3,192]{1,0:T(4,128)S(1)}, u32[]{:S(2)}, u32[]{:S(2)}) collective-permute-start(f32[3,192]{1,0:T(4,128)S(1)} %get-tuple-element.41), channel_id=1, source_target_pairs={{0,2},{1,3},{2,0},{3,1},{4,6},{5,7},{6,4},{7,5},{8,10},{9,11},{10,... | collective-permute-start | bytes 6920 | tf_op jit(solution)/shard_map/ppermute | solution.py:666
  21.3 3.0 %collective-permute-start.6 = (f32[3,192]{1,0:T(4,128)S(1)}, f32[3,192]{1,0:T(4,128)S(1)}, u32[]{:S(2)}, u32[]{:S(2)}) collective-permute-start(f32[3,192]{1,0:T(4,128)S(1)} %get-tuple-element.40), channel_id=1, source_target_pairs={{0,3},{1,2},{2,1},{3,0},{4,7},{5,6},{6,5},{7,4},{8,11},{9,10},{10,... | collective-permute-start | bytes 6920 | tf_op jit(solution)/shard_map/ppermute | solution.py:666
  24.3 6.5 %collective-permute-start.7 = (f32[3,192]{1,0:T(4,128)S(1)}, f32[3,192]{1,0:T(4,128)S(1)}, u32[]{:S(2)}, u32[]{:S(2)}) collective-permute-start(f32[3,192]{1,0:T(4,128)S(1)} %fusion), channel_id=1, source_target_pairs={{0,4},{4,0},{8,12},{12,8},{1,5},{5,1},{9,13},{13,9},{2,6},{6,2},{1... | collective-permute-start | bytes 6920 | tf_op jit(solution)/shard_map/ppermute | solution.py:666
  26.4 4.5 %collective-permute-start.8 = (f32[3,192]{1,0:T(4,128)S(1)}, f32[3,192]{1,0:T(4,128)S(1)}, u32[]{:S(2)}, u32[]{:S(2)}) collective-permute-start(f32[3,192]{1,0:T(4,128)S(1)} %fusion), channel_id=1, source_target_pairs={{0,8},{4,12},{8,0},{12,4},{1,9},{5,13},{9,1},{13,5},{2,10},{6,14},... | collective-permute-start | bytes 6920 | tf_op jit(solution)/shard_map/ppermute | solution.py:666
  26.9 5.4 %collective-permute-start.9 = (f32[3,192]{1,0:T(4,128)S(1)}, f32[3,192]{1,0:T(4,128)S(1)}, u32[]{:S(2)}, u32[]{:S(2)}) collective-permute-start(f32[3,192]{1,0:T(4,128)S(1)} %fusion), channel_id=1, source_target_pairs={{0,12},{4,8},{8,4},{12,0},{1,13},{5,9},{9,5},{13,1},{2,14},{6,10},... | collective-permute-start | bytes 6920 | tf_op jit(solution)/shard_map/ppermute | solution.py:666

commit v16 on v15

--- a/solution.py
+++ b/solution.py
@@ -37,7 +37,7 @@
 
 
 def partners(slabs):
-    return [(1, 1)] + [(shift + 1, shift) for shift in range(2, slabs, 2)]
+    return [(shift + 1, shift) for shift in range(2, slabs, 2)] + [(0, 1)]
 
 
 def send_kernel(region_hbm, density, *rest):
@@ -49,7 +49,6 @@
     core = lax.rem(lax.axis_index("atoms"), 2)
     slabs, size = region.shape
     owner_rows = density.shape[0]
-    rows = density.shape[-2]
     copies = []
     for number, ((low, high), out) in enumerate(zip([(0, 0)] + partners(slabs), outs)):
         slab = jnp.bitwise_xor(me, jnp.where(core == 0, low, high))
@@ -64,13 +63,10 @@
         after = jnp.minimum(base + 1, owner_rows - 1)
         lower = base == 0
         edge = jnp.where(jnp.logical_and(count == 2, jnp.logical_not(lower)), after, base)
-        kept = out.shape[1]
-        first = 0 if kept == rows else pl.multiple_of(core * kept, kept)
-        here = pl.ds(first, kept)
         pairs = (
-            (density.at[base, pl.ds(1, 2), here, :], out.at[pl.ds(0, 2)]),
-            (density.at[after, pl.ds(0, 2), here, :], out.at[pl.ds(2, 2)]),
-            (density.at[edge, jnp.where(lower, 0, 2), here, :], out.at[4]),
+            (density.at[base, pl.ds(1, 2)], out.at[pl.ds(0, 2)]),
+            (density.at[after, pl.ds(0, 2)], out.at[pl.ds(2, 2)]),
+            (density.at[edge, jnp.where(lower, 0, 2)], out.at[4]),
         )
         for part, (source, target) in enumerate(pairs):
             copies.append(pltpu.make_async_copy(source, target, sems.at[number, part]))
@@ -86,17 +82,16 @@
 
 def rows_to_send(region, density, slabs):
     size = density.shape[-1]
-    exchanges = partners(slabs)
-    kept = [size] + [size if low != high else size // 2 for low, high in exchanges]
+    count = 1 + len(partners(slabs))
     hbm = pl.BlockSpec(memory_space=pl.ANY)
     return pl.pallas_call(
         send_kernel,
-        out_shape=[jax.ShapeDtypeStruct((TRAVEL, rows, size), density.dtype) for rows in kept],
+        out_shape=[jax.ShapeDtypeStruct((TRAVEL, size, size), density.dtype)] * count,
         in_specs=[hbm, hbm],
-        out_specs=[pl.BlockSpec(memory_space=pltpu.VMEM)] * len(kept),
+        out_specs=[pl.BlockSpec(memory_space=pltpu.VMEM)] * count,
         scratch_shapes=[
             pltpu.SMEM(region.shape, jnp.int32),
-            pltpu.SemaphoreType.DMA((len(kept), 3)),
+            pltpu.SemaphoreType.DMA((count, 3)),
             pltpu.SemaphoreType.DMA,
         ],
         compiler_params=pltpu.CompilerParams(vmem_limit_bytes=VMEM_LIMIT),
@@ -108,7 +103,10 @@
     near = []
     for shifts, piece in zip(partners(slabs), outgoing):
         moves = [
-            (z * atom_devices + a, (z ^ shifts[a % 2]) * atom_devices + a) for z in range(slabs) for a in range(atom_devices)
+            (z * atom_devices + a, (z ^ shifts[a % 2]) * atom_devices + a)
+            for z in range(slabs)
+            for a in range(atom_devices)
+            if shifts[a % 2]
         ]
         near.append(lax.ppermute(piece, ("grid", "atoms"), moves))
     return own, near
@@ -119,16 +117,14 @@
     for place in range(TRAVEL):
         stage[place] = own[place]
     for (low, high), here, there in zip(partners(slabs), near, far):
-        kept = here.shape[1]
         mine = jnp.where(core == 0, low, high) * TRAVEL
         other = jnp.where(core == 0, high, low) * TRAVEL
         for place in range(TRAVEL):
-            if low != high:
+            if low:
                 stage[mine + place] = here[place]
                 stage[other + place] = there[place]
             else:
-                stage[mine + place, pl.ds(pl.multiple_of(core * kept, kept), kept), :] = here[place]
-                stage[mine + place, pl.ds(pl.multiple_of((1 - core) * kept, kept), kept), :] = there[place]
+                stage[high * TRAVEL + place] = jnp.where(core == 0, there[place], here[place])
 
 
 def block_major(x_ref, wide, points, blocks):
@@ -652,7 +648,8 @@
 def swap_halves(near, ready, atom_devices):
     near, ready = lax.optimization_barrier((near, ready))
     swap = [(i, i ^ 1) for i in range(atom_devices)]
-    return near, [lax.ppermute(piece, "atoms", swap) for piece in near], ready
+    moves = [swap] * (len(near) - 1) + [swap[1::2]]
+    return near, [lax.ppermute(piece, "atoms", pairs) for piece, pairs in zip(near, moves)], ready
 
 
 def tree_sum(values):
@@ -663,8 +660,9 @@
 
 
 def exchange_all(parts, axis, count):
-    moved = {d: lax.ppermute(parts[d], axis, [(i, i ^ d) for i in range(count)]) for d in range(1, count)}
-    return [parts[0]] + [moved[d] for d in range(1, count)]
+    moved = [lax.ppermute(parts[d], axis, [(i, i ^ d) for i in range(count)]) for d in range(count - 1, 0, -1)]
+    moved[:-1] = lax.optimization_barrier(tuple(moved[:-1]))
+    return [parts[0], *moved]
 
 
 def sum_parts(partial_grad, product, slabs, atom_devices):

time: 33.1 us -> 35.4 us (1.069)
  starting transfers between devices: 12.1 us -> 14.6 us
  waiting for transfers between devices: 4.38 us -> 4.02 us
    ppermute x2, starting transfers between devices: 0.57 us -> 2.41 us  [swap_halves(): lax.ppermute(piece, 'atoms', pairs)]
    ppermute x6, waiting for transfers between devices: 4.35 us -> 3.04 us  [exchange_all(): lax.ppermute(parts[d], axis, [(i, i ^ d) for i in range(count)])]
    ppermute x2, waiting for transfers between devices: 0.02 us -> 0.97 us  [swap_halves(): lax.ppermute(piece, 'atoms', pairs)]
    ppermute x2, starting transfers between devices: 5.12 us -> 5.78 us  [fetch_rows(): near.append(lax.ppermute(piece, ('grid', 'atoms'), moves))]
  transfers between devices with their start and end apart: 10 -> 10, of which waited for: 3 -> 3; matrix products, arithmetic and copies ran while one was open for 0% -> 0% of each run, Pallas kernels for 32% -> 30%
where the time goes in v16:
time: 35.4 us; the launch traced here: 35.1 us
  Pallas kernels  15.1 us (43%)
  starting transfers between devices  14.6 us (41%)
  waiting for transfers between devices  4.02 us (11%)
  between operations  0.81 us (2%)
  other arithmetic  0.6 us (2%)
    ppermute x6, starting transfers between devices, exchange_all(): lax.ppermute(parts[d], axis, [(i, i ^ d) for i in range(count)])  6.38 us
    ppermute x2, starting transfers between devices, fetch_rows(): near.append(lax.ppermute(piece, ('grid', 'atoms'), moves))  5.78 us
    pallas_call x1, Pallas kernels, reorder(): pl.pallas_call(reorder_kernel, out_shape=(ordered, ordered, jax.ShapeDtyp...  4.99 us
    ppermute x6, waiting for transfers between devices, exchange_all(): lax.ppermute(parts[d], axis, [(i, i ^ d) for i in range(count)])  3.04 us
    pallas_call x1, Pallas kernels, build_moments(): pl.pallas_call(moment_kernel, out_shape=jax.ShapeDtypeStruct((PARTS, bloc...  2.62 us
    pallas_call x1, Pallas kernels, combine(): pl.pallas_call(functools.partial(combine_kernel, owner_rows=owner_rows, s...  2.6 us
    ppermute x2, starting transfers between devices, swap_halves(): lax.ppermute(piece, 'atoms', pairs)  2.41 us
    pallas_call x1, Pallas kernels, write(): pl.pallas_call(write_kernel, out_shape=jax.ShapeDtypeStruct(shape, BF16),...  2.06 us
  transfers between devices with their start and end apart: 10, of which 3 were waited for; matrix products, arithmetic and copies ran while one was open for 0% of the time, Pallas kernels for 30%

profile of v16, /device:TPU:0, one launch (start us, length us, event | category | flops | bytes accessed | tf_op | source)
XLA Modules:
  0.0 35.1 jit_solution(17700195413182584482)
XLA Ops:
  0.6 1.9 %shard_map.113 = (bf16[5,128,128]{2,1,0:T(8,128)(2,1)S(1)}, bf16[5,128,128]{2,1,0:T(8,128)(2,1)S(1)}, bf16[5,128,128]{2,1,0:T(8,128)(2,1)S(1)}) custom-call(s32[4,4]{1,0:T(4,128)} %region.3, bf16[15,3,128,128]{3,2,1,0:T(8,128)(2,1)} %density.1), custom_call_target="tpu_custom_call" | custom-call | tf_op jit(solution)/shard_map/pallas_call | solution.py:87
  2.5 5.1 %collective-permute-start = (bf16[5,128,128]{2,1,0:T(8,128)(2,1)S(1)}, bf16[5,128,128]{2,1,0:T(8,128)(2,1)S(1)}, u32[]{:S(2)}, u32[]{:S(2)}) collective-permute-start(bf16[5,128,128]{2,1,0:T(8,128)(2,1)S(1)} %get-tuple-element.25), channel_id=1, source_target_pairs={{0,12},{1,9},{2,14},{3,11},{4,8},{5,13},{6,10},{7,15},{8,4},{9,1},... | collective-permute-start | bytes 491528 | tf_op jit(solution)/shard_map/ppermute | solution.py:111
  7.6 0.7 %collective-permute-start.1 = (bf16[5,128,128]{2,1,0:T(8,128)(2,1)S(1)}, bf16[5,128,128]{2,1,0:T(8,128)(2,1)S(1)}, u32[]{:S(2)}, u32[]{:S(2)}) collective-permute-start(bf16[5,128,128]{2,1,0:T(8,128)(2,1)S(1)} %get-tuple-element.26), channel_id=1, source_target_pairs={{1,5},{3,7},{5,1},{7,3},{9,13},{11,15},{13,9},{15,11},{17,21},{19,... | collective-permute-start | bytes 491528 | tf_op jit(solution)/shard_map/ppermute | solution.py:111
  8.3 5.0 %shard_map.114 = (bf16[16,4,128,128]{3,2,1,0:T(8,128)(2,1)S(1)}, bf16[16,4,128,128]{3,2,1,0:T(8,128)(2,1)S(1)}, bf16[4,2048,128]{2,1,0:T(8,128)(2,1)S(1)}, bf16[3,4,2048,128]{3,2,1,0:T(8,128)(2,1)S(1)}) custom-call(s32[4,16]{1,0:T(4,128)} %bitcast.17, bf16[16,512,128]{2,1,0:T(8,128)(2,1)} %bitcast.22, bf16[16,512,128]{2,1,0:T(8,128)(2,1)} %bitcast.23, ...), custom_call_target="tpu_custom_call" | custom-call | bytes 10485760 | tf_op jit(solution)/shard_map/pallas_call | solution.py:423
  13.3 0.0 copy-start
  13.3 0.0 copy-start.2
  13.3 0.0 copy-start.3
  13.3 0.0 copy-start.4
  13.3 2.6 %shard_map.115.moments = f32[3,512,512]{2,1,0:T(8,128)S(1)} custom-call(bf16[4,2048,128]{2,1,0:T(8,128)(2,1)S(1)} %get-tuple-element.29.weighted, bf16[3,4,2048,128]{3,2,1,0:T(8,128)(2,1)S(1)} %get-tuple-element.30.grads), custom_call_target="tpu_custom_call" | custom-call | flops 3221225472 | tf_op jit(solution)/shard_map/pallas_call | solution.py:466
  15.9 0.0 collective-permute-done.rest_1_
  16.0 0.0 collective-permute-done.1.rest_2_
  16.0 1.1 %collective-permute-start.2 = (bf16[5,128,128]{2,1,0:T(8,128)(2,1)S(1)}, bf16[5,128,128]{2,1,0:T(8,128)(2,1)S(1)}, u32[]{:S(2)}, u32[]{:S(2)}) collective-permute-start(bf16[5,128,128]{2,1,0:T(8,128)(2,1)S(1)} %collective-permute-done.rest_1_), channel_id=1, source_target_pairs={{0,1},{1,0},{2,3},{3,2},{4,5},{5,4},{6,7},{7,6},{8,9},{9,8},{10,11... | collective-permute-start | bytes 491528 | tf_op jit(solution)/shard_map/ppermute | solution.py:652
  17.1 1.3 %collective-permute-start.3 = (bf16[5,128,128]{2,1,0:T(8,128)(2,1)S(1)}, bf16[5,128,128]{2,1,0:T(8,128)(2,1)S(1)}, u32[]{:S(2)}, u32[]{:S(2)}) collective-permute-start(bf16[5,128,128]{2,1,0:T(8,128)(2,1)S(1)} %collective-permute-done.1.rest_2_), channel_id=1, source_target_pairs={{1,0},{3,2},{5,4},{7,6},{9,8},{11,10},{13,12},{15,14},{17,16},{19,... | collective-permute-start | bytes 491528 | tf_op jit(solution)/shard_map/ppermute | solution.py:652
  18.4 0.0 copy-done
  18.4 0.0 copy-done.2
  18.4 0.0 copy-done.3
  18.4 0.0 copy-done.4
  18.4 1.0 %shard_map.116 = (bf16[768,640]{1,0:T(8,128)(2,1)S(1)}, f32[3,128,128]{2,1,0:T(8,128)S(1)}) custom-call(s32[4,4]{1,0:T(4,128)S(1)} %copy-done, s32[60,128]{1,0:T(8,128)S(1)} %bitcast.19, s32[1,16]{1,0:T(1,128)S(1)} %bitcast.20, f32[3,16,128]{2,1,0:T(8,128)S(1)} %copy-done.3), custom_call_target="tpu_custom_call" | custom-call | flops 1000000000 | bytes 196608 | tf_op jit(solution)/shard_map/pallas_call | solution.py:500
  19.4 0.0 collective-permute-done.2.rest_3_
  19.4 1.0 %collective-permute-done.3.rest_4_ = bf16[5,128,128]{2,1,0:T(8,128)(2,1)S(1)} collective-permute-done((bf16[5,128,128]{2,1,0:T(8,128)(2,1)S(1)}, bf16[5,128,128]{2,1,0:T(8,128)(2,1)S(1)}, u32[]{:S(2)}, u32[]{:S(2)}) %collective-permute-start.3) | collective-permute-done | bytes 163872 | tf_op jit(solution)/shard_map/ppermute | solution.py:652
  20.4 0.0 copy-start.1
  20.4 2.6 %shard_map.117 = (bf16[16,4,128,128]{3,2,1,0:T(8,128)(2,1)S(1)}, f32[4,3,192]{2,1,0:T(4,128)S(1)}) custom-call(s32[4,4]{1,0:T(4,128)S(1)} %copy-done, bf16[16,4,128,128]{3,2,1,0:T(8,128)(2,1)S(1)} %get-tuple-element.31.basis, bf16[16,4,128,128]{3,2,1,0:T(8,128)(2,1)S(1)} %get-tuple-element.32.field, f32[3,512,512]{2,1,0:T(8,128)S(1)} %shard_map.115.moments, ...), custom_call_target="tpu_custom_call" | custom-call | tf_op jit(solution)/shard_map/pallas_call | solution.py:593
  23.0 1.3 %collective-permute-start.4 = (f32[3,192]{1,0:T(4,128)S(1)}, f32[3,192]{1,0:T(4,128)S(1)}, u32[]{:S(2)}, u32[]{:S(2)}) collective-permute-start(f32[3,192]{1,0:T(4,128)S(1)} %get-tuple-element.50), channel_id=1, source_target_pairs={{0,3},{1,2},{2,1},{3,0},{4,7},{5,6},{6,5},{7,4},{8,11},{9,10},{10,... | collective-permute-start | bytes 6920 | tf_op jit(solution)/shard_map/ppermute | solution.py:663
  24.4 0.5 %collective-permute-start.5 = (f32[3,192]{1,0:T(4,128)S(1)}, f32[3,192]{1,0:T(4,128)S(1)}, u32[]{:S(2)}, u32[]{:S(2)}) collective-permute-start(f32[3,192]{1,0:T(4,128)S(1)} %get-tuple-element.49), channel_id=1, source_target_pairs={{0,2},{1,3},{2,0},{3,1},{4,6},{5,7},{6,4},{7,5},{8,10},{9,11},{10,... | collective-permute-start | bytes 6920 | tf_op jit(solution)/shard_map/ppermute | solution.py:663
  24.9 0.0 collective-permute-start.6
  24.9 1.2 %collective-permute-done.4 = f32[3,192]{1,0:T(4,128)S(1)} collective-permute-done((f32[3,192]{1,0:T(4,128)S(1)}, f32[3,192]{1,0:T(4,128)S(1)}, u32[]{:S(2)}, u32[]{:S(2)}) %collective-permute-start.4) | collective-permute-done | bytes 2336 | tf_op jit(solution)/shard_map/ppermute | solution.py:663
  26.1 1.9 %collective-permute-done.5 = f32[3,192]{1,0:T(4,128)S(1)} collective-permute-done((f32[3,192]{1,0:T(4,128)S(1)}, f32[3,192]{1,0:T(4,128)S(1)}, u32[]{:S(2)}, u32[]{:S(2)}) %collective-permute-start.5) | collective-permute-done | bytes 2336 | tf_op jit(solution)/shard_map/ppermute | solution.py:663
  28.0 0.0 collective-permute-done.6
  28.0 0.7 %collective-permute-start.7 = (f32[3,192]{1,0:T(4,128)S(1)}, f32[3,192]{1,0:T(4,128)S(1)}, u32[]{:S(2)}, u32[]{:S(2)}) collective-permute-start(f32[3,192]{1,0:T(4,128)S(1)} %fusion), channel_id=1, source_target_pairs={{0,12},{4,8},{8,4},{12,0},{1,13},{5,9},{9,5},{13,1},{2,14},{6,10},... | collective-permute-start | bytes 6920 | tf_op jit(solution)/shard_map/ppermute | solution.py:663
  28.7 1.3 %collective-permute-start.8 = (f32[3,192]{1,0:T(4,128)S(1)}, f32[3,192]{1,0:T(4,128)S(1)}, u32[]{:S(2)}, u32[]{:S(2)}) collective-permute-start(f32[3,192]{1,0:T(4,128)S(1)} %fusion), channel_id=1, source_target_pairs={{0,8},{4,12},{8,0},{12,4},{1,9},{5,13},{9,1},{13,5},{2,10},{6,14},... | collective-permute-start | bytes 6920 | tf_op jit(solution)/shard_map/ppermute | solution.py:663
  30.0 2.4 %collective-permute-start.9 = (f32[3,192]{1,0:T(4,128)S(1)}, f32[3,192]{1,0:T(4,128)S(1)}, u32[]{:S(2)}, u32[]{:S(2)}) collective-permute-start(f32[3,192]{1,0:T(4,128)S(1)} %fusion), channel_id=1, source_target_pairs={{0,4},{4,0},{8,12},{12,8},{1,5},{5,1},{9,13},{13,9},{2,6},{6,2},{1... | collective-permute-start | bytes 6920 | tf_op jit(solution)/shard_map/ppermute | solution.py:663
  32.4 0.0 copy-done.1
  32.4 2.1 %shard_map.118 = bf16[16,512,128]{2,1,0:T(8,128)(2,1)} custom-call(s32[4,16]{1,0:T(4,128)S(1)} %bitcast.18, bf16[16,4,128,128]{3,2,1,0:T(8,128)(2,1)S(1)} %get-tuple-element.44.product), custom_call_target="tpu_custom_call" | custom-call | bytes 4194304 | tf_op jit(solution)/shard_map/pallas_call | solution.py:633
  34.5 0.0 collective-permute-done.7
  34.5 0.0 collective-permute-done.8
  34.5 0.0 collective-permute-done.9
  34.5 0.6 %add_add_fusion = f32[3,192]{1,0:T(4,128)} fusion(f32[3,192]{1,0:T(4,128)S(1)} %collective-permute-done.8, f32[3,192]{1,0:T(4,128)S(1)} %collective-permute-done.9, f32[3,192]{1,0:T(4,128)S(1)} %fusion, f32[3,192]{1,0:T(4,128)S(1)} %collective-permute-done.7), kind=kLoop, calls=%fused_computation.2 | loop fusion | flops 1728 | bytes 11520 | tf_op jit(solution)/shard_map/add | solution.py:659
  (2 shorter events, 0.0 us)
Async XLA Ops:
  2.5 13.5 %collective-permute-start = (bf16[5,128,128]{2,1,0:T(8,128)(2,1)S(1)}, bf16[5,128,128]{2,1,0:T(8,128)(2,1)S(1)}, u32[]{:S(2)}, u32[]{:S(2)}) collective-permute-start(bf16[5,128,128]{2,1,0:T(8,128)(2,1)S(1)} %get-tuple-element.25), channel_id=1, source_target_pairs={{0,12},{1,9},{2,14},{3,11},{4,8},{5,13},{6,10},{7,15},{8,4},{9,1},... | collective-permute-start | bytes 491528 | tf_op jit(solution)/shard_map/ppermute | solution.py:111
  7.6 8.4 %collective-permute-start.1 = (bf16[5,128,128]{2,1,0:T(8,128)(2,1)S(1)}, bf16[5,128,128]{2,1,0:T(8,128)(2,1)S(1)}, u32[]{:S(2)}, u32[]{:S(2)}) collective-permute-start(bf16[5,128,128]{2,1,0:T(8,128)(2,1)S(1)} %get-tuple-element.26), channel_id=1, source_target_pairs={{1,5},{3,7},{5,1},{7,3},{9,13},{11,15},{13,9},{15,11},{17,21},{19,... | collective-permute-start | bytes 491528 | tf_op jit(solution)/shard_map/ppermute | solution.py:111
  13.3 5.1 %copy-start = (s32[4,4]{1,0:T(4,128)S(1)}, s32[4,4]{1,0:T(4,128)}, u32[]{:S(2)}) copy-start(s32[4,4]{1,0:T(4,128)} %region.3) | copy-start | bytes 196
  13.3 5.1 %copy-start.2 = (s32[7680]{0:T(1024)S(1)}, s32[7680]{0:T(1024)}, u32[]{:S(2)}) copy-start(s32[7680]{0:T(1024)} %param.18) | copy-start | bytes 92164
  13.3 5.1 %copy-start.3 = (f32[3,16,128]{2,1,0:T(8,128)S(1)}, f32[3,16,128]{2,1,0:T(8,128)}, u32[]{:S(2)}) copy-start(f32[3,16,128]{2,1,0:T(8,128)} %weight_grad.1) | copy-start | bytes 73732
  13.3 5.1 %copy-start.4 = (s32[16]{0:T(128)S(1)}, s32[16]{0:T(128)}, u32[]{:S(2)}) copy-start(s32[16]{0:T(128)} %param.19) | copy-start | bytes 196
  16.0 3.4 %collective-permute-start.2 = (bf16[5,128,128]{2,1,0:T(8,128)(2,1)S(1)}, bf16[5,128,128]{2,1,0:T(8,128)(2,1)S(1)}, u32[]{:S(2)}, u32[]{:S(2)}) collective-permute-start(bf16[5,128,128]{2,1,0:T(8,128)(2,1)S(1)} %collective-permute-done.rest_1_), channel_id=1, source_target_pairs={{0,1},{1,0},{2,3},{3,2},{4,5},{5,4},{6,7},{7,6},{8,9},{9,8},{10,11... | collective-permute-start | bytes 491528 | tf_op jit(solution)/shard_map/ppermute | solution.py:652
  17.1 3.3 %collective-permute-start.3 = (bf16[5,128,128]{2,1,0:T(8,128)(2,1)S(1)}, bf16[5,128,128]{2,1,0:T(8,128)(2,1)S(1)}, u32[]{:S(2)}, u32[]{:S(2)}) collective-permute-start(bf16[5,128,128]{2,1,0:T(8,128)(2,1)S(1)} %collective-permute-done.1.rest_2_), channel_id=1, source_target_pairs={{1,0},{3,2},{5,4},{7,6},{9,8},{11,10},{13,12},{15,14},{17,16},{19,... | collective-permute-start | bytes 491528 | tf_op jit(solution)/shard_map/ppermute | solution.py:652
  20.4 12.1 %copy-start.1 = (s32[16,4]{0,1:T(4,128)S(1)}, s32[16,4]{0,1:T(4,128)}, u32[]{:S(2)}) copy-start(s32[16,4]{0,1:T(4,128)} %param.17) | copy-start | bytes 772
  23.0 3.1 %collective-permute-start.4 = (f32[3,192]{1,0:T(4,128)S(1)}, f32[3,192]{1,0:T(4,128)S(1)}, u32[]{:S(2)}, u32[]{:S(2)}) collective-permute-start(f32[3,192]{1,0:T(4,128)S(1)} %get-tuple-element.50), channel_id=1, source_target_pairs={{0,3},{1,2},{2,1},{3,0},{4,7},{5,6},{6,5},{7,4},{8,11},{9,10},{10,... | collective-permute-start | bytes 6920 | tf_op jit(solution)/shard_map/ppermute | solution.py:663
  24.4 3.6 %collective-permute-start.5 = (f32[3,192]{1,0:T(4,128)S(1)}, f32[3,192]{1,0:T(4,128)S(1)}, u32[]{:S(2)}, u32[]{:S(2)}) collective-permute-start(f32[3,192]{1,0:T(4,128)S(1)} %get-tuple-element.49), channel_id=1, source_target_pairs={{0,2},{1,3},{2,0},{3,1},{4,6},{5,7},{6,4},{7,5},{8,10},{9,11},{10,... | collective-permute-start | bytes 6920 | tf_op jit(solution)/shard_map/ppermute | solution.py:663
  24.9 3.1 %collective-permute-start.6 = (f32[3,192]{1,0:T(4,128)S(1)}, f32[3,192]{1,0:T(4,128)S(1)}, u32[]{:S(2)}, u32[]{:S(2)}) collective-permute-start(f32[3,192]{1,0:T(4,128)S(1)} %get-tuple-element.48), channel_id=1, source_target_pairs={{0,1},{1,0},{2,3},{3,2},{4,5},{5,4},{6,7},{7,6},{8,9},{9,8},{10,11... | collective-permute-start | bytes 6920 | tf_op jit(solution)/shard_map/ppermute | solution.py:663
  28.0 6.5 %collective-permute-start.7 = (f32[3,192]{1,0:T(4,128)S(1)}, f32[3,192]{1,0:T(4,128)S(1)}, u32[]{:S(2)}, u32[]{:S(2)}) collective-permute-start(f32[3,192]{1,0:T(4,128)S(1)} %fusion), channel_id=1, source_target_pairs={{0,12},{4,8},{8,4},{12,0},{1,13},{5,9},{9,5},{13,1},{2,14},{6,10},... | collective-permute-start | bytes 6920 | tf_op jit(solution)/shard_map/ppermute | solution.py:663
  28.7 5.8 %collective-permute-start.8 = (f32[3,192]{1,0:T(4,128)S(1)}, f32[3,192]{1,0:T(4,128)S(1)}, u32[]{:S(2)}, u32[]{:S(2)}) collective-permute-start(f32[3,192]{1,0:T(4,128)S(1)} %fusion), channel_id=1, source_target_pairs={{0,8},{4,12},{8,0},{12,4},{1,9},{5,13},{9,1},{13,5},{2,10},{6,14},... | collective-permute-start | bytes 6920 | tf_op jit(solution)/shard_map/ppermute | solution.py:663
  30.0 4.5 %collective-permute-start.9 = (f32[3,192]{1,0:T(4,128)S(1)}, f32[3,192]{1,0:T(4,128)S(1)}, u32[]{:S(2)}, u32[]{:S(2)}) collective-permute-start(f32[3,192]{1,0:T(4,128)S(1)} %fusion), channel_id=1, source_target_pairs={{0,4},{4,0},{8,12},{12,8},{1,5},{5,1},{9,13},{13,9},{2,6},{6,2},{1... | collective-permute-start | bytes 6920 | tf_op jit(solution)/shard_map/ppermute | solution.py:663

commit v17 on v15

--- a/solution.py
+++ b/solution.py
@@ -663,14 +663,17 @@
 
 
 def exchange_all(parts, axis, count):
-    moved = {d: lax.ppermute(parts[d], axis, [(i, i ^ d) for i in range(count)]) for d in range(1, count)}
-    return [parts[0]] + [moved[d] for d in range(1, count)]
-
-
-def sum_parts(partial_grad, product, slabs, atom_devices):
-    total = tree_sum(exchange_all([partial_grad[d] for d in range(atom_devices)], "atoms", atom_devices))
-    total, product = lax.optimization_barrier((total, product))
-    return tree_sum(exchange_all([total] * slabs, "grid", slabs)), product
+    return [parts[0]] + [
+        lax.ppermute(parts[d], axis, [(i, i ^ d) for i in range(count)]) for d in range(count - 1, 0, -1)
+    ]
+
+
+def sum_parts(partial_grad, contracted, slabs, atom_devices):
+    parts = exchange_all([partial_grad[d] for d in range(atom_devices)], "atoms", atom_devices)
+    parts, contracted = lax.optimization_barrier((parts, contracted))
+    own, *far, near = exchange_all([tree_sum(parts)] * slabs, "grid", slabs)
+    far = lax.optimization_barrier(far)
+    return tree_sum([own, *far, near]), contracted
 
 
 def local(
@@ -704,8 +707,7 @@
         hot, grad_columns = atom_matrix(region, fn_atom, batch_atom, weight_grad, blocks, size, atom_total)
         ready = (basis_wide, field_wide, moments, hot, grad_columns)
         product, partial_grad = combine(region, ready, [own, *near, *far], shapes)
-        gradient, product = sum_parts(partial_grad, product, slabs, atom_devices)
-        contracted = write(pattern, product)
+        gradient, contracted = sum_parts(partial_grad, write(pattern, product), slabs, atom_devices)
         return contracted.reshape(basis.shape), gradient
     ready = relayout(in_hbm(flat_basis), in_hbm(flat_field), points, blocks)
     near, far, (basis_wide, field_wide) = swap_halves(near, ready, atom_devices)
@@ -722,8 +724,8 @@
         [own, *near, *far],
         shapes,
     )
-    gradient, basis_wide = sum_parts(partial_grad, basis_wide, slabs, atom_devices)
     contracted = contract(region, pattern, basis_wide, tiles, points, blocks, width)
+    gradient, contracted = sum_parts(partial_grad, contracted, slabs, atom_devices)
     return contracted.reshape(basis.shape), gradient
 
 

time: 33.1 us -> 32.5 us (0.982)
  waiting for transfers between devices: 4.38 us -> 3.73 us
    ppermute x6, waiting for transfers between devices: 4.35 us -> 3.71 us  [exchange_all(): lax.ppermute(parts[d], axis, [(i, i ^ d) for i in range(count)])]
  transfers between devices with their start and end apart: 10 -> 10, of which waited for: 3 -> 4; matrix products, arithmetic and copies ran while one was open for 0% -> 0% of each run, Pallas kernels for 32% -> 33%
where the time goes in v17:
time: 32.5 us; the launch traced here: 32.3 us
  Pallas kernels  15 us (46%)
  starting transfers between devices  12.1 us (37%)
  waiting for transfers between devices  3.73 us (11%)
  between operations  0.76 us (2%)
  other arithmetic  0.6 us (2%)
    ppermute x6, starting transfers between devices, exchange_all(): lax.ppermute(parts[d], axis, [(i, i ^ d) for i in range(count)])  6.41 us
    ppermute x2, starting transfers between devices, fetch_rows(): near.append(lax.ppermute(piece, ('grid', 'atoms'), moves))  5.12 us
    pallas_call x1, Pallas kernels, reorder(): pl.pallas_call(reorder_kernel, out_shape=(ordered, ordered, jax.ShapeDtyp...  4.98 us
    ppermute x6, waiting for transfers between devices, exchange_all(): lax.ppermute(parts[d], axis, [(i, i ^ d) for i in range(count)])  3.71 us
    pallas_call x1, Pallas kernels, build_moments(): pl.pallas_call(moment_kernel, out_shape=jax.ShapeDtypeStruct((PARTS, bloc...  2.65 us
    pallas_call x1, Pallas kernels, combine(): pl.pallas_call(functools.partial(combine_kernel, owner_rows=owner_rows, s...  2.56 us
    pallas_call x1, Pallas kernels, write(): pl.pallas_call(write_kernel, out_shape=jax.ShapeDtypeStruct(shape, BF16),...  2.06 us
    pallas_call x1, Pallas kernels, rows_to_send(): pl.pallas_call(send_kernel, out_shape=[jax.ShapeDtypeStruct((TRAVEL, rows...  1.83 us
  transfers between devices with their start and end apart: 10, of which 4 were waited for; matrix products, arithmetic and copies ran while one was open for 0% of the time, Pallas kernels for 33%

profile of v17, /device:TPU:0, one launch (start us, length us, event | category | flops | bytes accessed | tf_op | source)
XLA Modules:
  0.0 32.3 jit_solution(6158544246692268958)
XLA Ops:
  0.6 1.8 %shard_map.113 = (bf16[5,128,128]{2,1,0:T(8,128)(2,1)S(1)}, bf16[5,64,128]{2,1,0:T(8,128)(2,1)S(1)}, bf16[5,128,128]{2,1,0:T(8,128)(2,1)S(1)}) custom-call(s32[4,4]{1,0:T(4,128)} %region.3, bf16[15,3,128,128]{3,2,1,0:T(8,128)(2,1)} %density.1), custom_call_target="tpu_custom_call" | custom-call | tf_op jit(solution)/shard_map/pallas_call | solution.py:92
  2.5 5.1 %collective-permute-start.1 = (bf16[5,128,128]{2,1,0:T(8,128)(2,1)S(1)}, bf16[5,128,128]{2,1,0:T(8,128)(2,1)S(1)}, u32[]{:S(2)}, u32[]{:S(2)}) collective-permute-start(bf16[5,128,128]{2,1,0:T(8,128)(2,1)S(1)} %get-tuple-element.27), channel_id=1, source_target_pairs={{0,12},{1,9},{2,14},{3,11},{4,8},{5,13},{6,10},{7,15},{8,4},{9,1},... | collective-permute-start | bytes 491528 | tf_op jit(solution)/shard_map/ppermute | solution.py:113
  7.6 0.0 collective-permute-start
  7.6 5.0 %shard_map.114 = (bf16[16,4,128,128]{3,2,1,0:T(8,128)(2,1)S(1)}, bf16[16,4,128,128]{3,2,1,0:T(8,128)(2,1)S(1)}, bf16[4,2048,128]{2,1,0:T(8,128)(2,1)S(1)}, bf16[3,4,2048,128]{3,2,1,0:T(8,128)(2,1)S(1)}) custom-call(s32[4,16]{1,0:T(4,128)} %bitcast.15, bf16[16,512,128]{2,1,0:T(8,128)(2,1)} %bitcast.20, bf16[16,512,128]{2,1,0:T(8,128)(2,1)} %bitcast.21, ...), custom_call_target="tpu_custom_call" | custom-call | bytes 10485760 | tf_op jit(solution)/shard_map/pallas_call | solution.py:427
  12.6 0.0 copy-start
  12.6 0.0 copy-start.2
  12.6 0.0 copy-start.3
  12.6 0.0 copy-start.4
  12.6 2.7 %shard_map.115.moments = f32[3,512,512]{2,1,0:T(8,128)S(1)} custom-call(bf16[4,2048,128]{2,1,0:T(8,128)(2,1)S(1)} %get-tuple-element.30.weighted, bf16[3,4,2048,128]{3,2,1,0:T(8,128)(2,1)S(1)} %get-tuple-element.31.grads), custom_call_target="tpu_custom_call" | custom-call | flops 3221225472 | tf_op jit(solution)/shard_map/pallas_call | solution.py:470
  15.3 0.0 collective-permute-done.rest_1_
  15.3 0.0 collective-permute-done.1.rest_2_
  15.3 0.1 collective-permute-start.3
  15.4 0.5 %collective-permute-start.2 = (bf16[5,64,128]{2,1,0:T(8,128)(2,1)S(1)}, bf16[5,64,128]{2,1,0:T(8,128)(2,1)S(1)}, u32[]{:S(2)}, u32[]{:S(2)}) collective-permute-start(bf16[5,64,128]{2,1,0:T(8,128)(2,1)S(1)} %collective-permute-done.rest_1_), channel_id=1, source_target_pairs={{0,1},{1,0},{2,3},{3,2},{4,5},{5,4},{6,7},{7,6},{8,9},{9,8},{10,11... | collective-permute-start | bytes 245768 | tf_op jit(solution)/shard_map/ppermute | solution.py:655
  15.9 0.0 copy-done
  15.9 0.0 copy-done.2
  15.9 0.0 copy-done.3
  15.9 0.0 copy-done.4
  15.9 1.0 %shard_map.116 = (bf16[768,640]{1,0:T(8,128)(2,1)S(1)}, f32[3,128,128]{2,1,0:T(8,128)S(1)}) custom-call(s32[4,4]{1,0:T(4,128)S(1)} %copy-done, s32[60,128]{1,0:T(8,128)S(1)} %bitcast.17, s32[1,16]{1,0:T(1,128)S(1)} %bitcast.18, f32[3,16,128]{2,1,0:T(8,128)S(1)} %copy-done.3), custom_call_target="tpu_custom_call" | custom-call | flops 1000000000 | bytes 196608 | tf_op jit(solution)/shard_map/pallas_call | solution.py:504
  16.9 0.0 collective-permute-done.2.rest_3_
  16.9 0.0 collective-permute-done.3.rest_4_
  16.9 0.0 copy-start.1
  16.9 2.6 %shard_map.117 = (bf16[16,4,128,128]{3,2,1,0:T(8,128)(2,1)S(1)}, f32[4,3,192]{2,1,0:T(4,128)S(1)}) custom-call(s32[4,4]{1,0:T(4,128)S(1)} %copy-done, bf16[16,4,128,128]{3,2,1,0:T(8,128)(2,1)S(1)} %get-tuple-element.32.basis, bf16[16,4,128,128]{3,2,1,0:T(8,128)(2,1)S(1)} %get-tuple-element.33.field, f32[3,512,512]{2,1,0:T(8,128)S(1)} %shard_map.115.moments, ...), custom_call_target="tpu_custom_call" | custom-call | tf_op jit(solution)/shard_map/pallas_call | solution.py:597
  19.5 1.4 %collective-permute-start.4 = (f32[3,192]{1,0:T(4,128)S(1)}, f32[3,192]{1,0:T(4,128)S(1)}, u32[]{:S(2)}, u32[]{:S(2)}) collective-permute-start(f32[3,192]{1,0:T(4,128)S(1)} %get-tuple-element.52), channel_id=1, source_target_pairs={{0,3},{1,2},{2,1},{3,0},{4,7},{5,6},{6,5},{7,4},{8,11},{9,10},{10,... | collective-permute-start | bytes 6920 | tf_op jit(solution)/shard_map/ppermute | solution.py:667
  20.9 0.5 %collective-permute-start.5 = (f32[3,192]{1,0:T(4,128)S(1)}, f32[3,192]{1,0:T(4,128)S(1)}, u32[]{:S(2)}, u32[]{:S(2)}) collective-permute-start(f32[3,192]{1,0:T(4,128)S(1)} %get-tuple-element.51), channel_id=1, source_target_pairs={{0,2},{1,3},{2,0},{3,1},{4,6},{5,7},{6,4},{7,5},{8,10},{9,11},{10,... | collective-permute-start | bytes 6920 | tf_op jit(solution)/shard_map/ppermute | solution.py:667
  21.4 0.0 collective-permute-start.6
  21.4 0.0 copy-done.1
  21.4 2.1 %shard_map.118 = bf16[16,512,128]{2,1,0:T(8,128)(2,1)} custom-call(s32[4,16]{1,0:T(4,128)S(1)} %bitcast.16, bf16[16,4,128,128]{3,2,1,0:T(8,128)(2,1)S(1)} %get-tuple-element.42.product), custom_call_target="tpu_custom_call" | custom-call | bytes 4194304 | tf_op jit(solution)/shard_map/pallas_call | solution.py:637
  23.5 0.0 collective-permute-done.4
  23.5 1.0 %collective-permute-done.5 = f32[3,192]{1,0:T(4,128)S(1)} collective-permute-done((f32[3,192]{1,0:T(4,128)S(1)}, f32[3,192]{1,0:T(4,128)S(1)}, u32[]{:S(2)}, u32[]{:S(2)}) %collective-permute-start.5) | collective-permute-done | bytes 2336 | tf_op jit(solution)/shard_map/ppermute | solution.py:667
  24.5 0.0 collective-permute-done.6
  24.5 2.1 %collective-permute-start.7 = (f32[3,192]{1,0:T(4,128)S(1)}, f32[3,192]{1,0:T(4,128)S(1)}, u32[]{:S(2)}, u32[]{:S(2)}) collective-permute-start(f32[3,192]{1,0:T(4,128)S(1)} %add_add_fusion.1), channel_id=1, source_target_pairs={{0,12},{4,8},{8,4},{12,0},{1,13},{5,9},{9,5},{13,1},{2,14},{6,10},... | collective-permute-start | bytes 6920 | tf_op jit(solution)/shard_map/ppermute | solution.py:667
  26.6 1.5 %collective-permute-start.8 = (f32[3,192]{1,0:T(4,128)S(1)}, f32[3,192]{1,0:T(4,128)S(1)}, u32[]{:S(2)}, u32[]{:S(2)}) collective-permute-start(f32[3,192]{1,0:T(4,128)S(1)} %add_add_fusion.1), channel_id=1, source_target_pairs={{0,8},{4,12},{8,0},{12,4},{1,9},{5,13},{9,1},{13,5},{2,10},{6,14},... | collective-permute-start | bytes 6920 | tf_op jit(solution)/shard_map/ppermute | solution.py:667
  28.1 0.9 %collective-permute-start.9 = (f32[3,192]{1,0:T(4,128)S(1)}, f32[3,192]{1,0:T(4,128)S(1)}, u32[]{:S(2)}, u32[]{:S(2)}) collective-permute-start(f32[3,192]{1,0:T(4,128)S(1)} %add_add_fusion.1), channel_id=1, source_target_pairs={{0,4},{4,0},{8,12},{12,8},{1,5},{5,1},{9,13},{13,9},{2,6},{6,2},{1... | collective-permute-start | bytes 6920 | tf_op jit(solution)/shard_map/ppermute | solution.py:667
  29.0 1.0 %collective-permute-done.7 = f32[3,192]{1,0:T(4,128)S(1)} collective-permute-done((f32[3,192]{1,0:T(4,128)S(1)}, f32[3,192]{1,0:T(4,128)S(1)}, u32[]{:S(2)}, u32[]{:S(2)}) %collective-permute-start.7) | collective-permute-done | bytes 2336 | tf_op jit(solution)/shard_map/ppermute | solution.py:667
  30.0 1.1 %collective-permute-done.8 = f32[3,192]{1,0:T(4,128)S(1)} collective-permute-done((f32[3,192]{1,0:T(4,128)S(1)}, f32[3,192]{1,0:T(4,128)S(1)}, u32[]{:S(2)}, u32[]{:S(2)}) %collective-permute-start.8) | collective-permute-done | bytes 2336 | tf_op jit(solution)/shard_map/ppermute | solution.py:667
  31.1 0.6 %collective-permute-done.9 = f32[3,192]{1,0:T(4,128)S(1)} collective-permute-done((f32[3,192]{1,0:T(4,128)S(1)}, f32[3,192]{1,0:T(4,128)S(1)}, u32[]{:S(2)}, u32[]{:S(2)}) %collective-permute-start.9) | collective-permute-done | bytes 2336 | tf_op jit(solution)/shard_map/ppermute | solution.py:667
  31.7 0.6 %add_add_fusion = f32[3,192]{1,0:T(4,128)} fusion(f32[3,192]{1,0:T(4,128)S(1)} %collective-permute-done.8, f32[3,192]{1,0:T(4,128)S(1)} %collective-permute-done.9, f32[3,192]{1,0:T(4,128)S(1)} %add_add_fusion.1, f32[3,192]{1,0:T(4,128)S(1)} %collective-permute-done.7), kind=kLoop, calls=%fused_computation | loop fusion | flops 1728 | bytes 11520 | tf_op jit(solution)/shard_map/add | solution.py:662
  (2 shorter events, 0.0 us)
Async XLA Ops:
  2.5 12.8 %collective-permute-start.1 = (bf16[5,128,128]{2,1,0:T(8,128)(2,1)S(1)}, bf16[5,128,128]{2,1,0:T(8,128)(2,1)S(1)}, u32[]{:S(2)}, u32[]{:S(2)}) collective-permute-start(bf16[5,128,128]{2,1,0:T(8,128)(2,1)S(1)} %get-tuple-element.27), channel_id=1, source_target_pairs={{0,12},{1,9},{2,14},{3,11},{4,8},{5,13},{6,10},{7,15},{8,4},{9,1},... | collective-permute-start | bytes 491528 | tf_op jit(solution)/shard_map/ppermute | solution.py:113
  7.6 7.7 %collective-permute-start = (bf16[5,64,128]{2,1,0:T(8,128)(2,1)S(1)}, bf16[5,64,128]{2,1,0:T(8,128)(2,1)S(1)}, u32[]{:S(2)}, u32[]{:S(2)}) collective-permute-start(bf16[5,64,128]{2,1,0:T(8,128)(2,1)S(1)} %get-tuple-element.26), channel_id=1, source_target_pairs={{0,4},{1,5},{2,6},{3,7},{4,0},{5,1},{6,2},{7,3},{8,12},{9,13},{10,... | collective-permute-start | bytes 245768 | tf_op jit(solution)/shard_map/ppermute | solution.py:113
  12.6 3.3 %copy-start = (s32[4,4]{1,0:T(4,128)S(1)}, s32[4,4]{1,0:T(4,128)}, u32[]{:S(2)}) copy-start(s32[4,4]{1,0:T(4,128)} %region.3) | copy-start | bytes 196
  12.6 3.3 %copy-start.2 = (s32[7680]{0:T(1024)S(1)}, s32[7680]{0:T(1024)}, u32[]{:S(2)}) copy-start(s32[7680]{0:T(1024)} %param.18) | copy-start | bytes 92164
  12.6 3.3 %copy-start.3 = (f32[3,16,128]{2,1,0:T(8,128)S(1)}, f32[3,16,128]{2,1,0:T(8,128)}, u32[]{:S(2)}) copy-start(f32[3,16,128]{2,1,0:T(8,128)} %weight_grad.1) | copy-start | bytes 73732
  12.6 3.3 %copy-start.4 = (s32[16]{0:T(128)S(1)}, s32[16]{0:T(128)}, u32[]{:S(2)}) copy-start(s32[16]{0:T(128)} %param.19) | copy-start | bytes 196
  15.3 1.6 %collective-permute-start.3 = (bf16[5,128,128]{2,1,0:T(8,128)(2,1)S(1)}, bf16[5,128,128]{2,1,0:T(8,128)(2,1)S(1)}, u32[]{:S(2)}, u32[]{:S(2)}) collective-permute-start(bf16[5,128,128]{2,1,0:T(8,128)(2,1)S(1)} %collective-permute-done.1.rest_2_), channel_id=1, source_target_pairs={{0,1},{1,0},{2,3},{3,2},{4,5},{5,4},{6,7},{7,6},{8,9},{9,8},{10,11... | collective-permute-start | bytes 491528 | tf_op jit(solution)/shard_map/ppermute | solution.py:655
  15.4 1.5 %collective-permute-start.2 = (bf16[5,64,128]{2,1,0:T(8,128)(2,1)S(1)}, bf16[5,64,128]{2,1,0:T(8,128)(2,1)S(1)}, u32[]{:S(2)}, u32[]{:S(2)}) collective-permute-start(bf16[5,64,128]{2,1,0:T(8,128)(2,1)S(1)} %collective-permute-done.rest_1_), channel_id=1, source_target_pairs={{0,1},{1,0},{2,3},{3,2},{4,5},{5,4},{6,7},{7,6},{8,9},{9,8},{10,11... | collective-permute-start | bytes 245768 | tf_op jit(solution)/shard_map/ppermute | solution.py:655
  16.9 4.6 %copy-start.1 = (s32[16,4]{0,1:T(4,128)S(1)}, s32[16,4]{0,1:T(4,128)}, u32[]{:S(2)}) copy-start(s32[16,4]{0,1:T(4,128)} %param.17) | copy-start | bytes 772
  19.5 4.0 %collective-permute-start.4 = (f32[3,192]{1,0:T(4,128)S(1)}, f32[3,192]{1,0:T(4,128)S(1)}, u32[]{:S(2)}, u32[]{:S(2)}) collective-permute-start(f32[3,192]{1,0:T(4,128)S(1)} %get-tuple-element.52), channel_id=1, source_target_pairs={{0,3},{1,2},{2,1},{3,0},{4,7},{5,6},{6,5},{7,4},{8,11},{9,10},{10,... | collective-permute-start | bytes 6920 | tf_op jit(solution)/shard_map/ppermute | solution.py:667
  20.9 3.6 %collective-permute-start.5 = (f32[3,192]{1,0:T(4,128)S(1)}, f32[3,192]{1,0:T(4,128)S(1)}, u32[]{:S(2)}, u32[]{:S(2)}) collective-permute-start(f32[3,192]{1,0:T(4,128)S(1)} %get-tuple-element.51), channel_id=1, source_target_pairs={{0,2},{1,3},{2,0},{3,1},{4,6},{5,7},{6,4},{7,5},{8,10},{9,11},{10,... | collective-permute-start | bytes 6920 | tf_op jit(solution)/shard_map/ppermute | solution.py:667
  21.4 3.1 %collective-permute-start.6 = (f32[3,192]{1,0:T(4,128)S(1)}, f32[3,192]{1,0:T(4,128)S(1)}, u32[]{:S(2)}, u32[]{:S(2)}) collective-permute-start(f32[3,192]{1,0:T(4,128)S(1)} %get-tuple-element.50), channel_id=1, source_target_pairs={{0,1},{1,0},{2,3},{3,2},{4,5},{5,4},{6,7},{7,6},{8,9},{9,8},{10,11... | collective-permute-start | bytes 6920 | tf_op jit(solution)/shard_map/ppermute | solution.py:667
  24.5 5.5 %collective-permute-start.7 = (f32[3,192]{1,0:T(4,128)S(1)}, f32[3,192]{1,0:T(4,128)S(1)}, u32[]{:S(2)}, u32[]{:S(2)}) collective-permute-start(f32[3,192]{1,0:T(4,128)S(1)} %add_add_fusion.1), channel_id=1, source_target_pairs={{0,12},{4,8},{8,4},{12,0},{1,13},{5,9},{9,5},{13,1},{2,14},{6,10},... | collective-permute-start | bytes 6920 | tf_op jit(solution)/shard_map/ppermute | solution.py:667
  26.6 4.5 %collective-permute-start.8 = (f32[3,192]{1,0:T(4,128)S(1)}, f32[3,192]{1,0:T(4,128)S(1)}, u32[]{:S(2)}, u32[]{:S(2)}) collective-permute-start(f32[3,192]{1,0:T(4,128)S(1)} %add_add_fusion.1), channel_id=1, source_target_pairs={{0,8},{4,12},{8,0},{12,4},{1,9},{5,13},{9,1},{13,5},{2,10},{6,14},... | collective-permute-start | bytes 6920 | tf_op jit(solution)/shard_map/ppermute | solution.py:667
  28.1 3.6 %collective-permute-start.9 = (f32[3,192]{1,0:T(4,128)S(1)}, f32[3,192]{1,0:T(4,128)S(1)}, u32[]{:S(2)}, u32[]{:S(2)}) collective-permute-start(f32[3,192]{1,0:T(4,128)S(1)} %add_add_fusion.1), channel_id=1, source_target_pairs={{0,4},{4,0},{8,12},{12,8},{1,5},{5,1},{9,13},{13,9},{2,6},{6,2},{1... | collective-permute-start | bytes 6920 | tf_op jit(solution)/shard_map/ppermute | solution.py:667

commit v18 on v17

--- a/solution.py
+++ b/solution.py
@@ -38,6 +38,12 @@
 
 def partners(slabs):
     return [(1, 1)] + [(shift + 1, shift) for shift in range(2, slabs, 2)]
+
+
+def moves_over_grid(shifts, slabs, atom_devices):
+    return [
+        (z * atom_devices + a, (z ^ shifts[a % 2]) * atom_devices + a) for z in range(slabs) for a in range(atom_devices)
+    ]
 
 
 def send_kernel(region_hbm, density, *rest):
@@ -107,10 +113,7 @@
     own, *outgoing = rows_to_send(region, density, slabs)
     near = []
     for shifts, piece in zip(partners(slabs), outgoing):
-        moves = [
-            (z * atom_devices + a, (z ^ shifts[a % 2]) * atom_devices + a) for z in range(slabs) for a in range(atom_devices)
-        ]
-        near.append(lax.ppermute(piece, ("grid", "atoms"), moves))
+        near.append(lax.ppermute(piece, ("grid", "atoms"), moves_over_grid(shifts, slabs, atom_devices)))
     return own, near
 
 
@@ -274,7 +277,9 @@
             for c in range(PARTS):
                 value = found[c : c + 1] + found[PARTS + c : PARTS + c + 1] + found[2 * PARTS + c : 2 * PARTS + c + 1]
                 value = value + jnp.sum(jnp.where(mine, scale[c], 0.0), axis=0, keepdims=True)
-                out[jnp.bitwise_xor(me_atoms, device), c : c + 1, :] = value
+                place = jnp.bitwise_xor(me_atoms, device)
+                out[place, 0, c : c + 1, :] = value
+                out[jnp.bitwise_xor(place, 1), 1, c : c + 1, :] = value
 
 
 def partial_gradient(
@@ -290,7 +295,7 @@
     block = pl.BlockSpec((1, points, columns), lambda b, *_: (b, 0, 0))
     whole = pl.BlockSpec(memory_space=pltpu.VMEM)
     tile_shape = (region_size * width + 1, size, size)
-    out_shape = (atom_devices, PARTS, atom_total // atom_devices)
+    out_shape = (atom_devices, 2, PARTS, atom_total // atom_devices)
     return pl.pallas_call(
         functools.partial(
             gradient_kernel, points=points, blocks=blocks, width=width, owner_rows=owner_rows, slabs=slabs
@@ -585,7 +590,9 @@
             left, hot[device * chunk : (device + 1) * chunk, :], NT, preferred_element_type=F32
         )
         value = sums[:PARTS] + sums[PARTS : 2 * PARTS] + sums[2 * PARTS : 3 * PARTS]
-        out[jnp.bitwise_xor(me_atoms, device)] = value
+        place = jnp.bitwise_xor(me_atoms, device)
+        out[place, 0] = value
+        out[jnp.bitwise_xor(place, 1), 1] = value
 
 
 def combine(region, prepared, pieces, shapes):
@@ -598,7 +605,7 @@
         functools.partial(combine_kernel, owner_rows=owner_rows, slabs=slabs, width=width, step=step),
         out_shape=(
             jax.ShapeDtypeStruct(basis.shape, BF16),
-            jax.ShapeDtypeStruct((atom_devices, PARTS, atom_total // atom_devices), F32),
+            jax.ShapeDtypeStruct((atom_devices, 2, PARTS, atom_total // atom_devices), F32),
         ),
         in_specs=[pl.BlockSpec(memory_space=pltpu.SMEM)] + [vmem] * (5 + len(pieces)),
         out_specs=(vmem, vmem),
@@ -662,18 +669,26 @@
     return tree_sum(values[:half]) + tree_sum(values[half:])
 
 
-def exchange_all(parts, axis, count):
-    return [parts[0]] + [
-        lax.ppermute(parts[d], axis, [(i, i ^ d) for i in range(count)]) for d in range(count - 1, 0, -1)
-    ]
+def pair_sums(values):
+    return [values[i] + values[i + 1] for i in range(0, len(values), 2)]
 
 
 def sum_parts(partial_grad, contracted, slabs, atom_devices):
-    parts = exchange_all([partial_grad[d] for d in range(atom_devices)], "atoms", atom_devices)
+    parts = [partial_grad[0]]
+    for d in range(1, atom_devices):
+        parts.append(lax.ppermute(partial_grad[d], "atoms", [(i, i ^ d) for i in range(atom_devices)]))
     parts, contracted = lax.optimization_barrier((parts, contracted))
-    own, *far, near = exchange_all([tree_sum(parts)] * slabs, "grid", slabs)
+    both = tree_sum(pair_sums(parts))
+    swap = [(i, i ^ 1) for i in range(atom_devices)]
+    far = []
+    for shifts in partners(slabs):
+        if shifts[0] != shifts[1]:
+            far.append(lax.ppermute(both, ("grid", "atoms"), moves_over_grid(shifts, slabs, atom_devices)))
+    near = lax.ppermute(both[0], "grid", [(i, i ^ 1) for i in range(slabs)])
     far = lax.optimization_barrier(far)
-    return tree_sum([own, *far, near]), contracted
+    swapped = [lax.ppermute(piece[1], "atoms", swap) for piece in far]
+    sums = [both[0] + near] + [piece[0] + other for piece, other in zip(far, swapped)]
+    return tree_sum(sums), contracted
 
 
 def local(

time: 32.5 us -> 31.9 us (0.982)
  starting transfers between devices: 12.1 us -> 9.8 us
  waiting for transfers between devices: 3.73 us -> 5.4 us
    ppermute x8, starting transfers between devices: 11.5 us -> 9.23 us  [the longest x2 5.12 us: fetch_rows(): lax.ppermute(piece, ('grid', 'atoms'), moves_over_grid(shifts, slabs, ato...]
    ppermute x8, waiting for transfers between devices: 3.71 us -> 5.38 us  [the longest x1 3.33 us: sum_parts(): lax.ppermute(both, ('grid', 'atoms'), moves_over_grid(shifts, slabs, atom...]
  transfers between devices with their start and end apart: 10 -> 10, of which waited for: 4 -> 4; matrix products, arithmetic and copies ran while one was open for 0% -> 0% of each run, Pallas kernels for 33% -> 34%
where the time goes in v18:
time: 31.9 us; the launch traced here: 31.7 us
  Pallas kernels  15 us (47%)
  starting transfers between devices  9.8 us (31%)
  waiting for transfers between devices  5.4 us (17%)
  between operations  0.77 us (2%)
  other arithmetic  0.6 us (2%)
    ppermute x2, starting transfers between devices, fetch_rows(): lax.ppermute(piece, ('grid', 'atoms'), moves_over_grid(shifts, slabs, ato...  5.12 us
    pallas_call x1, Pallas kernels, reorder(): pl.pallas_call(reorder_kernel, out_shape=(ordered, ordered, jax.ShapeDtyp...  4.98 us
    ppermute x1, waiting for transfers between devices, sum_parts(): lax.ppermute(both, ('grid', 'atoms'), moves_over_grid(shifts, slabs, atom...  3.33 us
    pallas_call x1, Pallas kernels, build_moments(): pl.pallas_call(moment_kernel, out_shape=jax.ShapeDtypeStruct((PARTS, bloc...  2.66 us
    pallas_call x1, Pallas kernels, combine(): pl.pallas_call(functools.partial(combine_kernel, owner_rows=owner_rows, s...  2.56 us
    pallas_call x1, Pallas kernels, write(): pl.pallas_call(write_kernel, out_shape=jax.ShapeDtypeStruct(shape, BF16),...  2.06 us
    ppermute x1, starting transfers between devices, sum_parts(): lax.ppermute(both, ('grid', 'atoms'), moves_over_grid(shifts, slabs, atom...  2.06 us
    ppermute x3, starting transfers between devices, sum_parts(): lax.ppermute(partial_grad[d], 'atoms', [(i, i ^ d) for i in range(atom_de...  1.93 us
  transfers between devices with their start and end apart: 10, of which 4 were waited for; matrix products, arithmetic and copies ran while one was open for 0% of the time, Pallas kernels for 34%

profile of v18, /device:TPU:0, one launch (start us, length us, event | category | flops | bytes accessed | tf_op | source)
XLA Modules:
  0.0 31.7 jit_solution(1737708827358520182)
XLA Ops:
  0.6 1.8 %shard_map.113 = (bf16[5,128,128]{2,1,0:T(8,128)(2,1)S(1)}, bf16[5,64,128]{2,1,0:T(8,128)(2,1)S(1)}, bf16[5,128,128]{2,1,0:T(8,128)(2,1)S(1)}) custom-call(s32[4,4]{1,0:T(4,128)} %region.3, bf16[15,3,128,128]{3,2,1,0:T(8,128)(2,1)} %density.1), custom_call_target="tpu_custom_call" | custom-call | tf_op jit(solution)/shard_map/pallas_call | solution.py:98
  2.5 5.1 %collective-permute-start.1 = (bf16[5,128,128]{2,1,0:T(8,128)(2,1)S(1)}, bf16[5,128,128]{2,1,0:T(8,128)(2,1)S(1)}, u32[]{:S(2)}, u32[]{:S(2)}) collective-permute-start(bf16[5,128,128]{2,1,0:T(8,128)(2,1)S(1)} %get-tuple-element.25), channel_id=1, source_target_pairs={{0,12},{1,9},{2,14},{3,11},{4,8},{5,13},{6,10},{7,15},{8,4},{9,1},... | collective-permute-start | bytes 491528 | tf_op jit(solution)/shard_map/ppermute | solution.py:116
  7.6 0.0 collective-permute-start
  7.6 5.0 %shard_map.114 = (bf16[16,4,128,128]{3,2,1,0:T(8,128)(2,1)S(1)}, bf16[16,4,128,128]{3,2,1,0:T(8,128)(2,1)S(1)}, bf16[4,2048,128]{2,1,0:T(8,128)(2,1)S(1)}, bf16[3,4,2048,128]{3,2,1,0:T(8,128)(2,1)S(1)}) custom-call(s32[4,16]{1,0:T(4,128)} %bitcast.27, bf16[16,512,128]{2,1,0:T(8,128)(2,1)} %bitcast.32, bf16[16,512,128]{2,1,0:T(8,128)(2,1)} %bitcast.33, ...), custom_call_target="tpu_custom_call" | custom-call | bytes 10485760 | tf_op jit(solution)/shard_map/pallas_call | solution.py:432
  12.6 0.0 copy-start
  12.6 0.0 copy-start.2
  12.6 0.0 copy-start.3
  12.6 0.0 copy-start.4
  12.6 2.7 %shard_map.115.moments = f32[3,512,512]{2,1,0:T(8,128)S(1)} custom-call(bf16[4,2048,128]{2,1,0:T(8,128)(2,1)S(1)} %get-tuple-element.28.weighted, bf16[3,4,2048,128]{3,2,1,0:T(8,128)(2,1)S(1)} %get-tuple-element.29.grads), custom_call_target="tpu_custom_call" | custom-call | flops 3221225472 | tf_op jit(solution)/shard_map/pallas_call | solution.py:475
  15.3 0.0 collective-permute-done.rest_1_
  15.3 0.0 collective-permute-done.1.rest_2_
  15.3 0.1 collective-permute-start.3
  15.4 0.5 %collective-permute-start.2 = (bf16[5,64,128]{2,1,0:T(8,128)(2,1)S(1)}, bf16[5,64,128]{2,1,0:T(8,128)(2,1)S(1)}, u32[]{:S(2)}, u32[]{:S(2)}) collective-permute-start(bf16[5,64,128]{2,1,0:T(8,128)(2,1)S(1)} %collective-permute-done.rest_1_), channel_id=1, source_target_pairs={{0,1},{1,0},{2,3},{3,2},{4,5},{5,4},{6,7},{7,6},{8,9},{9,8},{10,11... | collective-permute-start | bytes 245768 | tf_op jit(solution)/shard_map/ppermute | solution.py:662
  15.9 0.0 copy-done
  15.9 0.0 copy-done.2
  15.9 0.0 copy-done.3
  15.9 0.0 copy-done.4
  15.9 1.0 %shard_map.116 = (bf16[768,640]{1,0:T(8,128)(2,1)S(1)}, f32[3,128,128]{2,1,0:T(8,128)S(1)}) custom-call(s32[4,4]{1,0:T(4,128)S(1)} %copy-done, s32[60,128]{1,0:T(8,128)S(1)} %bitcast.29, s32[1,16]{1,0:T(1,128)S(1)} %bitcast.30, f32[3,16,128]{2,1,0:T(8,128)S(1)} %copy-done.3), custom_call_target="tpu_custom_call" | custom-call | flops 1000000000 | bytes 196608 | tf_op jit(solution)/shard_map/pallas_call | solution.py:509
  16.9 0.0 collective-permute-done.2.rest_3_
  16.9 0.0 collective-permute-done.3.rest_4_
  16.9 0.0 copy-start.1
  16.9 2.6 %shard_map.117 = (bf16[16,4,128,128]{3,2,1,0:T(8,128)(2,1)S(1)}, f32[4,2,3,192]{3,2,1,0:T(4,128)S(1)}) custom-call(s32[4,4]{1,0:T(4,128)S(1)} %copy-done, bf16[16,4,128,128]{3,2,1,0:T(8,128)(2,1)S(1)} %get-tuple-element.30.basis, bf16[16,4,128,128]{3,2,1,0:T(8,128)(2,1)S(1)} %get-tuple-element.31.field, f32[3,512,512]{2,1,0:T(8,128)S(1)} %shard_map.115.moments, ...), custom_call_target="tpu_custom_call" | custom-call | tf_op jit(solution)/shard_map/pallas_call | solution.py:604
  19.5 0.3 %collective-permute-start.4 = (f32[2,3,192]{2,1,0:T(4,128)S(1)}, f32[2,3,192]{2,1,0:T(4,128)S(1)}, u32[]{:S(2)}, u32[]{:S(2)}) collective-permute-start(f32[2,3,192]{2,1,0:T(4,128)S(1)} %get-tuple-element.48), channel_id=1, source_target_pairs={{0,1},{1,0},{2,3},{3,2},{4,5},{5,4},{6,7},{7,6},{8,9},{9,8},{10,11... | collective-permute-start | bytes 13832 | tf_op jit(solution)/shard_map/ppermute | solution.py:679
  19.8 1.5 %collective-permute-start.5 = (f32[2,3,192]{2,1,0:T(4,128)S(1)}, f32[2,3,192]{2,1,0:T(4,128)S(1)}, u32[]{:S(2)}, u32[]{:S(2)}) collective-permute-start(f32[2,3,192]{2,1,0:T(4,128)S(1)} %get-tuple-element.47), channel_id=1, source_target_pairs={{0,2},{1,3},{2,0},{3,1},{4,6},{5,7},{6,4},{7,5},{8,10},{9,11},{10,... | collective-permute-start | bytes 13832 | tf_op jit(solution)/shard_map/ppermute | solution.py:679
  21.3 0.1 collective-permute-start.6
  21.4 0.0 copy-done.1
  21.4 2.1 %shard_map.118 = bf16[16,512,128]{2,1,0:T(8,128)(2,1)} custom-call(s32[4,16]{1,0:T(4,128)S(1)} %bitcast.28, bf16[16,4,128,128]{3,2,1,0:T(8,128)(2,1)S(1)} %get-tuple-element.40.product), custom_call_target="tpu_custom_call" | custom-call | bytes 4194304 | tf_op jit(solution)/shard_map/pallas_call | solution.py:644
  23.5 0.0 collective-permute-done.4
  23.5 0.0 collective-permute-done.5
  23.5 0.9 %collective-permute-done.6 = f32[2,3,192]{2,1,0:T(4,128)S(1)} collective-permute-done((f32[2,3,192]{2,1,0:T(4,128)S(1)}, f32[2,3,192]{2,1,0:T(4,128)S(1)}, u32[]{:S(2)}, u32[]{:S(2)}) %collective-permute-start.6) | collective-permute-done | bytes 4640 | tf_op jit(solution)/shard_map/ppermute | solution.py:679
  24.4 2.1 %collective-permute-start.8 = (f32[2,3,192]{2,1,0:T(4,128)S(1)}, f32[2,3,192]{2,1,0:T(4,128)S(1)}, u32[]{:S(2)}, u32[]{:S(2)}) collective-permute-start(f32[2,3,192]{2,1,0:T(4,128)S(1)} %add_add_fusion), channel_id=1, source_target_pairs={{0,12},{1,9},{2,14},{3,11},{4,8},{5,13},{6,10},{7,15},{8,4},{9,1},... | collective-permute-start | bytes 13832 | tf_op jit(solution)/shard_map/ppermute | solution.py:686
  26.4 0.1 collective-permute-start.7
  26.6 3.3 %collective-permute-done.8 = f32[2,3,192]{2,1,0:T(4,128)S(1)} collective-permute-done((f32[2,3,192]{2,1,0:T(4,128)S(1)}, f32[2,3,192]{2,1,0:T(4,128)S(1)}, u32[]{:S(2)}, u32[]{:S(2)}) %collective-permute-start.8) | collective-permute-done | bytes 4640 | tf_op jit(solution)/shard_map/ppermute | solution.py:686
  29.9 0.0 collective-permute-start.9
  29.9 0.2 collective-permute-done.7
  30.1 1.0 %collective-permute-done.9 = f32[3,192]{1,0:T(4,128)S(1)} collective-permute-done((f32[3,192]{1,0:T(4,128)S(1)}, f32[3,192]{1,0:T(4,128)S(1)}, u32[]{:S(2)}, u32[]{:S(2)}) %collective-permute-start.9) | collective-permute-done | bytes 2336 | tf_op jit(solution)/shard_map/ppermute | solution.py:689
  31.1 0.6 %fusion.1 = f32[3,192]{1,0:T(4,128)} fusion(f32[3,192]{1,0:T(4,128)S(1)} %collective-permute-done.9, f32[2,3,192]{2,1,0:T(4,128)S(1)} %collective-permute-done.8, f32[3,192]{1,0:T(4,128)S(1)} %collective-permute-done.7, f32[2,3,192]{2,1,0:T(4,128)S(1)} %add_add_fusion), kind=kLoop, calls=%fused_computation.8 | loop fusion | flops 1728 | bytes 11520 | tf_op jit(solution)/shard_map/add | solution.py:669
  (4 shorter events, 0.0 us)
Async XLA Ops:
  2.5 12.8 %collective-permute-start.1 = (bf16[5,128,128]{2,1,0:T(8,128)(2,1)S(1)}, bf16[5,128,128]{2,1,0:T(8,128)(2,1)S(1)}, u32[]{:S(2)}, u32[]{:S(2)}) collective-permute-start(bf16[5,128,128]{2,1,0:T(8,128)(2,1)S(1)} %get-tuple-element.25), channel_id=1, source_target_pairs={{0,12},{1,9},{2,14},{3,11},{4,8},{5,13},{6,10},{7,15},{8,4},{9,1},... | collective-permute-start | bytes 491528 | tf_op jit(solution)/shard_map/ppermute | solution.py:116
  7.6 7.7 %collective-permute-start = (bf16[5,64,128]{2,1,0:T(8,128)(2,1)S(1)}, bf16[5,64,128]{2,1,0:T(8,128)(2,1)S(1)}, u32[]{:S(2)}, u32[]{:S(2)}) collective-permute-start(bf16[5,64,128]{2,1,0:T(8,128)(2,1)S(1)} %get-tuple-element.24), channel_id=1, source_target_pairs={{0,4},{1,5},{2,6},{3,7},{4,0},{5,1},{6,2},{7,3},{8,12},{9,13},{10,... | collective-permute-start | bytes 245768 | tf_op jit(solution)/shard_map/ppermute | solution.py:116
  12.6 3.3 %copy-start = (s32[4,4]{1,0:T(4,128)S(1)}, s32[4,4]{1,0:T(4,128)}, u32[]{:S(2)}) copy-start(s32[4,4]{1,0:T(4,128)} %region.3) | copy-start | bytes 196
  12.6 3.3 %copy-start.2 = (s32[7680]{0:T(1024)S(1)}, s32[7680]{0:T(1024)}, u32[]{:S(2)}) copy-start(s32[7680]{0:T(1024)} %param.18) | copy-start | bytes 92164
  12.6 3.3 %copy-start.3 = (f32[3,16,128]{2,1,0:T(8,128)S(1)}, f32[3,16,128]{2,1,0:T(8,128)}, u32[]{:S(2)}) copy-start(f32[3,16,128]{2,1,0:T(8,128)} %weight_grad.1) | copy-start | bytes 73732
  12.6 3.3 %copy-start.4 = (s32[16]{0:T(128)S(1)}, s32[16]{0:T(128)}, u32[]{:S(2)}) copy-start(s32[16]{0:T(128)} %param.19) | copy-start | bytes 196
  15.3 1.6 %collective-permute-start.3 = (bf16[5,128,128]{2,1,0:T(8,128)(2,1)S(1)}, bf16[5,128,128]{2,1,0:T(8,128)(2,1)S(1)}, u32[]{:S(2)}, u32[]{:S(2)}) collective-permute-start(bf16[5,128,128]{2,1,0:T(8,128)(2,1)S(1)} %collective-permute-done.1.rest_2_), channel_id=1, source_target_pairs={{0,1},{1,0},{2,3},{3,2},{4,5},{5,4},{6,7},{7,6},{8,9},{9,8},{10,11... | collective-permute-start | bytes 491528 | tf_op jit(solution)/shard_map/ppermute | solution.py:662
  15.4 1.5 %collective-permute-start.2 = (bf16[5,64,128]{2,1,0:T(8,128)(2,1)S(1)}, bf16[5,64,128]{2,1,0:T(8,128)(2,1)S(1)}, u32[]{:S(2)}, u32[]{:S(2)}) collective-permute-start(bf16[5,64,128]{2,1,0:T(8,128)(2,1)S(1)} %collective-permute-done.rest_1_), channel_id=1, source_target_pairs={{0,1},{1,0},{2,3},{3,2},{4,5},{5,4},{6,7},{7,6},{8,9},{9,8},{10,11... | collective-permute-start | bytes 245768 | tf_op jit(solution)/shard_map/ppermute | solution.py:662
  16.9 4.5 %copy-start.1 = (s32[16,4]{0,1:T(4,128)S(1)}, s32[16,4]{0,1:T(4,128)}, u32[]{:S(2)}) copy-start(s32[16,4]{0,1:T(4,128)} %param.17) | copy-start | bytes 772
  19.5 4.0 %collective-permute-start.4 = (f32[2,3,192]{2,1,0:T(4,128)S(1)}, f32[2,3,192]{2,1,0:T(4,128)S(1)}, u32[]{:S(2)}, u32[]{:S(2)}) collective-permute-start(f32[2,3,192]{2,1,0:T(4,128)S(1)} %get-tuple-element.48), channel_id=1, source_target_pairs={{0,1},{1,0},{2,3},{3,2},{4,5},{5,4},{6,7},{7,6},{8,9},{9,8},{10,11... | collective-permute-start | bytes 13832 | tf_op jit(solution)/shard_map/ppermute | solution.py:679
  19.8 3.7 %collective-permute-start.5 = (f32[2,3,192]{2,1,0:T(4,128)S(1)}, f32[2,3,192]{2,1,0:T(4,128)S(1)}, u32[]{:S(2)}, u32[]{:S(2)}) collective-permute-start(f32[2,3,192]{2,1,0:T(4,128)S(1)} %get-tuple-element.47), channel_id=1, source_target_pairs={{0,2},{1,3},{2,0},{3,1},{4,6},{5,7},{6,4},{7,5},{8,10},{9,11},{10,... | collective-permute-start | bytes 13832 | tf_op jit(solution)/shard_map/ppermute | solution.py:679
  21.3 3.1 %collective-permute-start.6 = (f32[2,3,192]{2,1,0:T(4,128)S(1)}, f32[2,3,192]{2,1,0:T(4,128)S(1)}, u32[]{:S(2)}, u32[]{:S(2)}) collective-permute-start(f32[2,3,192]{2,1,0:T(4,128)S(1)} %get-tuple-element.46), channel_id=1, source_target_pairs={{0,3},{1,2},{2,1},{3,0},{4,7},{5,6},{6,5},{7,4},{8,11},{9,10},{10,... | collective-permute-start | bytes 13832 | tf_op jit(solution)/shard_map/ppermute | solution.py:679
  24.4 5.5 %collective-permute-start.8 = (f32[2,3,192]{2,1,0:T(4,128)S(1)}, f32[2,3,192]{2,1,0:T(4,128)S(1)}, u32[]{:S(2)}, u32[]{:S(2)}) collective-permute-start(f32[2,3,192]{2,1,0:T(4,128)S(1)} %add_add_fusion), channel_id=1, source_target_pairs={{0,12},{1,9},{2,14},{3,11},{4,8},{5,13},{6,10},{7,15},{8,4},{9,1},... | collective-permute-start | bytes 13832 | tf_op jit(solution)/shard_map/ppermute | solution.py:686
  26.4 3.6 %collective-permute-start.7 = (f32[3,192]{1,0:T(4,128)S(1)}, f32[3,192]{1,0:T(4,128)S(1)}, u32[]{:S(2)}, u32[]{:S(2)}) collective-permute-start(f32[3,192]{1,0:T(4,128)S(1)} %slice_bitcast_fusion.6), channel_id=1, source_target_pairs={{0,4},{4,0},{8,12},{12,8},{1,5},{5,1},{9,13},{13,9},{2,6},{6,2},{1... | collective-permute-start | bytes 6920 | tf_op jit(solution)/shard_map/ppermute | solution.py:687
  29.9 1.2 %collective-permute-start.9 = (f32[3,192]{1,0:T(4,128)S(1)}, f32[3,192]{1,0:T(4,128)S(1)}, u32[]{:S(2)}, u32[]{:S(2)}) collective-permute-start(f32[3,192]{1,0:T(4,128)S(1)} %slice_bitcast_fusion.4), channel_id=1, source_target_pairs={{0,1},{1,0},{2,3},{3,2},{4,5},{5,4},{6,7},{7,6},{8,9},{9,8},{10,11... | collective-permute-start | bytes 6920 | tf_op jit(solution)/shard_map/ppermute | solution.py:689

commit v19 on v18

--- a/solution.py
+++ b/solution.py
@@ -47,17 +47,24 @@
 
 
 def send_kernel(region_hbm, density, *rest):
-    *outs, region, sems, region_sem = rest
+    *outs, region, held, region_sem, sems = rest
     fetch = pltpu.make_async_copy(region_hbm, region, region_sem)
     fetch.start()
+    count_here = density.shape[0] // sems.shape[0]
+    fetches = []
+    for part in range(sems.shape[0]):
+        here = pl.ds(part * count_here, count_here)
+        fetches.append(pltpu.make_async_copy(density.at[here], held.at[here], sems.at[part]))
+    for copy in fetches:
+        copy.start()
     fetch.wait()
     me = lax.axis_index("grid")
     core = lax.rem(lax.axis_index("atoms"), 2)
     slabs, size = region.shape
     owner_rows = density.shape[0]
     rows = density.shape[-2]
-    copies = []
-    for number, ((low, high), out) in enumerate(zip([(0, 0)] + partners(slabs), outs)):
+    picks = []
+    for low, high in [(0, 0)] + partners(slabs):
         slab = jnp.bitwise_xor(me, jnp.where(core == 0, low, high))
         base = jnp.int32(owner_rows)
         count = jnp.int32(0)
@@ -70,20 +77,16 @@
         after = jnp.minimum(base + 1, owner_rows - 1)
         lower = base == 0
         edge = jnp.where(jnp.logical_and(count == 2, jnp.logical_not(lower)), after, base)
+        picks.append(((base, 1), (base, 2), (after, 0), (after, 1), (edge, jnp.where(lower, 0, 2))))
+    for copy in fetches:
+        copy.wait()
+    for out, places in zip(outs, picks):
         kept = out.shape[1]
-        first = 0 if kept == rows else pl.multiple_of(core * kept, kept)
-        here = pl.ds(first, kept)
-        pairs = (
-            (density.at[base, pl.ds(1, 2), here, :], out.at[pl.ds(0, 2)]),
-            (density.at[after, pl.ds(0, 2), here, :], out.at[pl.ds(2, 2)]),
-            (density.at[edge, jnp.where(lower, 0, 2), here, :], out.at[4]),
-        )
-        for part, (source, target) in enumerate(pairs):
-            copies.append(pltpu.make_async_copy(source, target, sems.at[number, part]))
-    for copy in copies:
-        copy.start()
-    for copy in copies:
-        copy.wait()
+        for place, (row, k) in enumerate(places):
+            if kept == rows:
+                out[place] = held[row, k]
+            else:
+                out[place] = held[row, k, pl.ds(pl.multiple_of(core * kept, kept), kept), :]
 
 
 def in_hbm(array):
@@ -102,8 +105,9 @@
         out_specs=[pl.BlockSpec(memory_space=pltpu.VMEM)] * len(kept),
         scratch_shapes=[
             pltpu.SMEM(region.shape, jnp.int32),
-            pltpu.SemaphoreType.DMA((len(kept), 3)),
+            pltpu.VMEM(density.shape, density.dtype),
             pltpu.SemaphoreType.DMA,
+            pltpu.SemaphoreType.DMA((5 if density.shape[0] % 5 == 0 else 1,)),
         ],
         compiler_params=pltpu.CompilerParams(vmem_limit_bytes=VMEM_LIMIT),
     )(in_hbm(region), in_hbm(density))
@@ -370,6 +374,7 @@
     pattern,
     weights,
     columns,
+    gather,
     basis_in,
     field_in,
     grad_in,
@@ -403,6 +408,12 @@
     rows = jnp.concatenate([weights[...], jnp.zeros((size - batches, points), F32)], axis=0).T
     for batch in range(batches):
         columns[batch] = jnp.broadcast_to(rows[:, batch : batch + 1], (points, size))
+    depth = gather.shape[0]
+    some = depth // blocks
+    source = lax.broadcasted_iota(jnp.int32, (some, depth), 1)
+    target = lax.broadcasted_iota(jnp.int32, (some, depth), 0) * blocks
+    for s in range(blocks):
+        gather[s * some : (s + 1) * some, :] = jnp.where(source == target + s, 1.0, 0.0).astype(BF16)
 
     @pl.loop(0, batches)
     def _(batch):
@@ -410,18 +421,23 @@
             copy.wait()
         points_here = pl.ds(pl.multiple_of(batch * points, points), points)
         places = [pattern[s, batch] for s in range(blocks)]
-        wide[0] = field_in[batch].astype(F32)
-        wide[1] = basis_in[batch].astype(F32)
         for c in range(PARTS):
-            wide[2 + c] = grad_in[c, batch].astype(F32)
+            wide[c] = grad_in[c, batch].astype(F32)
+        for first in range(0, points, some):
+            here = pl.ds(first * blocks, depth)
+            both = jnp.concatenate([field_in[batch, here, :], basis_in[batch, here, :]], axis=1)
+            both = jnp.dot(gather[...], both, preferred_element_type=F32)
+            for s, place in enumerate(places):
+                values = both[s * some : (s + 1) * some, :size]
+                field_out[batch, place, pl.ds(first, some), :] = values.astype(BF16)
+                scaled = values * columns[batch, pl.ds(first, some), :]
+                weighted[place, pl.ds(pl.multiple_of(batch * points + first, some), some), :] = scaled.astype(BF16)
+                values = both[s * some : (s + 1) * some, size:]
+                basis_out[batch, place, pl.ds(first, some), :] = values.astype(BF16)
         for s, place in enumerate(places):
             strided = pl.ds(s, points, stride=blocks)
-            values = wide[0, strided, :]
-            field_out[batch, place] = values.astype(BF16)
-            weighted[place, points_here, :] = (values * columns[batch]).astype(BF16)
-            basis_out[batch, place] = wide[1, strided, :].astype(BF16)
             for c in range(PARTS):
-                grads[c, place, points_here, :] = wide[2 + c, strided, :].astype(BF16)
+                grads[c, place, points_here, :] = wide[c, strided, :].astype(BF16)
 
 
 def reorder(pattern, basis, field, basis_grad, weights, points, blocks):
@@ -443,10 +459,11 @@
             pltpu.SMEM((blocks, batches), jnp.int32),
             pltpu.VMEM(weights.shape, F32),
             pltpu.VMEM((batches, points, size), F32),
+            pltpu.VMEM((min(rows, 256), min(rows, 256)), BF16),
             pltpu.VMEM((batches, rows, size), BF16),
             pltpu.VMEM((batches, rows, size), BF16),
             pltpu.VMEM((PARTS, batches, rows, size), BF16),
-            pltpu.VMEM((2 + PARTS, rows, size), F32),
+            pltpu.VMEM((PARTS, rows, size), F32),
             pltpu.SemaphoreType.DMA((batches, 3)),
             pltpu.SemaphoreType.DMA((2,)),
         ],

time: 31.9 us -> 32.2 us (level)
  Pallas kernels: 15 us -> 15.4 us
    ppermute x1, starting transfers between devices: 2.06 us -> 1.24 us  [sum_parts(): lax.ppermute(both, ('grid', 'atoms'), moves_over_grid(shifts, slabs, atom...]
    pallas_call x1, Pallas kernels: 4.98 us -> 5.79 us  [reorder(): pl.pallas_call(reorder_kernel, out_shape=(ordered, ordered, jax.ShapeDtyp...]
    ppermute x1, starting transfers between devices: 0.12 us -> 0.93 us  [sum_parts(): near = lax.ppermute(both[0], 'grid', [(i, i ^ 1) for i in range(slabs)])]
    pallas_call x1, Pallas kernels: 1.82 us -> 1.4 us  [rows_to_send(): pl.pallas_call(send_kernel, out_shape=[jax.ShapeDtypeStruct((TRAVEL, rows...]
  transfers between devices with their start and end apart: 10 -> 10, of which waited for: 4 -> 3; matrix products, arithmetic and copies ran while one was open for 0% -> 0% of each run, Pallas kernels for 34% -> 36%
where the time goes in v19:
time: 32.2 us; the launch traced here: 32 us
  Pallas kernels  15.4 us (48%)
  starting transfers between devices  9.78 us (30%)
  waiting for transfers between devices  5.42 us (17%)
  between operations  0.77 us (2%)
  other arithmetic  0.6 us (2%)
    pallas_call x1, Pallas kernels, reorder(): pl.pallas_call(reorder_kernel, out_shape=(ordered, ordered, jax.ShapeDtyp...  5.79 us
    ppermute x2, starting transfers between devices, fetch_rows(): lax.ppermute(piece, ('grid', 'atoms'), moves_over_grid(shifts, slabs, ato...  5.12 us
    ppermute x1, waiting for transfers between devices, sum_parts(): lax.ppermute(both, ('grid', 'atoms'), moves_over_grid(shifts, slabs, atom...  3.34 us
    pallas_call x1, Pallas kernels, build_moments(): pl.pallas_call(moment_kernel, out_shape=jax.ShapeDtypeStruct((PARTS, bloc...  2.65 us
    pallas_call x1, Pallas kernels, combine(): pl.pallas_call(functools.partial(combine_kernel, owner_rows=owner_rows, s...  2.56 us
    pallas_call x1, Pallas kernels, write(): pl.pallas_call(write_kernel, out_shape=jax.ShapeDtypeStruct(shape, BF16),...  2.06 us
    ppermute x3, starting transfers between devices, sum_parts(): lax.ppermute(partial_grad[d], 'atoms', [(i, i ^ d) for i in range(atom_de...  1.93 us
    pallas_call x1, Pallas kernels, rows_to_send(): pl.pallas_call(send_kernel, out_shape=[jax.ShapeDtypeStruct((TRAVEL, rows...  1.4 us
  transfers between devices with their start and end apart: 10, of which 3 were waited for; matrix products, arithmetic and copies ran while one was open for 0% of the time, Pallas kernels for 36%

profile of v19, /device:TPU:0, one launch (start us, length us, event | category | flops | bytes accessed | tf_op | source)
XLA Modules:
  0.0 32.0 jit_solution(8316071384712746197)
XLA Ops:
  0.6 1.4 %shard_map.113 = (bf16[5,128,128]{2,1,0:T(8,128)(2,1)S(1)}, bf16[5,64,128]{2,1,0:T(8,128)(2,1)S(1)}, bf16[5,128,128]{2,1,0:T(8,128)(2,1)S(1)}) custom-call(s32[4,4]{1,0:T(4,128)} %region.3, bf16[15,3,128,128]{3,2,1,0:T(8,128)(2,1)} %density.1), custom_call_target="tpu_custom_call" | custom-call | tf_op jit(solution)/shard_map/pallas_call | solution.py:101
  2.0 5.1 %collective-permute-start.1 = (bf16[5,128,128]{2,1,0:T(8,128)(2,1)S(1)}, bf16[5,128,128]{2,1,0:T(8,128)(2,1)S(1)}, u32[]{:S(2)}, u32[]{:S(2)}) collective-permute-start(bf16[5,128,128]{2,1,0:T(8,128)(2,1)S(1)} %get-tuple-element.25), channel_id=1, source_target_pairs={{0,12},{1,9},{2,14},{3,11},{4,8},{5,13},{6,10},{7,15},{8,4},{9,1},... | collective-permute-start | bytes 491528 | tf_op jit(solution)/shard_map/ppermute | solution.py:120
  7.2 0.0 collective-permute-start
  7.2 5.8 %shard_map.114 = (bf16[16,4,128,128]{3,2,1,0:T(8,128)(2,1)S(1)}, bf16[16,4,128,128]{3,2,1,0:T(8,128)(2,1)S(1)}, bf16[4,2048,128]{2,1,0:T(8,128)(2,1)S(1)}, bf16[3,4,2048,128]{3,2,1,0:T(8,128)(2,1)S(1)}) custom-call(s32[4,16]{1,0:T(4,128)} %bitcast.27, bf16[16,512,128]{2,1,0:T(8,128)(2,1)} %bitcast.32, bf16[16,512,128]{2,1,0:T(8,128)(2,1)} %bitcast.33, ...), custom_call_target="tpu_custom_call" | custom-call | bytes 10485760 | tf_op jit(solution)/shard_map/pallas_call | solution.py:448
  12.9 0.0 copy-start
  13.0 0.0 copy-start.2
  13.0 0.0 copy-start.3
  13.0 0.0 copy-start.4
  13.0 2.7 %shard_map.115.moments = f32[3,512,512]{2,1,0:T(8,128)S(1)} custom-call(bf16[4,2048,128]{2,1,0:T(8,128)(2,1)S(1)} %get-tuple-element.28.weighted, bf16[3,4,2048,128]{3,2,1,0:T(8,128)(2,1)S(1)} %get-tuple-element.29.grads), custom_call_target="tpu_custom_call" | custom-call | flops 3221225472 | tf_op jit(solution)/shard_map/pallas_call | solution.py:492
  15.7 0.0 collective-permute-done.rest_1_
  15.7 0.0 collective-permute-done.1.rest_2_
  15.7 0.1 collective-permute-start.3
  15.8 0.5 %collective-permute-start.2 = (bf16[5,64,128]{2,1,0:T(8,128)(2,1)S(1)}, bf16[5,64,128]{2,1,0:T(8,128)(2,1)S(1)}, u32[]{:S(2)}, u32[]{:S(2)}) collective-permute-start(bf16[5,64,128]{2,1,0:T(8,128)(2,1)S(1)} %collective-permute-done.rest_1_), channel_id=1, source_target_pairs={{0,1},{1,0},{2,3},{3,2},{4,5},{5,4},{6,7},{7,6},{8,9},{9,8},{10,11... | collective-permute-start | bytes 245768 | tf_op jit(solution)/shard_map/ppermute | solution.py:679
  16.3 0.0 copy-done
  16.3 0.0 copy-done.2
  16.3 0.0 copy-done.3
  16.3 0.0 copy-done.4
  16.3 1.0 %shard_map.116 = (bf16[768,640]{1,0:T(8,128)(2,1)S(1)}, f32[3,128,128]{2,1,0:T(8,128)S(1)}) custom-call(s32[4,4]{1,0:T(4,128)S(1)} %copy-done, s32[60,128]{1,0:T(8,128)S(1)} %bitcast.29, s32[1,16]{1,0:T(1,128)S(1)} %bitcast.30, f32[3,16,128]{2,1,0:T(8,128)S(1)} %copy-done.3), custom_call_target="tpu_custom_call" | custom-call | flops 1000000000 | bytes 196608 | tf_op jit(solution)/shard_map/pallas_call | solution.py:526
  17.2 0.0 collective-permute-done.2.rest_3_
  17.3 0.0 collective-permute-done.3.rest_4_
  17.3 0.0 copy-start.1
  17.3 2.6 %shard_map.117 = (bf16[16,4,128,128]{3,2,1,0:T(8,128)(2,1)S(1)}, f32[4,2,3,192]{3,2,1,0:T(4,128)S(1)}) custom-call(s32[4,4]{1,0:T(4,128)S(1)} %copy-done, bf16[16,4,128,128]{3,2,1,0:T(8,128)(2,1)S(1)} %get-tuple-element.30.basis, bf16[16,4,128,128]{3,2,1,0:T(8,128)(2,1)S(1)} %get-tuple-element.31.field, f32[3,512,512]{2,1,0:T(8,128)S(1)} %shard_map.115.moments, ...), custom_call_target="tpu_custom_call" | custom-call | tf_op jit(solution)/shard_map/pallas_call | solution.py:621
  19.9 0.3 %collective-permute-start.4 = (f32[2,3,192]{2,1,0:T(4,128)S(1)}, f32[2,3,192]{2,1,0:T(4,128)S(1)}, u32[]{:S(2)}, u32[]{:S(2)}) collective-permute-start(f32[2,3,192]{2,1,0:T(4,128)S(1)} %get-tuple-element.48), channel_id=1, source_target_pairs={{0,1},{1,0},{2,3},{3,2},{4,5},{5,4},{6,7},{7,6},{8,9},{9,8},{10,11... | collective-permute-start | bytes 13832 | tf_op jit(solution)/shard_map/ppermute | solution.py:696
  20.2 1.5 %collective-permute-start.5 = (f32[2,3,192]{2,1,0:T(4,128)S(1)}, f32[2,3,192]{2,1,0:T(4,128)S(1)}, u32[]{:S(2)}, u32[]{:S(2)}) collective-permute-start(f32[2,3,192]{2,1,0:T(4,128)S(1)} %get-tuple-element.47), channel_id=1, source_target_pairs={{0,2},{1,3},{2,0},{3,1},{4,6},{5,7},{6,4},{7,5},{8,10},{9,11},{10,... | collective-permute-start | bytes 13832 | tf_op jit(solution)/shard_map/ppermute | solution.py:696
  21.7 0.1 collective-permute-start.6
  21.8 0.0 copy-done.1
  21.8 2.1 %shard_map.118 = bf16[16,512,128]{2,1,0:T(8,128)(2,1)} custom-call(s32[4,16]{1,0:T(4,128)S(1)} %bitcast.28, bf16[16,4,128,128]{3,2,1,0:T(8,128)(2,1)S(1)} %get-tuple-element.40.product), custom_call_target="tpu_custom_call" | custom-call | bytes 4194304 | tf_op jit(solution)/shard_map/pallas_call | solution.py:661
  23.9 0.0 collective-permute-done.4
  23.9 0.0 collective-permute-done.5
  23.9 0.9 %collective-permute-done.6 = f32[2,3,192]{2,1,0:T(4,128)S(1)} collective-permute-done((f32[2,3,192]{2,1,0:T(4,128)S(1)}, f32[2,3,192]{2,1,0:T(4,128)S(1)}, u32[]{:S(2)}, u32[]{:S(2)}) %collective-permute-start.6) | collective-permute-done | bytes 4640 | tf_op jit(solution)/shard_map/ppermute | solution.py:696
  24.8 1.2 %collective-permute-start.8 = (f32[2,3,192]{2,1,0:T(4,128)S(1)}, f32[2,3,192]{2,1,0:T(4,128)S(1)}, u32[]{:S(2)}, u32[]{:S(2)}) collective-permute-start(f32[2,3,192]{2,1,0:T(4,128)S(1)} %add_add_fusion), channel_id=1, source_target_pairs={{0,12},{1,9},{2,14},{3,11},{4,8},{5,13},{6,10},{7,15},{8,4},{9,1},... | collective-permute-start | bytes 13832 | tf_op jit(solution)/shard_map/ppermute | solution.py:703
  26.0 0.9 %collective-permute-start.7 = (f32[3,192]{1,0:T(4,128)S(1)}, f32[3,192]{1,0:T(4,128)S(1)}, u32[]{:S(2)}, u32[]{:S(2)}) collective-permute-start(f32[3,192]{1,0:T(4,128)S(1)} %slice_bitcast_fusion.6), channel_id=1, source_target_pairs={{0,4},{4,0},{8,12},{12,8},{1,5},{5,1},{9,13},{13,9},{2,6},{6,2},{1... | collective-permute-start | bytes 6920 | tf_op jit(solution)/shard_map/ppermute | solution.py:704
  26.9 3.3 %collective-permute-done.8 = f32[2,3,192]{2,1,0:T(4,128)S(1)} collective-permute-done((f32[2,3,192]{2,1,0:T(4,128)S(1)}, f32[2,3,192]{2,1,0:T(4,128)S(1)}, u32[]{:S(2)}, u32[]{:S(2)}) %collective-permute-start.8) | collective-permute-done | bytes 4640 | tf_op jit(solution)/shard_map/ppermute | solution.py:703
  30.3 0.0 collective-permute-start.9
  30.3 0.0 collective-permute-done.7
  30.3 1.2 %collective-permute-done.9 = f32[3,192]{1,0:T(4,128)S(1)} collective-permute-done((f32[3,192]{1,0:T(4,128)S(1)}, f32[3,192]{1,0:T(4,128)S(1)}, u32[]{:S(2)}, u32[]{:S(2)}) %collective-permute-start.9) | collective-permute-done | bytes 2336 | tf_op jit(solution)/shard_map/ppermute | solution.py:706
  31.5 0.6 %fusion.1 = f32[3,192]{1,0:T(4,128)} fusion(f32[3,192]{1,0:T(4,128)S(1)} %collective-permute-done.9, f32[2,3,192]{2,1,0:T(4,128)S(1)} %collective-permute-done.8, f32[3,192]{1,0:T(4,128)S(1)} %collective-permute-done.7, f32[2,3,192]{2,1,0:T(4,128)S(1)} %add_add_fusion), kind=kLoop, calls=%fused_computation.8 | loop fusion | flops 1728 | bytes 11520 | tf_op jit(solution)/shard_map/add | solution.py:686
  (4 shorter events, 0.0 us)
Async XLA Ops:
  2.0 13.6 %collective-permute-start.1 = (bf16[5,128,128]{2,1,0:T(8,128)(2,1)S(1)}, bf16[5,128,128]{2,1,0:T(8,128)(2,1)S(1)}, u32[]{:S(2)}, u32[]{:S(2)}) collective-permute-start(bf16[5,128,128]{2,1,0:T(8,128)(2,1)S(1)} %get-tuple-element.25), channel_id=1, source_target_pairs={{0,12},{1,9},{2,14},{3,11},{4,8},{5,13},{6,10},{7,15},{8,4},{9,1},... | collective-permute-start | bytes 491528 | tf_op jit(solution)/shard_map/ppermute | solution.py:120
  7.2 8.5 %collective-permute-start = (bf16[5,64,128]{2,1,0:T(8,128)(2,1)S(1)}, bf16[5,64,128]{2,1,0:T(8,128)(2,1)S(1)}, u32[]{:S(2)}, u32[]{:S(2)}) collective-permute-start(bf16[5,64,128]{2,1,0:T(8,128)(2,1)S(1)} %get-tuple-element.24), channel_id=1, source_target_pairs={{0,4},{1,5},{2,6},{3,7},{4,0},{5,1},{6,2},{7,3},{8,12},{9,13},{10,... | collective-permute-start | bytes 245768 | tf_op jit(solution)/shard_map/ppermute | solution.py:120
  12.9 3.3 %copy-start = (s32[4,4]{1,0:T(4,128)S(1)}, s32[4,4]{1,0:T(4,128)}, u32[]{:S(2)}) copy-start(s32[4,4]{1,0:T(4,128)} %region.3) | copy-start | bytes 196
  13.0 3.3 %copy-start.2 = (s32[7680]{0:T(1024)S(1)}, s32[7680]{0:T(1024)}, u32[]{:S(2)}) copy-start(s32[7680]{0:T(1024)} %param.18) | copy-start | bytes 92164
  13.0 3.3 %copy-start.3 = (f32[3,16,128]{2,1,0:T(8,128)S(1)}, f32[3,16,128]{2,1,0:T(8,128)}, u32[]{:S(2)}) copy-start(f32[3,16,128]{2,1,0:T(8,128)} %weight_grad.1) | copy-start | bytes 73732
  13.0 3.3 %copy-start.4 = (s32[16]{0:T(128)S(1)}, s32[16]{0:T(128)}, u32[]{:S(2)}) copy-start(s32[16]{0:T(128)} %param.19) | copy-start | bytes 196
  15.7 1.6 %collective-permute-start.3 = (bf16[5,128,128]{2,1,0:T(8,128)(2,1)S(1)}, bf16[5,128,128]{2,1,0:T(8,128)(2,1)S(1)}, u32[]{:S(2)}, u32[]{:S(2)}) collective-permute-start(bf16[5,128,128]{2,1,0:T(8,128)(2,1)S(1)} %collective-permute-done.1.rest_2_), channel_id=1, source_target_pairs={{0,1},{1,0},{2,3},{3,2},{4,5},{5,4},{6,7},{7,6},{8,9},{9,8},{10,11... | collective-permute-start | bytes 491528 | tf_op jit(solution)/shard_map/ppermute | solution.py:679
  15.8 1.5 %collective-permute-start.2 = (bf16[5,64,128]{2,1,0:T(8,128)(2,1)S(1)}, bf16[5,64,128]{2,1,0:T(8,128)(2,1)S(1)}, u32[]{:S(2)}, u32[]{:S(2)}) collective-permute-start(bf16[5,64,128]{2,1,0:T(8,128)(2,1)S(1)} %collective-permute-done.rest_1_), channel_id=1, source_target_pairs={{0,1},{1,0},{2,3},{3,2},{4,5},{5,4},{6,7},{7,6},{8,9},{9,8},{10,11... | collective-permute-start | bytes 245768 | tf_op jit(solution)/shard_map/ppermute | solution.py:679
  17.3 4.5 %copy-start.1 = (s32[16,4]{0,1:T(4,128)S(1)}, s32[16,4]{0,1:T(4,128)}, u32[]{:S(2)}) copy-start(s32[16,4]{0,1:T(4,128)} %param.17) | copy-start | bytes 772
  19.9 4.0 %collective-permute-start.4 = (f32[2,3,192]{2,1,0:T(4,128)S(1)}, f32[2,3,192]{2,1,0:T(4,128)S(1)}, u32[]{:S(2)}, u32[]{:S(2)}) collective-permute-start(f32[2,3,192]{2,1,0:T(4,128)S(1)} %get-tuple-element.48), channel_id=1, source_target_pairs={{0,1},{1,0},{2,3},{3,2},{4,5},{5,4},{6,7},{7,6},{8,9},{9,8},{10,11... | collective-permute-start | bytes 13832 | tf_op jit(solution)/shard_map/ppermute | solution.py:696
  20.2 3.7 %collective-permute-start.5 = (f32[2,3,192]{2,1,0:T(4,128)S(1)}, f32[2,3,192]{2,1,0:T(4,128)S(1)}, u32[]{:S(2)}, u32[]{:S(2)}) collective-permute-start(f32[2,3,192]{2,1,0:T(4,128)S(1)} %get-tuple-element.47), channel_id=1, source_target_pairs={{0,2},{1,3},{2,0},{3,1},{4,6},{5,7},{6,4},{7,5},{8,10},{9,11},{10,... | collective-permute-start | bytes 13832 | tf_op jit(solution)/shard_map/ppermute | solution.py:696
  21.7 3.1 %collective-permute-start.6 = (f32[2,3,192]{2,1,0:T(4,128)S(1)}, f32[2,3,192]{2,1,0:T(4,128)S(1)}, u32[]{:S(2)}, u32[]{:S(2)}) collective-permute-start(f32[2,3,192]{2,1,0:T(4,128)S(1)} %get-tuple-element.46), channel_id=1, source_target_pairs={{0,3},{1,2},{2,1},{3,0},{4,7},{5,6},{6,5},{7,4},{8,11},{9,10},{10,... | collective-permute-start | bytes 13832 | tf_op jit(solution)/shard_map/ppermute | solution.py:696
  24.8 5.5 %collective-permute-start.8 = (f32[2,3,192]{2,1,0:T(4,128)S(1)}, f32[2,3,192]{2,1,0:T(4,128)S(1)}, u32[]{:S(2)}, u32[]{:S(2)}) collective-permute-start(f32[2,3,192]{2,1,0:T(4,128)S(1)} %add_add_fusion), channel_id=1, source_target_pairs={{0,12},{1,9},{2,14},{3,11},{4,8},{5,13},{6,10},{7,15},{8,4},{9,1},... | collective-permute-start | bytes 13832 | tf_op jit(solution)/shard_map/ppermute | solution.py:703
  26.0 4.3 %collective-permute-start.7 = (f32[3,192]{1,0:T(4,128)S(1)}, f32[3,192]{1,0:T(4,128)S(1)}, u32[]{:S(2)}, u32[]{:S(2)}) collective-permute-start(f32[3,192]{1,0:T(4,128)S(1)} %slice_bitcast_fusion.6), channel_id=1, source_target_pairs={{0,4},{4,0},{8,12},{12,8},{1,5},{5,1},{9,13},{13,9},{2,6},{6,2},{1... | collective-permute-start | bytes 6920 | tf_op jit(solution)/shard_map/ppermute | solution.py:704
  30.3 1.2 %collective-permute-start.9 = (f32[3,192]{1,0:T(4,128)S(1)}, f32[3,192]{1,0:T(4,128)S(1)}, u32[]{:S(2)}, u32[]{:S(2)}) collective-permute-start(f32[3,192]{1,0:T(4,128)S(1)} %slice_bitcast_fusion.4), channel_id=1, source_target_pairs={{0,1},{1,0},{2,3},{3,2},{4,5},{5,4},{6,7},{7,6},{8,9},{9,8},{10,11... | collective-permute-start | bytes 6920 | tf_op jit(solution)/shard_map/ppermute | solution.py:706

commit v20 on v18

--- a/solution.py
+++ b/solution.py
@@ -47,17 +47,23 @@
 
 
 def send_kernel(region_hbm, density, *rest):
-    *outs, region, sems, region_sem = rest
+    *outs, region, held, region_sem, sems = rest
     fetch = pltpu.make_async_copy(region_hbm, region, region_sem)
     fetch.start()
+    count_here = density.shape[0] // sems.shape[0]
+    fetches = []
+    for part in range(sems.shape[0]):
+        here = pl.ds(part * count_here, count_here)
+        fetches.append(pltpu.make_async_copy(density.at[here], held.at[here], sems.at[part]))
+    for copy in fetches:
+        copy.start()
     fetch.wait()
     me = lax.axis_index("grid")
     core = lax.rem(lax.axis_index("atoms"), 2)
     slabs, size = region.shape
     owner_rows = density.shape[0]
-    rows = density.shape[-2]
-    copies = []
-    for number, ((low, high), out) in enumerate(zip([(0, 0)] + partners(slabs), outs)):
+    picks = []
+    for low, high in [(0, 0)] + partners(slabs):
         slab = jnp.bitwise_xor(me, jnp.where(core == 0, low, high))
         base = jnp.int32(owner_rows)
         count = jnp.int32(0)
@@ -70,20 +76,12 @@
         after = jnp.minimum(base + 1, owner_rows - 1)
         lower = base == 0
         edge = jnp.where(jnp.logical_and(count == 2, jnp.logical_not(lower)), after, base)
-        kept = out.shape[1]
-        first = 0 if kept == rows else pl.multiple_of(core * kept, kept)
-        here = pl.ds(first, kept)
-        pairs = (
-            (density.at[base, pl.ds(1, 2), here, :], out.at[pl.ds(0, 2)]),
-            (density.at[after, pl.ds(0, 2), here, :], out.at[pl.ds(2, 2)]),
-            (density.at[edge, jnp.where(lower, 0, 2), here, :], out.at[4]),
-        )
-        for part, (source, target) in enumerate(pairs):
-            copies.append(pltpu.make_async_copy(source, target, sems.at[number, part]))
-    for copy in copies:
-        copy.start()
-    for copy in copies:
+        picks.append(((base, 1), (base, 2), (after, 0), (after, 1), (edge, jnp.where(lower, 0, 2))))
+    for copy in fetches:
         copy.wait()
+    for out, places in zip(outs, picks):
+        for place, (row, k) in enumerate(places):
+            out[place] = held[row, k]
 
 
 def in_hbm(array):
@@ -92,18 +90,18 @@
 
 def rows_to_send(region, density, slabs):
     size = density.shape[-1]
-    exchanges = partners(slabs)
-    kept = [size] + [size if low != high else size // 2 for low, high in exchanges]
+    count = 1 + len(partners(slabs))
     hbm = pl.BlockSpec(memory_space=pl.ANY)
     return pl.pallas_call(
         send_kernel,
-        out_shape=[jax.ShapeDtypeStruct((TRAVEL, rows, size), density.dtype) for rows in kept],
+        out_shape=[jax.ShapeDtypeStruct((TRAVEL, size, size), density.dtype)] * count,
         in_specs=[hbm, hbm],
-        out_specs=[pl.BlockSpec(memory_space=pltpu.VMEM)] * len(kept),
+        out_specs=[pl.BlockSpec(memory_space=pltpu.VMEM)] * count,
         scratch_shapes=[
             pltpu.SMEM(region.shape, jnp.int32),
-            pltpu.SemaphoreType.DMA((len(kept), 3)),
+            pltpu.VMEM(density.shape, density.dtype),
             pltpu.SemaphoreType.DMA,
+            pltpu.SemaphoreType.DMA((5 if density.shape[0] % 5 == 0 else 1,)),
         ],
         compiler_params=pltpu.CompilerParams(vmem_limit_bytes=VMEM_LIMIT),
     )(in_hbm(region), in_hbm(density))
@@ -119,19 +117,16 @@
 
 def stage_rows(stage, own, near, far, slabs):
     core = lax.rem(lax.axis_index("atoms"), 2)
+    first, *pairs = partners(slabs)
     for place in range(TRAVEL):
         stage[place] = own[place]
-    for (low, high), here, there in zip(partners(slabs), near, far):
-        kept = here.shape[1]
+        stage[first[0] * TRAVEL + place] = near[0][place]
+    for (low, high), here, there in zip(pairs, near[1:], far):
         mine = jnp.where(core == 0, low, high) * TRAVEL
         other = jnp.where(core == 0, high, low) * TRAVEL
         for place in range(TRAVEL):
-            if low != high:
-                stage[mine + place] = here[place]
-                stage[other + place] = there[place]
-            else:
-                stage[mine + place, pl.ds(pl.multiple_of(core * kept, kept), kept), :] = here[place]
-                stage[mine + place, pl.ds(pl.multiple_of((1 - core) * kept, kept), kept), :] = there[place]
+            stage[mine + place] = here[place]
+            stage[other + place] = there[place]
 
 
 def block_major(x_ref, wide, points, blocks):
@@ -656,10 +651,10 @@
     )(pattern.T, product)
 
 
-def swap_halves(near, ready, atom_devices):
+def swap_between_cores(near, ready, atom_devices):
     near, ready = lax.optimization_barrier((near, ready))
     swap = [(i, i ^ 1) for i in range(atom_devices)]
-    return near, [lax.ppermute(piece, "atoms", swap) for piece in near], ready
+    return near, [lax.ppermute(piece, "atoms", swap) for piece in near[1:]], ready
 
 
 def tree_sum(values):
@@ -681,9 +676,8 @@
     both = tree_sum(pair_sums(parts))
     swap = [(i, i ^ 1) for i in range(atom_devices)]
     far = []
-    for shifts in partners(slabs):
-        if shifts[0] != shifts[1]:
-            far.append(lax.ppermute(both, ("grid", "atoms"), moves_over_grid(shifts, slabs, atom_devices)))
+    for shifts in partners(slabs)[1:]:
+        far.append(lax.ppermute(both, ("grid", "atoms"), moves_over_grid(shifts, slabs, atom_devices)))
     near = lax.ppermute(both[0], "grid", [(i, i ^ 1) for i in range(slabs)])
     far = lax.optimization_barrier(far)
     swapped = [lax.ppermute(piece[1], "atoms", swap) for piece in far]
@@ -718,14 +712,14 @@
             pattern, flat_basis, flat_field, flat_grad, weights, points, blocks
         )
         ready = (basis_wide, field_wide, build_moments(weighted, grads), batch_atom)
-        near, far, (basis_wide, field_wide, moments, batch_atom) = swap_halves(near, ready, atom_devices)
+        near, far, (basis_wide, field_wide, moments, batch_atom) = swap_between_cores(near, ready, atom_devices)
         hot, grad_columns = atom_matrix(region, fn_atom, batch_atom, weight_grad, blocks, size, atom_total)
         ready = (basis_wide, field_wide, moments, hot, grad_columns)
         product, partial_grad = combine(region, ready, [own, *near, *far], shapes)
         gradient, contracted = sum_parts(partial_grad, write(pattern, product), slabs, atom_devices)
         return contracted.reshape(basis.shape), gradient
     ready = relayout(in_hbm(flat_basis), in_hbm(flat_field), points, blocks)
-    near, far, (basis_wide, field_wide) = swap_halves(near, ready, atom_devices)
+    near, far, (basis_wide, field_wide) = swap_between_cores(near, ready, atom_devices)
     tiles, partial_grad = partial_gradient(
         region,
         pattern,

time: 31.9 us -> 31.6 us (level)
  Pallas kernels: 15 us -> 14.6 us
  waiting for transfers between devices: 5.4 us -> 5.72 us
    ppermute x1, starting transfers between devices: 2.06 us -> 1.41 us  [sum_parts(): lax.ppermute(both, ('grid', 'atoms'), moves_over_grid(shifts, slabs, atom...]
    ppermute x1, starting transfers between devices: 0.12 us -> 0.68 us  [sum_parts(): near = lax.ppermute(both[0], 'grid', [(i, i ^ 1) for i in range(slabs)])]
    ppermute x2 -> x1, starting transfers between devices: 0.57 us -> 0.07 us  [swap_between_cores(): lax.ppermute(piece, 'atoms', swap)]
    ppermute x2, starting transfers between devices: 5.12 us -> 5.56 us  [fetch_rows(): lax.ppermute(piece, ('grid', 'atoms'), moves_over_grid(shifts, slabs, ato...]
    pallas_call x1, Pallas kernels: 1.82 us -> 1.4 us  [rows_to_send(): pl.pallas_call(send_kernel, out_shape=[jax.ShapeDtypeStruct((TRAVEL, size...]
    ppermute x2 -> x1, waiting for transfers between devices: 0.02 us -> 0.37 us  [swap_between_cores(): lax.ppermute(piece, 'atoms', swap)]
  transfers between devices with their start and end apart: 10 -> 9, of which waited for: 4 -> 4; matrix products, arithmetic and copies ran while one was open for 0% -> 0% of each run, Pallas kernels for 34% -> 34%
where the time goes in v20:
time: 31.6 us; the launch traced here: 31.4 us
  Pallas kernels  14.6 us (46%)
  starting transfers between devices  9.66 us (31%)
  waiting for transfers between devices  5.72 us (18%)
  between operations  0.79 us (2%)
  other arithmetic  0.6 us (2%)
    ppermute x2, starting transfers between devices, fetch_rows(): lax.ppermute(piece, ('grid', 'atoms'), moves_over_grid(shifts, slabs, ato...  5.56 us
    pallas_call x1, Pallas kernels, reorder(): pl.pallas_call(reorder_kernel, out_shape=(ordered, ordered, jax.ShapeDtyp...  4.98 us
    ppermute x1, waiting for transfers between devices, sum_parts(): lax.ppermute(both, ('grid', 'atoms'), moves_over_grid(shifts, slabs, atom...  3.41 us
    pallas_call x1, Pallas kernels, build_moments(): pl.pallas_call(moment_kernel, out_shape=jax.ShapeDtypeStruct((PARTS, bloc...  2.62 us
    pallas_call x1, Pallas kernels, combine(): pl.pallas_call(functools.partial(combine_kernel, owner_rows=owner_rows, s...  2.58 us
    pallas_call x1, Pallas kernels, write(): pl.pallas_call(write_kernel, out_shape=jax.ShapeDtypeStruct(shape, BF16),...  2.06 us
    ppermute x3, starting transfers between devices, sum_parts(): lax.ppermute(partial_grad[d], 'atoms', [(i, i ^ d) for i in range(atom_de...  1.93 us
    ppermute x1, starting transfers between devices, sum_parts(): lax.ppermute(both, ('grid', 'atoms'), moves_over_grid(shifts, slabs, atom...  1.41 us
  transfers between devices with their start and end apart: 9, of which 4 were waited for; matrix products, arithmetic and copies ran while one was open for 0% of the time, Pallas kernels for 34%

profile of v20, /device:TPU:0, one launch (start us, length us, event | category | flops | bytes accessed | tf_op | source)
XLA Modules:
  0.0 31.4 jit_solution(5609537585509731977)
XLA Ops:
  0.6 1.4 %shard_map.113 = (bf16[5,128,128]{2,1,0:T(8,128)(2,1)S(1)}, bf16[5,128,128]{2,1,0:T(8,128)(2,1)S(1)}, bf16[5,128,128]{2,1,0:T(8,128)(2,1)S(1)}) custom-call(s32[4,4]{1,0:T(4,128)} %region.3, bf16[15,3,128,128]{3,2,1,0:T(8,128)(2,1)} %density.1), custom_call_target="tpu_custom_call" | custom-call | tf_op jit(solution)/shard_map/pallas_call | solution.py:95
  2.0 3.1 %collective-permute-start = (bf16[5,128,128]{2,1,0:T(8,128)(2,1)S(1)}, bf16[5,128,128]{2,1,0:T(8,128)(2,1)S(1)}, u32[]{:S(2)}, u32[]{:S(2)}) collective-permute-start(bf16[5,128,128]{2,1,0:T(8,128)(2,1)S(1)} %get-tuple-element.24), channel_id=1, source_target_pairs={{0,4},{1,5},{2,6},{3,7},{4,0},{5,1},{6,2},{7,3},{8,12},{9,13},{10,... | collective-permute-start | bytes 491528 | tf_op jit(solution)/shard_map/ppermute | solution.py:114
  5.1 2.5 %collective-permute-start.1 = (bf16[5,128,128]{2,1,0:T(8,128)(2,1)S(1)}, bf16[5,128,128]{2,1,0:T(8,128)(2,1)S(1)}, u32[]{:S(2)}, u32[]{:S(2)}) collective-permute-start(bf16[5,128,128]{2,1,0:T(8,128)(2,1)S(1)} %get-tuple-element.25), channel_id=1, source_target_pairs={{0,12},{1,9},{2,14},{3,11},{4,8},{5,13},{6,10},{7,15},{8,4},{9,1},... | collective-permute-start | bytes 491528 | tf_op jit(solution)/shard_map/ppermute | solution.py:114
  7.6 5.0 %shard_map.114 = (bf16[16,4,128,128]{3,2,1,0:T(8,128)(2,1)S(1)}, bf16[16,4,128,128]{3,2,1,0:T(8,128)(2,1)S(1)}, bf16[4,2048,128]{2,1,0:T(8,128)(2,1)S(1)}, bf16[3,4,2048,128]{3,2,1,0:T(8,128)(2,1)S(1)}) custom-call(s32[4,16]{1,0:T(4,128)} %bitcast.27, bf16[16,512,128]{2,1,0:T(8,128)(2,1)} %bitcast.32, bf16[16,512,128]{2,1,0:T(8,128)(2,1)} %bitcast.33, ...), custom_call_target="tpu_custom_call" | custom-call | bytes 10485760 | tf_op jit(solution)/shard_map/pallas_call | solution.py:427
  12.6 0.0 copy-start
  12.6 0.0 copy-start.2
  12.6 0.0 copy-start.3
  12.6 0.0 copy-start.4
  12.6 2.6 %shard_map.115.moments = f32[3,512,512]{2,1,0:T(8,128)S(1)} custom-call(bf16[4,2048,128]{2,1,0:T(8,128)(2,1)S(1)} %get-tuple-element.28.weighted, bf16[3,4,2048,128]{3,2,1,0:T(8,128)(2,1)S(1)} %get-tuple-element.29.grads), custom_call_target="tpu_custom_call" | custom-call | flops 3221225472 | tf_op jit(solution)/shard_map/pallas_call | solution.py:470
  15.3 0.0 collective-permute-done.rest_1_
  15.3 0.0 collective-permute-done.1.rest_2_
  15.3 0.1 collective-permute-start.2
  15.4 0.0 copy-done
  15.4 0.0 copy-done.2
  15.4 0.0 copy-done.3
  15.4 0.0 copy-done.4
  15.4 1.0 %shard_map.116 = (bf16[768,640]{1,0:T(8,128)(2,1)S(1)}, f32[3,128,128]{2,1,0:T(8,128)S(1)}) custom-call(s32[4,4]{1,0:T(4,128)S(1)} %copy-done, s32[60,128]{1,0:T(8,128)S(1)} %bitcast.29, s32[1,16]{1,0:T(1,128)S(1)} %bitcast.30, f32[3,16,128]{2,1,0:T(8,128)S(1)} %copy-done.3), custom_call_target="tpu_custom_call" | custom-call | flops 1000000000 | bytes 196608 | tf_op jit(solution)/shard_map/pallas_call | solution.py:504
  16.4 0.4 %collective-permute-done.2.rest_3_ = bf16[5,128,128]{2,1,0:T(8,128)(2,1)S(1)} collective-permute-done((bf16[5,128,128]{2,1,0:T(8,128)(2,1)S(1)}, bf16[5,128,128]{2,1,0:T(8,128)(2,1)S(1)}, u32[]{:S(2)}, u32[]{:S(2)}) %collective-permute-start.2) | collective-permute-done | bytes 163872 | tf_op jit(solution)/shard_map/ppermute | solution.py:657
  16.8 0.0 copy-start.1
  16.8 2.6 %shard_map.117 = (bf16[16,4,128,128]{3,2,1,0:T(8,128)(2,1)S(1)}, f32[4,2,3,192]{3,2,1,0:T(4,128)S(1)}) custom-call(s32[4,4]{1,0:T(4,128)S(1)} %copy-done, bf16[16,4,128,128]{3,2,1,0:T(8,128)(2,1)S(1)} %get-tuple-element.30.basis, bf16[16,4,128,128]{3,2,1,0:T(8,128)(2,1)S(1)} %get-tuple-element.31.field, f32[3,512,512]{2,1,0:T(8,128)S(1)} %shard_map.115.moments, ...), custom_call_target="tpu_custom_call" | custom-call | tf_op jit(solution)/shard_map/pallas_call | solution.py:599
  19.4 0.2 collective-permute-start.3
  19.6 1.5 %collective-permute-start.4 = (f32[2,3,192]{2,1,0:T(4,128)S(1)}, f32[2,3,192]{2,1,0:T(4,128)S(1)}, u32[]{:S(2)}, u32[]{:S(2)}) collective-permute-start(f32[2,3,192]{2,1,0:T(4,128)S(1)} %get-tuple-element.47), channel_id=1, source_target_pairs={{0,2},{1,3},{2,0},{3,1},{4,6},{5,7},{6,4},{7,5},{8,10},{9,11},{10,... | collective-permute-start | bytes 13832 | tf_op jit(solution)/shard_map/ppermute | solution.py:674
  21.1 0.2 collective-permute-start.5
  21.3 0.0 copy-done.1
  21.3 2.1 %shard_map.118 = bf16[16,512,128]{2,1,0:T(8,128)(2,1)} custom-call(s32[4,16]{1,0:T(4,128)S(1)} %bitcast.28, bf16[16,4,128,128]{3,2,1,0:T(8,128)(2,1)S(1)} %get-tuple-element.40.product), custom_call_target="tpu_custom_call" | custom-call | bytes 4194304 | tf_op jit(solution)/shard_map/pallas_call | solution.py:639
  23.4 0.0 collective-permute-done.3
  23.4 0.0 collective-permute-done.4
  23.4 0.8 %collective-permute-done.5 = f32[2,3,192]{2,1,0:T(4,128)S(1)} collective-permute-done((f32[2,3,192]{2,1,0:T(4,128)S(1)}, f32[2,3,192]{2,1,0:T(4,128)S(1)}, u32[]{:S(2)}, u32[]{:S(2)}) %collective-permute-start.5) | collective-permute-done | bytes 4640 | tf_op jit(solution)/shard_map/ppermute | solution.py:674
  24.2 1.4 %collective-permute-start.7 = (f32[2,3,192]{2,1,0:T(4,128)S(1)}, f32[2,3,192]{2,1,0:T(4,128)S(1)}, u32[]{:S(2)}, u32[]{:S(2)}) collective-permute-start(f32[2,3,192]{2,1,0:T(4,128)S(1)} %add_add_fusion), channel_id=1, source_target_pairs={{0,12},{1,9},{2,14},{3,11},{4,8},{5,13},{6,10},{7,15},{8,4},{9,1},... | collective-permute-start | bytes 13832 | tf_op jit(solution)/shard_map/ppermute | solution.py:680
  25.6 0.7 %collective-permute-start.6 = (f32[3,192]{1,0:T(4,128)S(1)}, f32[3,192]{1,0:T(4,128)S(1)}, u32[]{:S(2)}, u32[]{:S(2)}) collective-permute-start(f32[3,192]{1,0:T(4,128)S(1)} %slice_bitcast_fusion.6), channel_id=1, source_target_pairs={{0,4},{4,0},{8,12},{12,8},{1,5},{5,1},{9,13},{13,9},{2,6},{6,2},{1... | collective-permute-start | bytes 6920 | tf_op jit(solution)/shard_map/ppermute | solution.py:681
  26.3 3.4 %collective-permute-done.7 = f32[2,3,192]{2,1,0:T(4,128)S(1)} collective-permute-done((f32[2,3,192]{2,1,0:T(4,128)S(1)}, f32[2,3,192]{2,1,0:T(4,128)S(1)}, u32[]{:S(2)}, u32[]{:S(2)}) %collective-permute-start.7) | collective-permute-done | bytes 4640 | tf_op jit(solution)/shard_map/ppermute | solution.py:680
  29.7 0.0 collective-permute-start.8
  29.7 0.0 collective-permute-done.6
  29.7 1.2 %collective-permute-done.8 = f32[3,192]{1,0:T(4,128)S(1)} collective-permute-done((f32[3,192]{1,0:T(4,128)S(1)}, f32[3,192]{1,0:T(4,128)S(1)}, u32[]{:S(2)}, u32[]{:S(2)}) %collective-permute-start.8) | collective-permute-done | bytes 2336 | tf_op jit(solution)/shard_map/ppermute | solution.py:683
  30.8 0.6 %fusion.1 = f32[3,192]{1,0:T(4,128)} fusion(f32[3,192]{1,0:T(4,128)S(1)} %collective-permute-done.8, f32[2,3,192]{2,1,0:T(4,128)S(1)} %collective-permute-done.7, f32[3,192]{1,0:T(4,128)S(1)} %collective-permute-done.6, f32[2,3,192]{2,1,0:T(4,128)S(1)} %add_add_fusion), kind=kLoop, calls=%fused_computation.8 | loop fusion | flops 1728 | bytes 11520 | tf_op jit(solution)/shard_map/add | solution.py:664
  (4 shorter events, 0.0 us)
Async XLA Ops:
  2.0 13.2 %collective-permute-start = (bf16[5,128,128]{2,1,0:T(8,128)(2,1)S(1)}, bf16[5,128,128]{2,1,0:T(8,128)(2,1)S(1)}, u32[]{:S(2)}, u32[]{:S(2)}) collective-permute-start(bf16[5,128,128]{2,1,0:T(8,128)(2,1)S(1)} %get-tuple-element.24), channel_id=1, source_target_pairs={{0,4},{1,5},{2,6},{3,7},{4,0},{5,1},{6,2},{7,3},{8,12},{9,13},{10,... | collective-permute-start | bytes 491528 | tf_op jit(solution)/shard_map/ppermute | solution.py:114
  5.1 10.2 %collective-permute-start.1 = (bf16[5,128,128]{2,1,0:T(8,128)(2,1)S(1)}, bf16[5,128,128]{2,1,0:T(8,128)(2,1)S(1)}, u32[]{:S(2)}, u32[]{:S(2)}) collective-permute-start(bf16[5,128,128]{2,1,0:T(8,128)(2,1)S(1)} %get-tuple-element.25), channel_id=1, source_target_pairs={{0,12},{1,9},{2,14},{3,11},{4,8},{5,13},{6,10},{7,15},{8,4},{9,1},... | collective-permute-start | bytes 491528 | tf_op jit(solution)/shard_map/ppermute | solution.py:114
  12.6 2.8 %copy-start = (s32[4,4]{1,0:T(4,128)S(1)}, s32[4,4]{1,0:T(4,128)}, u32[]{:S(2)}) copy-start(s32[4,4]{1,0:T(4,128)} %region.3) | copy-start | bytes 196
  12.6 2.8 %copy-start.2 = (s32[7680]{0:T(1024)S(1)}, s32[7680]{0:T(1024)}, u32[]{:S(2)}) copy-start(s32[7680]{0:T(1024)} %param.18) | copy-start | bytes 92164
  12.6 2.8 %copy-start.3 = (f32[3,16,128]{2,1,0:T(8,128)S(1)}, f32[3,16,128]{2,1,0:T(8,128)}, u32[]{:S(2)}) copy-start(f32[3,16,128]{2,1,0:T(8,128)} %weight_grad.1) | copy-start | bytes 73732
  12.6 2.8 %copy-start.4 = (s32[16]{0:T(128)S(1)}, s32[16]{0:T(128)}, u32[]{:S(2)}) copy-start(s32[16]{0:T(128)} %param.19) | copy-start | bytes 196
  15.3 1.5 %collective-permute-start.2 = (bf16[5,128,128]{2,1,0:T(8,128)(2,1)S(1)}, bf16[5,128,128]{2,1,0:T(8,128)(2,1)S(1)}, u32[]{:S(2)}, u32[]{:S(2)}) collective-permute-start(bf16[5,128,128]{2,1,0:T(8,128)(2,1)S(1)} %collective-permute-done.1.rest_2_), channel_id=1, source_target_pairs={{0,1},{1,0},{2,3},{3,2},{4,5},{5,4},{6,7},{7,6},{8,9},{9,8},{10,11... | collective-permute-start | bytes 491528 | tf_op jit(solution)/shard_map/ppermute | solution.py:657
  16.8 4.5 %copy-start.1 = (s32[16,4]{0,1:T(4,128)S(1)}, s32[16,4]{0,1:T(4,128)}, u32[]{:S(2)}) copy-start(s32[16,4]{0,1:T(4,128)} %param.17) | copy-start | bytes 772
  19.4 4.0 %collective-permute-start.3 = (f32[2,3,192]{2,1,0:T(4,128)S(1)}, f32[2,3,192]{2,1,0:T(4,128)S(1)}, u32[]{:S(2)}, u32[]{:S(2)}) collective-permute-start(f32[2,3,192]{2,1,0:T(4,128)S(1)} %get-tuple-element.48), channel_id=1, source_target_pairs={{0,1},{1,0},{2,3},{3,2},{4,5},{5,4},{6,7},{7,6},{8,9},{9,8},{10,11... | collective-permute-start | bytes 13832 | tf_op jit(solution)/shard_map/ppermute | solution.py:674
  19.6 3.8 %collective-permute-start.4 = (f32[2,3,192]{2,1,0:T(4,128)S(1)}, f32[2,3,192]{2,1,0:T(4,128)S(1)}, u32[]{:S(2)}, u32[]{:S(2)}) collective-permute-start(f32[2,3,192]{2,1,0:T(4,128)S(1)} %get-tuple-element.47), channel_id=1, source_target_pairs={{0,2},{1,3},{2,0},{3,1},{4,6},{5,7},{6,4},{7,5},{8,10},{9,11},{10,... | collective-permute-start | bytes 13832 | tf_op jit(solution)/shard_map/ppermute | solution.py:674
  21.1 3.1 %collective-permute-start.5 = (f32[2,3,192]{2,1,0:T(4,128)S(1)}, f32[2,3,192]{2,1,0:T(4,128)S(1)}, u32[]{:S(2)}, u32[]{:S(2)}) collective-permute-start(f32[2,3,192]{2,1,0:T(4,128)S(1)} %get-tuple-element.46), channel_id=1, source_target_pairs={{0,3},{1,2},{2,1},{3,0},{4,7},{5,6},{6,5},{7,4},{8,11},{9,10},{10,... | collective-permute-start | bytes 13832 | tf_op jit(solution)/shard_map/ppermute | solution.py:674
  24.2 5.5 %collective-permute-start.7 = (f32[2,3,192]{2,1,0:T(4,128)S(1)}, f32[2,3,192]{2,1,0:T(4,128)S(1)}, u32[]{:S(2)}, u32[]{:S(2)}) collective-permute-start(f32[2,3,192]{2,1,0:T(4,128)S(1)} %add_add_fusion), channel_id=1, source_target_pairs={{0,12},{1,9},{2,14},{3,11},{4,8},{5,13},{6,10},{7,15},{8,4},{9,1},... | collective-permute-start | bytes 13832 | tf_op jit(solution)/shard_map/ppermute | solution.py:680
  25.6 4.1 %collective-permute-start.6 = (f32[3,192]{1,0:T(4,128)S(1)}, f32[3,192]{1,0:T(4,128)S(1)}, u32[]{:S(2)}, u32[]{:S(2)}) collective-permute-start(f32[3,192]{1,0:T(4,128)S(1)} %slice_bitcast_fusion.6), channel_id=1, source_target_pairs={{0,4},{4,0},{8,12},{12,8},{1,5},{5,1},{9,13},{13,9},{2,6},{6,2},{1... | collective-permute-start | bytes 6920 | tf_op jit(solution)/shard_map/ppermute | solution.py:681
  29.7 1.2 %collective-permute-start.8 = (f32[3,192]{1,0:T(4,128)S(1)}, f32[3,192]{1,0:T(4,128)S(1)}, u32[]{:S(2)}, u32[]{:S(2)}) collective-permute-start(f32[3,192]{1,0:T(4,128)S(1)} %slice_bitcast_fusion.4), channel_id=1, source_target_pairs={{0,1},{1,0},{2,3},{3,2},{4,5},{5,4},{6,7},{7,6},{8,9},{9,8},{10,11... | collective-permute-start | bytes 6920 | tf_op jit(solution)/shard_map/ppermute | solution.py:683

commit v21 on v20

--- a/solution.py
+++ b/solution.py
@@ -378,7 +378,10 @@
         return (
             pltpu.make_async_copy(field.at[batch], field_in.at[batch], sems.at[batch, 0]),
             pltpu.make_async_copy(basis.at[batch], basis_in.at[batch], sems.at[batch, 1]),
-            pltpu.make_async_copy(basis_grad.at[:, batch], grad_in.at[:, batch], sems.at[batch, 2]),
+            *(
+                pltpu.make_async_copy(basis_grad.at[c, batch], grad_in.at[c, batch], sems.at[batch, 2 + c])
+                for c in range(PARTS)
+            ),
         )
 
     small = (
@@ -442,7 +445,7 @@
             pltpu.VMEM((batches, rows, size), BF16),
             pltpu.VMEM((PARTS, batches, rows, size), BF16),
             pltpu.VMEM((2 + PARTS, rows, size), F32),
-            pltpu.SemaphoreType.DMA((batches, 3)),
+            pltpu.SemaphoreType.DMA((batches, 2 + PARTS)),
             pltpu.SemaphoreType.DMA((2,)),
         ],
         compiler_params=pltpu.CompilerParams(vmem_limit_bytes=VMEM_LIMIT),
@@ -515,9 +518,9 @@
 
 
 def combine_kernel(
-    region, basis, field, moments, hot, grad_columns, *rest, owner_rows, slabs, width, step
+    region, basis, field, moments, hot, grad_columns, *rest, owner_rows, slabs, width
 ):
-    *pieces, product_out, out, stage, matrix, energies = rest
+    *pieces, product_out, out, stage, matrix = rest
     batches, blocks, points, size = basis.shape
     me = lax.axis_index("grid")
     me_atoms = lax.axis_index("atoms")
@@ -550,31 +553,24 @@
         jnp.concatenate([jnp.sum(total, axis=0, keepdims=True) for total in totals[c]], axis=1) for c in range(PARTS)
     ]
 
-    energies[...] = jnp.zeros_like(energies)
+    energies = jnp.zeros((points, size), F32)
     lanes = lax.broadcasted_iota(jnp.int32, (points, size), 1)
-
-    @pl.loop(0, batches // step)
-    def _(group):
-        left = [
-            jnp.concatenate([basis[group * step + inner, p] for p in range(blocks)], axis=1) for inner in range(step)
-        ]
-        left = jnp.concatenate(left, axis=0)
-        energy = [jnp.zeros((points, size), F32) for _ in range(step)]
-        for q in range(0, blocks, 2):
-            product = jnp.dot(left, matrix[:, q * size : (q + 2) * size], preferred_element_type=F32)
-            for inner in range(step):
-                batch = group * step + inner
-                for column in range(2):
-                    part = product[inner * points : (inner + 1) * points, column * size : (column + 1) * size]
-                    product_out[batch, q + column] = part.astype(BF16)
-                    energy[inner] = energy[inner] + part * field[batch, q + column].astype(F32)
-        for inner in range(step):
-            total = jnp.sum(energy[inner], axis=1, keepdims=True)
-            energies[...] = jnp.where(lanes == group * step + inner, total, energies[...])
+    left = [jnp.concatenate([basis[batch, p] for p in range(blocks)], axis=1) for batch in range(batches)]
+    left = jnp.concatenate(left, axis=0)
+    energy = [jnp.zeros((points, size), F32) for _ in range(batches)]
+    for q in range(0, blocks, 2):
+        product = jnp.dot(left, matrix[:, q * size : (q + 2) * size], preferred_element_type=F32)
+        for batch in range(batches):
+            for column in range(2):
+                part = product[batch * points : (batch + 1) * points, column * size : (column + 1) * size]
+                product_out[batch, q + column] = part.astype(BF16)
+                energy[batch] = energy[batch] + part * field[batch, q + column].astype(F32)
+    for batch in range(batches):
+        energies = jnp.where(lanes == batch, jnp.sum(energy[batch], axis=1, keepdims=True), energies)
 
     lefts = []
     for c in range(PARTS):
-        term = jnp.sum(energies[...] * grad_columns[c], axis=0, keepdims=True)
+        term = jnp.sum(energies * grad_columns[c], axis=0, keepdims=True)
         lefts.append(jnp.concatenate([-2.0 * derivative[c], term], axis=1))
     left = jnp.concatenate(lefts, axis=0)
     high, middle, low = (piece.astype(F32) for piece in split(left))
@@ -594,10 +590,9 @@
     basis, field, moments, hot, grad_columns = prepared
     slabs, atom_devices, atom_total, points, blocks, width, owner_rows = shapes
     batches, _, _, size = basis.shape
-    step = 16 if batches % 16 == 0 else 1
     vmem = pl.BlockSpec(memory_space=pltpu.VMEM)
     return pl.pallas_call(
-        functools.partial(combine_kernel, owner_rows=owner_rows, slabs=slabs, width=width, step=step),
+        functools.partial(combine_kernel, owner_rows=owner_rows, slabs=slabs, width=width),
         out_shape=(
             jax.ShapeDtypeStruct(basis.shape, BF16),
             jax.ShapeDtypeStruct((atom_devices, 2, PARTS, atom_total // atom_devices), F32),
@@ -607,7 +602,6 @@
         scratch_shapes=[
             pltpu.VMEM((slabs * TRAVEL, size, size), BF16),
             pltpu.VMEM((blocks * size, blocks * size), BF16),
-            pltpu.VMEM((points, size), F32),
         ],
         compiler_params=pltpu.CompilerParams(vmem_limit_bytes=VMEM_LIMIT),
     )(region, basis, field, moments, hot, grad_columns, *pieces)

time: 31.6 us -> 32 us (1.013)
  Pallas kernels: 14.6 us -> 15 us
  starting transfers between devices: 9.66 us -> 9.28 us
  waiting for transfers between devices: 5.72 us -> 6.1 us
    ppermute x1, waiting for transfers between devices: 3.41 us -> 3.79 us  [sum_parts(): lax.ppermute(both, ('grid', 'atoms'), moves_over_grid(shifts, slabs, atom...]
    pallas_call x1, Pallas kernels: 4.98 us -> 5.35 us  [reorder(): pl.pallas_call(reorder_kernel, out_shape=(ordered, ordered, jax.ShapeDtyp...]
    ppermute x1, starting transfers between devices: 0.68 us -> 0.31 us  [sum_parts(): near = lax.ppermute(both[0], 'grid', [(i, i ^ 1) for i in range(slabs)])]
  transfers between devices with their start and end apart: 9 -> 9, of which waited for: 4 -> 4; matrix products, arithmetic and copies ran while one was open for 0% -> 0% of each run, Pallas kernels for 34% -> 35%
where the time goes in v21:
time: 32 us; the launch traced here: 31.8 us
  Pallas kernels  15 us (47%)
  starting transfers between devices  9.28 us (29%)
  waiting for transfers between devices  6.1 us (19%)
  between operations  0.79 us (2%)
  other arithmetic  0.6 us (2%)
    ppermute x2, starting transfers between devices, fetch_rows(): lax.ppermute(piece, ('grid', 'atoms'), moves_over_grid(shifts, slabs, ato...  5.56 us
    pallas_call x1, Pallas kernels, reorder(): pl.pallas_call(reorder_kernel, out_shape=(ordered, ordered, jax.ShapeDtyp...  5.35 us
    ppermute x1, waiting for transfers between devices, sum_parts(): lax.ppermute(both, ('grid', 'atoms'), moves_over_grid(shifts, slabs, atom...  3.79 us
    pallas_call x1, Pallas kernels, build_moments(): pl.pallas_call(moment_kernel, out_shape=jax.ShapeDtypeStruct((PARTS, bloc...  2.62 us
    pallas_call x1, Pallas kernels, combine(): pl.pallas_call(functools.partial(combine_kernel, owner_rows=owner_rows, s...  2.59 us
    pallas_call x1, Pallas kernels, write(): pl.pallas_call(write_kernel, out_shape=jax.ShapeDtypeStruct(shape, BF16),...  2.06 us
    ppermute x3, starting transfers between devices, sum_parts(): lax.ppermute(partial_grad[d], 'atoms', [(i, i ^ d) for i in range(atom_de...  1.93 us
    ppermute x1, starting transfers between devices, sum_parts(): lax.ppermute(both, ('grid', 'atoms'), moves_over_grid(shifts, slabs, atom...  1.41 us
  transfers between devices with their start and end apart: 9, of which 4 were waited for; matrix products, arithmetic and copies ran while one was open for 0% of the time, Pallas kernels for 35%

profile of v21, /device:TPU:0, one launch (start us, length us, event | category | flops | bytes accessed | tf_op | source)
XLA Modules:
  0.0 31.8 jit_solution(7628743686408140778)
XLA Ops:
  0.6 1.4 %shard_map.113 = (bf16[5,128,128]{2,1,0:T(8,128)(2,1)S(1)}, bf16[5,128,128]{2,1,0:T(8,128)(2,1)S(1)}, bf16[5,128,128]{2,1,0:T(8,128)(2,1)S(1)}) custom-call(s32[4,4]{1,0:T(4,128)} %region.3, bf16[15,3,128,128]{3,2,1,0:T(8,128)(2,1)} %density.1), custom_call_target="tpu_custom_call" | custom-call | tf_op jit(solution)/shard_map/pallas_call | solution.py:95
  2.0 3.1 %collective-permute-start = (bf16[5,128,128]{2,1,0:T(8,128)(2,1)S(1)}, bf16[5,128,128]{2,1,0:T(8,128)(2,1)S(1)}, u32[]{:S(2)}, u32[]{:S(2)}) collective-permute-start(bf16[5,128,128]{2,1,0:T(8,128)(2,1)S(1)} %get-tuple-element.24), channel_id=1, source_target_pairs={{0,4},{1,5},{2,6},{3,7},{4,0},{5,1},{6,2},{7,3},{8,12},{9,13},{10,... | collective-permute-start | bytes 491528 | tf_op jit(solution)/shard_map/ppermute | solution.py:114
  5.1 2.5 %collective-permute-start.1 = (bf16[5,128,128]{2,1,0:T(8,128)(2,1)S(1)}, bf16[5,128,128]{2,1,0:T(8,128)(2,1)S(1)}, u32[]{:S(2)}, u32[]{:S(2)}) collective-permute-start(bf16[5,128,128]{2,1,0:T(8,128)(2,1)S(1)} %get-tuple-element.25), channel_id=1, source_target_pairs={{0,12},{1,9},{2,14},{3,11},{4,8},{5,13},{6,10},{7,15},{8,4},{9,1},... | collective-permute-start | bytes 491528 | tf_op jit(solution)/shard_map/ppermute | solution.py:114
  7.6 5.3 %shard_map.114 = (bf16[16,4,128,128]{3,2,1,0:T(8,128)(2,1)S(1)}, bf16[16,4,128,128]{3,2,1,0:T(8,128)(2,1)S(1)}, bf16[4,2048,128]{2,1,0:T(8,128)(2,1)S(1)}, bf16[3,4,2048,128]{3,2,1,0:T(8,128)(2,1)S(1)}) custom-call(s32[4,16]{1,0:T(4,128)} %bitcast.27, bf16[16,512,128]{2,1,0:T(8,128)(2,1)} %bitcast.32, bf16[16,512,128]{2,1,0:T(8,128)(2,1)} %bitcast.33, ...), custom_call_target="tpu_custom_call" | custom-call | bytes 10485760 | tf_op jit(solution)/shard_map/pallas_call | solution.py:430
  13.0 0.0 copy-start
  13.0 0.0 copy-start.2
  13.0 0.0 copy-start.3
  13.0 0.0 copy-start.4
  13.0 2.6 %shard_map.115.moments = f32[3,512,512]{2,1,0:T(8,128)S(1)} custom-call(bf16[4,2048,128]{2,1,0:T(8,128)(2,1)S(1)} %get-tuple-element.28.weighted, bf16[3,4,2048,128]{3,2,1,0:T(8,128)(2,1)S(1)} %get-tuple-element.29.grads), custom_call_target="tpu_custom_call" | custom-call | flops 3221225472 | tf_op jit(solution)/shard_map/pallas_call | solution.py:473
  15.6 0.0 collective-permute-done.rest_1_
  15.6 0.0 collective-permute-done.1.rest_2_
  15.7 0.1 collective-permute-start.2
  15.7 0.0 copy-done
  15.7 0.0 copy-done.2
  15.8 0.0 copy-done.3
  15.8 0.0 copy-done.4
  15.8 1.0 %shard_map.116 = (bf16[768,640]{1,0:T(8,128)(2,1)S(1)}, f32[3,128,128]{2,1,0:T(8,128)S(1)}) custom-call(s32[4,4]{1,0:T(4,128)S(1)} %copy-done, s32[60,128]{1,0:T(8,128)S(1)} %bitcast.29, s32[1,16]{1,0:T(1,128)S(1)} %bitcast.30, f32[3,16,128]{2,1,0:T(8,128)S(1)} %copy-done.3), custom_call_target="tpu_custom_call" | custom-call | flops 1000000000 | bytes 196608 | tf_op jit(solution)/shard_map/pallas_call | solution.py:507
  16.7 0.4 %collective-permute-done.2.rest_3_ = bf16[5,128,128]{2,1,0:T(8,128)(2,1)S(1)} collective-permute-done((bf16[5,128,128]{2,1,0:T(8,128)(2,1)S(1)}, bf16[5,128,128]{2,1,0:T(8,128)(2,1)S(1)}, u32[]{:S(2)}, u32[]{:S(2)}) %collective-permute-start.2) | collective-permute-done | bytes 163872 | tf_op jit(solution)/shard_map/ppermute | solution.py:651
  17.1 0.0 copy-start.1
  17.1 2.6 %shard_map.117 = (bf16[16,4,128,128]{3,2,1,0:T(8,128)(2,1)S(1)}, f32[4,2,3,192]{3,2,1,0:T(4,128)S(1)}) custom-call(s32[4,4]{1,0:T(4,128)S(1)} %copy-done, bf16[16,4,128,128]{3,2,1,0:T(8,128)(2,1)S(1)} %get-tuple-element.30.basis, bf16[16,4,128,128]{3,2,1,0:T(8,128)(2,1)S(1)} %get-tuple-element.31.field, f32[3,512,512]{2,1,0:T(8,128)S(1)} %shard_map.115.moments, ...), custom_call_target="tpu_custom_call" | custom-call | tf_op jit(solution)/shard_map/pallas_call | solution.py:594
  19.7 0.2 collective-permute-start.3
  19.9 1.5 %collective-permute-start.4 = (f32[2,3,192]{2,1,0:T(4,128)S(1)}, f32[2,3,192]{2,1,0:T(4,128)S(1)}, u32[]{:S(2)}, u32[]{:S(2)}) collective-permute-start(f32[2,3,192]{2,1,0:T(4,128)S(1)} %get-tuple-element.47), channel_id=1, source_target_pairs={{0,2},{1,3},{2,0},{3,1},{4,6},{5,7},{6,4},{7,5},{8,10},{9,11},{10,... | collective-permute-start | bytes 13832 | tf_op jit(solution)/shard_map/ppermute | solution.py:668
  21.5 0.2 collective-permute-start.5
  21.7 0.0 copy-done.1
  21.7 2.1 %shard_map.118 = bf16[16,512,128]{2,1,0:T(8,128)(2,1)} custom-call(s32[4,16]{1,0:T(4,128)S(1)} %bitcast.28, bf16[16,4,128,128]{3,2,1,0:T(8,128)(2,1)S(1)} %get-tuple-element.40.product), custom_call_target="tpu_custom_call" | custom-call | bytes 4194304 | tf_op jit(solution)/shard_map/pallas_call | solution.py:633
  23.7 0.0 collective-permute-done.3
  23.7 0.0 collective-permute-done.4
  23.8 0.8 %collective-permute-done.5 = f32[2,3,192]{2,1,0:T(4,128)S(1)} collective-permute-done((f32[2,3,192]{2,1,0:T(4,128)S(1)}, f32[2,3,192]{2,1,0:T(4,128)S(1)}, u32[]{:S(2)}, u32[]{:S(2)}) %collective-permute-start.5) | collective-permute-done | bytes 4640 | tf_op jit(solution)/shard_map/ppermute | solution.py:668
  24.5 1.4 %collective-permute-start.7 = (f32[2,3,192]{2,1,0:T(4,128)S(1)}, f32[2,3,192]{2,1,0:T(4,128)S(1)}, u32[]{:S(2)}, u32[]{:S(2)}) collective-permute-start(f32[2,3,192]{2,1,0:T(4,128)S(1)} %add_add_fusion), channel_id=1, source_target_pairs={{0,12},{1,9},{2,14},{3,11},{4,8},{5,13},{6,10},{7,15},{8,4},{9,1},... | collective-permute-start | bytes 13832 | tf_op jit(solution)/shard_map/ppermute | solution.py:674
  25.9 0.3 collective-permute-start.6
  26.3 3.8 %collective-permute-done.7 = f32[2,3,192]{2,1,0:T(4,128)S(1)} collective-permute-done((f32[2,3,192]{2,1,0:T(4,128)S(1)}, f32[2,3,192]{2,1,0:T(4,128)S(1)}, u32[]{:S(2)}, u32[]{:S(2)}) %collective-permute-start.7) | collective-permute-done | bytes 4640 | tf_op jit(solution)/shard_map/ppermute | solution.py:674
  30.0 0.0 collective-permute-start.8
  30.1 0.0 collective-permute-done.6
  30.1 1.2 %collective-permute-done.8 = f32[3,192]{1,0:T(4,128)S(1)} collective-permute-done((f32[3,192]{1,0:T(4,128)S(1)}, f32[3,192]{1,0:T(4,128)S(1)}, u32[]{:S(2)}, u32[]{:S(2)}) %collective-permute-start.8) | collective-permute-done | bytes 2336 | tf_op jit(solution)/shard_map/ppermute | solution.py:677
  31.2 0.6 %fusion.1 = f32[3,192]{1,0:T(4,128)} fusion(f32[3,192]{1,0:T(4,128)S(1)} %collective-permute-done.8, f32[2,3,192]{2,1,0:T(4,128)S(1)} %collective-permute-done.7, f32[3,192]{1,0:T(4,128)S(1)} %collective-permute-done.6, f32[2,3,192]{2,1,0:T(4,128)S(1)} %add_add_fusion), kind=kLoop, calls=%fused_computation.8 | loop fusion | flops 1728 | bytes 11520 | tf_op jit(solution)/shard_map/add | solution.py:658
  (4 shorter events, 0.0 us)
Async XLA Ops:
  2.0 13.6 %collective-permute-start = (bf16[5,128,128]{2,1,0:T(8,128)(2,1)S(1)}, bf16[5,128,128]{2,1,0:T(8,128)(2,1)S(1)}, u32[]{:S(2)}, u32[]{:S(2)}) collective-permute-start(bf16[5,128,128]{2,1,0:T(8,128)(2,1)S(1)} %get-tuple-element.24), channel_id=1, source_target_pairs={{0,4},{1,5},{2,6},{3,7},{4,0},{5,1},{6,2},{7,3},{8,12},{9,13},{10,... | collective-permute-start | bytes 491528 | tf_op jit(solution)/shard_map/ppermute | solution.py:114
  5.1 10.5 %collective-permute-start.1 = (bf16[5,128,128]{2,1,0:T(8,128)(2,1)S(1)}, bf16[5,128,128]{2,1,0:T(8,128)(2,1)S(1)}, u32[]{:S(2)}, u32[]{:S(2)}) collective-permute-start(bf16[5,128,128]{2,1,0:T(8,128)(2,1)S(1)} %get-tuple-element.25), channel_id=1, source_target_pairs={{0,12},{1,9},{2,14},{3,11},{4,8},{5,13},{6,10},{7,15},{8,4},{9,1},... | collective-permute-start | bytes 491528 | tf_op jit(solution)/shard_map/ppermute | solution.py:114
  13.0 2.8 %copy-start = (s32[4,4]{1,0:T(4,128)S(1)}, s32[4,4]{1,0:T(4,128)}, u32[]{:S(2)}) copy-start(s32[4,4]{1,0:T(4,128)} %region.3) | copy-start | bytes 196
  13.0 2.8 %copy-start.2 = (s32[7680]{0:T(1024)S(1)}, s32[7680]{0:T(1024)}, u32[]{:S(2)}) copy-start(s32[7680]{0:T(1024)} %param.18) | copy-start | bytes 92164
  13.0 2.8 %copy-start.3 = (f32[3,16,128]{2,1,0:T(8,128)S(1)}, f32[3,16,128]{2,1,0:T(8,128)}, u32[]{:S(2)}) copy-start(f32[3,16,128]{2,1,0:T(8,128)} %weight_grad.1) | copy-start | bytes 73732
  13.0 2.8 %copy-start.4 = (s32[16]{0:T(128)S(1)}, s32[16]{0:T(128)}, u32[]{:S(2)}) copy-start(s32[16]{0:T(128)} %param.19) | copy-start | bytes 196
  15.7 1.5 %collective-permute-start.2 = (bf16[5,128,128]{2,1,0:T(8,128)(2,1)S(1)}, bf16[5,128,128]{2,1,0:T(8,128)(2,1)S(1)}, u32[]{:S(2)}, u32[]{:S(2)}) collective-permute-start(bf16[5,128,128]{2,1,0:T(8,128)(2,1)S(1)} %collective-permute-done.1.rest_2_), channel_id=1, source_target_pairs={{0,1},{1,0},{2,3},{3,2},{4,5},{5,4},{6,7},{7,6},{8,9},{9,8},{10,11... | collective-permute-start | bytes 491528 | tf_op jit(solution)/shard_map/ppermute | solution.py:651
  17.1 4.5 %copy-start.1 = (s32[16,4]{0,1:T(4,128)S(1)}, s32[16,4]{0,1:T(4,128)}, u32[]{:S(2)}) copy-start(s32[16,4]{0,1:T(4,128)} %param.17) | copy-start | bytes 772
  19.7 4.0 %collective-permute-start.3 = (f32[2,3,192]{2,1,0:T(4,128)S(1)}, f32[2,3,192]{2,1,0:T(4,128)S(1)}, u32[]{:S(2)}, u32[]{:S(2)}) collective-permute-start(f32[2,3,192]{2,1,0:T(4,128)S(1)} %get-tuple-element.48), channel_id=1, source_target_pairs={{0,1},{1,0},{2,3},{3,2},{4,5},{5,4},{6,7},{7,6},{8,9},{9,8},{10,11... | collective-permute-start | bytes 13832 | tf_op jit(solution)/shard_map/ppermute | solution.py:668
  19.9 3.8 %collective-permute-start.4 = (f32[2,3,192]{2,1,0:T(4,128)S(1)}, f32[2,3,192]{2,1,0:T(4,128)S(1)}, u32[]{:S(2)}, u32[]{:S(2)}) collective-permute-start(f32[2,3,192]{2,1,0:T(4,128)S(1)} %get-tuple-element.47), channel_id=1, source_target_pairs={{0,2},{1,3},{2,0},{3,1},{4,6},{5,7},{6,4},{7,5},{8,10},{9,11},{10,... | collective-permute-start | bytes 13832 | tf_op jit(solution)/shard_map/ppermute | solution.py:668
  21.5 3.1 %collective-permute-start.5 = (f32[2,3,192]{2,1,0:T(4,128)S(1)}, f32[2,3,192]{2,1,0:T(4,128)S(1)}, u32[]{:S(2)}, u32[]{:S(2)}) collective-permute-start(f32[2,3,192]{2,1,0:T(4,128)S(1)} %get-tuple-element.46), channel_id=1, source_target_pairs={{0,3},{1,2},{2,1},{3,0},{4,7},{5,6},{6,5},{7,4},{8,11},{9,10},{10,... | collective-permute-start | bytes 13832 | tf_op jit(solution)/shard_map/ppermute | solution.py:668
  24.5 5.5 %collective-permute-start.7 = (f32[2,3,192]{2,1,0:T(4,128)S(1)}, f32[2,3,192]{2,1,0:T(4,128)S(1)}, u32[]{:S(2)}, u32[]{:S(2)}) collective-permute-start(f32[2,3,192]{2,1,0:T(4,128)S(1)} %add_add_fusion), channel_id=1, source_target_pairs={{0,12},{1,9},{2,14},{3,11},{4,8},{5,13},{6,10},{7,15},{8,4},{9,1},... | collective-permute-start | bytes 13832 | tf_op jit(solution)/shard_map/ppermute | solution.py:674
  25.9 4.1 %collective-permute-start.6 = (f32[3,192]{1,0:T(4,128)S(1)}, f32[3,192]{1,0:T(4,128)S(1)}, u32[]{:S(2)}, u32[]{:S(2)}) collective-permute-start(f32[3,192]{1,0:T(4,128)S(1)} %slice_bitcast_fusion.6), channel_id=1, source_target_pairs={{0,4},{4,0},{8,12},{12,8},{1,5},{5,1},{9,13},{13,9},{2,6},{6,2},{1... | collective-permute-start | bytes 6920 | tf_op jit(solution)/shard_map/ppermute | solution.py:675
  30.0 1.2 %collective-permute-start.8 = (f32[3,192]{1,0:T(4,128)S(1)}, f32[3,192]{1,0:T(4,128)S(1)}, u32[]{:S(2)}, u32[]{:S(2)}) collective-permute-start(f32[3,192]{1,0:T(4,128)S(1)} %slice_bitcast_fusion.4), channel_id=1, source_target_pairs={{0,1},{1,0},{2,3},{3,2},{4,5},{5,4},{6,7},{7,6},{8,9},{9,8},{10,11... | collective-permute-start | bytes 6920 | tf_op jit(solution)/shard_map/ppermute | solution.py:677

commit v22 on v21

--- a/solution.py
+++ b/solution.py
@@ -365,9 +365,7 @@
     pattern,
     weights,
     columns,
-    basis_in,
-    field_in,
-    grad_in,
+    landed,
     wide,
     sems,
     small_sems,
@@ -376,12 +374,9 @@
 
     def copies(batch):
         return (
-            pltpu.make_async_copy(field.at[batch], field_in.at[batch], sems.at[batch, 0]),
-            pltpu.make_async_copy(basis.at[batch], basis_in.at[batch], sems.at[batch, 1]),
-            *(
-                pltpu.make_async_copy(basis_grad.at[c, batch], grad_in.at[c, batch], sems.at[batch, 2 + c])
-                for c in range(PARTS)
-            ),
+            pltpu.make_async_copy(field.at[batch], landed.at[batch, 0], sems.at[batch]),
+            pltpu.make_async_copy(basis.at[batch], landed.at[batch, 1], sems.at[batch]),
+            pltpu.make_async_copy(basis_grad.at[:, batch], landed.at[batch, pl.ds(2, PARTS)], sems.at[batch]),
         )
 
     small = (
@@ -404,14 +399,11 @@
 
     @pl.loop(0, batches)
     def _(batch):
-        for copy in copies(batch):
-            copy.wait()
+        pltpu.make_async_copy(landed.at[batch], landed.at[batch], sems.at[batch]).wait()
         points_here = pl.ds(pl.multiple_of(batch * points, points), points)
         places = [pattern[s, batch] for s in range(blocks)]
-        wide[0] = field_in[batch].astype(F32)
-        wide[1] = basis_in[batch].astype(F32)
-        for c in range(PARTS):
-            wide[2 + c] = grad_in[c, batch].astype(F32)
+        for array in range(2 + PARTS):
+            wide[array] = landed[batch, array].astype(F32)
         for s, place in enumerate(places):
             strided = pl.ds(s, points, stride=blocks)
             values = wide[0, strided, :]
@@ -441,11 +433,9 @@
             pltpu.SMEM((blocks, batches), jnp.int32),
             pltpu.VMEM(weights.shape, F32),
             pltpu.VMEM((batches, points, size), F32),
-            pltpu.VMEM((batches, rows, size), BF16),
-            pltpu.VMEM((batches, rows, size), BF16),
-            pltpu.VMEM((PARTS, batches, rows, size), BF16),
+            pltpu.VMEM((batches, 2 + PARTS, rows, size), BF16),
             pltpu.VMEM((2 + PARTS, rows, size), F32),
-            pltpu.SemaphoreType.DMA((batches, 2 + PARTS)),
+            pltpu.SemaphoreType.DMA((batches,)),
             pltpu.SemaphoreType.DMA((2,)),
         ],
         compiler_params=pltpu.CompilerParams(vmem_limit_bytes=VMEM_LIMIT),

time: 32 us -> 31.4 us (0.981)
  Pallas kernels: 15 us -> 14.3 us
  starting transfers between devices: 9.28 us -> 9.8 us
  waiting for transfers between devices: 6.1 us -> 5.73 us
    pallas_call x1, Pallas kernels: 5.35 us -> 4.65 us  [reorder(): pl.pallas_call(reorder_kernel, out_shape=(ordered, ordered, jax.ShapeDtyp...]
    ppermute x1, waiting for transfers between devices: 3.79 us -> 3.2 us  [sum_parts(): lax.ppermute(both, ('grid', 'atoms'), moves_over_grid(shifts, slabs, atom...]
    ppermute x1, starting transfers between devices: 0.31 us -> 0.77 us  [sum_parts(): near = lax.ppermute(both[0], 'grid', [(i, i ^ 1) for i in range(slabs)])]
  transfers between devices with their start and end apart: 9 -> 9, of which waited for: 4 -> 5; matrix products, arithmetic and copies ran while one was open for 0% -> 0% of each run, Pallas kernels for 35% -> 33%
where the time goes in v22:
time: 31.4 us; the launch traced here: 31.2 us
  Pallas kernels  14.3 us (46%)
  starting transfers between devices  9.8 us (31%)
  waiting for transfers between devices  5.73 us (18%)
  between operations  0.76 us (2%)
  other arithmetic  0.6 us (2%)
    ppermute x2, starting transfers between devices, fetch_rows(): lax.ppermute(piece, ('grid', 'atoms'), moves_over_grid(shifts, slabs, ato...  5.56 us
    pallas_call x1, Pallas kernels, reorder(): pl.pallas_call(reorder_kernel, out_shape=(ordered, ordered, jax.ShapeDtyp...  4.65 us
    ppermute x1, waiting for transfers between devices, sum_parts(): lax.ppermute(both, ('grid', 'atoms'), moves_over_grid(shifts, slabs, atom...  3.2 us
    pallas_call x1, Pallas kernels, build_moments(): pl.pallas_call(moment_kernel, out_shape=jax.ShapeDtypeStruct((PARTS, bloc...  2.62 us
    pallas_call x1, Pallas kernels, combine(): pl.pallas_call(functools.partial(combine_kernel, owner_rows=owner_rows, s...  2.58 us
    pallas_call x1, Pallas kernels, write(): pl.pallas_call(write_kernel, out_shape=jax.ShapeDtypeStruct(shape, BF16),...  2.06 us
    ppermute x3, starting transfers between devices, sum_parts(): lax.ppermute(partial_grad[d], 'atoms', [(i, i ^ d) for i in range(atom_de...  1.93 us
    ppermute x1, starting transfers between devices, sum_parts(): lax.ppermute(both, ('grid', 'atoms'), moves_over_grid(shifts, slabs, atom...  1.53 us
  transfers between devices with their start and end apart: 9, of which 5 were waited for; matrix products, arithmetic and copies ran while one was open for 0% of the time, Pallas kernels for 33%

profile of v22, /device:TPU:0, one launch (start us, length us, event | category | flops | bytes accessed | tf_op | source)
XLA Modules:
  0.0 31.2 jit_solution(6885737579745900776)
XLA Ops:
  0.6 1.4 %shard_map.113 = (bf16[5,128,128]{2,1,0:T(8,128)(2,1)S(1)}, bf16[5,128,128]{2,1,0:T(8,128)(2,1)S(1)}, bf16[5,128,128]{2,1,0:T(8,128)(2,1)S(1)}) custom-call(s32[4,4]{1,0:T(4,128)} %region.3, bf16[15,3,128,128]{3,2,1,0:T(8,128)(2,1)} %density.1), custom_call_target="tpu_custom_call" | custom-call | tf_op jit(solution)/shard_map/pallas_call | solution.py:95
  2.0 3.1 %collective-permute-start = (bf16[5,128,128]{2,1,0:T(8,128)(2,1)S(1)}, bf16[5,128,128]{2,1,0:T(8,128)(2,1)S(1)}, u32[]{:S(2)}, u32[]{:S(2)}) collective-permute-start(bf16[5,128,128]{2,1,0:T(8,128)(2,1)S(1)} %get-tuple-element.24), channel_id=1, source_target_pairs={{0,4},{1,5},{2,6},{3,7},{4,0},{5,1},{6,2},{7,3},{8,12},{9,13},{10,... | collective-permute-start | bytes 491528 | tf_op jit(solution)/shard_map/ppermute | solution.py:114
  5.1 2.5 %collective-permute-start.1 = (bf16[5,128,128]{2,1,0:T(8,128)(2,1)S(1)}, bf16[5,128,128]{2,1,0:T(8,128)(2,1)S(1)}, u32[]{:S(2)}, u32[]{:S(2)}) collective-permute-start(bf16[5,128,128]{2,1,0:T(8,128)(2,1)S(1)} %get-tuple-element.25), channel_id=1, source_target_pairs={{0,12},{1,9},{2,14},{3,11},{4,8},{5,13},{6,10},{7,15},{8,4},{9,1},... | collective-permute-start | bytes 491528 | tf_op jit(solution)/shard_map/ppermute | solution.py:114
  7.6 4.6 %shard_map.114 = (bf16[16,4,128,128]{3,2,1,0:T(8,128)(2,1)S(1)}, bf16[16,4,128,128]{3,2,1,0:T(8,128)(2,1)S(1)}, bf16[4,2048,128]{2,1,0:T(8,128)(2,1)S(1)}, bf16[3,4,2048,128]{3,2,1,0:T(8,128)(2,1)S(1)}) custom-call(s32[4,16]{1,0:T(4,128)} %bitcast.27, bf16[16,512,128]{2,1,0:T(8,128)(2,1)} %bitcast.32, bf16[16,512,128]{2,1,0:T(8,128)(2,1)} %bitcast.33, ...), custom_call_target="tpu_custom_call" | custom-call | bytes 10485760 | tf_op jit(solution)/shard_map/pallas_call | solution.py:422
  12.3 0.0 copy-start
  12.3 0.0 copy-start.2
  12.3 0.0 copy-start.3
  12.3 0.0 copy-start.4
  12.3 2.6 %shard_map.115.moments = f32[3,512,512]{2,1,0:T(8,128)S(1)} custom-call(bf16[4,2048,128]{2,1,0:T(8,128)(2,1)S(1)} %get-tuple-element.28.weighted, bf16[3,4,2048,128]{3,2,1,0:T(8,128)(2,1)S(1)} %get-tuple-element.29.grads), custom_call_target="tpu_custom_call" | custom-call | flops 3221225472 | tf_op jit(solution)/shard_map/pallas_call | solution.py:463
  14.9 0.0 collective-permute-done.rest_1_
  15.0 0.2 collective-permute-done.1.rest_2_
  15.1 0.0 collective-permute-start.2
  15.1 0.0 copy-done
  15.1 0.0 copy-done.2
  15.1 0.0 copy-done.3
  15.2 0.0 copy-done.4
  15.2 1.0 %shard_map.116 = (bf16[768,640]{1,0:T(8,128)(2,1)S(1)}, f32[3,128,128]{2,1,0:T(8,128)S(1)}) custom-call(s32[4,4]{1,0:T(4,128)S(1)} %copy-done, s32[60,128]{1,0:T(8,128)S(1)} %bitcast.29, s32[1,16]{1,0:T(1,128)S(1)} %bitcast.30, f32[3,16,128]{2,1,0:T(8,128)S(1)} %copy-done.3), custom_call_target="tpu_custom_call" | custom-call | flops 1000000000 | bytes 196608 | tf_op jit(solution)/shard_map/pallas_call | solution.py:497
  16.1 0.4 %collective-permute-done.2.rest_3_ = bf16[5,128,128]{2,1,0:T(8,128)(2,1)S(1)} collective-permute-done((bf16[5,128,128]{2,1,0:T(8,128)(2,1)S(1)}, bf16[5,128,128]{2,1,0:T(8,128)(2,1)S(1)}, u32[]{:S(2)}, u32[]{:S(2)}) %collective-permute-start.2) | collective-permute-done | bytes 163872 | tf_op jit(solution)/shard_map/ppermute | solution.py:641
  16.5 0.0 copy-start.1
  16.5 2.6 %shard_map.117 = (bf16[16,4,128,128]{3,2,1,0:T(8,128)(2,1)S(1)}, f32[4,2,3,192]{3,2,1,0:T(4,128)S(1)}) custom-call(s32[4,4]{1,0:T(4,128)S(1)} %copy-done, bf16[16,4,128,128]{3,2,1,0:T(8,128)(2,1)S(1)} %get-tuple-element.30.basis, bf16[16,4,128,128]{3,2,1,0:T(8,128)(2,1)S(1)} %get-tuple-element.31.field, f32[3,512,512]{2,1,0:T(8,128)S(1)} %shard_map.115.moments, ...), custom_call_target="tpu_custom_call" | custom-call | tf_op jit(solution)/shard_map/pallas_call | solution.py:584
  19.1 0.2 collective-permute-start.3
  19.4 1.5 %collective-permute-start.4 = (f32[2,3,192]{2,1,0:T(4,128)S(1)}, f32[2,3,192]{2,1,0:T(4,128)S(1)}, u32[]{:S(2)}, u32[]{:S(2)}) collective-permute-start(f32[2,3,192]{2,1,0:T(4,128)S(1)} %get-tuple-element.47), channel_id=1, source_target_pairs={{0,2},{1,3},{2,0},{3,1},{4,6},{5,7},{6,4},{7,5},{8,10},{9,11},{10,... | collective-permute-start | bytes 13832 | tf_op jit(solution)/shard_map/ppermute | solution.py:658
  20.9 0.2 collective-permute-start.5
  21.1 0.0 copy-done.1
  21.1 2.1 %shard_map.118 = bf16[16,512,128]{2,1,0:T(8,128)(2,1)} custom-call(s32[4,16]{1,0:T(4,128)S(1)} %bitcast.28, bf16[16,4,128,128]{3,2,1,0:T(8,128)(2,1)S(1)} %get-tuple-element.40.product), custom_call_target="tpu_custom_call" | custom-call | bytes 4194304 | tf_op jit(solution)/shard_map/pallas_call | solution.py:623
  23.1 0.0 collective-permute-done.3
  23.2 0.0 collective-permute-done.4
  23.2 0.8 %collective-permute-done.5 = f32[2,3,192]{2,1,0:T(4,128)S(1)} collective-permute-done((f32[2,3,192]{2,1,0:T(4,128)S(1)}, f32[2,3,192]{2,1,0:T(4,128)S(1)}, u32[]{:S(2)}, u32[]{:S(2)}) %collective-permute-start.5) | collective-permute-done | bytes 4640 | tf_op jit(solution)/shard_map/ppermute | solution.py:658
  24.0 1.5 %collective-permute-start.7 = (f32[2,3,192]{2,1,0:T(4,128)S(1)}, f32[2,3,192]{2,1,0:T(4,128)S(1)}, u32[]{:S(2)}, u32[]{:S(2)}) collective-permute-start(f32[2,3,192]{2,1,0:T(4,128)S(1)} %add_add_fusion), channel_id=1, source_target_pairs={{0,12},{1,9},{2,14},{3,11},{4,8},{5,13},{6,10},{7,15},{8,4},{9,1},... | collective-permute-start | bytes 13832 | tf_op jit(solution)/shard_map/ppermute | solution.py:664
  25.5 0.8 %collective-permute-start.6 = (f32[3,192]{1,0:T(4,128)S(1)}, f32[3,192]{1,0:T(4,128)S(1)}, u32[]{:S(2)}, u32[]{:S(2)}) collective-permute-start(f32[3,192]{1,0:T(4,128)S(1)} %slice_bitcast_fusion.6), channel_id=1, source_target_pairs={{0,4},{4,0},{8,12},{12,8},{1,5},{5,1},{9,13},{13,9},{2,6},{6,2},{1... | collective-permute-start | bytes 6920 | tf_op jit(solution)/shard_map/ppermute | solution.py:665
  26.3 3.2 %collective-permute-done.7 = f32[2,3,192]{2,1,0:T(4,128)S(1)} collective-permute-done((f32[2,3,192]{2,1,0:T(4,128)S(1)}, f32[2,3,192]{2,1,0:T(4,128)S(1)}, u32[]{:S(2)}, u32[]{:S(2)}) %collective-permute-start.7) | collective-permute-done | bytes 4640 | tf_op jit(solution)/shard_map/ppermute | solution.py:664
  29.5 0.0 collective-permute-start.8
  29.5 0.0 collective-permute-done.6
  29.5 1.2 %collective-permute-done.8 = f32[3,192]{1,0:T(4,128)S(1)} collective-permute-done((f32[3,192]{1,0:T(4,128)S(1)}, f32[3,192]{1,0:T(4,128)S(1)}, u32[]{:S(2)}, u32[]{:S(2)}) %collective-permute-start.8) | collective-permute-done | bytes 2336 | tf_op jit(solution)/shard_map/ppermute | solution.py:667
  30.6 0.6 %fusion.1 = f32[3,192]{1,0:T(4,128)} fusion(f32[3,192]{1,0:T(4,128)S(1)} %collective-permute-done.8, f32[2,3,192]{2,1,0:T(4,128)S(1)} %collective-permute-done.7, f32[3,192]{1,0:T(4,128)S(1)} %collective-permute-done.6, f32[2,3,192]{2,1,0:T(4,128)S(1)} %add_add_fusion), kind=kLoop, calls=%fused_computation.8 | loop fusion | flops 1728 | bytes 11520 | tf_op jit(solution)/shard_map/add | solution.py:648
  (4 shorter events, 0.0 us)
Async XLA Ops:
  2.0 12.9 %collective-permute-start = (bf16[5,128,128]{2,1,0:T(8,128)(2,1)S(1)}, bf16[5,128,128]{2,1,0:T(8,128)(2,1)S(1)}, u32[]{:S(2)}, u32[]{:S(2)}) collective-permute-start(bf16[5,128,128]{2,1,0:T(8,128)(2,1)S(1)} %get-tuple-element.24), channel_id=1, source_target_pairs={{0,4},{1,5},{2,6},{3,7},{4,0},{5,1},{6,2},{7,3},{8,12},{9,13},{10,... | collective-permute-start | bytes 491528 | tf_op jit(solution)/shard_map/ppermute | solution.py:114
  5.1 10.0 %collective-permute-start.1 = (bf16[5,128,128]{2,1,0:T(8,128)(2,1)S(1)}, bf16[5,128,128]{2,1,0:T(8,128)(2,1)S(1)}, u32[]{:S(2)}, u32[]{:S(2)}) collective-permute-start(bf16[5,128,128]{2,1,0:T(8,128)(2,1)S(1)} %get-tuple-element.25), channel_id=1, source_target_pairs={{0,12},{1,9},{2,14},{3,11},{4,8},{5,13},{6,10},{7,15},{8,4},{9,1},... | collective-permute-start | bytes 491528 | tf_op jit(solution)/shard_map/ppermute | solution.py:114
  12.3 2.9 %copy-start = (s32[4,4]{1,0:T(4,128)S(1)}, s32[4,4]{1,0:T(4,128)}, u32[]{:S(2)}) copy-start(s32[4,4]{1,0:T(4,128)} %region.3) | copy-start | bytes 196
  12.3 2.9 %copy-start.2 = (s32[7680]{0:T(1024)S(1)}, s32[7680]{0:T(1024)}, u32[]{:S(2)}) copy-start(s32[7680]{0:T(1024)} %param.18) | copy-start | bytes 92164
  12.3 2.9 %copy-start.3 = (f32[3,16,128]{2,1,0:T(8,128)S(1)}, f32[3,16,128]{2,1,0:T(8,128)}, u32[]{:S(2)}) copy-start(f32[3,16,128]{2,1,0:T(8,128)} %weight_grad.1) | copy-start | bytes 73732
  12.3 2.9 %copy-start.4 = (s32[16]{0:T(128)S(1)}, s32[16]{0:T(128)}, u32[]{:S(2)}) copy-start(s32[16]{0:T(128)} %param.19) | copy-start | bytes 196
  15.1 1.4 %collective-permute-start.2 = (bf16[5,128,128]{2,1,0:T(8,128)(2,1)S(1)}, bf16[5,128,128]{2,1,0:T(8,128)(2,1)S(1)}, u32[]{:S(2)}, u32[]{:S(2)}) collective-permute-start(bf16[5,128,128]{2,1,0:T(8,128)(2,1)S(1)} %collective-permute-done.1.rest_2_), channel_id=1, source_target_pairs={{0,1},{1,0},{2,3},{3,2},{4,5},{5,4},{6,7},{7,6},{8,9},{9,8},{10,11... | collective-permute-start | bytes 491528 | tf_op jit(solution)/shard_map/ppermute | solution.py:641
  16.5 4.5 %copy-start.1 = (s32[16,4]{0,1:T(4,128)S(1)}, s32[16,4]{0,1:T(4,128)}, u32[]{:S(2)}) copy-start(s32[16,4]{0,1:T(4,128)} %param.17) | copy-start | bytes 772
  19.1 4.0 %collective-permute-start.3 = (f32[2,3,192]{2,1,0:T(4,128)S(1)}, f32[2,3,192]{2,1,0:T(4,128)S(1)}, u32[]{:S(2)}, u32[]{:S(2)}) collective-permute-start(f32[2,3,192]{2,1,0:T(4,128)S(1)} %get-tuple-element.48), channel_id=1, source_target_pairs={{0,1},{1,0},{2,3},{3,2},{4,5},{5,4},{6,7},{7,6},{8,9},{9,8},{10,11... | collective-permute-start | bytes 13832 | tf_op jit(solution)/shard_map/ppermute | solution.py:658
  19.4 3.8 %collective-permute-start.4 = (f32[2,3,192]{2,1,0:T(4,128)S(1)}, f32[2,3,192]{2,1,0:T(4,128)S(1)}, u32[]{:S(2)}, u32[]{:S(2)}) collective-permute-start(f32[2,3,192]{2,1,0:T(4,128)S(1)} %get-tuple-element.47), channel_id=1, source_target_pairs={{0,2},{1,3},{2,0},{3,1},{4,6},{5,7},{6,4},{7,5},{8,10},{9,11},{10,... | collective-permute-start | bytes 13832 | tf_op jit(solution)/shard_map/ppermute | solution.py:658
  20.9 3.1 %collective-permute-start.5 = (f32[2,3,192]{2,1,0:T(4,128)S(1)}, f32[2,3,192]{2,1,0:T(4,128)S(1)}, u32[]{:S(2)}, u32[]{:S(2)}) collective-permute-start(f32[2,3,192]{2,1,0:T(4,128)S(1)} %get-tuple-element.46), channel_id=1, source_target_pairs={{0,3},{1,2},{2,1},{3,0},{4,7},{5,6},{6,5},{7,4},{8,11},{9,10},{10,... | collective-permute-start | bytes 13832 | tf_op jit(solution)/shard_map/ppermute | solution.py:658
  24.0 5.5 %collective-permute-start.7 = (f32[2,3,192]{2,1,0:T(4,128)S(1)}, f32[2,3,192]{2,1,0:T(4,128)S(1)}, u32[]{:S(2)}, u32[]{:S(2)}) collective-permute-start(f32[2,3,192]{2,1,0:T(4,128)S(1)} %add_add_fusion), channel_id=1, source_target_pairs={{0,12},{1,9},{2,14},{3,11},{4,8},{5,13},{6,10},{7,15},{8,4},{9,1},... | collective-permute-start | bytes 13832 | tf_op jit(solution)/shard_map/ppermute | solution.py:664
  25.5 4.0 %collective-permute-start.6 = (f32[3,192]{1,0:T(4,128)S(1)}, f32[3,192]{1,0:T(4,128)S(1)}, u32[]{:S(2)}, u32[]{:S(2)}) collective-permute-start(f32[3,192]{1,0:T(4,128)S(1)} %slice_bitcast_fusion.6), channel_id=1, source_target_pairs={{0,4},{4,0},{8,12},{12,8},{1,5},{5,1},{9,13},{13,9},{2,6},{6,2},{1... | collective-permute-start | bytes 6920 | tf_op jit(solution)/shard_map/ppermute | solution.py:665
  29.5 1.2 %collective-permute-start.8 = (f32[3,192]{1,0:T(4,128)S(1)}, f32[3,192]{1,0:T(4,128)S(1)}, u32[]{:S(2)}, u32[]{:S(2)}) collective-permute-start(f32[3,192]{1,0:T(4,128)S(1)} %slice_bitcast_fusion.4), channel_id=1, source_target_pairs={{0,1},{1,0},{2,3},{3,2},{4,5},{5,4},{6,7},{7,6},{8,9},{9,8},{10,11... | collective-permute-start | bytes 6920 | tf_op jit(solution)/shard_map/ppermute | solution.py:667

commit v23 on v22

--- a/solution.py
+++ b/solution.py
@@ -636,7 +636,8 @@
 
 
 def swap_between_cores(near, ready, atom_devices):
-    near, ready = lax.optimization_barrier((near, ready))
+    far, ready = lax.optimization_barrier((near[1:], ready))
+    near = [near[0], *far]
     swap = [(i, i ^ 1) for i in range(atom_devices)]
     return near, [lax.ppermute(piece, "atoms", swap) for piece in near[1:]], ready
 

time: 31.4 us -> 30.8 us (0.981)
  waiting for transfers between devices: 5.73 us -> 5.23 us
    ppermute x1, starting transfers between devices: 1.53 us -> 2.58 us  [sum_parts(): lax.ppermute(both, ('grid', 'atoms'), moves_over_grid(shifts, slabs, atom...]
    ppermute x1, starting transfers between devices: 0.77 us -> 0.01 us  [sum_parts(): near = lax.ppermute(both[0], 'grid', [(i, i ^ 1) for i in range(slabs)])]
    ppermute x1, waiting for transfers between devices: 0.01 us -> 0.68 us  [sum_parts(): near = lax.ppermute(both[0], 'grid', [(i, i ^ 1) for i in range(slabs)])]
    ppermute x1, waiting for transfers between devices: 1.16 us -> 0.49 us  [sum_parts(): swapped = [lax.ppermute(piece[1], 'atoms', swap) for piece in far]]
    ppermute x2, starting transfers between devices: 5.56 us -> 5.12 us  [fetch_rows(): lax.ppermute(piece, ('grid', 'atoms'), moves_over_grid(shifts, slabs, ato...]
  transfers between devices with their start and end apart: 9 -> 9, of which waited for: 5 -> 5; matrix products, arithmetic and copies ran while one was open for 0% -> 0% of each run, Pallas kernels for 33% -> 34%
where the time goes in v23:
time: 30.8 us; the launch traced here: 30.7 us
  Pallas kernels  14.3 us (46%)
  starting transfers between devices  9.7 us (31%)
  waiting for transfers between devices  5.23 us (17%)
  between operations  0.78 us (3%)
  other arithmetic  0.6 us (2%)
    ppermute x2, starting transfers between devices, fetch_rows(): lax.ppermute(piece, ('grid', 'atoms'), moves_over_grid(shifts, slabs, ato...  5.12 us
    pallas_call x1, Pallas kernels, reorder(): pl.pallas_call(reorder_kernel, out_shape=(ordered, ordered, jax.ShapeDtyp...  4.65 us
    ppermute x1, waiting for transfers between devices, sum_parts(): lax.ppermute(both, ('grid', 'atoms'), moves_over_grid(shifts, slabs, atom...  2.92 us
    pallas_call x1, Pallas kernels, build_moments(): pl.pallas_call(moment_kernel, out_shape=jax.ShapeDtypeStruct((PARTS, bloc...  2.62 us
    pallas_call x1, Pallas kernels, combine(): pl.pallas_call(functools.partial(combine_kernel, owner_rows=owner_rows, s...  2.58 us
    ppermute x1, starting transfers between devices, sum_parts(): lax.ppermute(both, ('grid', 'atoms'), moves_over_grid(shifts, slabs, atom...  2.58 us
    pallas_call x1, Pallas kernels, write(): pl.pallas_call(write_kernel, out_shape=jax.ShapeDtypeStruct(shape, BF16),...  2.06 us
    ppermute x3, starting transfers between devices, sum_parts(): lax.ppermute(partial_grad[d], 'atoms', [(i, i ^ d) for i in range(atom_de...  1.93 us
  transfers between devices with their start and end apart: 9, of which 5 were waited for; matrix products, arithmetic and copies ran while one was open for 0% of the time, Pallas kernels for 34%

profile of v23, /device:TPU:0, one launch (start us, length us, event | category | flops | bytes accessed | tf_op | source)
XLA Modules:
  0.0 30.7 jit_solution(3123393705702255453)
XLA Ops:
  0.6 1.4 %shard_map.113 = (bf16[5,128,128]{2,1,0:T(8,128)(2,1)S(1)}, bf16[5,128,128]{2,1,0:T(8,128)(2,1)S(1)}, bf16[5,128,128]{2,1,0:T(8,128)(2,1)S(1)}) custom-call(s32[4,4]{1,0:T(4,128)} %region.3, bf16[15,3,128,128]{3,2,1,0:T(8,128)(2,1)} %density.1), custom_call_target="tpu_custom_call" | custom-call | tf_op jit(solution)/shard_map/pallas_call | solution.py:95
  2.0 5.1 %collective-permute-start = (bf16[5,128,128]{2,1,0:T(8,128)(2,1)S(1)}, bf16[5,128,128]{2,1,0:T(8,128)(2,1)S(1)}, u32[]{:S(2)}, u32[]{:S(2)}) collective-permute-start(bf16[5,128,128]{2,1,0:T(8,128)(2,1)S(1)} %get-tuple-element.23), channel_id=1, source_target_pairs={{0,12},{1,9},{2,14},{3,11},{4,8},{5,13},{6,10},{7,15},{8,4},{9,1},... | collective-permute-start | bytes 491528 | tf_op jit(solution)/shard_map/ppermute | solution.py:114
  7.2 0.0 collective-permute-start.1
  7.2 4.7 %shard_map.114 = (bf16[16,4,128,128]{3,2,1,0:T(8,128)(2,1)S(1)}, bf16[16,4,128,128]{3,2,1,0:T(8,128)(2,1)S(1)}, bf16[4,2048,128]{2,1,0:T(8,128)(2,1)S(1)}, bf16[3,4,2048,128]{3,2,1,0:T(8,128)(2,1)S(1)}) custom-call(s32[4,16]{1,0:T(4,128)} %bitcast.27, bf16[16,512,128]{2,1,0:T(8,128)(2,1)} %bitcast.32, bf16[16,512,128]{2,1,0:T(8,128)(2,1)} %bitcast.33, ...), custom_call_target="tpu_custom_call" | custom-call | bytes 10485760 | tf_op jit(solution)/shard_map/pallas_call | solution.py:422
  11.8 0.0 copy-start
  11.8 0.0 copy-start.2
  11.8 0.0 copy-start.3
  11.9 0.0 copy-start.4
  11.9 2.6 %shard_map.115.moments = f32[3,512,512]{2,1,0:T(8,128)S(1)} custom-call(bf16[4,2048,128]{2,1,0:T(8,128)(2,1)S(1)} %get-tuple-element.26.weighted, bf16[3,4,2048,128]{3,2,1,0:T(8,128)(2,1)S(1)} %get-tuple-element.27.grads), custom_call_target="tpu_custom_call" | custom-call | flops 3221225472 | tf_op jit(solution)/shard_map/pallas_call | solution.py:463
  14.5 0.0 collective-permute-done.rest_2_
  14.5 0.1 collective-permute-start.2
  14.6 0.0 copy-done
  14.6 0.0 copy-done.2
  14.6 0.0 copy-done.3
  14.6 0.0 copy-done.4
  14.6 1.0 %shard_map.116 = (bf16[768,640]{1,0:T(8,128)(2,1)S(1)}, f32[3,128,128]{2,1,0:T(8,128)S(1)}) custom-call(s32[4,4]{1,0:T(4,128)S(1)} %copy-done, s32[60,128]{1,0:T(8,128)S(1)} %bitcast.29, s32[1,16]{1,0:T(1,128)S(1)} %bitcast.30, f32[3,16,128]{2,1,0:T(8,128)S(1)} %copy-done.3), custom_call_target="tpu_custom_call" | custom-call | flops 1000000000 | bytes 196608 | tf_op jit(solution)/shard_map/pallas_call | solution.py:497
  15.6 0.0 collective-permute-done.1.rest_1_
  15.6 0.4 %collective-permute-done.2.rest_3_ = bf16[5,128,128]{2,1,0:T(8,128)(2,1)S(1)} collective-permute-done((bf16[5,128,128]{2,1,0:T(8,128)(2,1)S(1)}, bf16[5,128,128]{2,1,0:T(8,128)(2,1)S(1)}, u32[]{:S(2)}, u32[]{:S(2)}) %collective-permute-start.2) | collective-permute-done | bytes 163872 | tf_op jit(solution)/shard_map/ppermute | solution.py:642
  16.0 0.0 copy-start.1
  16.0 2.6 %shard_map.117 = (bf16[16,4,128,128]{3,2,1,0:T(8,128)(2,1)S(1)}, f32[4,2,3,192]{3,2,1,0:T(4,128)S(1)}) custom-call(s32[4,4]{1,0:T(4,128)S(1)} %copy-done, bf16[16,4,128,128]{3,2,1,0:T(8,128)(2,1)S(1)} %get-tuple-element.28.basis, bf16[16,4,128,128]{3,2,1,0:T(8,128)(2,1)S(1)} %get-tuple-element.29.field, f32[3,512,512]{2,1,0:T(8,128)S(1)} %shard_map.115.moments, ...), custom_call_target="tpu_custom_call" | custom-call | tf_op jit(solution)/shard_map/pallas_call | solution.py:584
  18.6 0.2 collective-permute-start.3
  18.8 1.5 %collective-permute-start.4 = (f32[2,3,192]{2,1,0:T(4,128)S(1)}, f32[2,3,192]{2,1,0:T(4,128)S(1)}, u32[]{:S(2)}, u32[]{:S(2)}) collective-permute-start(f32[2,3,192]{2,1,0:T(4,128)S(1)} %get-tuple-element.45), channel_id=1, source_target_pairs={{0,2},{1,3},{2,0},{3,1},{4,6},{5,7},{6,4},{7,5},{8,10},{9,11},{10,... | collective-permute-start | bytes 13832 | tf_op jit(solution)/shard_map/ppermute | solution.py:659
  20.3 0.2 collective-permute-start.5
  20.5 0.0 copy-done.1
  20.5 2.1 %shard_map.118 = bf16[16,512,128]{2,1,0:T(8,128)(2,1)} custom-call(s32[4,16]{1,0:T(4,128)S(1)} %bitcast.28, bf16[16,4,128,128]{3,2,1,0:T(8,128)(2,1)S(1)} %get-tuple-element.38.product), custom_call_target="tpu_custom_call" | custom-call | bytes 4194304 | tf_op jit(solution)/shard_map/pallas_call | solution.py:623
  22.6 0.0 collective-permute-done.3
  22.6 0.0 collective-permute-done.4
  22.6 0.8 %collective-permute-done.5 = f32[2,3,192]{2,1,0:T(4,128)S(1)} collective-permute-done((f32[2,3,192]{2,1,0:T(4,128)S(1)}, f32[2,3,192]{2,1,0:T(4,128)S(1)}, u32[]{:S(2)}, u32[]{:S(2)}) %collective-permute-start.5) | collective-permute-done | bytes 4640 | tf_op jit(solution)/shard_map/ppermute | solution.py:659
  23.4 2.6 %collective-permute-start.7 = (f32[2,3,192]{2,1,0:T(4,128)S(1)}, f32[2,3,192]{2,1,0:T(4,128)S(1)}, u32[]{:S(2)}, u32[]{:S(2)}) collective-permute-start(f32[2,3,192]{2,1,0:T(4,128)S(1)} %add_add_fusion), channel_id=1, source_target_pairs={{0,12},{1,9},{2,14},{3,11},{4,8},{5,13},{6,10},{7,15},{8,4},{9,1},... | collective-permute-start | bytes 13832 | tf_op jit(solution)/shard_map/ppermute | solution.py:665
  26.0 0.0 collective-permute-start.6
  26.0 2.9 %collective-permute-done.7 = f32[2,3,192]{2,1,0:T(4,128)S(1)} collective-permute-done((f32[2,3,192]{2,1,0:T(4,128)S(1)}, f32[2,3,192]{2,1,0:T(4,128)S(1)}, u32[]{:S(2)}, u32[]{:S(2)}) %collective-permute-start.7) | collective-permute-done | bytes 4640 | tf_op jit(solution)/shard_map/ppermute | solution.py:665
  28.9 0.0 collective-permute-start.8
  28.9 0.7 %collective-permute-done.6 = f32[3,192]{1,0:T(4,128)S(1)} collective-permute-done((f32[3,192]{1,0:T(4,128)S(1)}, f32[3,192]{1,0:T(4,128)S(1)}, u32[]{:S(2)}, u32[]{:S(2)}) %collective-permute-start.6) | collective-permute-done | bytes 2336 | tf_op jit(solution)/shard_map/ppermute | solution.py:666
  29.6 0.5 %collective-permute-done.8 = f32[3,192]{1,0:T(4,128)S(1)} collective-permute-done((f32[3,192]{1,0:T(4,128)S(1)}, f32[3,192]{1,0:T(4,128)S(1)}, u32[]{:S(2)}, u32[]{:S(2)}) %collective-permute-start.8) | collective-permute-done | bytes 2336 | tf_op jit(solution)/shard_map/ppermute | solution.py:668
  30.1 0.6 %fusion.1 = f32[3,192]{1,0:T(4,128)} fusion(f32[3,192]{1,0:T(4,128)S(1)} %collective-permute-done.8, f32[2,3,192]{2,1,0:T(4,128)S(1)} %collective-permute-done.7, f32[3,192]{1,0:T(4,128)S(1)} %collective-permute-done.6, f32[2,3,192]{2,1,0:T(4,128)S(1)} %add_add_fusion), kind=kLoop, calls=%fused_computation.8 | loop fusion | flops 1728 | bytes 11520 | tf_op jit(solution)/shard_map/add | solution.py:649
  (4 shorter events, 0.0 us)
Async XLA Ops:
  2.0 12.5 %collective-permute-start = (bf16[5,128,128]{2,1,0:T(8,128)(2,1)S(1)}, bf16[5,128,128]{2,1,0:T(8,128)(2,1)S(1)}, u32[]{:S(2)}, u32[]{:S(2)}) collective-permute-start(bf16[5,128,128]{2,1,0:T(8,128)(2,1)S(1)} %get-tuple-element.23), channel_id=1, source_target_pairs={{0,12},{1,9},{2,14},{3,11},{4,8},{5,13},{6,10},{7,15},{8,4},{9,1},... | collective-permute-start | bytes 491528 | tf_op jit(solution)/shard_map/ppermute | solution.py:114
  7.2 8.4 %collective-permute-start.1 = (bf16[5,128,128]{2,1,0:T(8,128)(2,1)S(1)}, bf16[5,128,128]{2,1,0:T(8,128)(2,1)S(1)}, u32[]{:S(2)}, u32[]{:S(2)}) collective-permute-start(bf16[5,128,128]{2,1,0:T(8,128)(2,1)S(1)} %get-tuple-element.35), channel_id=1, source_target_pairs={{0,4},{1,5},{2,6},{3,7},{4,0},{5,1},{6,2},{7,3},{8,12},{9,13},{10,... | collective-permute-start | bytes 491528 | tf_op jit(solution)/shard_map/ppermute | solution.py:114
  11.8 2.8 %copy-start = (s32[4,4]{1,0:T(4,128)S(1)}, s32[4,4]{1,0:T(4,128)}, u32[]{:S(2)}) copy-start(s32[4,4]{1,0:T(4,128)} %region.3) | copy-start | bytes 196
  11.8 2.8 %copy-start.2 = (s32[7680]{0:T(1024)S(1)}, s32[7680]{0:T(1024)}, u32[]{:S(2)}) copy-start(s32[7680]{0:T(1024)} %param.18) | copy-start | bytes 92164
  11.8 2.8 %copy-start.3 = (f32[3,16,128]{2,1,0:T(8,128)S(1)}, f32[3,16,128]{2,1,0:T(8,128)}, u32[]{:S(2)}) copy-start(f32[3,16,128]{2,1,0:T(8,128)} %weight_grad.1) | copy-start | bytes 73732
  11.9 2.8 %copy-start.4 = (s32[16]{0:T(128)S(1)}, s32[16]{0:T(128)}, u32[]{:S(2)}) copy-start(s32[16]{0:T(128)} %param.19) | copy-start | bytes 196
  14.5 1.5 %collective-permute-start.2 = (bf16[5,128,128]{2,1,0:T(8,128)(2,1)S(1)}, bf16[5,128,128]{2,1,0:T(8,128)(2,1)S(1)}, u32[]{:S(2)}, u32[]{:S(2)}) collective-permute-start(bf16[5,128,128]{2,1,0:T(8,128)(2,1)S(1)} %collective-permute-done.rest_2_), channel_id=1, source_target_pairs={{0,1},{1,0},{2,3},{3,2},{4,5},{5,4},{6,7},{7,6},{8,9},{9,8},{10,11... | collective-permute-start | bytes 491528 | tf_op jit(solution)/shard_map/ppermute | solution.py:642
  16.0 4.5 %copy-start.1 = (s32[16,4]{0,1:T(4,128)S(1)}, s32[16,4]{0,1:T(4,128)}, u32[]{:S(2)}) copy-start(s32[16,4]{0,1:T(4,128)} %param.17) | copy-start | bytes 772
  18.6 4.0 %collective-permute-start.3 = (f32[2,3,192]{2,1,0:T(4,128)S(1)}, f32[2,3,192]{2,1,0:T(4,128)S(1)}, u32[]{:S(2)}, u32[]{:S(2)}) collective-permute-start(f32[2,3,192]{2,1,0:T(4,128)S(1)} %get-tuple-element.46), channel_id=1, source_target_pairs={{0,1},{1,0},{2,3},{3,2},{4,5},{5,4},{6,7},{7,6},{8,9},{9,8},{10,11... | collective-permute-start | bytes 13832 | tf_op jit(solution)/shard_map/ppermute | solution.py:659
  18.8 3.8 %collective-permute-start.4 = (f32[2,3,192]{2,1,0:T(4,128)S(1)}, f32[2,3,192]{2,1,0:T(4,128)S(1)}, u32[]{:S(2)}, u32[]{:S(2)}) collective-permute-start(f32[2,3,192]{2,1,0:T(4,128)S(1)} %get-tuple-element.45), channel_id=1, source_target_pairs={{0,2},{1,3},{2,0},{3,1},{4,6},{5,7},{6,4},{7,5},{8,10},{9,11},{10,... | collective-permute-start | bytes 13832 | tf_op jit(solution)/shard_map/ppermute | solution.py:659
  20.3 3.1 %collective-permute-start.5 = (f32[2,3,192]{2,1,0:T(4,128)S(1)}, f32[2,3,192]{2,1,0:T(4,128)S(1)}, u32[]{:S(2)}, u32[]{:S(2)}) collective-permute-start(f32[2,3,192]{2,1,0:T(4,128)S(1)} %get-tuple-element.44), channel_id=1, source_target_pairs={{0,3},{1,2},{2,1},{3,0},{4,7},{5,6},{6,5},{7,4},{8,11},{9,10},{10,... | collective-permute-start | bytes 13832 | tf_op jit(solution)/shard_map/ppermute | solution.py:659
  23.4 5.5 %collective-permute-start.7 = (f32[2,3,192]{2,1,0:T(4,128)S(1)}, f32[2,3,192]{2,1,0:T(4,128)S(1)}, u32[]{:S(2)}, u32[]{:S(2)}) collective-permute-start(f32[2,3,192]{2,1,0:T(4,128)S(1)} %add_add_fusion), channel_id=1, source_target_pairs={{0,12},{1,9},{2,14},{3,11},{4,8},{5,13},{6,10},{7,15},{8,4},{9,1},... | collective-permute-start | bytes 13832 | tf_op jit(solution)/shard_map/ppermute | solution.py:665
  26.0 3.6 %collective-permute-start.6 = (f32[3,192]{1,0:T(4,128)S(1)}, f32[3,192]{1,0:T(4,128)S(1)}, u32[]{:S(2)}, u32[]{:S(2)}) collective-permute-start(f32[3,192]{1,0:T(4,128)S(1)} %slice_bitcast_fusion.6), channel_id=1, source_target_pairs={{0,4},{4,0},{8,12},{12,8},{1,5},{5,1},{9,13},{13,9},{2,6},{6,2},{1... | collective-permute-start | bytes 6920 | tf_op jit(solution)/shard_map/ppermute | solution.py:666
  28.9 1.2 %collective-permute-start.8 = (f32[3,192]{1,0:T(4,128)S(1)}, f32[3,192]{1,0:T(4,128)S(1)}, u32[]{:S(2)}, u32[]{:S(2)}) collective-permute-start(f32[3,192]{1,0:T(4,128)S(1)} %slice_bitcast_fusion.4), channel_id=1, source_target_pairs={{0,1},{1,0},{2,3},{3,2},{4,5},{5,4},{6,7},{7,6},{8,9},{9,8},{10,11... | collective-permute-start | bytes 6920 | tf_op jit(solution)/shard_map/ppermute | solution.py:668

commit v24 on v23

--- a/solution.py
+++ b/solution.py
@@ -445,16 +445,23 @@
     )(in_hbm(pattern.T), in_hbm(basis), in_hbm(field), in_hbm(basis_grad), in_hbm(weights))
 
 
+def moment_terms(blocks):
+    return [(p, c) for p in range(0, blocks, 2) for c in range(PARTS)]
+
+
+def moment_term(weighted, grads, moments, p, c):
+    blocks, _, size = grads.shape[1:]
+    first, last = max(p - 1, 0), min(p + 3, blocks)
+    left = jnp.concatenate([weighted[place] for place in range(first, last)], axis=1)
+    right = jnp.concatenate([grads[c, p], grads[c, p + 1]], axis=1)
+    moments[c, first * size : last * size, p * size : (p + 2) * size] = lax.dot_general(
+        left, right, TN, preferred_element_type=F32
+    )
+
+
 def moment_kernel(weighted, grads, moments):
-    blocks, _, size = grads.shape[1:]
-    for p in range(0, blocks, 2):
-        first, last = max(p - 1, 0), min(p + 3, blocks)
-        left = jnp.concatenate([weighted[place] for place in range(first, last)], axis=1)
-        for c in range(PARTS):
-            right = jnp.concatenate([grads[c, p], grads[c, p + 1]], axis=1)
-            moments[c, first * size : last * size, p * size : (p + 2) * size] = lax.dot_general(
-                left, right, TN, preferred_element_type=F32
-            )
+    for p, c in moment_terms(grads.shape[1])[:-1]:
+        moment_term(weighted, grads, moments, p, c)
 
 
 def build_moments(weighted, grads):
@@ -472,7 +479,10 @@
     )(weighted, grads)
 
 
-def atom_kernel(region, fn_atom, batch_atom, weight_grad, hot, grad_columns):
+def atom_kernel(
+    region, fn_atom, batch_atom, weight_grad, before, weighted, grads, hot, grad_columns, moments
+):
+    moment_term(weighted, grads, moments, *moment_terms(grads.shape[1])[-1])
     batches, points = weight_grad.shape[1:]
     size = fn_atom.shape[1]
     blocks = region.shape[1]
@@ -492,19 +502,21 @@
         grad_columns[c] = jnp.concatenate([weight_grad[c], padding], axis=0).T
 
 
-def atom_matrix(region, fn_atom, batch_atom, weight_grad, blocks, size, atom_total):
+def atom_matrix(region, fn_atom, batch_atom, weight_grad, moments, weighted, grads, blocks, size, atom_total):
     vmem = pl.BlockSpec(memory_space=pltpu.VMEM)
     return pl.pallas_call(
         atom_kernel,
         out_shape=(
             jax.ShapeDtypeStruct((atom_total, (blocks + 1) * size), BF16),
             jax.ShapeDtypeStruct((PARTS, weight_grad.shape[2], size), F32),
-        ),
-        in_specs=[pl.BlockSpec(memory_space=pltpu.SMEM)] + [vmem] * 3,
-        out_specs=(vmem, vmem),
+            jax.ShapeDtypeStruct(moments.shape, F32),
+        ),
+        in_specs=[pl.BlockSpec(memory_space=pltpu.SMEM)] + [vmem] * 6,
+        out_specs=(vmem,) * 3,
+        input_output_aliases={4: 2},
         compiler_params=pltpu.CompilerParams(vmem_limit_bytes=VMEM_LIMIT),
         cost_estimate=pl.CostEstimate(flops=1000000000, bytes_accessed=2 * atom_total * size, transcendentals=0),
-    )(region, fn_atom.reshape(-1, size), batch_atom.reshape(1, -1), weight_grad)
+    )(region, fn_atom.reshape(-1, size), batch_atom.reshape(1, -1), weight_grad, moments, weighted, grads)
 
 
 def combine_kernel(
@@ -698,7 +710,9 @@
         )
         ready = (basis_wide, field_wide, build_moments(weighted, grads), batch_atom)
         near, far, (basis_wide, field_wide, moments, batch_atom) = swap_between_cores(near, ready, atom_devices)
-        hot, grad_columns = atom_matrix(region, fn_atom, batch_atom, weight_grad, blocks, size, atom_total)
+        hot, grad_columns, moments = atom_matrix(
+            region, fn_atom, batch_atom, weight_grad, moments, weighted, grads, blocks, size, atom_total
+        )
         ready = (basis_wide, field_wide, moments, hot, grad_columns)
         product, partial_grad = combine(region, ready, [own, *near, *far], shapes)
         gradient, contracted = sum_parts(partial_grad, write(pattern, product), slabs, atom_devices)

time: 30.8 us -> 31.2 us (1.013)
  starting transfers between devices: 9.7 us -> 10.3 us
  waiting for transfers between devices: 5.23 us -> 4.8 us
    pallas_call x1, Pallas kernels: 0.97 us -> 1.58 us  [atom_matrix(): pl.pallas_call(atom_kernel, out_shape=(jax.ShapeDtypeStruct((atom_total,...]
    pallas_call x1, Pallas kernels: 2.62 us -> 2.24 us  [build_moments(): pl.pallas_call(moment_kernel, out_shape=jax.ShapeDtypeStruct((PARTS, bloc...]
    ppermute x1, waiting for transfers between devices: 0.36 us -> 0.01 us  [swap_between_cores(): lax.ppermute(piece, 'atoms', swap)]
    ppermute x1, starting transfers between devices: 0.01 us -> 0.35 us  [sum_parts(): near = lax.ppermute(both[0], 'grid', [(i, i ^ 1) for i in range(slabs)])]
    ppermute x1, waiting for transfers between devices: 2.92 us -> 2.58 us  [sum_parts(): lax.ppermute(both, ('grid', 'atoms'), moves_over_grid(shifts, slabs, atom...]
  transfers between devices with their start and end apart: 9 -> 9, of which waited for: 5 -> 4; matrix products, arithmetic and copies ran while one was open for 0% -> 0% of each run, Pallas kernels for 34% -> 34%
where the time goes in v24:
time: 31.2 us; the launch traced here: 31 us
  Pallas kernels  14.4 us (46%)
  starting transfers between devices  10.3 us (33%)
  waiting for transfers between devices  4.8 us (15%)
  between operations  0.8 us (3%)
  other arithmetic  0.6 us (2%)
    ppermute x2, starting transfers between devices, fetch_rows(): lax.ppermute(piece, ('grid', 'atoms'), moves_over_grid(shifts, slabs, ato...  5.12 us
    pallas_call x1, Pallas kernels, reorder(): pl.pallas_call(reorder_kernel, out_shape=(ordered, ordered, jax.ShapeDtyp...  4.65 us
    ppermute x1, waiting for transfers between devices, sum_parts(): lax.ppermute(both, ('grid', 'atoms'), moves_over_grid(shifts, slabs, atom...  2.58 us
    ppermute x1, starting transfers between devices, sum_parts(): lax.ppermute(both, ('grid', 'atoms'), moves_over_grid(shifts, slabs, atom...  2.58 us
    pallas_call x1, Pallas kernels, combine(): pl.pallas_call(functools.partial(combine_kernel, owner_rows=owner_rows, s...  2.5 us
    pallas_call x1, Pallas kernels, build_moments(): pl.pallas_call(moment_kernel, out_shape=jax.ShapeDtypeStruct((PARTS, bloc...  2.24 us
    ppermute x3, starting transfers between devices, sum_parts(): lax.ppermute(partial_grad[d], 'atoms', [(i, i ^ d) for i in range(atom_de...  2.17 us
    pallas_call x1, Pallas kernels, write(): pl.pallas_call(write_kernel, out_shape=jax.ShapeDtypeStruct(shape, BF16),...  2.06 us
  transfers between devices with their start and end apart: 9, of which 4 were waited for; matrix products, arithmetic and copies ran while one was open for 0% of the time, Pallas kernels for 34%

profile of v24, /device:TPU:0, one launch (start us, length us, event | category | flops | bytes accessed | tf_op | source)
XLA Modules:
  0.0 31.0 jit_solution(8410246212714267110)
XLA Ops:
  0.6 1.4 %shard_map.113 = (bf16[5,128,128]{2,1,0:T(8,128)(2,1)S(1)}, bf16[5,128,128]{2,1,0:T(8,128)(2,1)S(1)}, bf16[5,128,128]{2,1,0:T(8,128)(2,1)S(1)}) custom-call(s32[4,4]{1,0:T(4,128)} %region.3, bf16[15,3,128,128]{3,2,1,0:T(8,128)(2,1)} %density.1), custom_call_target="tpu_custom_call" | custom-call | tf_op jit(solution)/shard_map/pallas_call | solution.py:95
  2.0 5.1 %collective-permute-start = (bf16[5,128,128]{2,1,0:T(8,128)(2,1)S(1)}, bf16[5,128,128]{2,1,0:T(8,128)(2,1)S(1)}, u32[]{:S(2)}, u32[]{:S(2)}) collective-permute-start(bf16[5,128,128]{2,1,0:T(8,128)(2,1)S(1)} %get-tuple-element.24), channel_id=1, source_target_pairs={{0,12},{1,9},{2,14},{3,11},{4,8},{5,13},{6,10},{7,15},{8,4},{9,1},... | collective-permute-start | bytes 491528 | tf_op jit(solution)/shard_map/ppermute | solution.py:114
  7.2 0.0 collective-permute-start.1
  7.2 4.7 %shard_map.114 = (bf16[16,4,128,128]{3,2,1,0:T(8,128)(2,1)S(1)}, bf16[16,4,128,128]{3,2,1,0:T(8,128)(2,1)S(1)}, bf16[4,2048,128]{2,1,0:T(8,128)(2,1)S(1)}, bf16[3,4,2048,128]{3,2,1,0:T(8,128)(2,1)S(1)}) custom-call(s32[4,16]{1,0:T(4,128)} %bitcast.28, bf16[16,512,128]{2,1,0:T(8,128)(2,1)} %bitcast.32, bf16[16,512,128]{2,1,0:T(8,128)(2,1)} %bitcast.33, ...), custom_call_target="tpu_custom_call" | custom-call | bytes 10485760 | tf_op jit(solution)/shard_map/pallas_call | solution.py:422
  11.8 0.0 copy-start
  11.8 0.0 copy-start.1
  11.8 0.0 copy-start.2
  11.9 0.0 copy-start.4
  11.9 2.2 %shard_map.115.before = f32[3,512,512]{2,1,0:T(8,128)S(1)} custom-call(bf16[4,2048,128]{2,1,0:T(8,128)(2,1)S(1)} %get-tuple-element.27.weighted, bf16[3,4,2048,128]{3,2,1,0:T(8,128)(2,1)S(1)} %get-tuple-element.28.grads), custom_call_target="tpu_custom_call" | custom-call | flops 3221225472 | tf_op jit(solution)/shard_map/pallas_call | solution.py:470
  14.1 0.0 collective-permute-done.rest_2_
  14.1 0.1 collective-permute-start.2
  14.2 0.0 copy-done
  14.2 0.0 copy-done.1
  14.2 0.0 copy-done.2
  14.2 0.0 copy-done.4
  14.2 1.6 %shard_map.116 = (bf16[768,640]{1,0:T(8,128)(2,1)S(1)}, f32[3,128,128]{2,1,0:T(8,128)S(1)}, f32[3,512,512]{2,1,0:T(8,128)S(1)}) custom-call(s32[4,4]{1,0:T(4,128)S(1)} %copy-done.2, s32[60,128]{1,0:T(8,128)S(1)} %bitcast.27, s32[1,16]{1,0:T(1,128)S(1)} %bitcast.30, f32[3,16,128]{2,1,0:T(8,128)S(1)} %copy-done.1, ...), custom_call_target="tpu_custom_call", output_to_operand_aliasing={{2}: (4, {})} | custom-call | flops 1000000000 | bytes 196608 | tf_op jit(solution)/shard_map/pallas_call | solution.py:507
  15.8 0.0 collective-permute-done.1.rest_1_
  15.8 0.0 collective-permute-done.2.rest_3_
  15.8 0.0 copy-start.3
  15.9 2.5 %shard_map.117 = (bf16[16,4,128,128]{3,2,1,0:T(8,128)(2,1)S(1)}, f32[4,2,3,192]{3,2,1,0:T(4,128)S(1)}) custom-call(s32[4,4]{1,0:T(4,128)S(1)} %copy-done.2, bf16[16,4,128,128]{3,2,1,0:T(8,128)(2,1)S(1)} %get-tuple-element.29.basis, bf16[16,4,128,128]{3,2,1,0:T(8,128)(2,1)S(1)} %get-tuple-element.30.field, f32[3,512,512]{2,1,0:T(8,128)S(1)} %get-tuple-element.33.moments, ...), custom_call_target="tpu_custom_call" | custom-call | tf_op jit(solution)/shard_map/pallas_call | solution.py:596
  18.4 1.6 %collective-permute-start.5 = (f32[2,3,192]{2,1,0:T(4,128)S(1)}, f32[2,3,192]{2,1,0:T(4,128)S(1)}, u32[]{:S(2)}, u32[]{:S(2)}) collective-permute-start(f32[2,3,192]{2,1,0:T(4,128)S(1)} %get-tuple-element.46), channel_id=1, source_target_pairs={{0,3},{1,2},{2,1},{3,0},{4,7},{5,6},{6,5},{7,4},{8,11},{9,10},{10,... | collective-permute-start | bytes 13832 | tf_op jit(solution)/shard_map/ppermute | solution.py:671
  20.0 0.5 %collective-permute-start.4 = (f32[2,3,192]{2,1,0:T(4,128)S(1)}, f32[2,3,192]{2,1,0:T(4,128)S(1)}, u32[]{:S(2)}, u32[]{:S(2)}) collective-permute-start(f32[2,3,192]{2,1,0:T(4,128)S(1)} %get-tuple-element.47), channel_id=1, source_target_pairs={{0,2},{1,3},{2,0},{3,1},{4,6},{5,7},{6,4},{7,5},{8,10},{9,11},{10,... | collective-permute-start | bytes 13832 | tf_op jit(solution)/shard_map/ppermute | solution.py:671
  20.6 0.0 collective-permute-start.3
  20.6 0.0 copy-done.3
  20.6 2.1 %shard_map.118 = bf16[16,512,128]{2,1,0:T(8,128)(2,1)} custom-call(s32[4,16]{1,0:T(4,128)S(1)} %bitcast.29, bf16[16,4,128,128]{3,2,1,0:T(8,128)(2,1)S(1)} %get-tuple-element.40.product), custom_call_target="tpu_custom_call" | custom-call | bytes 4194304 | tf_op jit(solution)/shard_map/pallas_call | solution.py:635
  22.6 0.0 collective-permute-done.5
  22.6 1.0 %collective-permute-done.4 = f32[2,3,192]{2,1,0:T(4,128)S(1)} collective-permute-done((f32[2,3,192]{2,1,0:T(4,128)S(1)}, f32[2,3,192]{2,1,0:T(4,128)S(1)}, u32[]{:S(2)}, u32[]{:S(2)}) %collective-permute-start.4) | collective-permute-done | bytes 4640 | tf_op jit(solution)/shard_map/ppermute | solution.py:671
  23.7 0.0 collective-permute-done.3
  23.7 2.6 %collective-permute-start.7 = (f32[2,3,192]{2,1,0:T(4,128)S(1)}, f32[2,3,192]{2,1,0:T(4,128)S(1)}, u32[]{:S(2)}, u32[]{:S(2)}) collective-permute-start(f32[2,3,192]{2,1,0:T(4,128)S(1)} %add_add_fusion), channel_id=1, source_target_pairs={{0,12},{1,9},{2,14},{3,11},{4,8},{5,13},{6,10},{7,15},{8,4},{9,1},... | collective-permute-start | bytes 13832 | tf_op jit(solution)/shard_map/ppermute | solution.py:677
  26.3 0.3 %collective-permute-start.6 = (f32[3,192]{1,0:T(4,128)S(1)}, f32[3,192]{1,0:T(4,128)S(1)}, u32[]{:S(2)}, u32[]{:S(2)}) collective-permute-start(f32[3,192]{1,0:T(4,128)S(1)} %slice_bitcast_fusion.6), channel_id=1, source_target_pairs={{0,4},{4,0},{8,12},{12,8},{1,5},{5,1},{9,13},{13,9},{2,6},{6,2},{1... | collective-permute-start | bytes 6920 | tf_op jit(solution)/shard_map/ppermute | solution.py:678
  26.6 2.6 %collective-permute-done.7 = f32[2,3,192]{2,1,0:T(4,128)S(1)} collective-permute-done((f32[2,3,192]{2,1,0:T(4,128)S(1)}, f32[2,3,192]{2,1,0:T(4,128)S(1)}, u32[]{:S(2)}, u32[]{:S(2)}) %collective-permute-start.7) | collective-permute-done | bytes 4640 | tf_op jit(solution)/shard_map/ppermute | solution.py:677
  29.2 0.0 collective-permute-start.8
  29.2 0.7 %collective-permute-done.6 = f32[3,192]{1,0:T(4,128)S(1)} collective-permute-done((f32[3,192]{1,0:T(4,128)S(1)}, f32[3,192]{1,0:T(4,128)S(1)}, u32[]{:S(2)}, u32[]{:S(2)}) %collective-permute-start.6) | collective-permute-done | bytes 2336 | tf_op jit(solution)/shard_map/ppermute | solution.py:678
  29.9 0.5 %collective-permute-done.8 = f32[3,192]{1,0:T(4,128)S(1)} collective-permute-done((f32[3,192]{1,0:T(4,128)S(1)}, f32[3,192]{1,0:T(4,128)S(1)}, u32[]{:S(2)}, u32[]{:S(2)}) %collective-permute-start.8) | collective-permute-done | bytes 2336 | tf_op jit(solution)/shard_map/ppermute | solution.py:680
  30.4 0.6 %fusion.1 = f32[3,192]{1,0:T(4,128)} fusion(f32[3,192]{1,0:T(4,128)S(1)} %collective-permute-done.8, f32[2,3,192]{2,1,0:T(4,128)S(1)} %collective-permute-done.7, f32[3,192]{1,0:T(4,128)S(1)} %collective-permute-done.6, f32[2,3,192]{2,1,0:T(4,128)S(1)} %add_add_fusion), kind=kLoop, calls=%fused_computation.8 | loop fusion | flops 1728 | bytes 11520 | tf_op jit(solution)/shard_map/add | solution.py:661
  (4 shorter events, 0.0 us)
Async XLA Ops:
  2.0 12.1 %collective-permute-start = (bf16[5,128,128]{2,1,0:T(8,128)(2,1)S(1)}, bf16[5,128,128]{2,1,0:T(8,128)(2,1)S(1)}, u32[]{:S(2)}, u32[]{:S(2)}) collective-permute-start(bf16[5,128,128]{2,1,0:T(8,128)(2,1)S(1)} %get-tuple-element.24), channel_id=1, source_target_pairs={{0,12},{1,9},{2,14},{3,11},{4,8},{5,13},{6,10},{7,15},{8,4},{9,1},... | collective-permute-start | bytes 491528 | tf_op jit(solution)/shard_map/ppermute | solution.py:114
  7.2 8.7 %collective-permute-start.1 = (bf16[5,128,128]{2,1,0:T(8,128)(2,1)S(1)}, bf16[5,128,128]{2,1,0:T(8,128)(2,1)S(1)}, u32[]{:S(2)}, u32[]{:S(2)}) collective-permute-start(bf16[5,128,128]{2,1,0:T(8,128)(2,1)S(1)} %get-tuple-element.37), channel_id=1, source_target_pairs={{0,4},{1,5},{2,6},{3,7},{4,0},{5,1},{6,2},{7,3},{8,12},{9,13},{10,... | collective-permute-start | bytes 491528 | tf_op jit(solution)/shard_map/ppermute | solution.py:114
  11.8 2.4 %copy-start = (s32[7680]{0:T(1024)S(1)}, s32[7680]{0:T(1024)}, u32[]{:S(2)}) copy-start(s32[7680]{0:T(1024)} %param.18) | copy-start | bytes 92164
  11.8 2.4 %copy-start.1 = (f32[3,16,128]{2,1,0:T(8,128)S(1)}, f32[3,16,128]{2,1,0:T(8,128)}, u32[]{:S(2)}) copy-start(f32[3,16,128]{2,1,0:T(8,128)} %weight_grad.1) | copy-start | bytes 73732
  11.8 2.4 %copy-start.2 = (s32[4,4]{1,0:T(4,128)S(1)}, s32[4,4]{1,0:T(4,128)}, u32[]{:S(2)}) copy-start(s32[4,4]{1,0:T(4,128)} %region.3) | copy-start | bytes 196
  11.9 2.4 %copy-start.4 = (s32[16]{0:T(128)S(1)}, s32[16]{0:T(128)}, u32[]{:S(2)}) copy-start(s32[16]{0:T(128)} %param.19) | copy-start | bytes 196
  14.1 1.7 %collective-permute-start.2 = (bf16[5,128,128]{2,1,0:T(8,128)(2,1)S(1)}, bf16[5,128,128]{2,1,0:T(8,128)(2,1)S(1)}, u32[]{:S(2)}, u32[]{:S(2)}) collective-permute-start(bf16[5,128,128]{2,1,0:T(8,128)(2,1)S(1)} %collective-permute-done.rest_2_), channel_id=1, source_target_pairs={{0,1},{1,0},{2,3},{3,2},{4,5},{5,4},{6,7},{7,6},{8,9},{9,8},{10,11... | collective-permute-start | bytes 491528 | tf_op jit(solution)/shard_map/ppermute | solution.py:654
  15.8 4.7 %copy-start.3 = (s32[16,4]{0,1:T(4,128)S(1)}, s32[16,4]{0,1:T(4,128)}, u32[]{:S(2)}) copy-start(s32[16,4]{0,1:T(4,128)} %param.17) | copy-start | bytes 772
  18.4 4.2 %collective-permute-start.5 = (f32[2,3,192]{2,1,0:T(4,128)S(1)}, f32[2,3,192]{2,1,0:T(4,128)S(1)}, u32[]{:S(2)}, u32[]{:S(2)}) collective-permute-start(f32[2,3,192]{2,1,0:T(4,128)S(1)} %get-tuple-element.46), channel_id=1, source_target_pairs={{0,3},{1,2},{2,1},{3,0},{4,7},{5,6},{6,5},{7,4},{8,11},{9,10},{10,... | collective-permute-start | bytes 13832 | tf_op jit(solution)/shard_map/ppermute | solution.py:671
  20.0 3.7 %collective-permute-start.4 = (f32[2,3,192]{2,1,0:T(4,128)S(1)}, f32[2,3,192]{2,1,0:T(4,128)S(1)}, u32[]{:S(2)}, u32[]{:S(2)}) collective-permute-start(f32[2,3,192]{2,1,0:T(4,128)S(1)} %get-tuple-element.47), channel_id=1, source_target_pairs={{0,2},{1,3},{2,0},{3,1},{4,6},{5,7},{6,4},{7,5},{8,10},{9,11},{10,... | collective-permute-start | bytes 13832 | tf_op jit(solution)/shard_map/ppermute | solution.py:671
  20.6 3.1 %collective-permute-start.3 = (f32[2,3,192]{2,1,0:T(4,128)S(1)}, f32[2,3,192]{2,1,0:T(4,128)S(1)}, u32[]{:S(2)}, u32[]{:S(2)}) collective-permute-start(f32[2,3,192]{2,1,0:T(4,128)S(1)} %get-tuple-element.48), channel_id=1, source_target_pairs={{0,1},{1,0},{2,3},{3,2},{4,5},{5,4},{6,7},{7,6},{8,9},{9,8},{10,11... | collective-permute-start | bytes 13832 | tf_op jit(solution)/shard_map/ppermute | solution.py:671
  23.7 5.5 %collective-permute-start.7 = (f32[2,3,192]{2,1,0:T(4,128)S(1)}, f32[2,3,192]{2,1,0:T(4,128)S(1)}, u32[]{:S(2)}, u32[]{:S(2)}) collective-permute-start(f32[2,3,192]{2,1,0:T(4,128)S(1)} %add_add_fusion), channel_id=1, source_target_pairs={{0,12},{1,9},{2,14},{3,11},{4,8},{5,13},{6,10},{7,15},{8,4},{9,1},... | collective-permute-start | bytes 13832 | tf_op jit(solution)/shard_map/ppermute | solution.py:677
  26.3 3.6 %collective-permute-start.6 = (f32[3,192]{1,0:T(4,128)S(1)}, f32[3,192]{1,0:T(4,128)S(1)}, u32[]{:S(2)}, u32[]{:S(2)}) collective-permute-start(f32[3,192]{1,0:T(4,128)S(1)} %slice_bitcast_fusion.6), channel_id=1, source_target_pairs={{0,4},{4,0},{8,12},{12,8},{1,5},{5,1},{9,13},{13,9},{2,6},{6,2},{1... | collective-permute-start | bytes 6920 | tf_op jit(solution)/shard_map/ppermute | solution.py:678
  29.2 1.2 %collective-permute-start.8 = (f32[3,192]{1,0:T(4,128)S(1)}, f32[3,192]{1,0:T(4,128)S(1)}, u32[]{:S(2)}, u32[]{:S(2)}) collective-permute-start(f32[3,192]{1,0:T(4,128)S(1)} %slice_bitcast_fusion.4), channel_id=1, source_target_pairs={{0,1},{1,0},{2,3},{3,2},{4,5},{5,4},{6,7},{7,6},{8,9},{9,8},{10,11... | collective-permute-start | bytes 6920 | tf_op jit(solution)/shard_map/ppermute | solution.py:680

commit v25 on v24

--- a/solution.py
+++ b/solution.py
@@ -669,7 +669,8 @@
     parts = [partial_grad[0]]
     for d in range(1, atom_devices):
         parts.append(lax.ppermute(partial_grad[d], "atoms", [(i, i ^ d) for i in range(atom_devices)]))
-    parts, contracted = lax.optimization_barrier((parts, contracted))
+    parts, contracted = lax.optimization_barrier((parts[::-1], contracted))
+    parts = parts[::-1]
     both = tree_sum(pair_sums(parts))
     swap = [(i, i ^ 1) for i in range(atom_devices)]
     far = []

time: 31.2 us -> 31 us (level)
  transfers between devices with their start and end apart: 9 -> 9, of which waited for: 4 -> 5; matrix products, arithmetic and copies ran while one was open for 0% -> 0% of each run, Pallas kernels for 34% -> 34%
where the time goes in v25:
time: 31 us; the launch traced here: 30.9 us
  Pallas kernels  14.4 us (46%)
  starting transfers between devices  10.2 us (33%)
  waiting for transfers between devices  4.81 us (16%)
  between operations  0.8 us (3%)
  other arithmetic  0.6 us (2%)
    ppermute x2, starting transfers between devices, fetch_rows(): lax.ppermute(piece, ('grid', 'atoms'), moves_over_grid(shifts, slabs, ato...  5.12 us
    pallas_call x1, Pallas kernels, reorder(): pl.pallas_call(reorder_kernel, out_shape=(ordered, ordered, jax.ShapeDtyp...  4.65 us
    ppermute x1, waiting for transfers between devices, sum_parts(): lax.ppermute(both, ('grid', 'atoms'), moves_over_grid(shifts, slabs, atom...  2.58 us
    ppermute x1, starting transfers between devices, sum_parts(): lax.ppermute(both, ('grid', 'atoms'), moves_over_grid(shifts, slabs, atom...  2.57 us
    pallas_call x1, Pallas kernels, combine(): pl.pallas_call(functools.partial(combine_kernel, owner_rows=owner_rows, s...  2.5 us
    pallas_call x1, Pallas kernels, build_moments(): pl.pallas_call(moment_kernel, out_shape=jax.ShapeDtypeStruct((PARTS, bloc...  2.24 us
    pallas_call x1, Pallas kernels, write(): pl.pallas_call(write_kernel, out_shape=jax.ShapeDtypeStruct(shape, BF16),...  2.06 us
    ppermute x3, starting transfers between devices, sum_parts(): lax.ppermute(partial_grad[d], 'atoms', [(i, i ^ d) for i in range(atom_de...  2.03 us
  transfers between devices with their start and end apart: 9, of which 5 were waited for; matrix products, arithmetic and copies ran while one was open for 0% of the time, Pallas kernels for 34%

profile of v25, /device:TPU:0, one launch (start us, length us, event | category | flops | bytes accessed | tf_op | source)
XLA Modules:
  0.0 30.9 jit_solution(12262003125070239328)
XLA Ops:
  0.6 1.4 %shard_map.113 = (bf16[5,128,128]{2,1,0:T(8,128)(2,1)S(1)}, bf16[5,128,128]{2,1,0:T(8,128)(2,1)S(1)}, bf16[5,128,128]{2,1,0:T(8,128)(2,1)S(1)}) custom-call(s32[4,4]{1,0:T(4,128)} %region.3, bf16[15,3,128,128]{3,2,1,0:T(8,128)(2,1)} %density.1), custom_call_target="tpu_custom_call" | custom-call | tf_op jit(solution)/shard_map/pallas_call | solution.py:95
  2.0 5.1 %collective-permute-start = (bf16[5,128,128]{2,1,0:T(8,128)(2,1)S(1)}, bf16[5,128,128]{2,1,0:T(8,128)(2,1)S(1)}, u32[]{:S(2)}, u32[]{:S(2)}) collective-permute-start(bf16[5,128,128]{2,1,0:T(8,128)(2,1)S(1)} %get-tuple-element.24), channel_id=1, source_target_pairs={{0,12},{1,9},{2,14},{3,11},{4,8},{5,13},{6,10},{7,15},{8,4},{9,1},... | collective-permute-start | bytes 491528 | tf_op jit(solution)/shard_map/ppermute | solution.py:114
  7.2 0.0 collective-permute-start.1
  7.2 4.7 %shard_map.114 = (bf16[16,4,128,128]{3,2,1,0:T(8,128)(2,1)S(1)}, bf16[16,4,128,128]{3,2,1,0:T(8,128)(2,1)S(1)}, bf16[4,2048,128]{2,1,0:T(8,128)(2,1)S(1)}, bf16[3,4,2048,128]{3,2,1,0:T(8,128)(2,1)S(1)}) custom-call(s32[4,16]{1,0:T(4,128)} %bitcast.28, bf16[16,512,128]{2,1,0:T(8,128)(2,1)} %bitcast.32, bf16[16,512,128]{2,1,0:T(8,128)(2,1)} %bitcast.33, ...), custom_call_target="tpu_custom_call" | custom-call | bytes 10485760 | tf_op jit(solution)/shard_map/pallas_call | solution.py:422
  11.8 0.0 copy-start
  11.8 0.0 copy-start.1
  11.8 0.0 copy-start.2
  11.9 0.0 copy-start.4
  11.9 2.2 %shard_map.115.before = f32[3,512,512]{2,1,0:T(8,128)S(1)} custom-call(bf16[4,2048,128]{2,1,0:T(8,128)(2,1)S(1)} %get-tuple-element.27.weighted, bf16[3,4,2048,128]{3,2,1,0:T(8,128)(2,1)S(1)} %get-tuple-element.28.grads), custom_call_target="tpu_custom_call" | custom-call | flops 3221225472 | tf_op jit(solution)/shard_map/pallas_call | solution.py:470
  14.1 0.0 collective-permute-done.rest_2_
  14.1 0.1 collective-permute-start.2
  14.2 0.0 copy-done
  14.2 0.0 copy-done.1
  14.2 0.0 copy-done.2
  14.2 0.0 copy-done.4
  14.2 1.6 %shard_map.116 = (bf16[768,640]{1,0:T(8,128)(2,1)S(1)}, f32[3,128,128]{2,1,0:T(8,128)S(1)}, f32[3,512,512]{2,1,0:T(8,128)S(1)}) custom-call(s32[4,4]{1,0:T(4,128)S(1)} %copy-done.2, s32[60,128]{1,0:T(8,128)S(1)} %bitcast.27, s32[1,16]{1,0:T(1,128)S(1)} %bitcast.30, f32[3,16,128]{2,1,0:T(8,128)S(1)} %copy-done.1, ...), custom_call_target="tpu_custom_call", output_to_operand_aliasing={{2}: (4, {})} | custom-call | flops 1000000000 | bytes 196608 | tf_op jit(solution)/shard_map/pallas_call | solution.py:507
  15.8 0.0 collective-permute-done.1.rest_1_
  15.8 0.0 collective-permute-done.2.rest_3_
  15.8 0.0 copy-start.3
  15.9 2.5 %shard_map.117 = (bf16[16,4,128,128]{3,2,1,0:T(8,128)(2,1)S(1)}, f32[4,2,3,192]{3,2,1,0:T(4,128)S(1)}) custom-call(s32[4,4]{1,0:T(4,128)S(1)} %copy-done.2, bf16[16,4,128,128]{3,2,1,0:T(8,128)(2,1)S(1)} %get-tuple-element.29.basis, bf16[16,4,128,128]{3,2,1,0:T(8,128)(2,1)S(1)} %get-tuple-element.30.field, f32[3,512,512]{2,1,0:T(8,128)S(1)} %get-tuple-element.33.moments, ...), custom_call_target="tpu_custom_call" | custom-call | tf_op jit(solution)/shard_map/pallas_call | solution.py:596
  18.4 0.5 %collective-permute-start.5 = (f32[2,3,192]{2,1,0:T(4,128)S(1)}, f32[2,3,192]{2,1,0:T(4,128)S(1)}, u32[]{:S(2)}, u32[]{:S(2)}) collective-permute-start(f32[2,3,192]{2,1,0:T(4,128)S(1)} %get-tuple-element.47), channel_id=1, source_target_pairs={{0,1},{1,0},{2,3},{3,2},{4,5},{5,4},{6,7},{7,6},{8,9},{9,8},{10,11... | collective-permute-start | bytes 13832 | tf_op jit(solution)/shard_map/ppermute | solution.py:671
  18.9 1.5 %collective-permute-start.4 = (f32[2,3,192]{2,1,0:T(4,128)S(1)}, f32[2,3,192]{2,1,0:T(4,128)S(1)}, u32[]{:S(2)}, u32[]{:S(2)}) collective-permute-start(f32[2,3,192]{2,1,0:T(4,128)S(1)} %get-tuple-element.48), channel_id=1, source_target_pairs={{0,2},{1,3},{2,0},{3,1},{4,6},{5,7},{6,4},{7,5},{8,10},{9,11},{10,... | collective-permute-start | bytes 13832 | tf_op jit(solution)/shard_map/ppermute | solution.py:671
  20.4 0.0 collective-permute-start.3
  20.4 0.0 copy-done.3
  20.4 2.1 %shard_map.118 = bf16[16,512,128]{2,1,0:T(8,128)(2,1)} custom-call(s32[4,16]{1,0:T(4,128)S(1)} %bitcast.29, bf16[16,4,128,128]{3,2,1,0:T(8,128)(2,1)S(1)} %get-tuple-element.40.product), custom_call_target="tpu_custom_call" | custom-call | bytes 4194304 | tf_op jit(solution)/shard_map/pallas_call | solution.py:635
  22.5 0.0 collective-permute-done.5
  22.5 0.1 collective-permute-done.4
  22.6 1.0 %collective-permute-done.3 = f32[2,3,192]{2,1,0:T(4,128)S(1)} collective-permute-done((f32[2,3,192]{2,1,0:T(4,128)S(1)}, f32[2,3,192]{2,1,0:T(4,128)S(1)}, u32[]{:S(2)}, u32[]{:S(2)}) %collective-permute-start.3) | collective-permute-done | bytes 4640 | tf_op jit(solution)/shard_map/ppermute | solution.py:671
  23.6 2.6 %collective-permute-start.7 = (f32[2,3,192]{2,1,0:T(4,128)S(1)}, f32[2,3,192]{2,1,0:T(4,128)S(1)}, u32[]{:S(2)}, u32[]{:S(2)}) collective-permute-start(f32[2,3,192]{2,1,0:T(4,128)S(1)} %add_add_fusion), channel_id=1, source_target_pairs={{0,12},{1,9},{2,14},{3,11},{4,8},{5,13},{6,10},{7,15},{8,4},{9,1},... | collective-permute-start | bytes 13832 | tf_op jit(solution)/shard_map/ppermute | solution.py:678
  26.2 0.4 %collective-permute-start.6 = (f32[3,192]{1,0:T(4,128)S(1)}, f32[3,192]{1,0:T(4,128)S(1)}, u32[]{:S(2)}, u32[]{:S(2)}) collective-permute-start(f32[3,192]{1,0:T(4,128)S(1)} %slice_bitcast_fusion.6), channel_id=1, source_target_pairs={{0,4},{4,0},{8,12},{12,8},{1,5},{5,1},{9,13},{13,9},{2,6},{6,2},{1... | collective-permute-start | bytes 6920 | tf_op jit(solution)/shard_map/ppermute | solution.py:679
  26.5 2.6 %collective-permute-done.7 = f32[2,3,192]{2,1,0:T(4,128)S(1)} collective-permute-done((f32[2,3,192]{2,1,0:T(4,128)S(1)}, f32[2,3,192]{2,1,0:T(4,128)S(1)}, u32[]{:S(2)}, u32[]{:S(2)}) %collective-permute-start.7) | collective-permute-done | bytes 4640 | tf_op jit(solution)/shard_map/ppermute | solution.py:678
  29.1 0.0 collective-permute-start.8
  29.1 0.7 %collective-permute-done.6 = f32[3,192]{1,0:T(4,128)S(1)} collective-permute-done((f32[3,192]{1,0:T(4,128)S(1)}, f32[3,192]{1,0:T(4,128)S(1)}, u32[]{:S(2)}, u32[]{:S(2)}) %collective-permute-start.6) | collective-permute-done | bytes 2336 | tf_op jit(solution)/shard_map/ppermute | solution.py:679
  29.8 0.5 %collective-permute-done.8 = f32[3,192]{1,0:T(4,128)S(1)} collective-permute-done((f32[3,192]{1,0:T(4,128)S(1)}, f32[3,192]{1,0:T(4,128)S(1)}, u32[]{:S(2)}, u32[]{:S(2)}) %collective-permute-start.8) | collective-permute-done | bytes 2336 | tf_op jit(solution)/shard_map/ppermute | solution.py:681
  30.3 0.6 %fusion.1 = f32[3,192]{1,0:T(4,128)} fusion(f32[3,192]{1,0:T(4,128)S(1)} %collective-permute-done.8, f32[2,3,192]{2,1,0:T(4,128)S(1)} %collective-permute-done.7, f32[3,192]{1,0:T(4,128)S(1)} %collective-permute-done.6, f32[2,3,192]{2,1,0:T(4,128)S(1)} %add_add_fusion), kind=kLoop, calls=%fused_computation.8 | loop fusion | flops 1728 | bytes 11520 | tf_op jit(solution)/shard_map/add | solution.py:661
  (4 shorter events, 0.0 us)
Async XLA Ops:
  2.0 12.1 %collective-permute-start = (bf16[5,128,128]{2,1,0:T(8,128)(2,1)S(1)}, bf16[5,128,128]{2,1,0:T(8,128)(2,1)S(1)}, u32[]{:S(2)}, u32[]{:S(2)}) collective-permute-start(bf16[5,128,128]{2,1,0:T(8,128)(2,1)S(1)} %get-tuple-element.24), channel_id=1, source_target_pairs={{0,12},{1,9},{2,14},{3,11},{4,8},{5,13},{6,10},{7,15},{8,4},{9,1},... | collective-permute-start | bytes 491528 | tf_op jit(solution)/shard_map/ppermute | solution.py:114
  7.2 8.7 %collective-permute-start.1 = (bf16[5,128,128]{2,1,0:T(8,128)(2,1)S(1)}, bf16[5,128,128]{2,1,0:T(8,128)(2,1)S(1)}, u32[]{:S(2)}, u32[]{:S(2)}) collective-permute-start(bf16[5,128,128]{2,1,0:T(8,128)(2,1)S(1)} %get-tuple-element.37), channel_id=1, source_target_pairs={{0,4},{1,5},{2,6},{3,7},{4,0},{5,1},{6,2},{7,3},{8,12},{9,13},{10,... | collective-permute-start | bytes 491528 | tf_op jit(solution)/shard_map/ppermute | solution.py:114
  11.8 2.4 %copy-start = (s32[7680]{0:T(1024)S(1)}, s32[7680]{0:T(1024)}, u32[]{:S(2)}) copy-start(s32[7680]{0:T(1024)} %param.18) | copy-start | bytes 92164
  11.8 2.4 %copy-start.1 = (f32[3,16,128]{2,1,0:T(8,128)S(1)}, f32[3,16,128]{2,1,0:T(8,128)}, u32[]{:S(2)}) copy-start(f32[3,16,128]{2,1,0:T(8,128)} %weight_grad.1) | copy-start | bytes 73732
  11.8 2.4 %copy-start.2 = (s32[4,4]{1,0:T(4,128)S(1)}, s32[4,4]{1,0:T(4,128)}, u32[]{:S(2)}) copy-start(s32[4,4]{1,0:T(4,128)} %region.3) | copy-start | bytes 196
  11.9 2.4 %copy-start.4 = (s32[16]{0:T(128)S(1)}, s32[16]{0:T(128)}, u32[]{:S(2)}) copy-start(s32[16]{0:T(128)} %param.19) | copy-start | bytes 196
  14.1 1.7 %collective-permute-start.2 = (bf16[5,128,128]{2,1,0:T(8,128)(2,1)S(1)}, bf16[5,128,128]{2,1,0:T(8,128)(2,1)S(1)}, u32[]{:S(2)}, u32[]{:S(2)}) collective-permute-start(bf16[5,128,128]{2,1,0:T(8,128)(2,1)S(1)} %collective-permute-done.rest_2_), channel_id=1, source_target_pairs={{0,1},{1,0},{2,3},{3,2},{4,5},{5,4},{6,7},{7,6},{8,9},{9,8},{10,11... | collective-permute-start | bytes 491528 | tf_op jit(solution)/shard_map/ppermute | solution.py:654
  15.8 4.6 %copy-start.3 = (s32[16,4]{0,1:T(4,128)S(1)}, s32[16,4]{0,1:T(4,128)}, u32[]{:S(2)}) copy-start(s32[16,4]{0,1:T(4,128)} %param.17) | copy-start | bytes 772
  18.4 4.1 %collective-permute-start.5 = (f32[2,3,192]{2,1,0:T(4,128)S(1)}, f32[2,3,192]{2,1,0:T(4,128)S(1)}, u32[]{:S(2)}, u32[]{:S(2)}) collective-permute-start(f32[2,3,192]{2,1,0:T(4,128)S(1)} %get-tuple-element.47), channel_id=1, source_target_pairs={{0,1},{1,0},{2,3},{3,2},{4,5},{5,4},{6,7},{7,6},{8,9},{9,8},{10,11... | collective-permute-start | bytes 13832 | tf_op jit(solution)/shard_map/ppermute | solution.py:671
  18.9 3.7 %collective-permute-start.4 = (f32[2,3,192]{2,1,0:T(4,128)S(1)}, f32[2,3,192]{2,1,0:T(4,128)S(1)}, u32[]{:S(2)}, u32[]{:S(2)}) collective-permute-start(f32[2,3,192]{2,1,0:T(4,128)S(1)} %get-tuple-element.48), channel_id=1, source_target_pairs={{0,2},{1,3},{2,0},{3,1},{4,6},{5,7},{6,4},{7,5},{8,10},{9,11},{10,... | collective-permute-start | bytes 13832 | tf_op jit(solution)/shard_map/ppermute | solution.py:671
  20.4 3.1 %collective-permute-start.3 = (f32[2,3,192]{2,1,0:T(4,128)S(1)}, f32[2,3,192]{2,1,0:T(4,128)S(1)}, u32[]{:S(2)}, u32[]{:S(2)}) collective-permute-start(f32[2,3,192]{2,1,0:T(4,128)S(1)} %get-tuple-element.49), channel_id=1, source_target_pairs={{0,3},{1,2},{2,1},{3,0},{4,7},{5,6},{6,5},{7,4},{8,11},{9,10},{10,... | collective-permute-start | bytes 13832 | tf_op jit(solution)/shard_map/ppermute | solution.py:671
  23.6 5.5 %collective-permute-start.7 = (f32[2,3,192]{2,1,0:T(4,128)S(1)}, f32[2,3,192]{2,1,0:T(4,128)S(1)}, u32[]{:S(2)}, u32[]{:S(2)}) collective-permute-start(f32[2,3,192]{2,1,0:T(4,128)S(1)} %add_add_fusion), channel_id=1, source_target_pairs={{0,12},{1,9},{2,14},{3,11},{4,8},{5,13},{6,10},{7,15},{8,4},{9,1},... | collective-permute-start | bytes 13832 | tf_op jit(solution)/shard_map/ppermute | solution.py:678
  26.2 3.6 %collective-permute-start.6 = (f32[3,192]{1,0:T(4,128)S(1)}, f32[3,192]{1,0:T(4,128)S(1)}, u32[]{:S(2)}, u32[]{:S(2)}) collective-permute-start(f32[3,192]{1,0:T(4,128)S(1)} %slice_bitcast_fusion.6), channel_id=1, source_target_pairs={{0,4},{4,0},{8,12},{12,8},{1,5},{5,1},{9,13},{13,9},{2,6},{6,2},{1... | collective-permute-start | bytes 6920 | tf_op jit(solution)/shard_map/ppermute | solution.py:679
  29.1 1.2 %collective-permute-start.8 = (f32[3,192]{1,0:T(4,128)S(1)}, f32[3,192]{1,0:T(4,128)S(1)}, u32[]{:S(2)}, u32[]{:S(2)}) collective-permute-start(f32[3,192]{1,0:T(4,128)S(1)} %slice_bitcast_fusion.4), channel_id=1, source_target_pairs={{0,1},{1,0},{2,3},{3,2},{4,5},{5,4},{6,7},{7,6},{8,9},{9,8},{10,11... | collective-permute-start | bytes 6920 | tf_op jit(solution)/shard_map/ppermute | solution.py:681

commit v26 on v23

--- a/solution.py
+++ b/solution.py
@@ -397,7 +397,7 @@
     for batch in range(batches):
         columns[batch] = jnp.broadcast_to(rows[:, batch : batch + 1], (points, size))
 
-    @pl.loop(0, batches)
+    @pl.loop(0, batches, unroll=2)
     def _(batch):
         pltpu.make_async_copy(landed.at[batch], landed.at[batch], sems.at[batch]).wait()
         points_here = pl.ds(pl.multiple_of(batch * points, points), points)

time: 30.8 us -> 30.8 us (level)
  no operation moved by 1% of the time
where the time goes in v26:
time: 30.8 us; the launch traced here: 30.7 us
  Pallas kernels  14.3 us (46%)
  starting transfers between devices  9.7 us (31%)
  waiting for transfers between devices  5.24 us (17%)
  between operations  0.78 us (3%)
  other arithmetic  0.6 us (2%)
    ppermute x2, starting transfers between devices, fetch_rows(): lax.ppermute(piece, ('grid', 'atoms'), moves_over_grid(shifts, slabs, ato...  5.12 us
    pallas_call x1, Pallas kernels, reorder(): pl.pallas_call(reorder_kernel, out_shape=(ordered, ordered, jax.ShapeDtyp...  4.64 us
    ppermute x1, waiting for transfers between devices, sum_parts(): lax.ppermute(both, ('grid', 'atoms'), moves_over_grid(shifts, slabs, atom...  2.92 us
    pallas_call x1, Pallas kernels, build_moments(): pl.pallas_call(moment_kernel, out_shape=jax.ShapeDtypeStruct((PARTS, bloc...  2.62 us
    ppermute x1, starting transfers between devices, sum_parts(): lax.ppermute(both, ('grid', 'atoms'), moves_over_grid(shifts, slabs, atom...  2.58 us
    pallas_call x1, Pallas kernels, combine(): pl.pallas_call(functools.partial(combine_kernel, owner_rows=owner_rows, s...  2.58 us
    pallas_call x1, Pallas kernels, write(): pl.pallas_call(write_kernel, out_shape=jax.ShapeDtypeStruct(shape, BF16),...  2.06 us
    ppermute x3, starting transfers between devices, sum_parts(): lax.ppermute(partial_grad[d], 'atoms', [(i, i ^ d) for i in range(atom_de...  1.93 us
  transfers between devices with their start and end apart: 9, of which 5 were waited for; matrix products, arithmetic and copies ran while one was open for 0% of the time, Pallas kernels for 34%

profile of v26, /device:TPU:0, one launch (start us, length us, event | category | flops | bytes accessed | tf_op | source)
XLA Modules:
  0.0 30.7 jit_solution(11716187970202464395)
XLA Ops:
  0.6 1.4 %shard_map.113 = (bf16[5,128,128]{2,1,0:T(8,128)(2,1)S(1)}, bf16[5,128,128]{2,1,0:T(8,128)(2,1)S(1)}, bf16[5,128,128]{2,1,0:T(8,128)(2,1)S(1)}) custom-call(s32[4,4]{1,0:T(4,128)} %region.3, bf16[15,3,128,128]{3,2,1,0:T(8,128)(2,1)} %density.1), custom_call_target="tpu_custom_call" | custom-call | tf_op jit(solution)/shard_map/pallas_call | solution.py:95
  2.0 5.1 %collective-permute-start = (bf16[5,128,128]{2,1,0:T(8,128)(2,1)S(1)}, bf16[5,128,128]{2,1,0:T(8,128)(2,1)S(1)}, u32[]{:S(2)}, u32[]{:S(2)}) collective-permute-start(bf16[5,128,128]{2,1,0:T(8,128)(2,1)S(1)} %get-tuple-element.23), channel_id=1, source_target_pairs={{0,12},{1,9},{2,14},{3,11},{4,8},{5,13},{6,10},{7,15},{8,4},{9,1},... | collective-permute-start | bytes 491528 | tf_op jit(solution)/shard_map/ppermute | solution.py:114
  7.2 0.0 collective-permute-start.1
  7.2 4.6 %shard_map.114 = (bf16[16,4,128,128]{3,2,1,0:T(8,128)(2,1)S(1)}, bf16[16,4,128,128]{3,2,1,0:T(8,128)(2,1)S(1)}, bf16[4,2048,128]{2,1,0:T(8,128)(2,1)S(1)}, bf16[3,4,2048,128]{3,2,1,0:T(8,128)(2,1)S(1)}) custom-call(s32[4,16]{1,0:T(4,128)} %bitcast.27, bf16[16,512,128]{2,1,0:T(8,128)(2,1)} %bitcast.32, bf16[16,512,128]{2,1,0:T(8,128)(2,1)} %bitcast.33, ...), custom_call_target="tpu_custom_call" | custom-call | bytes 10485760 | tf_op jit(solution)/shard_map/pallas_call | solution.py:422
  11.8 0.0 copy-start
  11.8 0.0 copy-start.2
  11.8 0.0 copy-start.3
  11.8 0.0 copy-start.4
  11.9 2.6 %shard_map.115.moments = f32[3,512,512]{2,1,0:T(8,128)S(1)} custom-call(bf16[4,2048,128]{2,1,0:T(8,128)(2,1)S(1)} %get-tuple-element.26.weighted, bf16[3,4,2048,128]{3,2,1,0:T(8,128)(2,1)S(1)} %get-tuple-element.27.grads), custom_call_target="tpu_custom_call" | custom-call | flops 3221225472 | tf_op jit(solution)/shard_map/pallas_call | solution.py:463
  14.5 0.0 collective-permute-done.rest_2_
  14.5 0.1 collective-permute-start.2
  14.6 0.0 copy-done
  14.6 0.0 copy-done.2
  14.6 0.0 copy-done.3
  14.6 0.0 copy-done.4
  14.6 1.0 %shard_map.116 = (bf16[768,640]{1,0:T(8,128)(2,1)S(1)}, f32[3,128,128]{2,1,0:T(8,128)S(1)}) custom-call(s32[4,4]{1,0:T(4,128)S(1)} %copy-done, s32[60,128]{1,0:T(8,128)S(1)} %bitcast.29, s32[1,16]{1,0:T(1,128)S(1)} %bitcast.30, f32[3,16,128]{2,1,0:T(8,128)S(1)} %copy-done.3), custom_call_target="tpu_custom_call" | custom-call | flops 1000000000 | bytes 196608 | tf_op jit(solution)/shard_map/pallas_call | solution.py:497
  15.6 0.0 collective-permute-done.1.rest_1_
  15.6 0.4 %collective-permute-done.2.rest_3_ = bf16[5,128,128]{2,1,0:T(8,128)(2,1)S(1)} collective-permute-done((bf16[5,128,128]{2,1,0:T(8,128)(2,1)S(1)}, bf16[5,128,128]{2,1,0:T(8,128)(2,1)S(1)}, u32[]{:S(2)}, u32[]{:S(2)}) %collective-permute-start.2) | collective-permute-done | bytes 163872 | tf_op jit(solution)/shard_map/ppermute | solution.py:642
  16.0 0.0 copy-start.1
  16.0 2.6 %shard_map.117 = (bf16[16,4,128,128]{3,2,1,0:T(8,128)(2,1)S(1)}, f32[4,2,3,192]{3,2,1,0:T(4,128)S(1)}) custom-call(s32[4,4]{1,0:T(4,128)S(1)} %copy-done, bf16[16,4,128,128]{3,2,1,0:T(8,128)(2,1)S(1)} %get-tuple-element.28.basis, bf16[16,4,128,128]{3,2,1,0:T(8,128)(2,1)S(1)} %get-tuple-element.29.field, f32[3,512,512]{2,1,0:T(8,128)S(1)} %shard_map.115.moments, ...), custom_call_target="tpu_custom_call" | custom-call | tf_op jit(solution)/shard_map/pallas_call | solution.py:584
  18.6 0.2 collective-permute-start.3
  18.8 1.5 %collective-permute-start.4 = (f32[2,3,192]{2,1,0:T(4,128)S(1)}, f32[2,3,192]{2,1,0:T(4,128)S(1)}, u32[]{:S(2)}, u32[]{:S(2)}) collective-permute-start(f32[2,3,192]{2,1,0:T(4,128)S(1)} %get-tuple-element.45), channel_id=1, source_target_pairs={{0,2},{1,3},{2,0},{3,1},{4,6},{5,7},{6,4},{7,5},{8,10},{9,11},{10,... | collective-permute-start | bytes 13832 | tf_op jit(solution)/shard_map/ppermute | solution.py:659
  20.3 0.2 collective-permute-start.5
  20.5 0.0 copy-done.1
  20.5 2.1 %shard_map.118 = bf16[16,512,128]{2,1,0:T(8,128)(2,1)} custom-call(s32[4,16]{1,0:T(4,128)S(1)} %bitcast.28, bf16[16,4,128,128]{3,2,1,0:T(8,128)(2,1)S(1)} %get-tuple-element.38.product), custom_call_target="tpu_custom_call" | custom-call | bytes 4194304 | tf_op jit(solution)/shard_map/pallas_call | solution.py:623
  22.6 0.0 collective-permute-done.3
  22.6 0.0 collective-permute-done.4
  22.6 0.8 %collective-permute-done.5 = f32[2,3,192]{2,1,0:T(4,128)S(1)} collective-permute-done((f32[2,3,192]{2,1,0:T(4,128)S(1)}, f32[2,3,192]{2,1,0:T(4,128)S(1)}, u32[]{:S(2)}, u32[]{:S(2)}) %collective-permute-start.5) | collective-permute-done | bytes 4640 | tf_op jit(solution)/shard_map/ppermute | solution.py:659
  23.4 2.6 %collective-permute-start.7 = (f32[2,3,192]{2,1,0:T(4,128)S(1)}, f32[2,3,192]{2,1,0:T(4,128)S(1)}, u32[]{:S(2)}, u32[]{:S(2)}) collective-permute-start(f32[2,3,192]{2,1,0:T(4,128)S(1)} %add_add_fusion), channel_id=1, source_target_pairs={{0,12},{1,9},{2,14},{3,11},{4,8},{5,13},{6,10},{7,15},{8,4},{9,1},... | collective-permute-start | bytes 13832 | tf_op jit(solution)/shard_map/ppermute | solution.py:665
  26.0 0.0 collective-permute-start.6
  26.0 2.9 %collective-permute-done.7 = f32[2,3,192]{2,1,0:T(4,128)S(1)} collective-permute-done((f32[2,3,192]{2,1,0:T(4,128)S(1)}, f32[2,3,192]{2,1,0:T(4,128)S(1)}, u32[]{:S(2)}, u32[]{:S(2)}) %collective-permute-start.7) | collective-permute-done | bytes 4640 | tf_op jit(solution)/shard_map/ppermute | solution.py:665
  28.9 0.0 collective-permute-start.8
  28.9 0.7 %collective-permute-done.6 = f32[3,192]{1,0:T(4,128)S(1)} collective-permute-done((f32[3,192]{1,0:T(4,128)S(1)}, f32[3,192]{1,0:T(4,128)S(1)}, u32[]{:S(2)}, u32[]{:S(2)}) %collective-permute-start.6) | collective-permute-done | bytes 2336 | tf_op jit(solution)/shard_map/ppermute | solution.py:666
  29.6 0.5 %collective-permute-done.8 = f32[3,192]{1,0:T(4,128)S(1)} collective-permute-done((f32[3,192]{1,0:T(4,128)S(1)}, f32[3,192]{1,0:T(4,128)S(1)}, u32[]{:S(2)}, u32[]{:S(2)}) %collective-permute-start.8) | collective-permute-done | bytes 2336 | tf_op jit(solution)/shard_map/ppermute | solution.py:668
  30.1 0.6 %fusion.1 = f32[3,192]{1,0:T(4,128)} fusion(f32[3,192]{1,0:T(4,128)S(1)} %collective-permute-done.8, f32[2,3,192]{2,1,0:T(4,128)S(1)} %collective-permute-done.7, f32[3,192]{1,0:T(4,128)S(1)} %collective-permute-done.6, f32[2,3,192]{2,1,0:T(4,128)S(1)} %add_add_fusion), kind=kLoop, calls=%fused_computation.8 | loop fusion | flops 1728 | bytes 11520 | tf_op jit(solution)/shard_map/add | solution.py:649
  (4 shorter events, 0.0 us)
Async XLA Ops:
  2.0 12.5 %collective-permute-start = (bf16[5,128,128]{2,1,0:T(8,128)(2,1)S(1)}, bf16[5,128,128]{2,1,0:T(8,128)(2,1)S(1)}, u32[]{:S(2)}, u32[]{:S(2)}) collective-permute-start(bf16[5,128,128]{2,1,0:T(8,128)(2,1)S(1)} %get-tuple-element.23), channel_id=1, source_target_pairs={{0,12},{1,9},{2,14},{3,11},{4,8},{5,13},{6,10},{7,15},{8,4},{9,1},... | collective-permute-start | bytes 491528 | tf_op jit(solution)/shard_map/ppermute | solution.py:114
  7.2 8.4 %collective-permute-start.1 = (bf16[5,128,128]{2,1,0:T(8,128)(2,1)S(1)}, bf16[5,128,128]{2,1,0:T(8,128)(2,1)S(1)}, u32[]{:S(2)}, u32[]{:S(2)}) collective-permute-start(bf16[5,128,128]{2,1,0:T(8,128)(2,1)S(1)} %get-tuple-element.35), channel_id=1, source_target_pairs={{0,4},{1,5},{2,6},{3,7},{4,0},{5,1},{6,2},{7,3},{8,12},{9,13},{10,... | collective-permute-start | bytes 491528 | tf_op jit(solution)/shard_map/ppermute | solution.py:114
  11.8 2.8 %copy-start = (s32[4,4]{1,0:T(4,128)S(1)}, s32[4,4]{1,0:T(4,128)}, u32[]{:S(2)}) copy-start(s32[4,4]{1,0:T(4,128)} %region.3) | copy-start | bytes 196
  11.8 2.8 %copy-start.2 = (s32[7680]{0:T(1024)S(1)}, s32[7680]{0:T(1024)}, u32[]{:S(2)}) copy-start(s32[7680]{0:T(1024)} %param.18) | copy-start | bytes 92164
  11.8 2.8 %copy-start.3 = (f32[3,16,128]{2,1,0:T(8,128)S(1)}, f32[3,16,128]{2,1,0:T(8,128)}, u32[]{:S(2)}) copy-start(f32[3,16,128]{2,1,0:T(8,128)} %weight_grad.1) | copy-start | bytes 73732
  11.8 2.8 %copy-start.4 = (s32[16]{0:T(128)S(1)}, s32[16]{0:T(128)}, u32[]{:S(2)}) copy-start(s32[16]{0:T(128)} %param.19) | copy-start | bytes 196
  14.5 1.5 %collective-permute-start.2 = (bf16[5,128,128]{2,1,0:T(8,128)(2,1)S(1)}, bf16[5,128,128]{2,1,0:T(8,128)(2,1)S(1)}, u32[]{:S(2)}, u32[]{:S(2)}) collective-permute-start(bf16[5,128,128]{2,1,0:T(8,128)(2,1)S(1)} %collective-permute-done.rest_2_), channel_id=1, source_target_pairs={{0,1},{1,0},{2,3},{3,2},{4,5},{5,4},{6,7},{7,6},{8,9},{9,8},{10,11... | collective-permute-start | bytes 491528 | tf_op jit(solution)/shard_map/ppermute | solution.py:642
  16.0 4.5 %copy-start.1 = (s32[16,4]{0,1:T(4,128)S(1)}, s32[16,4]{0,1:T(4,128)}, u32[]{:S(2)}) copy-start(s32[16,4]{0,1:T(4,128)} %param.17) | copy-start | bytes 772
  18.6 4.0 %collective-permute-start.3 = (f32[2,3,192]{2,1,0:T(4,128)S(1)}, f32[2,3,192]{2,1,0:T(4,128)S(1)}, u32[]{:S(2)}, u32[]{:S(2)}) collective-permute-start(f32[2,3,192]{2,1,0:T(4,128)S(1)} %get-tuple-element.46), channel_id=1, source_target_pairs={{0,1},{1,0},{2,3},{3,2},{4,5},{5,4},{6,7},{7,6},{8,9},{9,8},{10,11... | collective-permute-start | bytes 13832 | tf_op jit(solution)/shard_map/ppermute | solution.py:659
  18.8 3.8 %collective-permute-start.4 = (f32[2,3,192]{2,1,0:T(4,128)S(1)}, f32[2,3,192]{2,1,0:T(4,128)S(1)}, u32[]{:S(2)}, u32[]{:S(2)}) collective-permute-start(f32[2,3,192]{2,1,0:T(4,128)S(1)} %get-tuple-element.45), channel_id=1, source_target_pairs={{0,2},{1,3},{2,0},{3,1},{4,6},{5,7},{6,4},{7,5},{8,10},{9,11},{10,... | collective-permute-start | bytes 13832 | tf_op jit(solution)/shard_map/ppermute | solution.py:659
  20.3 3.1 %collective-permute-start.5 = (f32[2,3,192]{2,1,0:T(4,128)S(1)}, f32[2,3,192]{2,1,0:T(4,128)S(1)}, u32[]{:S(2)}, u32[]{:S(2)}) collective-permute-start(f32[2,3,192]{2,1,0:T(4,128)S(1)} %get-tuple-element.44), channel_id=1, source_target_pairs={{0,3},{1,2},{2,1},{3,0},{4,7},{5,6},{6,5},{7,4},{8,11},{9,10},{10,... | collective-permute-start | bytes 13832 | tf_op jit(solution)/shard_map/ppermute | solution.py:659
  23.4 5.5 %collective-permute-start.7 = (f32[2,3,192]{2,1,0:T(4,128)S(1)}, f32[2,3,192]{2,1,0:T(4,128)S(1)}, u32[]{:S(2)}, u32[]{:S(2)}) collective-permute-start(f32[2,3,192]{2,1,0:T(4,128)S(1)} %add_add_fusion), channel_id=1, source_target_pairs={{0,12},{1,9},{2,14},{3,11},{4,8},{5,13},{6,10},{7,15},{8,4},{9,1},... | collective-permute-start | bytes 13832 | tf_op jit(solution)/shard_map/ppermute | solution.py:665
  26.0 3.6 %collective-permute-start.6 = (f32[3,192]{1,0:T(4,128)S(1)}, f32[3,192]{1,0:T(4,128)S(1)}, u32[]{:S(2)}, u32[]{:S(2)}) collective-permute-start(f32[3,192]{1,0:T(4,128)S(1)} %slice_bitcast_fusion.6), channel_id=1, source_target_pairs={{0,4},{4,0},{8,12},{12,8},{1,5},{5,1},{9,13},{13,9},{2,6},{6,2},{1... | collective-permute-start | bytes 6920 | tf_op jit(solution)/shard_map/ppermute | solution.py:666
  28.9 1.2 %collective-permute-start.8 = (f32[3,192]{1,0:T(4,128)S(1)}, f32[3,192]{1,0:T(4,128)S(1)}, u32[]{:S(2)}, u32[]{:S(2)}) collective-permute-start(f32[3,192]{1,0:T(4,128)S(1)} %slice_bitcast_fusion.4), channel_id=1, source_target_pairs={{0,1},{1,0},{2,3},{3,2},{4,5},{5,4},{6,7},{7,6},{8,9},{9,8},{10,11... | collective-permute-start | bytes 6920 | tf_op jit(solution)/shard_map/ppermute | solution.py:668
